TPU v7x, 256 devices: a whole 4x4x8 slice. The times are simulated.
256 devices in a mesh: dp: 16 (over y_lo, z), shard: 16 (over x, y_hi, core).
Axes of the slice: x: 4, y: 4 (y_hi: 2, y_lo: 2; y = y_hi * 2 + y_lo), z: 8, core: 2. Of those that a mesh axis runs over, the one named last changes fastest.
Arguments:
- train_ids: int32 [4096], P('dp'), may hold values from 0 to 31999, as said below
- query_ids: int32 [2048], P('dp'), may hold values from 0 to 31999, as said below
- embed: bfloat16 [32000, 2048], P('shard'), as said below
- norm_gain: float32 [2048], replicated, may hold values from 0.1 to 1.9
- w_gate: bfloat16 [2048, 5504], P(None, 'shard'), may hold values from -0.125 to 0.125
- w_up: bfloat16 [2048, 5504], P(None, 'shard'), may hold values from -0.125 to 0.125
- cotangent: bfloat16 [2048, 2048], P('dp'), as said below
Outputs:
- solution: float32 [5504, 2048], P('shard', 'dp')
Inputs may be any that keep to these rules, and one draw needn't show every extreme that they name: `train_ids`: token ids of the vocabulary. `query_ids`: token ids of the vocabulary. `embed`: real values, drawn afresh for every entry. `cotangent`: real values, drawn afresh for every entry.
All inputs are finite; a program needn't handle non-finite values.
Results may differ from a plain program's by a relative error of at most 0.0061.
Values may be sent and summed in bfloat16 or wider, within the bound.
No kernel may reach another device: no remote copies, remote signals or barrier semaphores. Data moves between devices by JAX's collectives and lax.ppermute only.
A program may use at most 64 MiB of HBM per device.

v0:
```python
import math

import jax
import jax.numpy as jnp
from jax import lax
from jax.sharding import PartitionSpec as P

ITERS = 3


norm_eps = 1e-05
damping = 0.1


def hidden_acts(rows, norm_gain, w_gate, w_up):
    inv_scale = lax.rsqrt(jnp.mean(rows * rows, axis=-1, keepdims=True) + norm_eps)
    normed = (rows * inv_scale * norm_gain).astype(jnp.bfloat16)
    gate_out = jnp.dot(normed, w_gate, preferred_element_type=jnp.float32)
    upward = jnp.dot(normed, w_up, preferred_element_type=jnp.float32)
    return (jax.nn.silu(gate_out) * upward).astype(jnp.bfloat16)


def table_rows(token_ids, table):
    height = table.shape[0]
    offset_ids = token_ids - lax.axis_index("shard") * height
    inside = (offset_ids >= 0) & (offset_ids < height)
    picked = jnp.take(table, jnp.clip(offset_ids, 0, height - 1), axis=0).astype(jnp.float32)
    return jnp.where(inside[:, None], picked, jnp.zeros_like(picked))


def units_transposed(hidden_vals, right):
    return lax.dot_general(
        hidden_vals, right, (((0,), (0,)), ((), ())), preferred_element_type=jnp.float32
    )


def column_share(partial_terms):
    return lax.psum_scatter(partial_terms, "dp", scatter_dimension=1, tiled=True)


def global_total(value):
    return lax.psum(value, ("dp", "shard"))


def tangent_total(partial_terms):
    return lax.psum(partial_terms, "shard").astype(jnp.bfloat16)


def body(train_ids, query_ids, embed, norm_gain, w_gate, w_up, cotangent):
    rows_part = table_rows(train_ids, embed)
    query_part = table_rows(query_ids, embed)
    rows_sum, query_sum = (
        lax.psum(rows_part.astype(jnp.bfloat16), "shard").astype(jnp.float32),
        lax.psum(query_part.astype(jnp.bfloat16), "shard").astype(jnp.float32),
    )
    hidden_vals = hidden_acts(rows_sum, norm_gain, w_gate, w_up)
    query_vals = hidden_acts(query_sum, norm_gain, w_gate, w_up)
    query_total = query_ids.shape[0] * lax.axis_size("dp")
    tokens_total = train_ids.shape[0] * lax.axis_size("dp")
    target_vec = column_share(units_transposed(query_vals, cotangent)) / math.sqrt(query_total)
    solution = jnp.zeros_like(target_vec)
    residual = target_vec
    direction = target_vec
    norm_now = global_total(jnp.sum(residual * residual))
    for turn_index in range(ITERS):
        projected = jnp.dot(
            hidden_vals,
            lax.all_gather(direction.astype(jnp.bfloat16), "dp", axis=1, tiled=True),
            preferred_element_type=jnp.float32,
        )
        tangent = tangent_total(projected)
        curved = (
            column_share(units_transposed(hidden_vals, tangent)) / tokens_total
            + damping * direction
        )
        step_size = norm_now / global_total(jnp.sum(direction * curved))
        solution = solution + step_size * direction
        residual = residual - step_size * curved
        norm_next = global_total(jnp.sum(residual * residual))
        direction = residual + norm_next / norm_now * direction
        norm_now = norm_next
    return solution


def solution(mesh):
    placed = (
        P("dp"),
        P("dp"),
        P("shard", None),
        P(),
        P(None, "shard"),
        P(None, "shard"),
        P("dp", None),
    )
    return jax.shard_map(
        body, mesh=mesh, in_specs=placed, out_specs=P("shard", "dp"), check_vma=False
    )
```

profile of v0, /device:TPU:1, one launch (start us, length us, event | category | flops | bytes accessed | tf_op | source)
XLA Modules:
  0.0 1312.3 jit_solution(7112634386722985562)
XLA Ops:
  8.0 5.8 gather_fusion
  13.9 6.7 gather_fusion.1
  23.1 151.2 %all-reduce.7.cloned.1.call-done = (bf16[128,2048]{1,0:T(8,128)(2,1)}, bf16[256,2048]{1,0:T(8,128)(2,1)}) async-done(((bf16[128,2048]{1,0:T(8,128)(2,1)}, bf16[256,2048]{1,0:T(8,128)(2,1)}), (bf16[128,2048]{1,0:T(8,128)(2,1)}, bf16[256,2048]{1,0:T(8,128)(2,1)})) %all-reduce.7.cloned.1.call-update) | async-done | bytes 1572880 | tf_op jit(solution)/shard_map/psum | solution.py:54
  175.6 2.1 fusion.25
  177.8 3.3 fusion.5
  181.2 68.8 %reduce-scatter.5.cloned.1.call-done = f32[344,128]{1,0:T(8,128)} async-done(((f32[344,2048]{1,0:T(8,128)}), f32[344,128]{1,0:T(8,128)}) %reduce-scatter.5.cloned.1.call-update) | async-done | bytes 176144 | tf_op jit(solution)/shard_map/reduce_scatter | solution.py:38
  252.0 2.1 fusion.16
  254.8 59.1 %all-gather.4.cloned.1.call-done = bf16[344,2048]{1,0:T(8,128)(2,1)} async-done(((bf16[344,128]{1,0:T(8,128)(2,1)}), bf16[344,2048]{1,0:T(8,128)(2,1)}) %all-gather.4.cloned.1.call-update) | async-done | bytes 1409040 | tf_op jit(solution)/shard_map/all_gather | solution.py:68
  313.8 3.4 fusion.31
  317.3 84.3 %all-reduce.8 = bf16[256,2048]{1,0:T(8,128)(2,1)S(1)} all-reduce(f32[256,2048]{1,0:T(8,128)} %fusion.31), channel_id=1, replica_groups=mesh['dp'=16,'shard'=16] {'shard'}, use_global_device_ids=true, to_apply=%region_7.8 | all-reduce | flops 524288 | bytes 3145728 | tf_op jit(solution)/shard_map/psum | solution.py:46
  401.6 2.1 fusion.36
  403.7 66.5 %reduce-scatter.7.cloned.1.call-done = f32[344,128]{1,0:T(8,128)} async-done(((f32[344,2048]{1,0:T(8,128)}), f32[344,128]{1,0:T(8,128)}) %reduce-scatter.7.cloned.1.call-update) | async-done | bytes 176144 | tf_op jit(solution)/shard_map/reduce_scatter | solution.py:38
  470.2 1.6 multiply_reduce_fusion.4
  471.8 84.3 %all-reduce = (f32[]{:T(128)}, f32[]{:T(128)}) all-reduce(f32[]{:T(128)} %get-tuple-element.6, f32[]{:T(128)} %get-tuple-element.5), channel_id=1, replica_groups=mesh['dp'=16,'shard'=16] {'dp','shard'}, use_global_device_ids=true, to_apply=%region_4.5 | all-reduce | flops 2 | bytes 16 | tf_op jit(solution)/shard_map/psum | solution.py:42
  557.5 1.6 multiply_reduce_fusion.3
  559.1 73.7 %psum.82 = f32[]{:T(128)} all-reduce(f32[]{:T(128)} %multiply_reduce_fusion.3), channel_id=1, replica_groups=mesh['dp'=16,'shard'=16] {'dp','shard'}, use_global_device_ids=true, to_apply=%region_12.13 | all-reduce | flops 1 | bytes 8 | tf_op jit(solution)/shard_map/psum | solution.py:42
  634.2 1.6 fusion.30
  635.9 52.3 %all-gather.6.cloned.1.call-done = bf16[344,2048]{1,0:T(8,128)(2,1)} async-done(((bf16[344,128]{1,0:T(8,128)(2,1)}), bf16[344,2048]{1,0:T(8,128)(2,1)}) %all-gather.6.cloned.1.call-update) | async-done | bytes 1409040 | tf_op jit(solution)/shard_map/all_gather | solution.py:68
  688.2 3.4 fusion.32
  691.7 84.3 %all-reduce.9 = bf16[256,2048]{1,0:T(8,128)(2,1)S(1)} all-reduce(f32[256,2048]{1,0:T(8,128)} %fusion.32), channel_id=1, replica_groups=mesh['dp'=16,'shard'=16] {'shard'}, use_global_device_ids=true, to_apply=%region_13.14 | all-reduce | flops 524288 | bytes 3145728 | tf_op jit(solution)/shard_map/psum | solution.py:46
  776.0 2.1 fusion.35
  778.2 66.3 %reduce-scatter.9.cloned.1.call-done = f32[344,128]{1,0:T(8,128)} async-done(((f32[344,2048]{1,0:T(8,128)}), f32[344,128]{1,0:T(8,128)}) %reduce-scatter.9.cloned.1.call-update) | async-done | bytes 176144 | tf_op jit(solution)/shard_map/reduce_scatter | solution.py:38
  846.1 84.1 %psum.84 = f32[]{:T(128)} all-reduce(f32[]{:T(128)} %multiply_reduce_fusion.2), channel_id=1, replica_groups=mesh['dp'=16,'shard'=16] {'dp','shard'}, use_global_device_ids=true, to_apply=%region_16.17 | all-reduce | flops 1 | bytes 8 | tf_op jit(solution)/shard_map/psum | solution.py:42
  931.6 1.6 multiply_reduce_fusion.1
  933.2 73.5 %psum.85 = f32[]{:T(128)} all-reduce(f32[]{:T(128)} %get-tuple-element.11), channel_id=1, replica_groups=mesh['dp'=16,'shard'=16] {'dp','shard'}, use_global_device_ids=true, to_apply=%region_18.19 | all-reduce | flops 1 | bytes 8 | tf_op jit(solution)/shard_map/psum | solution.py:42
  1008.9 52.6 %all-gather.8.cloned.1.call-done = bf16[344,2048]{1,0:T(8,128)(2,1)} async-done(((bf16[344,128]{1,0:T(8,128)(2,1)}), bf16[344,2048]{1,0:T(8,128)(2,1)}) %all-gather.8.cloned.1.call-update) | async-done | bytes 1409040 | tf_op jit(solution)/shard_map/all_gather | solution.py:68
  1061.4 3.4 fusion.33
  1064.8 84.3 %all-reduce.10 = bf16[256,2048]{1,0:T(8,128)(2,1)S(1)} all-reduce(f32[256,2048]{1,0:T(8,128)} %fusion.33), channel_id=1, replica_groups=mesh['dp'=16,'shard'=16] {'shard'}, use_global_device_ids=true, to_apply=%region_19.20 | all-reduce | flops 524288 | bytes 3145728 | tf_op jit(solution)/shard_map/psum | solution.py:46
  1149.1 2.1 fusion.34
  1151.3 66.4 %reduce-scatter.11.cloned.1.call-done = f32[344,128]{1,0:T(8,128)} async-done(((f32[344,2048]{1,0:T(8,128)}), f32[344,128]{1,0:T(8,128)}) %reduce-scatter.11.cloned.1.call-update) | async-done | bytes 176144 | tf_op jit(solution)/shard_map/reduce_scatter | solution.py:38
  1217.7 1.6 multiply_reduce_fusion
  1219.3 84.1 %psum.87 = f32[]{:T(128)} all-reduce(f32[]{:T(128)} %multiply_reduce_fusion), channel_id=1, replica_groups=mesh['dp'=16,'shard'=16] {'dp','shard'}, use_global_device_ids=true, to_apply=%region_22.23 | all-reduce | flops 1 | bytes 8 | tf_op jit(solution)/shard_map/psum | solution.py:42
  (45 shorter events, 11.2 us)
Async XLA Ops:
  6.5 171.2 %copy-start = (bf16[2048,344]{0,1:T(8,128)(2,1)S(1)}, bf16[2048,344]{0,1:T(8,128)(2,1)}, u32[]{:S(2)}) copy-start(bf16[2048,344]{0,1:T(8,128)(2,1)} %param.12) | copy-start | bytes 4227076
  6.5 167.8 %all-reduce.7.cloned.1.call-start = ((), (), s32[]{:S(2)}) async-start(), calls=%async_computation.11 | async-start | bytes 3145728 | tf_op jit(solution)/shard_map/psum | solution.py:54
  21.7 153.9 %copy-start.6 = (f32[2048]{0:T(1024)S(1)}, f32[2048]{0:T(1024)}, u32[]{:S(2)}) copy-start(f32[2048]{0:T(1024)} %param.10) | copy-start | bytes 24580
  23.0 154.8 %copy-start.5 = (bf16[128,2048]{1,0:T(8,128)(2,1)S(1)}, bf16[128,2048]{1,0:T(8,128)(2,1)}, u32[]{:S(2)}) copy-start(bf16[128,2048]{1,0:T(8,128)(2,1)} %param.13) | copy-start | bytes 1572868
  23.1 226.9 %reduce-scatter.5.cloned.1.call-start = ((), (), s32[]{:S(2)}) async-start(), calls=%async_computation.4 | async-start | bytes 2994176 | tf_op jit(solution)/shard_map/reduce_scatter | solution.py:38
  174.3 3.5 copy-start.3
  181.1 70.6 %copy-start.4 = (bf16[256,2048]{1,0:T(8,128)(2,1)S(1)}, bf16[256,2048]{1,0:T(8,128)(2,1)}, u32[]{:S(2)}) copy-start(bf16[256,2048]{1,0:T(8,128)(2,1)} %get-tuple-element.10) | copy-start | bytes 3145732
  181.1 132.7 %all-gather.4.cloned.1.call-start = ((), (), s32[]{:S(2)}) async-start(), calls=%async_computation.5 | async-start | bytes 1497088 | tf_op jit(solution)/shard_map/all_gather | solution.py:68
  251.6 218.6 %reduce-scatter.7.cloned.1.call-start = ((), (), s32[]{:S(2)}) async-start(), calls=%async_computation.6 | async-start | bytes 2994176 | tf_op jit(solution)/shard_map/reduce_scatter | solution.py:38
  403.7 66.5 %copy-start.1 = (f32[344,128]{1,0:T(8,128)S(1)}, f32[344,128]{1,0:T(8,128)}, u32[]{:S(2)}) copy-start(f32[344,128]{1,0:T(8,128)} %reduce-scatter.5.cloned.1.call-done) | copy-start | bytes 528388
  403.7 284.5 %all-gather.6.cloned.1.call-start = ((), (), s32[]{:S(2)}) async-start(), calls=%async_computation.7 | async-start | bytes 1497088 | tf_op jit(solution)/shard_map/all_gather | solution.py:68
  635.9 208.6 %reduce-scatter.9.cloned.1.call-start = ((), (), s32[]{:S(2)}) async-start(), calls=%async_computation.8 | async-start | bytes 2994176 | tf_op jit(solution)/shard_map/reduce_scatter | solution.py:38
  778.1 153.5 %copy-start.2 = (f32[344,128]{1,0:T(8,128)S(1)}, f32[344,128]{1,0:T(8,128)}, u32[]{:S(2)}) copy-start(f32[344,128]{1,0:T(8,128)} %reduce-scatter.7.cloned.1.call-done) | copy-start | bytes 528388
  778.1 283.3 %all-gather.8.cloned.1.call-start = ((), (), s32[]{:S(2)}) async-start(), calls=%async_computation.9 | async-start | bytes 1497088 | tf_op jit(solution)/shard_map/all_gather | solution.py:68
  1008.8 208.9 %reduce-scatter.11.cloned.1.call-start = ((), (), s32[]{:S(2)}) async-start(), calls=%async_computation.10 | async-start | bytes 2994176 | tf_op jit(solution)/shard_map/reduce_scatter | solution.py:38
Sparse Core Ops, SparseCore 0:
  23.2 151.0 all-reduce.6
  181.2 68.7 reduce-scatter.4
  251.8 61.9 all-gather.3
  403.8 66.3 reduce-scatter.6
  636.0 52.2 all-gather.5
  778.2 66.2 reduce-scatter.8
  1008.9 52.4 all-gather.7
  1151.4 66.2 reduce-scatter.10
where the time goes:
time: 1310 us
  blocking collectives  653 us (50%)
  waiting for transfers between devices  583 us (45%)
  matrix products  24.9 us (2%)
  between operations  20.5 us (2%)
  other arithmetic  18 us (1%)
    psum x5, blocking collectives, global_total(): return lax.psum(value, ('dp', 'shard'))  400 us
    reduce_scatter x4, waiting for transfers between devices, column_share(): lax.psum_scatter(partial_terms, 'dp', scatter_dimension=1, tiled=True)  268 us
    psum x3, blocking collectives, tangent_total(): return lax.psum(partial_terms, 'shard').astype(jnp.bfloat16)  253 us
    all_gather x3, waiting for transfers between devices, body(): lax.all_gather(direction.astype(jnp.bfloat16), 'dp', axis=1, tiled=True)  164 us
    psum x1, waiting for transfers between devices, body(): lax.psum(query_part.astype(jnp.bfloat16), 'shard').astype(jnp.float32)  151 us
  transfers between devices with their start and end apart: 8, of which 8 were waited for; matrix products, arithmetic and copies ran while one was open for 0% of the time, Pallas kernels for 0%

commit v1 on v0

v1 whole, which is shorter than its diff:
```python
import math

import jax
import jax.numpy as jnp
from jax import lax
from jax.sharding import PartitionSpec as P

norm_eps = 1e-05
damping = 0.1

bf16 = jnp.bfloat16
f32 = jnp.float32

CHIPS = [[c + 2 * i for i in range(8)] for c in range(2)]
CORE = [(i, i ^ 1) for i in range(16)]
YLO = [(i, i ^ 8) for i in range(16)]


def z_shift(step):
    return [(i, (i & 8) | ((i + step) & 7)) for i in range(16)]


def swap_core(v):
    return lax.ppermute(v, "shard", CORE)


def scatter_chips(v):
    return lax.all_to_all(v, "shard", 0, 0, axis_index_groups=CHIPS, tiled=True)


def share_chips(v):
    spread = jnp.broadcast_to(v[None], (8,) + v.shape)
    return lax.all_to_all(spread, "shard", 0, 0, axis_index_groups=CHIPS, tiled=True)


def split3(v):
    hi = v.astype(bf16).astype(f32)
    mid = (v - hi).astype(bf16).astype(f32)
    low = v - hi - mid
    return jnp.stack([hi, mid, low]).astype(bf16)


def guarded(top, bottom):
    fine = bottom > 0
    return jnp.where(fine, top / jnp.where(fine, bottom, 1.0), 0.0)


def dot_t(a, b):
    return lax.dot_general(a, b, (((0,), (0,)), ((), ())), preferred_element_type=f32)


def dot(a, b):
    return jnp.dot(a, b, preferred_element_type=f32)


def embedding_rows(train_ids, query_ids, embed, core):
    height = embed.shape[0]
    ids = jnp.concatenate([train_ids.reshape(2, -1), query_ids.reshape(2, -1)], axis=1)
    ids = jnp.where(core == 0, ids, ids[::-1])
    offset = ids - lax.axis_index("shard") * height
    inside = (offset >= 0) & (offset < height)
    picked = jnp.take(embed, jnp.clip(offset, 0, height - 1).reshape(-1), axis=0)
    picked = jnp.where(inside.reshape(-1)[:, None], picked, jnp.zeros_like(picked))
    half = picked.shape[0] // 2
    other = swap_core(picked[half:])
    mine = picked[:half] + other
    parts = scatter_chips(mine.reshape(8, half // 8, -1))
    return jnp.sum(parts.astype(f32), axis=0)


def normalise(rows, norm_gain):
    inv_scale = lax.rsqrt(jnp.mean(rows * rows, axis=-1, keepdims=True) + norm_eps)
    return (rows * inv_scale * norm_gain).astype(bf16)


def hidden_transposed(normed, w_gate, w_up):
    def product(w):
        return lax.dot_general(w, normed, (((0,), (1,)), ((), ())), preferred_element_type=f32)

    return (jax.nn.silu(product(w_gate)) * product(w_up)).astype(bf16)


def gather_groups(own):
    pair = jnp.stack([own, lax.ppermute(own, "dp", YLO)])
    ups, downs = [pair], [pair]
    for _ in range(3):
        ups.append(lax.ppermute(ups[-1], "dp", z_shift(1)))
        downs.append(lax.ppermute(downs[-1], "dp", z_shift(-1)))
    last_up = lax.ppermute(ups[-1][0], "dp", z_shift(1))
    last_down = lax.ppermute(downs[-1][1], "dp", z_shift(-1))
    blocks = [pair[0], pair[1]]
    for i in range(1, 4):
        blocks += [ups[i][0], ups[i][1], downs[i][0], downs[i][1]]
    return blocks + [last_up, last_down]


def group_order():
    me = lax.axis_index("dp")
    y, z = me // 8, me % 8
    steps = [0]
    for i in range(1, 4):
        steps += [-i, i]
    steps.append(4)
    order = []
    for step in steps:
        for flip in range(2):
            order.append((y ^ flip) * 8 + (z + step) % 8)
    return jnp.stack(order)


def body(train_ids, query_ids, embed, norm_gain, w_gate, w_up, cotangent):
    core = lax.axis_index("shard") % 2
    tokens_total = train_ids.shape[0] * 16
    query_total = query_ids.shape[0] * 16
    units = w_gate.shape[1]
    w_gate_other, w_up_other = swap_core(w_gate), swap_core(w_up)

    with jax.named_scope("rows"):
        rows = embedding_rows(train_ids, query_ids, embed, core)
    with jax.named_scope("normed"):
        normed = normalise(rows, norm_gain)
        normed = share_chips(normed).reshape(-1, rows.shape[1])
    with jax.named_scope("acts"):
        own = hidden_transposed(normed, w_gate, w_up)
        other = hidden_transposed(normed, w_gate_other, w_up_other)
        n_train = train_ids.shape[0] // 2
        package = jnp.concatenate(
            [
                own[:, :n_train],
                other[:, :n_train],
                jnp.concatenate([own[:, n_train:], other[:, n_train:]], axis=1),
            ],
            axis=0,
        )
    with jax.named_scope("groups"):
        blocks = gather_groups(package)
        acts = jnp.concatenate([b[: 2 * units] for b in blocks], axis=1)
        query = jnp.concatenate([b[2 * units :] for b in blocks], axis=1)
    with jax.named_scope("cotangent"):
        n_query = query_ids.shape[0] // 2
        mine = lax.dynamic_slice_in_dim(cotangent, core * n_query, n_query, axis=0)
        columns = lax.all_to_all(
            mine.reshape(n_query, 16, -1).transpose(1, 0, 2), "dp", 0, 0, tiled=True
        )
        columns = jnp.take(columns, group_order(), axis=0)
        empty = jnp.zeros_like(columns)
        wide = jnp.concatenate(
            [
                jnp.concatenate([columns, empty], axis=2),
                jnp.concatenate([empty, columns], axis=2),
            ],
            axis=1,
        ).reshape(-1, 2 * columns.shape[2])

    def across_cores(pair):
        return pair + swap_core(pair[::-1])

    with jax.named_scope("rhs"):
        part = dot(query, wide)
        width = part.shape[1] // 2
        part = jnp.stack([part[:, :width], part[:, width:]]) / math.sqrt(query_total)
        residual = across_cores(part)

    def scattered_tangent(res):
        partial = dot_t(acts, res.reshape(-1, width).astype(bf16)).astype(bf16)
        parts = scatter_chips(partial.reshape(8, -1, width))
        return jnp.sum(parts.astype(f32), axis=0)

    def shared_tangent(block, scalars):
        extra = split3(scalars)
        extra = jnp.pad(extra, ((0, 16 - extra.shape[0]), (0, width - extra.shape[1])))
        message = jnp.concatenate([block.astype(bf16), extra], axis=0)
        got = share_chips(message).reshape(8, -1, width)
        rows = block.shape[0]
        sums = jnp.sum(got[:, rows : rows + 3, : scalars.shape[0]].astype(f32), axis=(0, 1))
        return got[:, :rows].reshape(-1, width), sums

    def curved_product(tangent):
        return across_cores(dot(acts, tangent).reshape(2, -1, width)) / tokens_total

    with jax.named_scope("first"):
        r0 = residual
        block0 = scattered_tangent(r0)
        block0 = block0.astype(bf16).astype(f32)
        t0, sums = shared_tangent(block0, jnp.stack([jnp.sum(r0 * r0), jnp.sum(block0 * block0)]))
        rr0, tt0 = sums[0], sums[1]
        tt0 = tt0 + swap_core(tt0)
        pp0 = rr0
        inv_alpha0 = guarded(tt0 / tokens_total + damping * pp0, rr0)
        alpha0 = guarded(1.0, inv_alpha0)
        p0 = r0
        r1 = r0 - alpha0 * (curved_product(t0) + damping * p0)
    with jax.named_scope("second"):
        block1 = scattered_tangent(r1)
        block1 = block1.astype(bf16).astype(f32)
        w1, sums = shared_tangent(
            block1,
            jnp.stack([jnp.sum(r1 * r1), jnp.sum(block1 * block1), jnp.sum(block1 * block0)]),
        )
        rr1 = sums[0]
        cross = sums[1:]
        cross = cross + swap_core(cross)
        beta0 = guarded(rr1, rr0)
        tt1 = cross[0] + 2 * beta0 * cross[1] + beta0 * beta0 * tt0
        pp1 = rr1 + beta0 * beta0 * pp0
        inv_alpha1 = guarded(tt1 / tokens_total + damping * pp1, rr1)
        alpha1 = guarded(1.0, inv_alpha1)
        t1 = (w1.astype(f32) + beta0 * t0.astype(f32)).astype(bf16)
        p1 = r1 + beta0 * p0
        r2 = r1 - alpha1 * (curved_product(t1) + damping * p1)
    with jax.named_scope("third"):
        block2 = scattered_tangent(r2)
        step1 = block1 + beta0 * block0
        partials = jnp.stack(
            [0.5 * jnp.sum(r2 * r2), jnp.sum(block2 * block2), jnp.sum(block2 * step1)]
        )
        got = lax.all_to_all(jnp.broadcast_to(partials[None], (16, 3)), "shard", 0, 0, tiled=True)
        sums = jnp.sum(got, axis=0)
        rr2 = sums[0]
        beta1 = guarded(rr2, rr1)
        tt2 = sums[1] + 2 * beta1 * sums[2] + beta1 * beta1 * tt1
        pp2 = rr2 + beta1 * beta1 * pp1
        inv_alpha2 = guarded(tt2 / tokens_total + damping * pp2, rr2)

    with jax.named_scope("whole"):
        mine = jnp.stack([rr0, rr1, rr2, inv_alpha0, inv_alpha1, inv_alpha2, beta0, beta1])
        every = lax.all_to_all(jnp.broadcast_to(mine[None], (16, 8)), "dp", 0, 0, tiled=True)
        norms = every[:, 0:3]
        ia0, ia1, ia2 = every[:, 3], every[:, 4], every[:, 5]
        b0, b1 = every[:, 6], every[:, 7]

        def apply_whole(u):
            u0, u1, u2 = u[:, 0], u[:, 1], u[:, 2]
            s2 = u2
            s1 = u1 - b1 * s2
            s0 = u0 - b0 * u1
            return jnp.stack([s0 * ia0, s1 * ia1 - s0 * ia0, s2 * ia2 - s1 * ia1], axis=1)

        def inner(u, v):
            return jnp.sum(u * v * norms)

        answer = jnp.zeros_like(norms)
        res = jnp.concatenate([jnp.ones_like(norms[:, :1]), jnp.zeros_like(norms[:, :2])], axis=1)
        direction = res
        norm_now = inner(res, res)
        for turn in range(3):
            curved = apply_whole(direction)
            step = norm_now / inner(direction, curved)
            answer = answer + step * direction
            if turn < 2:
                res = res - step * curved
                norm_next = inner(res, res)
                direction = res + norm_next / norm_now * direction
                norm_now = norm_next
        mix = lax.dynamic_slice_in_dim(answer, lax.axis_index("dp"), 1, axis=0)[0]
        return mix[0] * r0[0] + mix[1] * r1[0] + mix[2] * r2[0]


def solution(mesh):
    placed = (
        P("dp"),
        P("dp"),
        P("shard", None),
        P(),
        P(None, "shard"),
        P(None, "shard"),
        P("dp", None),
    )
    return jax.shard_map(
        body, mesh=mesh, in_specs=placed, out_specs=P("shard", "dp"), check_vma=False
    )
```

time: 1310 us -> 337 us (0.26)
  blocking collectives: 653 us -> 38.4 us
  waiting for transfers between devices: 583 us -> 83.9 us
  starting transfers between devices: 0.29 us -> 70.4 us
  local copies, waits for them, and re-layouts: 12.6 us -> 82 us
    psum x8 -> x0, blocking collectives: 653 us -> none  [the longest x5 400 us: global_total(): return lax.psum(value, ('dp', 'shard'))]
    reduce_scatter x4 -> x0, waiting for transfers between devices: 268 us -> none  [column_share(): lax.psum_scatter(partial_terms, 'dp', scatter_dimension=1, tiled=True)]
    all_gather x3 -> x0, waiting for transfers between devices: 164 us -> none  [body(): lax.all_gather(direction.astype(jnp.bfloat16), 'dp', axis=1, tiled=True)]
    psum x1 -> x0, waiting for transfers between devices: 151 us -> none  [body(): lax.psum(query_part.astype(jnp.bfloat16), 'shard').astype(jnp.float32)]
    all_to_all x0 -> x7, waiting for transfers between devices: none -> 58.7 us  [the longest x3 28.8 us: scatter_chips(): return lax.all_to_all(v, 'shard', 0, 0, axis_index_groups=CHIPS, tiled=True)]
    unnamed x14 -> x89, local copies, waits for them, and re-layouts: 0.03 us -> 50.3 us
    all_to_all x0 -> x7, starting transfers between devices: none -> 43.4 us  [the longest x3 20.3 us: scatter_chips(): return lax.all_to_all(v, 'shard', 0, 0, axis_index_groups=CHIPS, tiled=True)]
    all_to_all x0 -> x3, blocking collectives: none -> 38.4 us  [the longest x1 13.8 us: share_chips(): lax.all_to_all(spread, 'shard', 0, 0, axis_index_groups=CHIPS, tiled=True)]
  transfers between devices with their start and end apart: 8 -> 24, of which waited for: 8 -> 14; matrix products, arithmetic and copies ran while one was open for 0% -> 15% of each run, Pallas kernels for 0% -> 0%
where the time goes in v1:
time: 337 us; the launch traced here: 335 us
  waiting for transfers between devices  83.9 us (25%)
  local copies, waits for them, and re-layouts  82 us (24%)
  starting transfers between devices  70.4 us (21%)
  blocking collectives  38.4 us (11%)
  matrix products  22.5 us (7%)
  other arithmetic  20.3 us (6%)
  between operations  17.5 us (5%)
    unnamed x89, local copies, waits for them, and re-layouts  50.3 us
    all_to_all x3, waiting for transfers between devices, scatter_chips(): return lax.all_to_all(v, 'shard', 0, 0, axis_index_groups=CHIPS, tiled=True)  28.8 us
    all_to_all x3, starting transfers between devices, scatter_chips(): return lax.all_to_all(v, 'shard', 0, 0, axis_index_groups=CHIPS, tiled=True)  20.3 us
    ppermute x3, waiting for transfers between devices, gather_groups(): downs.append(lax.ppermute(downs[-1], 'dp', z_shift(-1)))  17.7 us
    all_to_all x2, waiting for transfers between devices, share_chips(): lax.all_to_all(spread, 'shard', 0, 0, axis_index_groups=CHIPS, tiled=True)  15.2 us
    ppermute x8, starting transfers between devices, swap_core(): return lax.ppermute(v, 'shard', CORE)  14.4 us
    all_to_all x1, blocking collectives, share_chips(): lax.all_to_all(spread, 'shard', 0, 0, axis_index_groups=CHIPS, tiled=True)  13.8 us
    all_to_all x1, blocking collectives, scatter_chips(): return lax.all_to_all(v, 'shard', 0, 0, axis_index_groups=CHIPS, tiled=True)  13.1 us
  transfers between devices with their start and end apart: 24, of which 14 were waited for; matrix products, arithmetic and copies ran while one was open for 15% of the time, Pallas kernels for 0%

profile of v1, /device:TPU:1, one launch (start us, length us, event | category | flops | bytes accessed | tf_op | source)
XLA Modules:
  0.0 335.0 jit_solution(5219784753272952866)
XLA Ops:
  3.2 8.8 %gather_fusion = bf16[384,2048]{1,0:T(8,128)(2,1)S(1)} fusion(bf16[2000,2048]{1,0:T(8,128)(2,1)} %param.9, s32[1024]{0:T(1024)S(1)} %pad_clamp_fusion.1), kind=kCustom, calls=%fused_computation | custom fusion | bytes 3147264 | tf_op jit(solution)/shard_map/rows/jit(_take)/gather | solution.py:62
  12.4 3.3 collective-permute-start
  18.6 4.9 %all-to-all-start = ((bf16[8,24,2048]{2,1,0:T(8,128)(2,1)}), bf16[8,24,2048]{2,1,0:T(8,128)(2,1)S(1)}, u32[]{:S(2)}, u32[]{:S(2)}) async-start(bf16[8,24,2048]{2,1,0:T(8,128)(2,1)} %bitcast.1), calls=%async_computation | async-start | bytes 1572864 | tf_op jit(solution)/shard_map/rows/all_to_all | solution.py:28
  25.2 11.2 %all-to-all-done = bf16[8,24,2048]{2,1,0:T(8,128)(2,1)S(1)} async-done(((bf16[8,24,2048]{2,1,0:T(8,128)(2,1)}), bf16[8,24,2048]{2,1,0:T(8,128)(2,1)S(1)}, u32[]{:S(2)}, u32[]{:S(2)}) %all-to-all-start) | async-done | bytes 786464 | tf_op jit(solution)/shard_map/rows/all_to_all | solution.py:28
  36.4 8.4 %all-to-all-start.2 = ((bf16[16,64,128]{2,1,0:T(8,128)(2,1)}), bf16[16,64,128]{2,1,0:T(8,128)(2,1)S(1)}, u32[]{:S(2)}, u32[]{:S(2)}) async-start(bf16[16,64,128]{2,1,0:T(8,128)(2,1)} %bitcast_bitcast_fusion), calls=%async_computation.2 | async-start | bytes 524288 | tf_op jit(solution)/shard_map/cotangent/all_to_all | solution.py:142
  45.2 7.5 %all-to-all-done.2 = bf16[16,64,128]{2,1,0:T(8,128)(2,1)S(1)} async-done(((bf16[16,64,128]{2,1,0:T(8,128)(2,1)}), bf16[16,64,128]{2,1,0:T(8,128)(2,1)S(1)}, u32[]{:S(2)}, u32[]{:S(2)}) %all-to-all-start.2) | async-done | bytes 262176 | tf_op jit(solution)/shard_map/cotangent/all_to_all | solution.py:142
  53.7 5.3 %all-to-all-start.1 = ((bf16[8,24,2048]{2,1,0:T(8,128)(2,1)}), bf16[8,24,2048]{2,1,0:T(8,128)(2,1)S(1)}, u32[]{:S(2)}, u32[]{:S(2)}) async-start(bf16[8,24,2048]{2,1,0:T(8,128)(2,1)} %broadcast_in_dim.71), calls=%async_computation.1 | async-start | bytes 1572864 | tf_op jit(solution)/shard_map/normed/all_to_all | solution.py:33
  59.8 9.1 %all-to-all-done.1 = bf16[8,24,2048]{2,1,0:T(8,128)(2,1)S(1)} async-done(((bf16[8,24,2048]{2,1,0:T(8,128)(2,1)}), bf16[8,24,2048]{2,1,0:T(8,128)(2,1)S(1)}, u32[]{:S(2)}, u32[]{:S(2)}) %all-to-all-start.1) | async-done | bytes 786464 | tf_op jit(solution)/shard_map/normed/all_to_all | solution.py:33
  79.1 3.8 %collective-permute-done.3 = bf16[1032,128]{0,1:T(8,128)(2,1)S(1)} collective-permute-done((bf16[1032,128]{0,1:T(8,128)(2,1)S(1)}, bf16[1032,128]{0,1:T(8,128)(2,1)S(1)}, u32[]{:S(2)}, u32[]{:S(2)}) %collective-permute-start.3) | collective-permute-done | bytes 264224 | tf_op jit(solution)/shard_map/groups/ppermute | solution.py:84
  83.2 2.5 collective-permute-start.5
  89.9 5.8 %collective-permute-done.5 = bf16[2,1032,128]{2,1,0:T(8,128)(2,1)} collective-permute-done((bf16[2,1032,128]{2,1,0:T(8,128)(2,1)S(1)}, bf16[2,1032,128]{2,1,0:T(8,128)(2,1)}, u32[]{:S(2)}, u32[]{:S(2)}) %collective-permute-start.5) | collective-permute-done | bytes 528416 | tf_op jit(solution)/shard_map/groups/ppermute | solution.py:88
  112.0 5.5 %collective-permute-done.7 = bf16[2,1032,128]{2,1,0:T(8,128)(2,1)S(1)} collective-permute-done((bf16[2,1032,128]{2,1,0:T(8,128)(2,1)}, bf16[2,1032,128]{2,1,0:T(8,128)(2,1)S(1)}, u32[]{:S(2)}, u32[]{:S(2)}) %collective-permute-start.7) | collective-permute-done | bytes 528416 | tf_op jit(solution)/shard_map/groups/ppermute | solution.py:88
  129.4 3.7 %collective-permute-start.8 = (bf16[2,1032,128]{2,1,0:T(8,128)(2,1)}, bf16[2,1032,128]{2,1,0:T(8,128)(2,1)S(1)}, u32[]{:S(2)}, u32[]{:S(2)}) collective-permute-start(bf16[2,1032,128]{2,1,0:T(8,128)(2,1)} %copy-done.5), channel_id=1, source_target_pairs={{0,16},{16,32},{32,48},{48,64},{64,80},{80,96},{96,112},{112,0},{1... | collective-permute-start | bytes 1585160 | tf_op jit(solution)/shard_map/groups/ppermute | solution.py:87
  135.1 6.5 %collective-permute-done.9 = bf16[2,1032,128]{2,1,0:T(8,128)(2,1)S(1)} collective-permute-done((bf16[2,1032,128]{2,1,0:T(8,128)(2,1)}, bf16[2,1032,128]{2,1,0:T(8,128)(2,1)S(1)}, u32[]{:S(2)}, u32[]{:S(2)}) %collective-permute-start.9) | collective-permute-done | bytes 528416 | tf_op jit(solution)/shard_map/groups/ppermute | solution.py:88
  168.2 5.4 %collective-permute-start.12 = (f32[2,344,128]{2,1,0:T(8,128)S(1)}, f32[2,344,128]{2,1,0:T(8,128)S(1)}, u32[]{:S(2)}, u32[]{:S(2)}) collective-permute-start(f32[2,344,128]{2,1,0:T(8,128)S(1)} %reverse_multiply_fusion), channel_id=1, source_target_pairs={{0,1},{1,0},{2,3},{3,2},{4,5},{5,4},{6,7},{7,6},{8,9},{9,8},{10,11... | collective-permute-start | bytes 1056776 | tf_op jit(solution)/shard_map/rhs/ppermute | solution.py:24
  178.2 11.9 %all-to-all-start.3 = ((bf16[8,256,128]{2,1,0:T(8,128)(2,1)}), bf16[8,256,128]{2,1,0:T(8,128)(2,1)S(1)}, u32[]{:S(2)}, u32[]{:S(2)}) async-start(bf16[8,256,128]{2,1,0:T(8,128)(2,1)} %bitcast.73), calls=%async_computation.3 | async-start | bytes 1048576 | tf_op jit(solution)/shard_map/first/all_to_all | solution.py:28
  192.9 7.7 %all-to-all-done.3 = bf16[8,256,128]{2,1,0:T(8,128)(2,1)S(1)} async-done(((bf16[8,256,128]{2,1,0:T(8,128)(2,1)}), bf16[8,256,128]{2,1,0:T(8,128)(2,1)S(1)}, u32[]{:S(2)}, u32[]{:S(2)}) %all-to-all-start.3) | async-done | bytes 524320 | tf_op jit(solution)/shard_map/first/all_to_all | solution.py:28
  203.6 3.8 %all-to-all-start.4 = ((bf16[8,272,128]{2,1,0:T(8,128)(2,1)}), bf16[8,272,128]{2,1,0:T(8,128)(2,1)S(1)}, u32[]{:S(2)}, u32[]{:S(2)}) async-start(bf16[8,272,128]{2,1,0:T(8,128)(2,1)} %broadcast_in_dim.74), calls=%async_computation.4 | async-start | bytes 1114112 | tf_op jit(solution)/shard_map/first/all_to_all | solution.py:33
  211.3 6.1 %all-to-all-done.4 = bf16[8,272,128]{2,1,0:T(8,128)(2,1)S(1)} async-done(((bf16[8,272,128]{2,1,0:T(8,128)(2,1)}), bf16[8,272,128]{2,1,0:T(8,128)(2,1)S(1)}, u32[]{:S(2)}, u32[]{:S(2)}) %all-to-all-start.4) | async-done | bytes 557088 | tf_op jit(solution)/shard_map/first/all_to_all | solution.py:33
  217.4 2.7 fusion.66
  227.5 2.9 convolution_convert_fusion.1
  230.4 13.1 %all_to_all.55 = bf16[8,256,128]{2,1,0:T(8,128)(2,1)S(1)} all-to-all(bf16[8,256,128]{2,1,0:T(8,128)(2,1)S(1)} %bitcast.195), channel_id=1, replica_groups={{0,2,4,6,8,10,12,14},{1,3,5,7,9,11,13,15},{16,18,20,22,24,26,28,30},{17..., dimensions={0} | all-to-all | bytes 1048576 | tf_op jit(solution)/shard_map/second/all_to_all | solution.py:28
  246.2 13.8 %all_to_all.56 = bf16[8,272,128]{2,1,0:T(8,128)(2,1)S(1)} all-to-all(bf16[8,272,128]{2,1,0:T(8,128)(2,1)S(1)} %broadcast_in_dim.75), channel_id=1, replica_groups={{0,2,4,6,8,10,12,14},{1,3,5,7,9,11,13,15},{16,18,20,22,24,26,28,30},{17..., dimensions={0} | all-to-all | bytes 1114112 | tf_op jit(solution)/shard_map/second/all_to_all | solution.py:33
  260.1 2.7 fusion.7
  262.9 2.8 collective-permute-start.16
  270.7 3.7 %convolution_convert_fusion = bf16[2048,128]{1,0:T(8,128)(2,1)} fusion(bf16[688,2048]{0,1:T(8,128)(2,1)} %copy-done.2, bf16[688,128]{1,0:T(8,128)(2,1)S(1)} %bitcast.212), kind=kOutput, calls=%fused_computation.2 | convolution fusion | flops 360972288 | bytes 3518464 | tf_op jit(solution)/shard_map/third/dot_general | solution.py:49
  274.4 3.5 %all-to-all-start.7 = ((bf16[8,256,128]{2,1,0:T(8,128)(2,1)}), bf16[8,256,128]{2,1,0:T(8,128)(2,1)S(1)}, u32[]{:S(2)}, u32[]{:S(2)}) async-start(bf16[8,256,128]{2,1,0:T(8,128)(2,1)} %bitcast.108), calls=%async_computation.7 | async-start | bytes 1048576 | tf_op jit(solution)/shard_map/third/all_to_all | solution.py:28
  278.4 9.9 %all-to-all-done.7 = bf16[8,256,128]{2,1,0:T(8,128)(2,1)S(1)} async-done(((bf16[8,256,128]{2,1,0:T(8,128)(2,1)}), bf16[8,256,128]{2,1,0:T(8,128)(2,1)S(1)}, u32[]{:S(2)}, u32[]{:S(2)}) %all-to-all-start.7) | async-done | bytes 524320 | tf_op jit(solution)/shard_map/third/all_to_all | solution.py:28
  290.4 11.5 %all_to_all.57 = f32[16,1,3]{2,1,0:T(1,128)S(1)} all-to-all(f32[16,1,3]{2,1,0:T(1,128)S(1)} %broadcast_in_dim.76), channel_id=1, replica_groups=mesh['dp'=16,'shard'=16] {'shard'}, dimensions={0} | all-to-all | bytes 384 | tf_op jit(solution)/shard_map/third/all_to_all | solution.py:217
  308.4 5.7 %all-to-all-start.9 = ((f32[16,1,8]{2,1,0:T(1,128)}), f32[16,1,8]{2,1,0:T(1,128)S(1)}, u32[]{:S(2)}, u32[]{:S(2)}) async-start(f32[16,1,8]{2,1,0:T(1,128)} %broadcast_in_dim.77), calls=%async_computation.9 | async-start | bytes 16384 | tf_op jit(solution)/shard_map/whole/all_to_all | solution.py:227
  314.1 7.2 %all-to-all-done.9 = f32[16,1,8]{2,1,0:T(1,128)S(1)} async-done(((f32[16,1,8]{2,1,0:T(1,128)}), f32[16,1,8]{2,1,0:T(1,128)S(1)}, u32[]{:S(2)}, u32[]{:S(2)}) %all-to-all-start.9) | async-done | bytes 544 | tf_op jit(solution)/shard_map/whole/all_to_all | solution.py:227
  332.3 2.6 fusion.11
  (235 shorter events, 114.4 us)
Async XLA Ops:
  0.0 24.4 %copy-start = (bf16[128,2048]{1,0:T(8,128)(2,1)S(1)}, bf16[128,2048]{1,0:T(8,128)(2,1)}, u32[]{:S(2)}) copy-start(bf16[128,2048]{1,0:T(8,128)(2,1)} %param.13) | copy-start | bytes 1572868
  12.3 11.2 %copy-start.3 = (bf16[2048,344]{0,1:T(8,128)(2,1)S(1)}, bf16[2048,344]{0,1:T(8,128)(2,1)}, u32[]{:S(2)}) copy-start(bf16[2048,344]{0,1:T(8,128)(2,1)} %param.11) | copy-start | bytes 4227076
  12.3 32.8 %copy-start.9 = (f32[2048]{0:T(1024)S(1)}, f32[2048]{0:T(1024)}, u32[]{:S(2)}) copy-start(f32[2048]{0:T(1024)} %param.10) | copy-start | bytes 24580
  12.4 5.2 %collective-permute-start = (bf16[192,2048]{1,0:T(8,128)(2,1)S(1)}, bf16[192,2048]{1,0:T(8,128)(2,1)S(1)}, u32[]{:S(2)}, u32[]{:S(2)}) collective-permute-start(bf16[192,2048]{1,0:T(8,128)(2,1)S(1)} %slice.426), channel_id=1, source_target_pairs={{0,1},{1,0},{2,3},{3,2},{4,5},{5,4},{6,7},{7,6},{8,9},{9,8},{10,11... | collective-permute-start | bytes 2359304 | tf_op jit(solution)/shard_map/rows/ppermute | solution.py:24
  18.6 17.9 %all-to-all-start = ((bf16[8,24,2048]{2,1,0:T(8,128)(2,1)}), bf16[8,24,2048]{2,1,0:T(8,128)(2,1)S(1)}, u32[]{:S(2)}, u32[]{:S(2)}) async-start(bf16[8,24,2048]{2,1,0:T(8,128)(2,1)} %bitcast.1), calls=%async_computation | async-start | bytes 1572864 | tf_op jit(solution)/shard_map/rows/all_to_all | solution.py:28
  23.5 48.8 %collective-permute-start.1 = (bf16[2048,344]{0,1:T(8,128)(2,1)S(1)}, bf16[2048,344]{0,1:T(8,128)(2,1)}, u32[]{:S(2)}, u32[]{:S(2)}) collective-permute-start(bf16[2048,344]{0,1:T(8,128)(2,1)S(1)} %copy-done.3), channel_id=1, source_target_pairs={{0,1},{1,0},{2,3},{3,2},{4,5},{5,4},{6,7},{7,6},{8,9},{9,8},{10,11... | collective-permute-start | bytes 4227080 | tf_op jit(solution)/shard_map/ppermute | solution.py:24
  24.2 50.0 %collective-permute-start.2 = (bf16[2048,344]{0,1:T(8,128)(2,1)}, bf16[2048,344]{0,1:T(8,128)(2,1)}, u32[]{:S(2)}, u32[]{:S(2)}) collective-permute-start(bf16[2048,344]{0,1:T(8,128)(2,1)} %param.12), channel_id=1, source_target_pairs={{0,1},{1,0},{2,3},{3,2},{4,5},{5,4},{6,7},{7,6},{8,9},{9,8},{10,11... | collective-permute-start | bytes 4227080 | tf_op jit(solution)/shard_map/ppermute | solution.py:24
  36.4 16.3 %all-to-all-start.2 = ((bf16[16,64,128]{2,1,0:T(8,128)(2,1)}), bf16[16,64,128]{2,1,0:T(8,128)(2,1)S(1)}, u32[]{:S(2)}, u32[]{:S(2)}) async-start(bf16[16,64,128]{2,1,0:T(8,128)(2,1)} %bitcast_bitcast_fusion), calls=%async_computation.2 | async-start | bytes 524288 | tf_op jit(solution)/shard_map/cotangent/all_to_all | solution.py:142
  53.7 15.2 %all-to-all-start.1 = ((bf16[8,24,2048]{2,1,0:T(8,128)(2,1)}), bf16[8,24,2048]{2,1,0:T(8,128)(2,1)S(1)}, u32[]{:S(2)}, u32[]{:S(2)}) async-start(bf16[8,24,2048]{2,1,0:T(8,128)(2,1)} %broadcast_in_dim.71), calls=%async_computation.1 | async-start | bytes 1572864 | tf_op jit(solution)/shard_map/normed/all_to_all | solution.py:33
  77.2 5.7 %collective-permute-start.3 = (bf16[1032,128]{0,1:T(8,128)(2,1)S(1)}, bf16[1032,128]{0,1:T(8,128)(2,1)S(1)}, u32[]{:S(2)}, u32[]{:S(2)}) collective-permute-start(bf16[1032,128]{0,1:T(8,128)(2,1)S(1)} %concatenate.145), channel_id=1, source_target_pairs={{0,128},{16,144},{32,160},{48,176},{64,192},{80,208},{96,224},{112... | collective-permute-start | bytes 792584 | tf_op jit(solution)/shard_map/groups/ppermute | solution.py:84
  83.2 12.4 %collective-permute-start.5 = (bf16[2,1032,128]{2,1,0:T(8,128)(2,1)S(1)}, bf16[2,1032,128]{2,1,0:T(8,128)(2,1)}, u32[]{:S(2)}, u32[]{:S(2)}) collective-permute-start(bf16[2,1032,128]{2,1,0:T(8,128)(2,1)S(1)} %copy.196), channel_id=1, source_target_pairs={{0,112},{16,0},{32,16},{48,32},{64,48},{80,64},{96,80},{112,96},{1... | collective-permute-start | bytes 1585160 | tf_op jit(solution)/shard_map/groups/ppermute | solution.py:88
  85.7 12.5 %collective-permute-start.4 = (bf16[2,1032,128]{2,1,0:T(8,128)(2,1)S(1)}, bf16[2,1032,128]{2,1,0:T(8,128)(2,1)}, u32[]{:S(2)}, u32[]{:S(2)}) collective-permute-start(bf16[2,1032,128]{2,1,0:T(8,128)(2,1)S(1)} %copy.196), channel_id=1, source_target_pairs={{0,16},{16,32},{32,48},{48,64},{64,80},{80,96},{96,112},{112,0},{1... | collective-permute-start | bytes 1585160 | tf_op jit(solution)/shard_map/groups/ppermute | solution.py:87
  108.5 9.1 %collective-permute-start.7 = (bf16[2,1032,128]{2,1,0:T(8,128)(2,1)}, bf16[2,1032,128]{2,1,0:T(8,128)(2,1)S(1)}, u32[]{:S(2)}, u32[]{:S(2)}) collective-permute-start(bf16[2,1032,128]{2,1,0:T(8,128)(2,1)} %collective-permute-done.5), channel_id=1, source_target_pairs={{0,112},{16,0},{32,16},{48,32},{64,48},{80,64},{96,80},{112,96},{1... | collective-permute-start | bytes 1585160 | tf_op jit(solution)/shard_map/groups/ppermute | solution.py:88
  108.5 12.0 %collective-permute-start.6 = (bf16[2,1032,128]{2,1,0:T(8,128)(2,1)}, bf16[2,1032,128]{2,1,0:T(8,128)(2,1)S(1)}, u32[]{:S(2)}, u32[]{:S(2)}) collective-permute-start(bf16[2,1032,128]{2,1,0:T(8,128)(2,1)} %collective-permute-done.4), channel_id=1, source_target_pairs={{0,16},{16,32},{32,48},{48,64},{64,80},{80,96},{96,112},{112,0},{1... | collective-permute-start | bytes 1585160 | tf_op jit(solution)/shard_map/groups/ppermute | solution.py:87
  119.1 6.5 %copy-start.7 = (bf16[1,344,128]{1,2,0:T(8,128)(2,1)S(1)}, bf16[1,344,128]{1,2,0:T(8,128)(2,1)}, u32[]{:S(2)}) copy-start(bf16[1,344,128]{1,2,0:T(8,128)(2,1)} %copy.250) | copy-start | bytes 264196
  120.5 1.7 copy-start.5
  128.4 13.2 %collective-permute-start.9 = (bf16[2,1032,128]{2,1,0:T(8,128)(2,1)}, bf16[2,1032,128]{2,1,0:T(8,128)(2,1)S(1)}, u32[]{:S(2)}, u32[]{:S(2)}) collective-permute-start(bf16[2,1032,128]{2,1,0:T(8,128)(2,1)} %copy-done.6), channel_id=1, source_target_pairs={{0,112},{16,0},{32,16},{48,32},{64,48},{80,64},{96,80},{112,96},{1... | collective-permute-start | bytes 1585160 | tf_op jit(solution)/shard_map/groups/ppermute | solution.py:88
  129.4 18.3 %collective-permute-start.8 = (bf16[2,1032,128]{2,1,0:T(8,128)(2,1)}, bf16[2,1032,128]{2,1,0:T(8,128)(2,1)S(1)}, u32[]{:S(2)}, u32[]{:S(2)}) collective-permute-start(bf16[2,1032,128]{2,1,0:T(8,128)(2,1)} %copy-done.5), channel_id=1, source_target_pairs={{0,16},{16,32},{32,48},{48,64},{64,80},{80,96},{96,112},{112,0},{1... | collective-permute-start | bytes 1585160 | tf_op jit(solution)/shard_map/groups/ppermute | solution.py:87
  147.7 16.7 %collective-permute-start.11 = (bf16[1032,128]{0,1:T(8,128)(2,1)}, bf16[1032,128]{0,1:T(8,128)(2,1)}, u32[]{:S(2)}, u32[]{:S(2)}) collective-permute-start(bf16[1032,128]{0,1:T(8,128)(2,1)} %bitcast.22), channel_id=1, source_target_pairs={{0,112},{16,0},{32,16},{48,32},{64,48},{80,64},{96,80},{112,96},{1... | collective-permute-start | bytes 792584 | tf_op jit(solution)/shard_map/groups/ppermute | solution.py:90
  150.5 11.9 %collective-permute-start.10 = (bf16[1032,128]{0,1:T(8,128)(2,1)}, bf16[1032,128]{0,1:T(8,128)(2,1)}, u32[]{:S(2)}, u32[]{:S(2)}) collective-permute-start(bf16[1032,128]{0,1:T(8,128)(2,1)} %bitcast.220), channel_id=1, source_target_pairs={{0,16},{16,32},{32,48},{48,64},{64,80},{80,96},{96,112},{112,0},{1... | collective-permute-start | bytes 792584 | tf_op jit(solution)/shard_map/groups/ppermute | solution.py:89
  161.8 11.7 %copy-start.1 = (bf16[688,2048]{0,1:T(8,128)(2,1)S(1)}, bf16[688,2048]{0,1:T(8,128)(2,1)}, u32[]{:S(2)}) copy-start(bf16[688,2048]{0,1:T(8,128)(2,1)} %bitcast_dynamic-update-slice_fusion) | copy-start | bytes 8454148
  168.2 7.3 %collective-permute-start.12 = (f32[2,344,128]{2,1,0:T(8,128)S(1)}, f32[2,344,128]{2,1,0:T(8,128)S(1)}, u32[]{:S(2)}, u32[]{:S(2)}) collective-permute-start(f32[2,344,128]{2,1,0:T(8,128)S(1)} %reverse_multiply_fusion), channel_id=1, source_target_pairs={{0,1},{1,0},{2,3},{3,2},{4,5},{5,4},{6,7},{7,6},{8,9},{9,8},{10,11... | collective-permute-start | bytes 1056776 | tf_op jit(solution)/shard_map/rhs/ppermute | solution.py:24
  175.5 2.7 copy-start.2
  178.2 22.4 %all-to-all-start.3 = ((bf16[8,256,128]{2,1,0:T(8,128)(2,1)}), bf16[8,256,128]{2,1,0:T(8,128)(2,1)S(1)}, u32[]{:S(2)}, u32[]{:S(2)}) async-start(bf16[8,256,128]{2,1,0:T(8,128)(2,1)} %bitcast.73), calls=%async_computation.3 | async-start | bytes 1048576 | tf_op jit(solution)/shard_map/first/all_to_all | solution.py:28
  203.6 13.8 %all-to-all-start.4 = ((bf16[8,272,128]{2,1,0:T(8,128)(2,1)}), bf16[8,272,128]{2,1,0:T(8,128)(2,1)S(1)}, u32[]{:S(2)}, u32[]{:S(2)}) async-start(bf16[8,272,128]{2,1,0:T(8,128)(2,1)} %broadcast_in_dim.74), calls=%async_computation.4 | async-start | bytes 1114112 | tf_op jit(solution)/shard_map/first/all_to_all | solution.py:33
  220.2 6.5 %collective-permute-start.14 = (f32[2,344,128]{2,1,0:T(8,128)S(1)}, f32[2,344,128]{2,1,0:T(8,128)S(1)}, u32[]{:S(2)}, u32[]{:S(2)}) collective-permute-start(f32[2,344,128]{2,1,0:T(8,128)S(1)} %rev.14), channel_id=1, source_target_pairs={{0,1},{1,0},{2,3},{3,2},{4,5},{5,4},{6,7},{7,6},{8,9},{9,8},{10,11... | collective-permute-start | bytes 1056776 | tf_op jit(solution)/shard_map/first/ppermute | solution.py:24
  223.9 1.3 collective-permute-start.13
  262.9 7.0 %collective-permute-start.16 = (f32[2,344,128]{2,1,0:T(8,128)S(1)}, f32[2,344,128]{2,1,0:T(8,128)S(1)}, u32[]{:S(2)}, u32[]{:S(2)}) collective-permute-start(f32[2,344,128]{2,1,0:T(8,128)S(1)} %rev.15), channel_id=1, source_target_pairs={{0,1},{1,0},{2,3},{3,2},{4,5},{5,4},{6,7},{7,6},{8,9},{9,8},{10,11... | collective-permute-start | bytes 1056776 | tf_op jit(solution)/shard_map/second/ppermute | solution.py:24
  266.5 1.2 collective-permute-start.15
  270.7 50.7 %copy-start.8 = (f32[16,3]{0,1:T(4,128)S(1)}, f32[16,3]{0,1:T(4,128)}, u32[]{:S(2)}) copy-start(f32[16,3]{0,1:T(4,128)} %constant.177.clone.1) | copy-start | bytes 580
  274.4 13.9 %all-to-all-start.7 = ((bf16[8,256,128]{2,1,0:T(8,128)(2,1)}), bf16[8,256,128]{2,1,0:T(8,128)(2,1)S(1)}, u32[]{:S(2)}, u32[]{:S(2)}) async-start(bf16[8,256,128]{2,1,0:T(8,128)(2,1)} %bitcast.108), calls=%async_computation.7 | async-start | bytes 1048576 | tf_op jit(solution)/shard_map/third/all_to_all | solution.py:28
  308.4 12.9 %all-to-all-start.9 = ((f32[16,1,8]{2,1,0:T(1,128)}), f32[16,1,8]{2,1,0:T(1,128)S(1)}, u32[]{:S(2)}, u32[]{:S(2)}) async-start(f32[16,1,8]{2,1,0:T(1,128)} %broadcast_in_dim.77), calls=%async_computation.9 | async-start | bytes 16384 | tf_op jit(solution)/shard_map/whole/all_to_all | solution.py:227
  (2 other events, 1.7 us)

commit v2 on v0

v2 whole, which is shorter than its diff:
```python
import functools
import math

import jax
import jax.numpy as jnp
from jax import lax
from jax.experimental import pallas as pl
from jax.experimental.pallas import tpu as pltpu
from jax.sharding import PartitionSpec as P

norm_eps = 1e-05
damping = 0.1

bf16 = jnp.bfloat16
f32 = jnp.float32

CHIPS = [[c + 2 * i for i in range(8)] for c in range(2)]
CORE = [(i, i ^ 1) for i in range(16)]
YLO = [(i, i ^ 8) for i in range(16)]
VMEM = pl.BlockSpec(memory_space=pltpu.VMEM)
SMEM = pl.BlockSpec(memory_space=pltpu.SMEM)
UNITS = 344
BOTH = 2 * UNITS
PACK = 1040
TOKENS = 4096
HALF = TOKENS // 2


def z_shift(step):
    return [(i, (i & 8) | ((i + step) & 7)) for i in range(16)]


def swap_core(v):
    return lax.ppermute(v, "shard", CORE)


def exchange_chips(v):
    return lax.all_to_all(v, "shard", 0, 0, axis_index_groups=CHIPS, tiled=True)


def local_call(kernel, outs, *args, specs=None, **more):
    return pl.pallas_call(
        kernel,
        out_shape=outs,
        in_specs=specs or [VMEM] * len(args),
        out_specs=jax.tree.map(lambda _: VMEM, outs),
        compiler_params=pltpu.CompilerParams(vmem_limit_bytes=48 * 2**20),
        **more,
    )(*args)


def shape(dims, dtype):
    return jax.ShapeDtypeStruct(dims, dtype)


def guarded(top, bottom):
    fine = bottom > 0
    return jnp.where(fine, top / jnp.where(fine, bottom, 1.0), 0.0)


def dot(a, b):
    return jnp.dot(a, b, preferred_element_type=f32)


def total(v):
    return jnp.sum(v, axis=(0, 1), keepdims=True)


def lanes(values, dims):
    lane = lax.broadcasted_iota(jnp.int32, dims, 1)
    row = lax.broadcasted_iota(jnp.int32, dims, 0)
    out = jnp.zeros(dims, f32)
    for i, v in enumerate(values):
        out = jnp.where((lane == i) & (row == 0), v, out)
    return out


def lookup_kernel(place, train, query, table, mine, other, hot):
    height = table.shape[0]

    @pl.when(pl.program_id(0) == 0)
    def _():
        core, shard = place[0], place[1]

        def column(row):
            return jnp.broadcast_to(row, (128, 128)).T

        own_train = column(train[pl.ds(core, 1), :])
        other_train = column(train[pl.ds(1 - core, 1), :])
        asked = column(query[...])
        first = core == 0
        own_query = jnp.where(first, asked[:64], asked[64:])
        other_query = jnp.where(first, asked[64:], asked[:64])
        ids = jnp.concatenate([own_train, own_query, other_train, other_query], axis=0)
        ids = ids - shard * height
        lane = lax.broadcasted_iota(jnp.int32, ids.shape, 1)
        for start in range(0, height, 128):
            wide = min(128, height - start)
            hit = jnp.where(ids == lane + start, 1.0, 0.0).astype(bf16)
            hot[:, start : start + wide] = hit[:, :wide]

    found = dot(hot[...], table[...]).astype(bf16)
    mine[...] = found[:192]
    other[...] = found[192:]


def lookup(train_ids, query_ids, embed, core):
    height, wide = embed.shape
    step = 256
    place = jnp.stack([core, lax.axis_index("shard")])
    out = shape((192, wide), bf16)
    return pl.pallas_call(
        lookup_kernel,
        grid=(wide // step,),
        out_shape=(out, out),
        in_specs=[SMEM, VMEM, VMEM, pl.BlockSpec((height, step), lambda j: (0, j))],
        out_specs=[pl.BlockSpec((192, step), lambda j: (0, j))] * 2,
        scratch_shapes=[pltpu.VMEM((384, height), bf16)],
        compiler_params=pltpu.CompilerParams(vmem_limit_bytes=48 * 2**20),
    )(place, train_ids.reshape(2, 128), query_ids.reshape(1, 128), embed)


def norm_kernel(parts, gain, out):
    rows = jnp.sum(parts[...].astype(f32), axis=0)
    inv_scale = lax.rsqrt(jnp.mean(rows * rows, axis=-1, keepdims=True) + norm_eps)
    normed = (rows * inv_scale * gain[...]).astype(bf16)
    for i in range(8):
        out[i] = normed


def acts_kernel(normed, w_gate, w_up, w_gate_other, w_up_other, out):
    rows = normed[...]

    def hidden(gate_w, up_w):
        gate = dot(rows, gate_w[...])
        return (gate / (1.0 + jnp.exp(-gate))) * dot(rows, up_w[...])

    own = hidden(w_gate, w_up)
    other = hidden(w_gate_other, w_up_other)
    asked = jnp.concatenate([own[128:], other[128:]], axis=0)
    fill = jnp.zeros((PACK - 3 * UNITS, 128), f32)
    out[...] = jnp.concatenate([own[:128].T, other[:128].T, asked.T, fill], axis=0).astype(bf16)


def gather_groups(own):
    partner = lax.ppermute(own, "dp", YLO)
    pair = jnp.stack([own, partner])
    ups, downs = [pair], [pair]
    for _ in range(3):
        ups.append(lax.ppermute(ups[-1], "dp", z_shift(1)))
        downs.append(lax.ppermute(downs[-1], "dp", z_shift(-1)))
    last_up = lax.ppermute(ups[-1][0], "dp", z_shift(1))
    last_down = lax.ppermute(downs[-1][1], "dp", z_shift(-1))
    return pair, [pair] + [b for i in range(1, 4) for b in (ups[i], downs[i])], [last_up, last_down]


def group_order():
    me = lax.axis_index("dp")
    y, z = me // 8, me % 8
    order = []
    for step in (0, -1, 1, -2, 2, -3, 3, 4):
        for flip in range(2):
            order.append((y ^ flip) * 8 + (z + step) % 8)
    return jnp.stack(order)


def rhs_kernel(scale, *refs):
    pairs, singles, wide, part, flip, acts = refs[:7], refs[7:9], refs[9], refs[10], refs[11], refs[12]
    blocks = [(p, i) for p in pairs for i in range(2)]
    out = jnp.zeros((PACK - BOTH, 256), f32)
    for b in range(16):
        block = blocks[b][0][blocks[b][1]] if b < 14 else singles[b - 14][...]
        acts[:, b * 128 : (b + 1) * 128] = block[:BOTH]
        out = out + dot(block[BOTH:], wide[b])
    out = out * scale
    part[:UNITS] = out[:UNITS, :128]
    part[UNITS:] = out[:UNITS, 128:]
    flip[:UNITS] = out[:UNITS, 128:]
    flip[UNITS:] = out[:UNITS, :128]


def spread_tangent(res, acts, tangent):
    res_t = res.T.astype(bf16)
    for i in range(8):
        tangent[i] = dot(res_t, acts[:, i * 256 : (i + 1) * 256]).astype(bf16)


def first_kernel(part, got, acts, res_out, sums, tangent):
    res = part[...] + got[...]
    res_out[...] = res
    sums[...] = lanes([total(res * res)], (8, 128))
    spread_tangent(res, acts, tangent)


def share_kernel(parts, sums, *refs):
    earlier, (block_out, message) = refs[:-2], refs[-2:]
    block = jnp.sum(parts[...].astype(f32), axis=0).astype(bf16)
    block_out[...] = block
    block = block.astype(f32)
    values = [sums[0:1, 0:1], total(block * block)]
    if earlier:
        values.append(total(block * earlier[0][...].astype(f32)))
    extra = lanes(values, (16, 256))
    hi = extra.astype(bf16).astype(f32)
    mid = (extra - hi).astype(bf16).astype(f32)
    low = extra - hi - mid
    row = lax.broadcasted_iota(jnp.int32, (16, 256), 0)
    first_row = jnp.where(row == 0, hi, 0.0)
    mid = jnp.broadcast_to(mid[0:1], (16, 256))
    low = jnp.broadcast_to(low[0:1], (16, 256))
    extra = jnp.where(row == 1, mid, jnp.where(row == 2, low, first_row))
    whole = jnp.concatenate([block, extra], axis=0).astype(bf16)
    for i in range(8):
        message[i] = whole


def curve_kernel(got, acts, *refs):
    if len(refs) == 4:
        tangent_out, part, flip, sums_out = refs
    else:
        past, state, part, flip, sums_out = refs
    extra = got[0, 128:144, :].astype(f32)
    for i in range(1, 8):
        extra = extra + got[i, 128:144, :].astype(f32)
    sums = jnp.sum(extra, axis=0, keepdims=True)[:, :128]
    if len(refs) == 5:
        beta = guarded(sums[:, 0:1], state[0:1, 1:2])
    out = jnp.zeros((BOTH, 128), f32)
    for i in range(8):
        tangent = got[i, :128, :]
        if len(refs) == 4:
            tangent_out[i] = tangent
        else:
            tangent = (tangent.astype(f32) + beta * past[i].astype(f32)).astype(bf16)
        out = out + lax.dot_general(
            acts[:, i * 256 : (i + 1) * 256],
            tangent,
            (((1,), (1,)), ((), ())),
            preferred_element_type=f32,
        )
    row = lax.broadcasted_iota(jnp.int32, (8, 128), 0)
    sums = jnp.where(row == 0, jnp.broadcast_to(sums, (8, 128)), 0.0)
    sums_out[...] = sums
    part[...] = out
    flip[:UNITS] = out[UNITS:]
    flip[UNITS:BOTH] = out[:UNITS]
    flip[BOTH:] = sums


def second_kernel(part, got, sums, res, acts, res_out, state, tangent):
    rr = sums[0:1, 0:1]
    tt = sums[0:1, 1:2] + got[BOTH : BOTH + 1, 1:2]
    inv_alpha = guarded(tt / TOKENS + damping * rr, rr)
    alpha = guarded(jnp.ones_like(inv_alpha), inv_alpha)
    old = res[...]
    new = old - alpha * ((part[...] + got[:BOTH]) / TOKENS + damping * old)
    res_out[...] = new
    state[...] = lanes([total(new * new), rr, tt, rr, inv_alpha], (8, 128))
    spread_tangent(new, acts, tangent)


def third_kernel(part, got, sums, past, res, res_before, acts, res_out, state, tangent):
    rr = sums[0:1, 0:1]
    ww = sums[0:1, 1:2] + got[BOTH : BOTH + 1, 1:2]
    cross = sums[0:1, 2:3] + got[BOTH : BOTH + 1, 2:3]
    rr0, tt0, pp0, inv_alpha0 = (past[0:1, i : i + 1] for i in range(1, 5))
    beta = guarded(rr, rr0)
    tt = ww + 2.0 * beta * cross + beta * beta * tt0
    pp = rr + beta * beta * pp0
    inv_alpha = guarded(tt / TOKENS + damping * pp, rr)
    alpha = guarded(jnp.ones_like(inv_alpha), inv_alpha)
    old = res[...]
    direction = old + beta * res_before[...]
    new = old - alpha * ((part[...] + got[:BOTH]) / TOKENS + damping * direction)
    res_out[...] = new
    state[...] = lanes(
        [total(new * new), rr0, rr, tt, pp, inv_alpha0, inv_alpha, beta], (8, 128)
    )
    spread_tangent(new, acts, tangent)


def partial_kernel(parts, state, block0, block1, message):
    block2 = jnp.sum(parts[...].astype(f32), axis=0)
    beta = state[0:1, 7:8]
    step1 = block1[...].astype(f32) + beta * block0[...].astype(f32)
    out = lanes([0.5 * state[0:1, 0:1], total(block2 * block2), total(block2 * step1)], (8, 128))
    for i in range(16):
        message[i] = out


def group_kernel(got, state, message):
    sums = jnp.sum(jnp.sum(got[...], axis=0), axis=0, keepdims=True)
    rr0, rr1, tt1, pp1, inv_alpha0, inv_alpha1, beta0 = (state[0:1, i : i + 1] for i in range(1, 8))
    rr2 = sums[:, 0:1]
    beta1 = guarded(rr2, rr1)
    tt2 = sums[:, 1:2] + 2.0 * beta1 * sums[:, 2:3] + beta1 * beta1 * tt1
    pp2 = rr2 + beta1 * beta1 * pp1
    inv_alpha2 = guarded(tt2 / TOKENS + damping * pp2, rr2)
    out = lanes([rr0, rr1, rr2, inv_alpha0, inv_alpha1, inv_alpha2, beta0, beta1], (8, 128))
    for i in range(16):
        message[i] = out


def whole_kernel(me, got, res0, res1, res2, out):
    every = jnp.sum(got[...], axis=1)
    n0, n1, n2, ia0, ia1, ia2, b0, b1 = (every[:, i : i + 1] for i in range(8))

    def apply_whole(u):
        u0, u1, u2 = u
        s0, s1, s2 = u0 - b0 * u1, u1 - b1 * u2, u2
        return s0 * ia0, s1 * ia1 - s0 * ia0, s2 * ia2 - s1 * ia1

    def inner(u, v):
        terms = u[0] * v[0] * n0 + u[1] * v[1] * n1 + u[2] * v[2] * n2
        return jnp.sum(terms, axis=0, keepdims=True)

    zero = jnp.zeros_like(n0)
    answer = (zero, zero, zero)
    res = (jnp.ones_like(n0), zero, zero)
    direction = res
    norm_now = inner(res, res)
    for turn in range(3):
        curved = apply_whole(direction)
        step = norm_now / inner(direction, curved)
        answer = tuple(a + step * d for a, d in zip(answer, direction))
        if turn < 2:
            res = tuple(r - step * c for r, c in zip(res, curved))
            norm_next = inner(res, res)
            ratio = norm_next / norm_now
            direction = tuple(r + ratio * d for r, d in zip(res, direction))
            norm_now = norm_next
    chosen = lax.broadcasted_iota(jnp.int32, n0.shape, 0) == me[0]
    mix = [jnp.sum(jnp.where(chosen, a, 0.0), axis=0, keepdims=True) for a in answer]
    out[...] = mix[0] * res0[:UNITS] + mix[1] * res1[:UNITS] + mix[2] * res2[:UNITS]


def body(train_ids, query_ids, embed, norm_gain, w_gate, w_up, cotangent):
    core = lax.axis_index("shard") % 2
    wide = embed.shape[1]
    w_gate_other, w_up_other = swap_core(w_gate), swap_core(w_up)

    with jax.named_scope("rows"):
        mine, other = lookup(train_ids, query_ids, embed, core)
        rows = (mine + swap_core(other)).reshape(8, 24, wide)
        rows = exchange_chips(rows)
    with jax.named_scope("normed"):
        normed = local_call(norm_kernel, shape((8, 24, wide), bf16), rows, norm_gain.reshape(1, wide))
        normed = exchange_chips(normed).reshape(192, wide)
    with jax.named_scope("acts"):
        package = local_call(
            acts_kernel, shape((PACK, 128), bf16), normed, w_gate, w_up, w_gate_other, w_up_other
        )
    with jax.named_scope("groups"):
        pair, pairs, singles = gather_groups(package)
    with jax.named_scope("cotangent"):
        cotangent, _ = lax.optimization_barrier((cotangent, pair))
        mine = lax.dynamic_slice_in_dim(cotangent, core * 64, 64, axis=0)
        columns = lax.all_to_all(
            mine.reshape(64, 16, 128).transpose(1, 0, 2), "dp", 0, 0, tiled=True
        )
        columns = jnp.take(columns, group_order(), axis=0)
        empty = jnp.zeros_like(columns)
        columns = jnp.concatenate(
            [
                jnp.concatenate([columns, empty], axis=2),
                jnp.concatenate([empty, columns], axis=2),
            ],
            axis=1,
        )

    vector = shape((BOTH, 128), f32)
    longer = shape((BOTH + 8, 128), f32)
    small = shape((8, 128), f32)
    spread = shape((8, 128, 256), bf16)
    block = shape((128, 256), bf16)
    message = shape((8, 144, 256), bf16)
    table = shape((16, 8, 128), f32)

    with jax.named_scope("rhs"):
        part, flip, acts = local_call(
            functools.partial(rhs_kernel, 1.0 / math.sqrt(2048)),
            (vector, vector, shape((BOTH, HALF), bf16)),
            *pairs,
            *singles,
            columns,
        )
        got = swap_core(flip)
    with jax.named_scope("first"):
        res0, sums, tangent = local_call(first_kernel, (vector, small, spread), part, got, acts)
        parts = exchange_chips(tangent)
        block0, shared = local_call(share_kernel, (block, message), parts, sums)
        shared = exchange_chips(shared)
        tangent0, part, flip, sums = local_call(
            curve_kernel, (spread, vector, longer, small), shared, acts
        )
        got = swap_core(flip)
    with jax.named_scope("second"):
        res1, state, tangent = local_call(
            second_kernel, (vector, small, spread), part, got, sums, res0, acts
        )
        parts = exchange_chips(tangent)
        block1, shared = local_call(share_kernel, (block, message), parts, state, block0)
        shared = exchange_chips(shared)
        past = state
        part, flip, sums = local_call(
            curve_kernel, (vector, longer, small), shared, acts, tangent0, state
        )
        got = swap_core(flip)
    with jax.named_scope("third"):
        res2, state, tangent = local_call(
            third_kernel, (vector, small, spread), part, got, sums, past, res1, res0, acts
        )
        parts = exchange_chips(tangent)
        partials = local_call(partial_kernel, table, parts, state, block0, block1)
        partials = lax.all_to_all(partials, "shard", 0, 0, tiled=True)
    with jax.named_scope("whole"):
        mine = local_call(group_kernel, table, partials, state)
        every = lax.all_to_all(mine, "dp", 0, 0, tiled=True)
        return local_call(
            whole_kernel,
            shape((UNITS, 128), f32),
            lax.axis_index("dp").reshape(1),
            every,
            res0,
            res1,
            res2,
            specs=[SMEM] + [VMEM] * 4,
        )


def solution(mesh):
    placed = (
        P("dp"),
        P("dp"),
        P("shard", None),
        P(),
        P(None, "shard"),
        P(None, "shard"),
        P("dp", None),
    )
    return jax.shard_map(
        body, mesh=mesh, in_specs=placed, out_specs=P("shard", "dp"), check_vma=False
    )
```

time: 1310 us -> 239 us (0.18)
  blocking collectives: 653 us -> 108 us
  waiting for transfers between devices: 583 us -> 42.8 us
  starting transfers between devices: 0.29 us -> 44 us
  matrix products: 24.9 us -> 0 us
  Pallas kernels: 0 us -> 24.4 us
  between operations: 20.5 us -> 0.21 us
  other arithmetic: 18 us -> 0.62 us
    psum x8 -> x0, blocking collectives: 653 us -> none  [the longest x5 400 us: global_total(): return lax.psum(value, ('dp', 'shard'))]
    reduce_scatter x4 -> x0, waiting for transfers between devices: 268 us -> none  [column_share(): lax.psum_scatter(partial_terms, 'dp', scatter_dimension=1, tiled=True)]
    all_gather x3 -> x0, waiting for transfers between devices: 164 us -> none  [body(): lax.all_gather(direction.astype(jnp.bfloat16), 'dp', axis=1, tiled=True)]
    psum x1 -> x0, waiting for transfers between devices: 151 us -> none  [body(): lax.psum(query_part.astype(jnp.bfloat16), 'shard').astype(jnp.float32)]
    all_to_all x0 -> x8, blocking collectives: none -> 108 us  [the longest x6 85.6 us: exchange_chips(): return lax.all_to_all(v, 'shard', 0, 0, axis_index_groups=CHIPS, tiled=True)]
    ppermute x0 -> x15, waiting for transfers between devices: none -> 36.7 us  [the longest x3 16.9 us: gather_groups(): downs.append(lax.ppermute(downs[-1], 'dp', z_shift(-1)))]
    ppermute x0 -> x15, starting transfers between devices: none -> 36 us  [the longest x6 19.3 us: swap_core(): return lax.ppermute(v, 'shard', CORE)]
    dot_general x10 -> x0, matrix products: 24.9 us -> none  [the longest x3 10.3 us: body(): jnp.dot(hidden_vals, lax.all_gather(direction.astype(jnp.bfloat16), 'dp',...]
  transfers between devices with their start and end apart: 8 -> 17, of which waited for: 8 -> 12; matrix products, arithmetic and copies ran while one was open for 0% -> 5% of each run, Pallas kernels for 0% -> 0%
where the time goes in v2:
time: 239 us; the launch traced here: 238 us
  blocking collectives  108 us (45%)
  starting transfers between devices  44 us (18%)
  waiting for transfers between devices  42.8 us (18%)
  Pallas kernels  24.4 us (10%)
  local copies, waits for them, and re-layouts  18.1 us (8%)
    all_to_all x6, blocking collectives, exchange_chips(): return lax.all_to_all(v, 'shard', 0, 0, axis_index_groups=CHIPS, tiled=True)  85.6 us
    ppermute x6, starting transfers between devices, swap_core(): return lax.ppermute(v, 'shard', CORE)  19.3 us
    ppermute x3, waiting for transfers between devices, gather_groups(): downs.append(lax.ppermute(downs[-1], 'dp', z_shift(-1)))  16.9 us
    pallas_call x13, Pallas kernels, local_call(): pl.pallas_call(kernel, out_shape=outs, in_specs=specs or [VMEM] * len(arg...  15.9 us
    ppermute x3, starting transfers between devices, gather_groups(): downs.append(lax.ppermute(downs[-1], 'dp', z_shift(-1)))  12.6 us
    all_to_all x1, blocking collectives, body(): partials = lax.all_to_all(partials, 'shard', 0, 0, tiled=True)  12.2 us
    unnamed x18, local copies, waits for them, and re-layouts  10.4 us
    all_to_all x1, blocking collectives, body(): every = lax.all_to_all(mine, 'dp', 0, 0, tiled=True)  10.1 us
  transfers between devices with their start and end apart: 17, of which 12 were waited for; matrix products, arithmetic and copies ran while one was open for 5% of the time, Pallas kernels for 0%

profile of v2, /device:TPU:1, one launch (start us, length us, event | category | flops | bytes accessed | tf_op | source)
XLA Modules:
  0.0 238.0 jit_solution(8546337541847692650)
XLA Ops:
  1.5 8.5 %rows.1 = (bf16[192,2048]{1,0:T(8,128)(2,1)S(1)}, bf16[192,2048]{1,0:T(8,128)(2,1)S(1)}) custom-call(s32[2]{0:T(128)S(1)} %pad_add_fusion.place, s32[2,128]{1,0:T(2,128)S(1)} %bitcast.58, s32[1,128]{1,0:T(1,128)S(1)} %bitcast.59, bf16[2000,2048]{1,0:T(8,128)(2,1)} %table.1), custom_call_target="tpu_custom_call" | custom-call | tf_op jit(solution)/shard_map/rows/pallas_call | solution.py:112
  10.0 3.3 %collective-permute-start = (bf16[192,2048]{1,0:T(8,128)(2,1)S(1)}, bf16[192,2048]{1,0:T(8,128)(2,1)S(1)}, u32[]{:S(2)}, u32[]{:S(2)}) collective-permute-start(bf16[192,2048]{1,0:T(8,128)(2,1)S(1)} %get-tuple-element.32), channel_id=1, source_target_pairs={{0,1},{1,0},{2,3},{3,2},{4,5},{5,4},{6,7},{7,6},{8,9},{9,8},{10,11... | collective-permute-start | bytes 2359304 | tf_op jit(solution)/shard_map/rows/ppermute | solution.py:34
  15.6 17.5 %all_to_all.50.parts = bf16[8,24,2048]{2,1,0:T(8,128)(2,1)S(1)} all-to-all(bf16[8,24,2048]{2,1,0:T(8,128)(2,1)S(1)} %bitcast.60), channel_id=1, replica_groups={{0,2,4,6,8,10,12,14},{1,3,5,7,9,11,13,15},{16,18,20,22,24,26,28,30},{17..., dimensions={0} | all-to-all | bytes 1572864 | tf_op jit(solution)/shard_map/rows/all_to_all | solution.py:38
  34.3 3.9 %all-to-all-start.1 = ((bf16[8,24,2048]{2,1,0:T(8,128)(2,1)}), bf16[8,24,2048]{2,1,0:T(8,128)(2,1)S(1)}, u32[]{:S(2)}, u32[]{:S(2)}) async-start(bf16[8,24,2048]{2,1,0:T(8,128)(2,1)} %normed.1), calls=%async_computation.1 | async-start | bytes 1572864 | tf_op jit(solution)/shard_map/normed/all_to_all | solution.py:38
  38.1 1.8 copy.21.w_gate
  40.0 2.6 %copy.22.w_up = bf16[2048,344]{1,0:T(8,128)(2,1)} copy(bf16[2048,344]{0,1:T(8,128)(2,1)} %param.12) | data formatting | bytes 2818048 | tf_op args[5]
  42.6 2.6 %copy.23.w_gate_other = bf16[2048,344]{1,0:T(8,128)(2,1)} copy(bf16[2048,344]{0,1:T(8,128)(2,1)} %collective-permute-done.1) | data formatting | bytes 2818048 | tf_op jit(solution)/shard_map/ppermute | solution.py:34
  45.1 2.6 %copy.24.w_up_other = bf16[2048,344]{1,0:T(8,128)(2,1)} copy(bf16[2048,344]{0,1:T(8,128)(2,1)} %collective-permute-done.2) | data formatting | bytes 2818048 | tf_op jit(solution)/shard_map/ppermute | solution.py:34
  47.7 2.4 %all-to-all-done.1 = bf16[8,24,2048]{2,1,0:T(8,128)(2,1)S(1)} async-done(((bf16[8,24,2048]{2,1,0:T(8,128)(2,1)}), bf16[8,24,2048]{2,1,0:T(8,128)(2,1)S(1)}, u32[]{:S(2)}, u32[]{:S(2)}) %all-to-all-start.1) | async-done | bytes 786464 | tf_op jit(solution)/shard_map/normed/all_to_all | solution.py:38
  52.9 3.3 %acts.1 = bf16[1040,128]{1,0:T(8,128)(2,1)S(1)} custom-call(bf16[192,2048]{1,0:T(8,128)(2,1)S(1)} %bitcast.55, bf16[2048,344]{1,0:T(8,128)(2,1)S(1)} %copy.21.w_gate, bf16[2048,344]{1,0:T(8,128)(2,1)S(1)} %copy-done.3, bf16[2048,344]{1,0:T(8,128)(2,1)S(1)} %copy-done.4, bf16[2048,344]{1,0:T(8,128)(2,1)} %copy.24.w_up_other), custom_call_target="tpu_custom_call" | custom-call | tf_op jit(solution)/shard_map/acts/pallas_call | solution.py:42
  56.7 4.9 %collective-permute-done.3 = bf16[1040,128]{1,0:T(8,128)(2,1)S(1)} collective-permute-done((bf16[1040,128]{1,0:T(8,128)(2,1)S(1)}, bf16[1040,128]{1,0:T(8,128)(2,1)S(1)}, u32[]{:S(2)}, u32[]{:S(2)}) %collective-permute-start.3) | collective-permute-done | bytes 266272 | tf_op jit(solution)/shard_map/groups/ppermute | solution.py:146
  61.6 5.7 %collective-permute-start.5 = (bf16[2,1040,128]{2,1,0:T(8,128)(2,1)S(1)}, bf16[2,1040,128]{2,1,0:T(8,128)(2,1)S(1)}, u32[]{:S(2)}, u32[]{:S(2)}) collective-permute-start(bf16[2,1040,128]{2,1,0:T(8,128)(2,1)S(1)} %pad_maximum_fusion.refs_0_), channel_id=1, source_target_pairs={{0,112},{16,0},{32,16},{48,32},{64,48},{80,64},{96,80},{112,96},{1... | collective-permute-start | bytes 1597448 | tf_op jit(solution)/shard_map/groups/ppermute | solution.py:151
  67.3 7.8 %collective-permute-done.5.refs_2_ = bf16[2,1040,128]{2,1,0:T(8,128)(2,1)S(1)} collective-permute-done((bf16[2,1040,128]{2,1,0:T(8,128)(2,1)S(1)}, bf16[2,1040,128]{2,1,0:T(8,128)(2,1)S(1)}, u32[]{:S(2)}, u32[]{:S(2)}) %collective-permute-start.5) | collective-permute-done | bytes 532512 | tf_op jit(solution)/shard_map/groups/ppermute | solution.py:151
  75.1 3.4 %collective-permute-start.7 = (bf16[2,1040,128]{2,1,0:T(8,128)(2,1)S(1)}, bf16[2,1040,128]{2,1,0:T(8,128)(2,1)}, u32[]{:S(2)}, u32[]{:S(2)}) collective-permute-start(bf16[2,1040,128]{2,1,0:T(8,128)(2,1)S(1)} %collective-permute-done.5.refs_2_), channel_id=1, source_target_pairs={{0,112},{16,0},{32,16},{48,32},{64,48},{80,64},{96,80},{112,96},{1... | collective-permute-start | bytes 1597448 | tf_op jit(solution)/shard_map/groups/ppermute | solution.py:151
  79.6 4.2 %all-to-all-start.2 = ((bf16[16,64,128]{2,1,0:T(8,128)(2,1)}), bf16[16,64,128]{2,1,0:T(8,128)(2,1)}, u32[]{:S(2)}, u32[]{:S(2)}) async-start(bf16[16,64,128]{2,1,0:T(8,128)(2,1)} %bitcast_bitcast_fusion), calls=%async_computation.2 | async-start | bytes 524288 | tf_op jit(solution)/shard_map/cotangent/all_to_all | solution.py:358
  85.6 3.5 %collective-permute-start.9 = (bf16[2,1040,128]{2,1,0:T(8,128)(2,1)}, bf16[2,1040,128]{2,1,0:T(8,128)(2,1)S(1)}, u32[]{:S(2)}, u32[]{:S(2)}) collective-permute-start(bf16[2,1040,128]{2,1,0:T(8,128)(2,1)} %collective-permute-done.7.refs_4_), channel_id=1, source_target_pairs={{0,112},{16,0},{32,16},{48,32},{64,48},{80,64},{96,80},{112,96},{1... | collective-permute-start | bytes 1597448 | tf_op jit(solution)/shard_map/groups/ppermute | solution.py:151
  89.5 3.7 %all-to-all-done.2 = bf16[16,64,128]{2,1,0:T(8,128)(2,1)} async-done(((bf16[16,64,128]{2,1,0:T(8,128)(2,1)}), bf16[16,64,128]{2,1,0:T(8,128)(2,1)}, u32[]{:S(2)}, u32[]{:S(2)}) %all-to-all-start.2) | async-done | bytes 262176 | tf_op jit(solution)/shard_map/cotangent/all_to_all | solution.py:358
  94.7 7.3 %collective-permute-done.9.refs_6_ = bf16[2,1040,128]{2,1,0:T(8,128)(2,1)S(1)} collective-permute-done((bf16[2,1040,128]{2,1,0:T(8,128)(2,1)}, bf16[2,1040,128]{2,1,0:T(8,128)(2,1)S(1)}, u32[]{:S(2)}, u32[]{:S(2)}) %collective-permute-start.9) | collective-permute-done | bytes 532512 | tf_op jit(solution)/shard_map/groups/ppermute | solution.py:151
  102.1 3.1 %collective-permute-start.11 = (bf16[1040,128]{1,0:T(8,128)(2,1)S(1)}, bf16[1040,128]{1,0:T(8,128)(2,1)S(1)}, u32[]{:S(2)}, u32[]{:S(2)}) collective-permute-start(bf16[1040,128]{1,0:T(8,128)(2,1)S(1)} %slice_bitcast_fusion), channel_id=1, source_target_pairs={{0,112},{16,0},{32,16},{48,32},{64,48},{80,64},{96,80},{112,96},{1... | collective-permute-start | bytes 798728 | tf_op jit(solution)/shard_map/groups/ppermute | solution.py:153
  105.5 5.9 %collective-permute-done.11.refs_8_ = bf16[1040,128]{1,0:T(8,128)(2,1)S(1)} collective-permute-done((bf16[1040,128]{1,0:T(8,128)(2,1)S(1)}, bf16[1040,128]{1,0:T(8,128)(2,1)S(1)}, u32[]{:S(2)}, u32[]{:S(2)}) %collective-permute-start.11) | collective-permute-done | bytes 266272 | tf_op jit(solution)/shard_map/groups/ppermute | solution.py:153
  111.4 3.5 %collective-permute-done.10.refs_7_ = bf16[1040,128]{1,0:T(8,128)(2,1)S(1)} collective-permute-done((bf16[1040,128]{1,0:T(8,128)(2,1)S(1)}, bf16[1040,128]{1,0:T(8,128)(2,1)S(1)}, u32[]{:S(2)}, u32[]{:S(2)}) %collective-permute-start.10) | collective-permute-done | bytes 266272 | tf_op jit(solution)/shard_map/groups/ppermute | solution.py:152
  114.9 4.4 %rhs.1 = (f32[688,128]{1,0:T(8,128)S(1)}, f32[688,128]{1,0:T(8,128)S(1)}, bf16[688,2048]{1,0:T(8,128)(2,1)}) custom-call(bf16[2,1040,128]{2,1,0:T(8,128)(2,1)S(1)} %pad_maximum_fusion.refs_0_, bf16[2,1040,128]{2,1,0:T(8,128)(2,1)S(1)} %collective-permute-done.4.refs_1_, bf16[2,1040,128]{2,1,0:T(8,128)(2,1)S(1)} %collective-permute-done.5.refs_2_, ...), custom_call_target="tpu_custom_call" | custom-call | tf_op jit(solution)/shard_map/rhs/pallas_call | solution.py:42
  119.3 9.5 %collective-permute-start.12 = (f32[688,128]{1,0:T(8,128)S(1)}, f32[688,128]{1,0:T(8,128)S(1)}, u32[]{:S(2)}, u32[]{:S(2)}) collective-permute-start(f32[688,128]{1,0:T(8,128)S(1)} %get-tuple-element.35), channel_id=1, source_target_pairs={{0,1},{1,0},{2,3},{3,2},{4,5},{5,4},{6,7},{7,6},{8,9},{9,8},{10,11... | collective-permute-start | bytes 1056776 | tf_op jit(solution)/shard_map/rhs/ppermute | solution.py:34
  132.5 15.2 %all_to_all.51.parts = bf16[8,128,256]{2,1,0:T(8,128)(2,1)S(1)} all-to-all(bf16[8,128,256]{2,1,0:T(8,128)(2,1)S(1)} %get-tuple-element.37), channel_id=1, replica_groups={{0,2,4,6,8,10,12,14},{1,3,5,7,9,11,13,15},{16,18,20,22,24,26,28,30},{17..., dimensions={0} | all-to-all | bytes 1048576 | tf_op jit(solution)/shard_map/first/all_to_all | solution.py:38
  148.0 14.0 %all_to_all.52.got = bf16[8,144,256]{2,1,0:T(8,128)(2,1)S(1)} all-to-all(bf16[8,144,256]{2,1,0:T(8,128)(2,1)S(1)} %get-tuple-element.39), channel_id=1, replica_groups={{0,2,4,6,8,10,12,14},{1,3,5,7,9,11,13,15},{16,18,20,22,24,26,28,30},{17..., dimensions={0} | all-to-all | bytes 1179648 | tf_op jit(solution)/shard_map/first/all_to_all | solution.py:38
  163.0 3.0 %collective-permute-start.13 = (f32[696,128]{1,0:T(8,128)S(1)}, f32[696,128]{1,0:T(8,128)S(1)}, u32[]{:S(2)}, u32[]{:S(2)}) collective-permute-start(f32[696,128]{1,0:T(8,128)S(1)} %get-tuple-element.41), channel_id=1, source_target_pairs={{0,1},{1,0},{2,3},{3,2},{4,5},{5,4},{6,7},{7,6},{8,9},{9,8},{10,11... | collective-permute-start | bytes 1069064 | tf_op jit(solution)/shard_map/first/ppermute | solution.py:34
  168.1 12.7 %all_to_all.53.parts = bf16[8,128,256]{2,1,0:T(8,128)(2,1)S(1)} all-to-all(bf16[8,128,256]{2,1,0:T(8,128)(2,1)S(1)} %get-tuple-element.44), channel_id=1, replica_groups={{0,2,4,6,8,10,12,14},{1,3,5,7,9,11,13,15},{16,18,20,22,24,26,28,30},{17..., dimensions={0} | all-to-all | bytes 1048576 | tf_op jit(solution)/shard_map/second/all_to_all | solution.py:38
  181.0 13.5 %all_to_all.54.got = bf16[8,144,256]{2,1,0:T(8,128)(2,1)S(1)} all-to-all(bf16[8,144,256]{2,1,0:T(8,128)(2,1)S(1)} %get-tuple-element.47), channel_id=1, replica_groups={{0,2,4,6,8,10,12,14},{1,3,5,7,9,11,13,15},{16,18,20,22,24,26,28,30},{17..., dimensions={0} | all-to-all | bytes 1179648 | tf_op jit(solution)/shard_map/second/all_to_all | solution.py:38
  195.7 3.1 %collective-permute-start.14 = (f32[696,128]{1,0:T(8,128)S(1)}, f32[696,128]{1,0:T(8,128)S(1)}, u32[]{:S(2)}, u32[]{:S(2)}) collective-permute-start(f32[696,128]{1,0:T(8,128)S(1)} %get-tuple-element.50), channel_id=1, source_target_pairs={{0,1},{1,0},{2,3},{3,2},{4,5},{5,4},{6,7},{7,6},{8,9},{9,8},{10,11... | collective-permute-start | bytes 1069064 | tf_op jit(solution)/shard_map/second/ppermute | solution.py:34
  201.2 12.7 %all_to_all.55.parts = bf16[8,128,256]{2,1,0:T(8,128)(2,1)S(1)} all-to-all(bf16[8,128,256]{2,1,0:T(8,128)(2,1)S(1)} %get-tuple-element.53), channel_id=1, replica_groups={{0,2,4,6,8,10,12,14},{1,3,5,7,9,11,13,15},{16,18,20,22,24,26,28,30},{17..., dimensions={0} | all-to-all | bytes 1048576 | tf_op jit(solution)/shard_map/third/all_to_all | solution.py:38
  214.2 12.2 %all_to_all.56.got = f32[16,8,128]{2,1,0:T(8,128)S(1)} all-to-all(f32[16,8,128]{2,1,0:T(8,128)S(1)} %third.3), channel_id=1, replica_groups=mesh['dp'=16,'shard'=16] {'shard'}, dimensions={0} | all-to-all | bytes 131072 | tf_op jit(solution)/shard_map/third/all_to_all | solution.py:415
  226.7 10.1 %all_to_all.57.got = f32[16,8,128]{2,1,0:T(8,128)S(1)} all-to-all(f32[16,8,128]{2,1,0:T(8,128)S(1)} %whole.2), channel_id=1, replica_groups=mesh['dp'=16,'shard'=16] {'dp'}, dimensions={0} | all-to-all | bytes 131072 | tf_op jit(solution)/shard_map/whole/all_to_all | solution.py:418
  (58 shorter events, 26.0 us)
Async XLA Ops:
  0.0 78.8 %copy-start = (bf16[128,2048]{1,0:T(8,128)(2,1)S(1)}, bf16[128,2048]{1,0:T(8,128)(2,1)}, u32[]{:S(2)}) copy-start(bf16[128,2048]{1,0:T(8,128)(2,1)} %param.13) | copy-start | bytes 1572868
  0.1 0.7 copy-start.6
  0.8 0.7 copy-start.7
  10.0 23.1 %copy-start.5 = (f32[2048]{0:T(1024)S(1)}, f32[2048]{0:T(1024)}, u32[]{:S(2)}) copy-start(f32[2048]{0:T(1024)} %param.10) | copy-start | bytes 24580
  10.0 5.4 %collective-permute-start = (bf16[192,2048]{1,0:T(8,128)(2,1)S(1)}, bf16[192,2048]{1,0:T(8,128)(2,1)S(1)}, u32[]{:S(2)}, u32[]{:S(2)}) collective-permute-start(bf16[192,2048]{1,0:T(8,128)(2,1)S(1)} %get-tuple-element.32), channel_id=1, source_target_pairs={{0,1},{1,0},{2,3},{3,2},{4,5},{5,4},{6,7},{7,6},{8,9},{9,8},{10,11... | collective-permute-start | bytes 2359304 | tf_op jit(solution)/shard_map/rows/ppermute | solution.py:34
  13.3 29.2 %collective-permute-start.1 = (bf16[2048,344]{0,1:T(8,128)(2,1)}, bf16[2048,344]{0,1:T(8,128)(2,1)}, u32[]{:S(2)}, u32[]{:S(2)}) collective-permute-start(bf16[2048,344]{0,1:T(8,128)(2,1)} %param.11), channel_id=1, source_target_pairs={{0,1},{1,0},{2,3},{3,2},{4,5},{5,4},{6,7},{7,6},{8,9},{9,8},{10,11... | collective-permute-start | bytes 4227080 | tf_op jit(solution)/shard_map/ppermute | solution.py:34
  13.4 31.7 %collective-permute-start.2 = (bf16[2048,344]{0,1:T(8,128)(2,1)}, bf16[2048,344]{0,1:T(8,128)(2,1)}, u32[]{:S(2)}, u32[]{:S(2)}) collective-permute-start(bf16[2048,344]{0,1:T(8,128)(2,1)} %param.12), channel_id=1, source_target_pairs={{0,1},{1,0},{2,3},{3,2},{4,5},{5,4},{6,7},{7,6},{8,9},{9,8},{10,11... | collective-permute-start | bytes 4227080 | tf_op jit(solution)/shard_map/ppermute | solution.py:34
  34.3 15.9 %all-to-all-start.1 = ((bf16[8,24,2048]{2,1,0:T(8,128)(2,1)}), bf16[8,24,2048]{2,1,0:T(8,128)(2,1)S(1)}, u32[]{:S(2)}, u32[]{:S(2)}) async-start(bf16[8,24,2048]{2,1,0:T(8,128)(2,1)} %normed.1), calls=%async_computation.1 | async-start | bytes 1572864 | tf_op jit(solution)/shard_map/normed/all_to_all | solution.py:38
  50.1 1.4 copy-start.3
  51.5 1.4 copy-start.4
  56.2 5.4 %collective-permute-start.3 = (bf16[1040,128]{1,0:T(8,128)(2,1)S(1)}, bf16[1040,128]{1,0:T(8,128)(2,1)S(1)}, u32[]{:S(2)}, u32[]{:S(2)}) collective-permute-start(bf16[1040,128]{1,0:T(8,128)(2,1)S(1)} %acts.1), channel_id=1, source_target_pairs={{0,128},{16,144},{32,160},{48,176},{64,192},{80,208},{96,224},{112... | collective-permute-start | bytes 798728 | tf_op jit(solution)/shard_map/groups/ppermute | solution.py:146
  61.6 13.4 %collective-permute-start.5 = (bf16[2,1040,128]{2,1,0:T(8,128)(2,1)S(1)}, bf16[2,1040,128]{2,1,0:T(8,128)(2,1)S(1)}, u32[]{:S(2)}, u32[]{:S(2)}) collective-permute-start(bf16[2,1040,128]{2,1,0:T(8,128)(2,1)S(1)} %pad_maximum_fusion.refs_0_), channel_id=1, source_target_pairs={{0,112},{16,0},{32,16},{48,32},{64,48},{80,64},{96,80},{112,96},{1... | collective-permute-start | bytes 1597448 | tf_op jit(solution)/shard_map/groups/ppermute | solution.py:151
  67.3 11.4 %collective-permute-start.4 = (bf16[2,1040,128]{2,1,0:T(8,128)(2,1)S(1)}, bf16[2,1040,128]{2,1,0:T(8,128)(2,1)S(1)}, u32[]{:S(2)}, u32[]{:S(2)}) collective-permute-start(bf16[2,1040,128]{2,1,0:T(8,128)(2,1)S(1)} %pad_maximum_fusion.refs_0_), channel_id=1, source_target_pairs={{0,16},{16,32},{32,48},{48,64},{64,80},{80,96},{96,112},{112,0},{1... | collective-permute-start | bytes 1597448 | tf_op jit(solution)/shard_map/groups/ppermute | solution.py:150
  75.1 10.6 %collective-permute-start.7 = (bf16[2,1040,128]{2,1,0:T(8,128)(2,1)S(1)}, bf16[2,1040,128]{2,1,0:T(8,128)(2,1)}, u32[]{:S(2)}, u32[]{:S(2)}) collective-permute-start(bf16[2,1040,128]{2,1,0:T(8,128)(2,1)S(1)} %collective-permute-done.5.refs_2_), channel_id=1, source_target_pairs={{0,112},{16,0},{32,16},{48,32},{64,48},{80,64},{96,80},{112,96},{1... | collective-permute-start | bytes 1597448 | tf_op jit(solution)/shard_map/groups/ppermute | solution.py:151
  78.7 10.5 %collective-permute-start.6 = (bf16[2,1040,128]{2,1,0:T(8,128)(2,1)S(1)}, bf16[2,1040,128]{2,1,0:T(8,128)(2,1)}, u32[]{:S(2)}, u32[]{:S(2)}) collective-permute-start(bf16[2,1040,128]{2,1,0:T(8,128)(2,1)S(1)} %collective-permute-done.4.refs_1_), channel_id=1, source_target_pairs={{0,16},{16,32},{32,48},{48,64},{64,80},{80,96},{96,112},{112,0},{1... | collective-permute-start | bytes 1597448 | tf_op jit(solution)/shard_map/groups/ppermute | solution.py:150
  79.6 13.6 %all-to-all-start.2 = ((bf16[16,64,128]{2,1,0:T(8,128)(2,1)}), bf16[16,64,128]{2,1,0:T(8,128)(2,1)}, u32[]{:S(2)}, u32[]{:S(2)}) async-start(bf16[16,64,128]{2,1,0:T(8,128)(2,1)} %bitcast_bitcast_fusion), calls=%async_computation.2 | async-start | bytes 524288 | tf_op jit(solution)/shard_map/cotangent/all_to_all | solution.py:358
  85.6 16.4 %collective-permute-start.9 = (bf16[2,1040,128]{2,1,0:T(8,128)(2,1)}, bf16[2,1040,128]{2,1,0:T(8,128)(2,1)S(1)}, u32[]{:S(2)}, u32[]{:S(2)}) collective-permute-start(bf16[2,1040,128]{2,1,0:T(8,128)(2,1)} %collective-permute-done.7.refs_4_), channel_id=1, source_target_pairs={{0,112},{16,0},{32,16},{48,32},{64,48},{80,64},{96,80},{112,96},{1... | collective-permute-start | bytes 1597448 | tf_op jit(solution)/shard_map/groups/ppermute | solution.py:151
  89.2 16.0 %collective-permute-start.8 = (bf16[2,1040,128]{2,1,0:T(8,128)(2,1)}, bf16[2,1040,128]{2,1,0:T(8,128)(2,1)S(1)}, u32[]{:S(2)}, u32[]{:S(2)}) collective-permute-start(bf16[2,1040,128]{2,1,0:T(8,128)(2,1)} %collective-permute-done.6.refs_3_), channel_id=1, source_target_pairs={{0,16},{16,32},{32,48},{48,64},{64,80},{80,96},{96,112},{112,0},{1... | collective-permute-start | bytes 1597448 | tf_op jit(solution)/shard_map/groups/ppermute | solution.py:150
  102.1 9.4 %collective-permute-start.11 = (bf16[1040,128]{1,0:T(8,128)(2,1)S(1)}, bf16[1040,128]{1,0:T(8,128)(2,1)S(1)}, u32[]{:S(2)}, u32[]{:S(2)}) collective-permute-start(bf16[1040,128]{1,0:T(8,128)(2,1)S(1)} %slice_bitcast_fusion), channel_id=1, source_target_pairs={{0,112},{16,0},{32,16},{48,32},{64,48},{80,64},{96,80},{112,96},{1... | collective-permute-start | bytes 798728 | tf_op jit(solution)/shard_map/groups/ppermute | solution.py:153
  105.2 9.8 %collective-permute-start.10 = (bf16[1040,128]{1,0:T(8,128)(2,1)S(1)}, bf16[1040,128]{1,0:T(8,128)(2,1)S(1)}, u32[]{:S(2)}, u32[]{:S(2)}) collective-permute-start(bf16[1040,128]{1,0:T(8,128)(2,1)S(1)} %slice_bitcast_fusion.1), channel_id=1, source_target_pairs={{0,16},{16,32},{32,48},{48,64},{64,80},{80,96},{96,112},{112,0},{1... | collective-permute-start | bytes 798728 | tf_op jit(solution)/shard_map/groups/ppermute | solution.py:152
  119.3 10.7 %collective-permute-start.12 = (f32[688,128]{1,0:T(8,128)S(1)}, f32[688,128]{1,0:T(8,128)S(1)}, u32[]{:S(2)}, u32[]{:S(2)}) collective-permute-start(f32[688,128]{1,0:T(8,128)S(1)} %get-tuple-element.35), channel_id=1, source_target_pairs={{0,1},{1,0},{2,3},{3,2},{4,5},{5,4},{6,7},{7,6},{8,9},{9,8},{10,11... | collective-permute-start | bytes 1056776 | tf_op jit(solution)/shard_map/rhs/ppermute | solution.py:34
  130.1 1.8 copy-start.1
  131.9 30.2 %copy-start.2 = (bf16[688,2048]{1,0:T(8,128)(2,1)S(1)}, bf16[688,2048]{1,0:T(8,128)(2,1)}, u32[]{:S(2)}) copy-start(bf16[688,2048]{1,0:T(8,128)(2,1)} %get-tuple-element.36.acts) | copy-start | bytes 8454148
  163.0 4.3 %collective-permute-start.13 = (f32[696,128]{1,0:T(8,128)S(1)}, f32[696,128]{1,0:T(8,128)S(1)}, u32[]{:S(2)}, u32[]{:S(2)}) collective-permute-start(f32[696,128]{1,0:T(8,128)S(1)} %get-tuple-element.41), channel_id=1, source_target_pairs={{0,1},{1,0},{2,3},{3,2},{4,5},{5,4},{6,7},{7,6},{8,9},{9,8},{10,11... | collective-permute-start | bytes 1069064 | tf_op jit(solution)/shard_map/first/ppermute | solution.py:34
  195.7 4.4 %collective-permute-start.14 = (f32[696,128]{1,0:T(8,128)S(1)}, f32[696,128]{1,0:T(8,128)S(1)}, u32[]{:S(2)}, u32[]{:S(2)}) collective-permute-start(f32[696,128]{1,0:T(8,128)S(1)} %get-tuple-element.50), channel_id=1, source_target_pairs={{0,1},{1,0},{2,3},{3,2},{4,5},{5,4},{6,7},{7,6},{8,9},{9,8},{10,11... | collective-permute-start | bytes 1069064 | tf_op jit(solution)/shard_map/second/ppermute | solution.py:34

commit v3 on v2

--- a/solution.py
+++ b/solution.py
@@ -14,6 +14,7 @@
 bf16 = jnp.bfloat16
 f32 = jnp.float32
 
+STEPS = (0, -1, 1, -2, 2, -3, 3, 4)
 CHIPS = [[c + 2 * i for i in range(8)] for c in range(2)]
 CORE = [(i, i ^ 1) for i in range(16)]
 YLO = [(i, i ^ 8) for i in range(16)]
@@ -23,7 +24,6 @@
 BOTH = 2 * UNITS
 PACK = 1040
 TOKENS = 4096
-HALF = TOKENS // 2
 
 
 def z_shift(step):
@@ -44,7 +44,7 @@
         out_shape=outs,
         in_specs=specs or [VMEM] * len(args),
         out_specs=jax.tree.map(lambda _: VMEM, outs),
-        compiler_params=pltpu.CompilerParams(vmem_limit_bytes=48 * 2**20),
+        compiler_params=pltpu.CompilerParams(vmem_limit_bytes=24 * 2**20),
         **more,
     )(*args)
 
@@ -116,7 +116,7 @@
         in_specs=[SMEM, VMEM, VMEM, pl.BlockSpec((height, step), lambda j: (0, j))],
         out_specs=[pl.BlockSpec((192, step), lambda j: (0, j))] * 2,
         scratch_shapes=[pltpu.VMEM((384, height), bf16)],
-        compiler_params=pltpu.CompilerParams(vmem_limit_bytes=48 * 2**20),
+        compiler_params=pltpu.CompilerParams(vmem_limit_bytes=24 * 2**20),
     )(place, train_ids.reshape(2, 128), query_ids.reshape(1, 128), embed)
 
 
@@ -131,47 +131,60 @@
 def acts_kernel(normed, w_gate, w_up, w_gate_other, w_up_other, out):
     rows = normed[...]
 
+    def product(w):
+        return lax.dot_general(
+            w[...], rows, (((1,), (1,)), ((), ())), preferred_element_type=f32
+        )
+
     def hidden(gate_w, up_w):
-        gate = dot(rows, gate_w[...])
-        return (gate / (1.0 + jnp.exp(-gate))) * dot(rows, up_w[...])
+        gate = product(gate_w)
+        return (gate / (1.0 + jnp.exp(-gate))) * product(up_w)
 
     own = hidden(w_gate, w_up)
     other = hidden(w_gate_other, w_up_other)
-    asked = jnp.concatenate([own[128:], other[128:]], axis=0)
+    asked = jnp.concatenate([own[:, 128:], other[:, 128:]], axis=1)
     fill = jnp.zeros((PACK - 3 * UNITS, 128), f32)
-    out[...] = jnp.concatenate([own[:128].T, other[:128].T, asked.T, fill], axis=0).astype(bf16)
+    out[...] = jnp.concatenate([own[:, :128], other[:, :128], asked, fill], axis=0).astype(bf16)
 
 
 def gather_groups(own):
-    partner = lax.ppermute(own, "dp", YLO)
-    pair = jnp.stack([own, partner])
-    ups, downs = [pair], [pair]
-    for _ in range(3):
-        ups.append(lax.ppermute(ups[-1], "dp", z_shift(1)))
-        downs.append(lax.ppermute(downs[-1], "dp", z_shift(-1)))
-    last_up = lax.ppermute(ups[-1][0], "dp", z_shift(1))
-    last_down = lax.ppermute(downs[-1][1], "dp", z_shift(-1))
-    return pair, [pair] + [b for i in range(1, 4) for b in (ups[i], downs[i])], [last_up, last_down]
+    def up(v):
+        return lax.ppermute(v, "dp", z_shift(1))
+
+    def down(v):
+        return lax.ppermute(v, "dp", z_shift(-1))
+
+    def across(v):
+        return lax.ppermute(v, "dp", YLO)
+
+    same, twin = {0: own}, {0: across(own)}
+    same[-1], same[1] = up(own), down(own)
+    twin[1], twin[-1] = across(same[1]), up(twin[0])
+    same[-2], same[2] = up(same[-1]), down(same[1])
+    twin[2], twin[-2] = across(same[2]), up(twin[-1])
+    same[-3], same[3] = up(same[-2]), down(same[2])
+    twin[3] = across(same[3])
+    same[4] = down(same[3])
+    twin[-3] = across(same[-3])
+    twin[4] = down(twin[3])
+    return [group[step] for step in STEPS for group in (same, twin)]
 
 
 def group_order():
     me = lax.axis_index("dp")
     y, z = me // 8, me % 8
     order = []
-    for step in (0, -1, 1, -2, 2, -3, 3, 4):
+    for step in STEPS:
         for flip in range(2):
             order.append((y ^ flip) * 8 + (z + step) % 8)
     return jnp.stack(order)
 
 
 def rhs_kernel(scale, *refs):
-    pairs, singles, wide, part, flip, acts = refs[:7], refs[7:9], refs[9], refs[10], refs[11], refs[12]
-    blocks = [(p, i) for p in pairs for i in range(2)]
+    blocks, (wide, part, flip) = refs[:16], refs[16:]
     out = jnp.zeros((PACK - BOTH, 256), f32)
     for b in range(16):
-        block = blocks[b][0][blocks[b][1]] if b < 14 else singles[b - 14][...]
-        acts[:, b * 128 : (b + 1) * 128] = block[:BOTH]
-        out = out + dot(block[BOTH:], wide[b])
+        out = out + dot(blocks[b][BOTH:, :], wide[b])
     out = out * scale
     part[:UNITS] = out[:UNITS, :128]
     part[UNITS:] = out[:UNITS, 128:]
@@ -179,17 +192,19 @@
     flip[UNITS:] = out[:UNITS, :128]
 
 
-def spread_tangent(res, acts, tangent):
+def spread_tangent(res, blocks, tangent):
     res_t = res.T.astype(bf16)
     for i in range(8):
-        tangent[i] = dot(res_t, acts[:, i * 256 : (i + 1) * 256]).astype(bf16)
-
-
-def first_kernel(part, got, acts, res_out, sums, tangent):
+        acts = jnp.concatenate([blocks[2 * i][:BOTH, :], blocks[2 * i + 1][:BOTH, :]], axis=1)
+        tangent[i] = dot(res_t, acts).astype(bf16)
+
+
+def first_kernel(*refs):
+    blocks, (part, got, res_out, sums, tangent) = refs[:16], refs[16:]
     res = part[...] + got[...]
     res_out[...] = res
     sums[...] = lanes([total(res * res)], (8, 128))
-    spread_tangent(res, acts, tangent)
+    spread_tangent(res, blocks, tangent)
 
 
 def share_kernel(parts, sums, *refs):
@@ -214,7 +229,8 @@
         message[i] = whole
 
 
-def curve_kernel(got, acts, *refs):
+def curve_kernel(*refs):
+    blocks, got, refs = refs[:16], refs[16], refs[17:]
     if len(refs) == 4:
         tangent_out, part, flip, sums_out = refs
     else:
@@ -232,11 +248,9 @@
             tangent_out[i] = tangent
         else:
             tangent = (tangent.astype(f32) + beta * past[i].astype(f32)).astype(bf16)
+        acts = jnp.concatenate([blocks[2 * i][:BOTH, :], blocks[2 * i + 1][:BOTH, :]], axis=1)
         out = out + lax.dot_general(
-            acts[:, i * 256 : (i + 1) * 256],
-            tangent,
-            (((1,), (1,)), ((), ())),
-            preferred_element_type=f32,
+            acts, tangent, (((1,), (1,)), ((), ())), preferred_element_type=f32
         )
     row = lax.broadcasted_iota(jnp.int32, (8, 128), 0)
     sums = jnp.where(row == 0, jnp.broadcast_to(sums, (8, 128)), 0.0)
@@ -247,7 +261,8 @@
     flip[BOTH:] = sums
 
 
-def second_kernel(part, got, sums, res, acts, res_out, state, tangent):
+def second_kernel(*refs):
+    blocks, (part, got, sums, res, res_out, state, tangent) = refs[:16], refs[16:]
     rr = sums[0:1, 0:1]
     tt = sums[0:1, 1:2] + got[BOTH : BOTH + 1, 1:2]
     inv_alpha = guarded(tt / TOKENS + damping * rr, rr)
@@ -256,10 +271,12 @@
     new = old - alpha * ((part[...] + got[:BOTH]) / TOKENS + damping * old)
     res_out[...] = new
     state[...] = lanes([total(new * new), rr, tt, rr, inv_alpha], (8, 128))
-    spread_tangent(new, acts, tangent)
-
-
-def third_kernel(part, got, sums, past, res, res_before, acts, res_out, state, tangent):
+    spread_tangent(new, blocks, tangent)
+
+
+def third_kernel(*refs):
+    blocks, refs = refs[:16], refs[16:]
+    part, got, sums, past, res, res_before, res_out, state, tangent = refs
     rr = sums[0:1, 0:1]
     ww = sums[0:1, 1:2] + got[BOTH : BOTH + 1, 1:2]
     cross = sums[0:1, 2:3] + got[BOTH : BOTH + 1, 2:3]
@@ -276,7 +293,7 @@
     state[...] = lanes(
         [total(new * new), rr0, rr, tt, pp, inv_alpha0, inv_alpha, beta], (8, 128)
     )
-    spread_tangent(new, acts, tangent)
+    spread_tangent(new, blocks, tangent)
 
 
 def partial_kernel(parts, state, block0, block1, message):
@@ -337,6 +354,7 @@
 def body(train_ids, query_ids, embed, norm_gain, w_gate, w_up, cotangent):
     core = lax.axis_index("shard") % 2
     wide = embed.shape[1]
+    w_gate, w_up = w_gate.T, w_up.T
     w_gate_other, w_up_other = swap_core(w_gate), swap_core(w_up)
 
     with jax.named_scope("rows"):
@@ -351,9 +369,9 @@
             acts_kernel, shape((PACK, 128), bf16), normed, w_gate, w_up, w_gate_other, w_up_other
         )
     with jax.named_scope("groups"):
-        pair, pairs, singles = gather_groups(package)
+        blocks = gather_groups(package)
     with jax.named_scope("cotangent"):
-        cotangent, _ = lax.optimization_barrier((cotangent, pair))
+        cotangent, _ = lax.optimization_barrier((cotangent, package))
         mine = lax.dynamic_slice_in_dim(cotangent, core * 64, 64, axis=0)
         columns = lax.all_to_all(
             mine.reshape(64, 16, 128).transpose(1, 0, 2), "dp", 0, 0, tiled=True
@@ -377,38 +395,45 @@
     table = shape((16, 8, 128), f32)
 
     with jax.named_scope("rhs"):
-        part, flip, acts = local_call(
+        part, flip = local_call(
             functools.partial(rhs_kernel, 1.0 / math.sqrt(2048)),
-            (vector, vector, shape((BOTH, HALF), bf16)),
-            *pairs,
-            *singles,
+            (vector, vector),
+            *blocks,
             columns,
         )
         got = swap_core(flip)
     with jax.named_scope("first"):
-        res0, sums, tangent = local_call(first_kernel, (vector, small, spread), part, got, acts)
+        res0, sums, tangent = local_call(first_kernel, (vector, small, spread), *blocks, part, got)
         parts = exchange_chips(tangent)
         block0, shared = local_call(share_kernel, (block, message), parts, sums)
         shared = exchange_chips(shared)
         tangent0, part, flip, sums = local_call(
-            curve_kernel, (spread, vector, longer, small), shared, acts
+            curve_kernel, (spread, vector, longer, small), *blocks, shared
         )
         got = swap_core(flip)
     with jax.named_scope("second"):
         res1, state, tangent = local_call(
-            second_kernel, (vector, small, spread), part, got, sums, res0, acts
+            second_kernel, (vector, small, spread), *blocks, part, got, sums, res0
         )
         parts = exchange_chips(tangent)
         block1, shared = local_call(share_kernel, (block, message), parts, state, block0)
         shared = exchange_chips(shared)
         past = state
         part, flip, sums = local_call(
-            curve_kernel, (vector, longer, small), shared, acts, tangent0, state
+            curve_kernel, (vector, longer, small), *blocks, shared, tangent0, state
         )
         got = swap_core(flip)
     with jax.named_scope("third"):
         res2, state, tangent = local_call(
-            third_kernel, (vector, small, spread), part, got, sums, past, res1, res0, acts
+            third_kernel,
+            (vector, small, spread),
+            *blocks,
+            part,
+            got,
+            sums,
+            past,
+            res1,
+            res0,
         )
         parts = exchange_chips(tangent)
         partials = local_call(partial_kernel, table, parts, state, block0, block1)

time: 239 us -> 224 us (0.937)
  local copies, waits for them, and re-layouts: 18.1 us -> 7.9 us
  waiting for transfers between devices: 42.8 us -> 34.4 us
  Pallas kernels: 24.4 us -> 19.9 us
  starting transfers between devices: 44 us -> 48 us
  blocking collectives: 108 us -> 111 us
    ppermute x9 -> x15, waiting for transfers between devices: 31.3 us -> 13.3 us  [the longest x5 6.14 us: down(): return lax.ppermute(v, 'dp', z_shift(-1))]
    all_to_all x1, waiting for transfers between devices: 2.43 us -> 12 us  [exchange_chips(): return lax.all_to_all(v, 'shard', 0, 0, axis_index_groups=CHIPS, tiled=True)]
    unnamed x18 -> x12, local copies, waits for them, and re-layouts: 10.4 us -> 4.72 us
    ppermute x9 -> x15, starting transfers between devices: 16.6 us -> 21.7 us  [the longest x5 13.7 us: down(): return lax.ppermute(v, 'dp', z_shift(-1))]
    ppermute x2 -> x0, local copies, waits for them, and re-layouts: 5.12 us -> none  [swap_core(): return lax.ppermute(v, 'shard', CORE)]
    pallas_call x13, Pallas kernels: 15.9 us -> 13.1 us  [local_call(): pl.pallas_call(kernel, out_shape=outs, in_specs=specs or [VMEM] * len(arg...]
  transfers between devices with their start and end apart: 17 -> 23, of which waited for: 12 -> 11; matrix products, arithmetic and copies ran while one was open for 5% -> 2% of each run, Pallas kernels for 0% -> 1%
where the time goes in v3:
time: 224 us; the launch traced here: 223 us
  blocking collectives  111 us (50%)
  starting transfers between devices  48 us (21%)
  waiting for transfers between devices  34.4 us (15%)
  Pallas kernels  19.9 us (9%)
  local copies, waits for them, and re-layouts  7.9 us (4%)
    all_to_all x6, blocking collectives, exchange_chips(): return lax.all_to_all(v, 'shard', 0, 0, axis_index_groups=CHIPS, tiled=True)  87.2 us
    ppermute x6, starting transfers between devices, swap_core(): return lax.ppermute(v, 'shard', CORE)  18.2 us
    ppermute x5, starting transfers between devices, down(): return lax.ppermute(v, 'dp', z_shift(-1))  13.7 us
    pallas_call x13, Pallas kernels, local_call(): pl.pallas_call(kernel, out_shape=outs, in_specs=specs or [VMEM] * len(arg...  13.1 us
    all_to_all x1, blocking collectives, body(): partials = lax.all_to_all(partials, 'shard', 0, 0, tiled=True)  12.1 us
    all_to_all x1, waiting for transfers between devices, exchange_chips(): return lax.all_to_all(v, 'shard', 0, 0, axis_index_groups=CHIPS, tiled=True)  12 us
    all_to_all x1, blocking collectives, body(): every = lax.all_to_all(mine, 'dp', 0, 0, tiled=True)  11.8 us
    pallas_call x1, Pallas kernels, lookup(): pl.pallas_call(lookup_kernel, grid=(wide // step,), out_shape=(out, out),...  6.82 us
  transfers between devices with their start and end apart: 23, of which 11 were waited for; matrix products, arithmetic and copies ran while one was open for 2% of the time, Pallas kernels for 1%

profile of v3, /device:TPU:1, one launch (start us, length us, event | category | flops | bytes accessed | tf_op | source)
XLA Modules:
  0.0 223.0 jit_solution(528640490044867712)
XLA Ops:
  0.1 3.4 %copy-done.1 = bf16[2000,2048]{1,0:T(8,128)(2,1)S(1)} copy-done((bf16[2000,2048]{1,0:T(8,128)(2,1)S(1)}, bf16[2000,2048]{1,0:T(8,128)(2,1)}, u32[]{:S(2)}) %copy-start.1) | copy-done | bytes 8192024
  4.8 6.8 %rows.1 = (bf16[192,2048]{1,0:T(8,128)(2,1)S(1)}, bf16[192,2048]{1,0:T(8,128)(2,1)S(1)}) custom-call(s32[2]{0:T(128)S(1)} %pad_add_fusion.place, s32[2,128]{1,0:T(2,128)S(1)} %bitcast.55, s32[1,128]{1,0:T(1,128)S(1)} %bitcast.56, bf16[2000,2048]{1,0:T(8,128)(2,1)S(1)} %copy-done.1), custom_call_target="tpu_custom_call" | custom-call | tf_op jit(solution)/shard_map/rows/pallas_call | solution.py:112
  11.6 3.3 %collective-permute-start = (bf16[192,2048]{1,0:T(8,128)(2,1)S(1)}, bf16[192,2048]{1,0:T(8,128)(2,1)S(1)}, u32[]{:S(2)}, u32[]{:S(2)}) collective-permute-start(bf16[192,2048]{1,0:T(8,128)(2,1)S(1)} %get-tuple-element.31), channel_id=1, source_target_pairs={{0,1},{1,0},{2,3},{3,2},{4,5},{5,4},{6,7},{7,6},{8,9},{9,8},{10,11... | collective-permute-start | bytes 2359304 | tf_op jit(solution)/shard_map/rows/ppermute | solution.py:34
  15.5 1.4 collective-permute-done
  17.2 17.5 %all_to_all.50.parts = bf16[8,24,2048]{2,1,0:T(8,128)(2,1)S(1)} all-to-all(bf16[8,24,2048]{2,1,0:T(8,128)(2,1)S(1)} %bitcast.57), channel_id=1, replica_groups={{0,2,4,6,8,10,12,14},{1,3,5,7,9,11,13,15},{16,18,20,22,24,26,28,30},{17..., dimensions={0} | all-to-all | bytes 1572864 | tf_op jit(solution)/shard_map/rows/all_to_all | solution.py:38
  35.8 3.9 %all-to-all-start.1 = ((bf16[8,24,2048]{2,1,0:T(8,128)(2,1)}), bf16[8,24,2048]{2,1,0:T(8,128)(2,1)S(1)}, u32[]{:S(2)}, u32[]{:S(2)}) async-start(bf16[8,24,2048]{2,1,0:T(8,128)(2,1)} %normed.1), calls=%async_computation.1 | async-start | bytes 1572864 | tf_op jit(solution)/shard_map/normed/all_to_all | solution.py:38
  39.7 12.0 %all-to-all-done.1 = bf16[8,24,2048]{2,1,0:T(8,128)(2,1)S(1)} async-done(((bf16[8,24,2048]{2,1,0:T(8,128)(2,1)}), bf16[8,24,2048]{2,1,0:T(8,128)(2,1)S(1)}, u32[]{:S(2)}, u32[]{:S(2)}) %all-to-all-start.1) | async-done | bytes 786464 | tf_op jit(solution)/shard_map/normed/all_to_all | solution.py:38
  51.6 4.0 %acts.1.refs_0_ = bf16[1040,128]{1,0:T(8,128)(2,1)S(1)} custom-call(bf16[192,2048]{1,0:T(8,128)(2,1)S(1)} %bitcast.51, bf16[344,2048]{1,0:T(8,128)(2,1)S(1)} %bitcast.53, bf16[344,2048]{1,0:T(8,128)(2,1)} %bitcast.9.w_up, bf16[344,2048]{1,0:T(8,128)(2,1)} %collective-permute-done.1.w_gate_other, bf16[344,2048]{1,0:T(8,128)(2,1)} %collective-permute-done.2.w_up_other), custom_call_target="tpu_custom_call" | custom-call | tf_op jit(solution)/shard_map/acts/pallas_call | solution.py:42
  55.6 5.7 %collective-permute-start.6 = (bf16[1040,128]{1,0:T(8,128)(2,1)S(1)}, bf16[1040,128]{1,0:T(8,128)(2,1)S(1)}, u32[]{:S(2)}, u32[]{:S(2)}) collective-permute-start(bf16[1040,128]{1,0:T(8,128)(2,1)S(1)} %acts.1.refs_0_), channel_id=1, source_target_pairs={{0,112},{16,0},{32,16},{48,32},{64,48},{80,64},{96,80},{112,96},{1... | collective-permute-start | bytes 798728 | tf_op jit(solution)/shard_map/groups/ppermute | solution.py:155
  61.3 3.4 %collective-permute-done.6.refs_4_ = bf16[1040,128]{1,0:T(8,128)(2,1)S(1)} collective-permute-done((bf16[1040,128]{1,0:T(8,128)(2,1)S(1)}, bf16[1040,128]{1,0:T(8,128)(2,1)S(1)}, u32[]{:S(2)}, u32[]{:S(2)}) %collective-permute-start.6) | collective-permute-done | bytes 266272 | tf_op jit(solution)/shard_map/groups/ppermute | solution.py:155
  64.6 3.1 %collective-permute-start.10 = (bf16[1040,128]{1,0:T(8,128)(2,1)S(1)}, bf16[1040,128]{1,0:T(8,128)(2,1)S(1)}, u32[]{:S(2)}, u32[]{:S(2)}) collective-permute-start(bf16[1040,128]{1,0:T(8,128)(2,1)S(1)} %collective-permute-done.6.refs_4_), channel_id=1, source_target_pairs={{0,112},{16,0},{32,16},{48,32},{64,48},{80,64},{96,80},{112,96},{1... | collective-permute-start | bytes 798728 | tf_op jit(solution)/shard_map/groups/ppermute | solution.py:155
  68.3 2.8 %collective-permute-done.10.refs_8_ = bf16[1040,128]{1,0:T(8,128)(2,1)S(1)} collective-permute-done((bf16[1040,128]{1,0:T(8,128)(2,1)S(1)}, bf16[1040,128]{1,0:T(8,128)(2,1)S(1)}, u32[]{:S(2)}, u32[]{:S(2)}) %collective-permute-start.10) | collective-permute-done | bytes 266272 | tf_op jit(solution)/shard_map/groups/ppermute | solution.py:155
  71.1 3.1 %collective-permute-start.14 = (bf16[1040,128]{1,0:T(8,128)(2,1)S(1)}, bf16[1040,128]{1,0:T(8,128)(2,1)S(1)}, u32[]{:S(2)}, u32[]{:S(2)}) collective-permute-start(bf16[1040,128]{1,0:T(8,128)(2,1)S(1)} %collective-permute-done.10.refs_8_), channel_id=1, source_target_pairs={{0,112},{16,0},{32,16},{48,32},{64,48},{80,64},{96,80},{112,96},{1... | collective-permute-start | bytes 798728 | tf_op jit(solution)/shard_map/groups/ppermute | solution.py:155
  75.0 4.2 %all-to-all-start.2 = ((bf16[16,64,128]{2,1,0:T(8,128)(2,1)}), bf16[16,64,128]{2,1,0:T(8,128)(2,1)}, u32[]{:S(2)}, u32[]{:S(2)}) async-start(bf16[16,64,128]{2,1,0:T(8,128)(2,1)} %bitcast_bitcast_fusion), calls=%async_computation.2 | async-start | bytes 524288 | tf_op jit(solution)/shard_map/cotangent/all_to_all | solution.py:376
  79.2 1.3 collective-permute-start.7
  83.2 3.7 %all-to-all-done.2 = bf16[16,64,128]{2,1,0:T(8,128)(2,1)} async-done(((bf16[16,64,128]{2,1,0:T(8,128)(2,1)}), bf16[16,64,128]{2,1,0:T(8,128)(2,1)}, u32[]{:S(2)}, u32[]{:S(2)}) %all-to-all-start.2) | async-done | bytes 262176 | tf_op jit(solution)/shard_map/cotangent/all_to_all | solution.py:376
  87.0 2.2 gather_fusion
  89.9 1.7 collective-permute-start.9
  92.6 3.3 %collective-permute-done.12.refs_10_ = bf16[1040,128]{1,0:T(8,128)(2,1)S(1)} collective-permute-done((bf16[1040,128]{1,0:T(8,128)(2,1)S(1)}, bf16[1040,128]{1,0:T(8,128)(2,1)S(1)}, u32[]{:S(2)}, u32[]{:S(2)}) %collective-permute-start.12) | collective-permute-done | bytes 266272 | tf_op jit(solution)/shard_map/groups/ppermute | solution.py:152
  99.1 2.5 %collective-permute-done.9.refs_7_ = bf16[1040,128]{1,0:T(8,128)(2,1)S(1)} collective-permute-done((bf16[1040,128]{1,0:T(8,128)(2,1)S(1)}, bf16[1040,128]{1,0:T(8,128)(2,1)S(1)}, u32[]{:S(2)}, u32[]{:S(2)}) %collective-permute-start.9) | collective-permute-done | bytes 266272 | tf_op jit(solution)/shard_map/groups/ppermute | solution.py:152
  101.5 1.5 collective-permute-done.13.refs_11_
  103.9 8.3 %collective-permute-start.18 = (f32[688,128]{1,0:T(8,128)S(1)}, f32[688,128]{1,0:T(8,128)S(1)}, u32[]{:S(2)}, u32[]{:S(2)}) collective-permute-start(f32[688,128]{1,0:T(8,128)S(1)} %get-tuple-element.34), channel_id=1, source_target_pairs={{0,1},{1,0},{2,3},{3,2},{4,5},{5,4},{6,7},{7,6},{8,9},{9,8},{10,11... | collective-permute-start | bytes 1056776 | tf_op jit(solution)/shard_map/rhs/ppermute | solution.py:34
  114.2 16.8 %all_to_all.51.parts = bf16[8,128,256]{2,1,0:T(8,128)(2,1)S(1)} all-to-all(bf16[8,128,256]{2,1,0:T(8,128)(2,1)S(1)} %get-tuple-element.35), channel_id=1, replica_groups={{0,2,4,6,8,10,12,14},{1,3,5,7,9,11,13,15},{16,18,20,22,24,26,28,30},{17..., dimensions={0} | all-to-all | bytes 1048576 | tf_op jit(solution)/shard_map/first/all_to_all | solution.py:38
  131.2 14.0 %all_to_all.52.refs_16_ = bf16[8,144,256]{2,1,0:T(8,128)(2,1)S(1)} all-to-all(bf16[8,144,256]{2,1,0:T(8,128)(2,1)S(1)} %get-tuple-element.37), channel_id=1, replica_groups={{0,2,4,6,8,10,12,14},{1,3,5,7,9,11,13,15},{16,18,20,22,24,26,28,30},{17..., dimensions={0} | all-to-all | bytes 1179648 | tf_op jit(solution)/shard_map/first/all_to_all | solution.py:38
  146.2 3.0 %collective-permute-start.19 = (f32[696,128]{1,0:T(8,128)S(1)}, f32[696,128]{1,0:T(8,128)S(1)}, u32[]{:S(2)}, u32[]{:S(2)}) collective-permute-start(f32[696,128]{1,0:T(8,128)S(1)} %get-tuple-element.39), channel_id=1, source_target_pairs={{0,1},{1,0},{2,3},{3,2},{4,5},{5,4},{6,7},{7,6},{8,9},{9,8},{10,11... | collective-permute-start | bytes 1069064 | tf_op jit(solution)/shard_map/first/ppermute | solution.py:34
  149.1 1.3 collective-permute-done.19.refs_17_
  151.3 12.7 %all_to_all.53.parts = bf16[8,128,256]{2,1,0:T(8,128)(2,1)S(1)} all-to-all(bf16[8,128,256]{2,1,0:T(8,128)(2,1)S(1)} %get-tuple-element.42), channel_id=1, replica_groups={{0,2,4,6,8,10,12,14},{1,3,5,7,9,11,13,15},{16,18,20,22,24,26,28,30},{17..., dimensions={0} | all-to-all | bytes 1048576 | tf_op jit(solution)/shard_map/second/all_to_all | solution.py:38
  164.3 13.5 %all_to_all.54.refs_16_ = bf16[8,144,256]{2,1,0:T(8,128)(2,1)S(1)} all-to-all(bf16[8,144,256]{2,1,0:T(8,128)(2,1)S(1)} %get-tuple-element.45), channel_id=1, replica_groups={{0,2,4,6,8,10,12,14},{1,3,5,7,9,11,13,15},{16,18,20,22,24,26,28,30},{17..., dimensions={0} | all-to-all | bytes 1179648 | tf_op jit(solution)/shard_map/second/all_to_all | solution.py:38
  179.0 3.1 %collective-permute-start.20 = (f32[696,128]{1,0:T(8,128)S(1)}, f32[696,128]{1,0:T(8,128)S(1)}, u32[]{:S(2)}, u32[]{:S(2)}) collective-permute-start(f32[696,128]{1,0:T(8,128)S(1)} %get-tuple-element.48), channel_id=1, source_target_pairs={{0,1},{1,0},{2,3},{3,2},{4,5},{5,4},{6,7},{7,6},{8,9},{9,8},{10,11... | collective-permute-start | bytes 1069064 | tf_op jit(solution)/shard_map/second/ppermute | solution.py:34
  184.4 12.7 %all_to_all.55.parts = bf16[8,128,256]{2,1,0:T(8,128)(2,1)S(1)} all-to-all(bf16[8,128,256]{2,1,0:T(8,128)(2,1)S(1)} %get-tuple-element.51), channel_id=1, replica_groups={{0,2,4,6,8,10,12,14},{1,3,5,7,9,11,13,15},{16,18,20,22,24,26,28,30},{17..., dimensions={0} | all-to-all | bytes 1048576 | tf_op jit(solution)/shard_map/third/all_to_all | solution.py:38
  197.4 12.1 %all_to_all.56.got = f32[16,8,128]{2,1,0:T(8,128)S(1)} all-to-all(f32[16,8,128]{2,1,0:T(8,128)S(1)} %third.3), channel_id=1, replica_groups=mesh['dp'=16,'shard'=16] {'shard'}, dimensions={0} | all-to-all | bytes 131072 | tf_op jit(solution)/shard_map/third/all_to_all | solution.py:440
  210.0 11.8 %all_to_all.57.got = f32[16,8,128]{2,1,0:T(8,128)S(1)} all-to-all(f32[16,8,128]{2,1,0:T(8,128)S(1)} %whole.2), channel_id=1, replica_groups=mesh['dp'=16,'shard'=16] {'dp'}, dimensions={0} | all-to-all | bytes 131072 | tf_op jit(solution)/shard_map/whole/all_to_all | solution.py:443
  (59 shorter events, 22.9 us)
Async XLA Ops:
  0.0 74.2 %copy-start = (bf16[128,2048]{1,0:T(8,128)(2,1)S(1)}, bf16[128,2048]{1,0:T(8,128)(2,1)}, u32[]{:S(2)}) copy-start(bf16[128,2048]{1,0:T(8,128)(2,1)} %param.13) | copy-start | bytes 1572868
  0.1 3.4 %copy-start.1 = (bf16[2000,2048]{1,0:T(8,128)(2,1)S(1)}, bf16[2000,2048]{1,0:T(8,128)(2,1)}, u32[]{:S(2)}) copy-start(bf16[2000,2048]{1,0:T(8,128)(2,1)} %table.1) | copy-start | bytes 24576004
  3.4 0.7 copy-start.4
  4.1 0.7 copy-start.5
  4.8 10.2 %copy-start.2 = (bf16[2048,344]{0,1:T(8,128)(2,1)S(1)}, bf16[2048,344]{0,1:T(8,128)(2,1)}, u32[]{:S(2)}) copy-start(bf16[2048,344]{0,1:T(8,128)(2,1)} %param.11) | copy-start | bytes 4227076
  11.6 23.0 %copy-start.3 = (f32[2048]{0:T(1024)S(1)}, f32[2048]{0:T(1024)}, u32[]{:S(2)}) copy-start(f32[2048]{0:T(1024)} %param.10) | copy-start | bytes 24580
  11.6 5.3 %collective-permute-start = (bf16[192,2048]{1,0:T(8,128)(2,1)S(1)}, bf16[192,2048]{1,0:T(8,128)(2,1)S(1)}, u32[]{:S(2)}, u32[]{:S(2)}) collective-permute-start(bf16[192,2048]{1,0:T(8,128)(2,1)S(1)} %get-tuple-element.31), channel_id=1, source_target_pairs={{0,1},{1,0},{2,3},{3,2},{4,5},{5,4},{6,7},{7,6},{8,9},{9,8},{10,11... | collective-permute-start | bytes 2359304 | tf_op jit(solution)/shard_map/rows/ppermute | solution.py:34
  15.0 24.7 %collective-permute-start.1 = (bf16[344,2048]{1,0:T(8,128)(2,1)S(1)}, bf16[344,2048]{1,0:T(8,128)(2,1)}, u32[]{:S(2)}, u32[]{:S(2)}) collective-permute-start(bf16[344,2048]{1,0:T(8,128)(2,1)S(1)} %bitcast.52), channel_id=1, source_target_pairs={{0,1},{1,0},{2,3},{3,2},{4,5},{5,4},{6,7},{7,6},{8,9},{9,8},{10,11... | collective-permute-start | bytes 4227080 | tf_op jit(solution)/shard_map/ppermute | solution.py:34
  15.1 24.6 %collective-permute-start.2 = (bf16[344,2048]{1,0:T(8,128)(2,1)}, bf16[344,2048]{1,0:T(8,128)(2,1)}, u32[]{:S(2)}, u32[]{:S(2)}) collective-permute-start(bf16[344,2048]{1,0:T(8,128)(2,1)} %bitcast.9.w_up), channel_id=1, source_target_pairs={{0,1},{1,0},{2,3},{3,2},{4,5},{5,4},{6,7},{7,6},{8,9},{9,8},{10,11... | collective-permute-start | bytes 4227080 | tf_op jit(solution)/shard_map/ppermute | solution.py:34
  35.8 15.9 %all-to-all-start.1 = ((bf16[8,24,2048]{2,1,0:T(8,128)(2,1)}), bf16[8,24,2048]{2,1,0:T(8,128)(2,1)S(1)}, u32[]{:S(2)}, u32[]{:S(2)}) async-start(bf16[8,24,2048]{2,1,0:T(8,128)(2,1)} %normed.1), calls=%async_computation.1 | async-start | bytes 1572864 | tf_op jit(solution)/shard_map/normed/all_to_all | solution.py:38
  55.6 9.0 %collective-permute-start.6 = (bf16[1040,128]{1,0:T(8,128)(2,1)S(1)}, bf16[1040,128]{1,0:T(8,128)(2,1)S(1)}, u32[]{:S(2)}, u32[]{:S(2)}) collective-permute-start(bf16[1040,128]{1,0:T(8,128)(2,1)S(1)} %acts.1.refs_0_), channel_id=1, source_target_pairs={{0,112},{16,0},{32,16},{48,32},{64,48},{80,64},{96,80},{112,96},{1... | collective-permute-start | bytes 798728 | tf_op jit(solution)/shard_map/groups/ppermute | solution.py:155
  61.3 7.1 %collective-permute-start.4 = (bf16[1040,128]{1,0:T(8,128)(2,1)S(1)}, bf16[1040,128]{1,0:T(8,128)(2,1)S(1)}, u32[]{:S(2)}, u32[]{:S(2)}) collective-permute-start(bf16[1040,128]{1,0:T(8,128)(2,1)S(1)} %acts.1.refs_0_), channel_id=1, source_target_pairs={{0,16},{16,32},{32,48},{48,64},{64,80},{80,96},{96,112},{112,0},{1... | collective-permute-start | bytes 798728 | tf_op jit(solution)/shard_map/groups/ppermute | solution.py:152
  64.6 6.5 %collective-permute-start.10 = (bf16[1040,128]{1,0:T(8,128)(2,1)S(1)}, bf16[1040,128]{1,0:T(8,128)(2,1)S(1)}, u32[]{:S(2)}, u32[]{:S(2)}) collective-permute-start(bf16[1040,128]{1,0:T(8,128)(2,1)S(1)} %collective-permute-done.6.refs_4_), channel_id=1, source_target_pairs={{0,112},{16,0},{32,16},{48,32},{64,48},{80,64},{96,80},{112,96},{1... | collective-permute-start | bytes 798728 | tf_op jit(solution)/shard_map/groups/ppermute | solution.py:155
  67.8 12.7 %collective-permute-start.3 = (bf16[1040,128]{1,0:T(8,128)(2,1)S(1)}, bf16[1040,128]{1,0:T(8,128)(2,1)S(1)}, u32[]{:S(2)}, u32[]{:S(2)}) collective-permute-start(bf16[1040,128]{1,0:T(8,128)(2,1)S(1)} %acts.1.refs_0_), channel_id=1, source_target_pairs={{0,128},{16,144},{32,160},{48,176},{64,192},{80,208},{96,224},{112... | collective-permute-start | bytes 798728 | tf_op jit(solution)/shard_map/groups/ppermute | solution.py:158
  68.3 13.4 %collective-permute-start.8 = (bf16[1040,128]{1,0:T(8,128)(2,1)S(1)}, bf16[1040,128]{1,0:T(8,128)(2,1)S(1)}, u32[]{:S(2)}, u32[]{:S(2)}) collective-permute-start(bf16[1040,128]{1,0:T(8,128)(2,1)S(1)} %collective-permute-done.4.refs_2_), channel_id=1, source_target_pairs={{0,16},{16,32},{32,48},{48,64},{64,80},{80,96},{96,112},{112,0},{1... | collective-permute-start | bytes 798728 | tf_op jit(solution)/shard_map/groups/ppermute | solution.py:152
  71.1 11.8 %collective-permute-start.14 = (bf16[1040,128]{1,0:T(8,128)(2,1)S(1)}, bf16[1040,128]{1,0:T(8,128)(2,1)S(1)}, u32[]{:S(2)}, u32[]{:S(2)}) collective-permute-start(bf16[1040,128]{1,0:T(8,128)(2,1)S(1)} %collective-permute-done.10.refs_8_), channel_id=1, source_target_pairs={{0,112},{16,0},{32,16},{48,32},{64,48},{80,64},{96,80},{112,96},{1... | collective-permute-start | bytes 798728 | tf_op jit(solution)/shard_map/groups/ppermute | solution.py:155
  75.0 12.0 %all-to-all-start.2 = ((bf16[16,64,128]{2,1,0:T(8,128)(2,1)}), bf16[16,64,128]{2,1,0:T(8,128)(2,1)}, u32[]{:S(2)}, u32[]{:S(2)}) async-start(bf16[16,64,128]{2,1,0:T(8,128)(2,1)} %bitcast_bitcast_fusion), calls=%async_computation.2 | async-start | bytes 524288 | tf_op jit(solution)/shard_map/cotangent/all_to_all | solution.py:376
  79.2 12.4 %collective-permute-start.7 = (bf16[1040,128]{1,0:T(8,128)(2,1)S(1)}, bf16[1040,128]{1,0:T(8,128)(2,1)S(1)}, u32[]{:S(2)}, u32[]{:S(2)}) collective-permute-start(bf16[1040,128]{1,0:T(8,128)(2,1)S(1)} %collective-permute-done.6.refs_4_), channel_id=1, source_target_pairs={{0,128},{16,144},{32,160},{48,176},{64,192},{80,208},{96,224},{112... | collective-permute-start | bytes 798728 | tf_op jit(solution)/shard_map/groups/ppermute | solution.py:158
  80.5 9.4 %collective-permute-start.5 = (bf16[1040,128]{1,0:T(8,128)(2,1)S(1)}, bf16[1040,128]{1,0:T(8,128)(2,1)S(1)}, u32[]{:S(2)}, u32[]{:S(2)}) collective-permute-start(bf16[1040,128]{1,0:T(8,128)(2,1)S(1)} %collective-permute-done.3.refs_1_), channel_id=1, source_target_pairs={{0,16},{16,32},{32,48},{48,64},{64,80},{80,96},{96,112},{112,0},{1... | collective-permute-start | bytes 798728 | tf_op jit(solution)/shard_map/groups/ppermute | solution.py:152
  81.7 14.1 %collective-permute-start.12 = (bf16[1040,128]{1,0:T(8,128)(2,1)S(1)}, bf16[1040,128]{1,0:T(8,128)(2,1)S(1)}, u32[]{:S(2)}, u32[]{:S(2)}) collective-permute-start(bf16[1040,128]{1,0:T(8,128)(2,1)S(1)} %collective-permute-done.8.refs_6_), channel_id=1, source_target_pairs={{0,16},{16,32},{32,48},{48,64},{64,80},{80,96},{96,112},{112,0},{1... | collective-permute-start | bytes 798728 | tf_op jit(solution)/shard_map/groups/ppermute | solution.py:152
  82.9 14.2 %collective-permute-start.15 = (bf16[1040,128]{1,0:T(8,128)(2,1)S(1)}, bf16[1040,128]{1,0:T(8,128)(2,1)S(1)}, u32[]{:S(2)}, u32[]{:S(2)}) collective-permute-start(bf16[1040,128]{1,0:T(8,128)(2,1)S(1)} %collective-permute-done.14.refs_12_), channel_id=1, source_target_pairs={{0,128},{16,144},{32,160},{48,176},{64,192},{80,208},{96,224},{112... | collective-permute-start | bytes 798728 | tf_op jit(solution)/shard_map/groups/ppermute | solution.py:158
  89.2 9.9 %collective-permute-start.11 = (bf16[1040,128]{1,0:T(8,128)(2,1)S(1)}, bf16[1040,128]{1,0:T(8,128)(2,1)S(1)}, u32[]{:S(2)}, u32[]{:S(2)}) collective-permute-start(bf16[1040,128]{1,0:T(8,128)(2,1)S(1)} %collective-permute-done.10.refs_8_), channel_id=1, source_target_pairs={{0,128},{16,144},{32,160},{48,176},{64,192},{80,208},{96,224},{112... | collective-permute-start | bytes 798728 | tf_op jit(solution)/shard_map/groups/ppermute | solution.py:158
  89.9 11.6 %collective-permute-start.9 = (bf16[1040,128]{1,0:T(8,128)(2,1)S(1)}, bf16[1040,128]{1,0:T(8,128)(2,1)S(1)}, u32[]{:S(2)}, u32[]{:S(2)}) collective-permute-start(bf16[1040,128]{1,0:T(8,128)(2,1)S(1)} %collective-permute-done.5.refs_3_), channel_id=1, source_target_pairs={{0,16},{16,32},{32,48},{48,64},{64,80},{80,96},{96,112},{112,0},{1... | collective-permute-start | bytes 798728 | tf_op jit(solution)/shard_map/groups/ppermute | solution.py:152
  91.6 9.9 %collective-permute-start.16 = (bf16[1040,128]{1,0:T(8,128)(2,1)S(1)}, bf16[1040,128]{1,0:T(8,128)(2,1)S(1)}, u32[]{:S(2)}, u32[]{:S(2)}) collective-permute-start(bf16[1040,128]{1,0:T(8,128)(2,1)S(1)} %collective-permute-done.14.refs_12_), channel_id=1, source_target_pairs={{0,112},{16,0},{32,16},{48,32},{64,48},{80,64},{96,80},{112,96},{1... | collective-permute-start | bytes 798728 | tf_op jit(solution)/shard_map/groups/ppermute | solution.py:155
  95.8 7.2 %collective-permute-start.13 = (bf16[1040,128]{1,0:T(8,128)(2,1)S(1)}, bf16[1040,128]{1,0:T(8,128)(2,1)S(1)}, u32[]{:S(2)}, u32[]{:S(2)}) collective-permute-start(bf16[1040,128]{1,0:T(8,128)(2,1)S(1)} %collective-permute-done.12.refs_10_), channel_id=1, source_target_pairs={{0,128},{16,144},{32,160},{48,176},{64,192},{80,208},{96,224},{112... | collective-permute-start | bytes 798728 | tf_op jit(solution)/shard_map/groups/ppermute | solution.py:158
  97.1 5.9 %collective-permute-start.17 = (bf16[1040,128]{1,0:T(8,128)(2,1)S(1)}, bf16[1040,128]{1,0:T(8,128)(2,1)S(1)}, u32[]{:S(2)}, u32[]{:S(2)}) collective-permute-start(bf16[1040,128]{1,0:T(8,128)(2,1)S(1)} %collective-permute-done.15.refs_13_), channel_id=1, source_target_pairs={{0,112},{16,0},{32,16},{48,32},{64,48},{80,64},{96,80},{112,96},{1... | collective-permute-start | bytes 798728 | tf_op jit(solution)/shard_map/groups/ppermute | solution.py:155
  103.9 9.6 %collective-permute-start.18 = (f32[688,128]{1,0:T(8,128)S(1)}, f32[688,128]{1,0:T(8,128)S(1)}, u32[]{:S(2)}, u32[]{:S(2)}) collective-permute-start(f32[688,128]{1,0:T(8,128)S(1)} %get-tuple-element.34), channel_id=1, source_target_pairs={{0,1},{1,0},{2,3},{3,2},{4,5},{5,4},{6,7},{7,6},{8,9},{9,8},{10,11... | collective-permute-start | bytes 1056776 | tf_op jit(solution)/shard_map/rhs/ppermute | solution.py:34
  146.2 4.3 %collective-permute-start.19 = (f32[696,128]{1,0:T(8,128)S(1)}, f32[696,128]{1,0:T(8,128)S(1)}, u32[]{:S(2)}, u32[]{:S(2)}) collective-permute-start(f32[696,128]{1,0:T(8,128)S(1)} %get-tuple-element.39), channel_id=1, source_target_pairs={{0,1},{1,0},{2,3},{3,2},{4,5},{5,4},{6,7},{7,6},{8,9},{9,8},{10,11... | collective-permute-start | bytes 1069064 | tf_op jit(solution)/shard_map/first/ppermute | solution.py:34
  179.0 4.4 %collective-permute-start.20 = (f32[696,128]{1,0:T(8,128)S(1)}, f32[696,128]{1,0:T(8,128)S(1)}, u32[]{:S(2)}, u32[]{:S(2)}) collective-permute-start(f32[696,128]{1,0:T(8,128)S(1)} %get-tuple-element.48), channel_id=1, source_target_pairs={{0,1},{1,0},{2,3},{3,2},{4,5},{5,4},{6,7},{7,6},{8,9},{9,8},{10,11... | collective-permute-start | bytes 1069064 | tf_op jit(solution)/shard_map/second/ppermute | solution.py:34

commit v4 on v3

--- a/solution.py
+++ b/solution.py
@@ -20,6 +20,7 @@
 YLO = [(i, i ^ 8) for i in range(16)]
 VMEM = pl.BlockSpec(memory_space=pltpu.VMEM)
 SMEM = pl.BlockSpec(memory_space=pltpu.SMEM)
+HBM = pl.BlockSpec(memory_space=pltpu.HBM)
 UNITS = 344
 BOTH = 2 * UNITS
 PACK = 1040
@@ -75,49 +76,71 @@
     return out
 
 
-def lookup_kernel(place, train, query, table, mine, other, hot):
-    height = table.shape[0]
-
-    @pl.when(pl.program_id(0) == 0)
-    def _():
-        core, shard = place[0], place[1]
-
-        def column(row):
-            return jnp.broadcast_to(row, (128, 128)).T
-
-        own_train = column(train[pl.ds(core, 1), :])
-        other_train = column(train[pl.ds(1 - core, 1), :])
-        asked = column(query[...])
-        first = core == 0
-        own_query = jnp.where(first, asked[:64], asked[64:])
-        other_query = jnp.where(first, asked[64:], asked[:64])
-        ids = jnp.concatenate([own_train, own_query, other_train, other_query], axis=0)
-        ids = ids - shard * height
-        lane = lax.broadcasted_iota(jnp.int32, ids.shape, 1)
-        for start in range(0, height, 128):
-            wide = min(128, height - start)
-            hit = jnp.where(ids == lane + start, 1.0, 0.0).astype(bf16)
-            hot[:, start : start + wide] = hit[:, :wide]
-
-    found = dot(hot[...], table[...]).astype(bf16)
-    mine[...] = found[:192]
-    other[...] = found[192:]
-
-
-def lookup(train_ids, query_ids, embed, core):
+LOOKUP_STEPS = 4
+
+
+def lookup_kernel(place, train_hbm, query_hbm, table_hbm, mine, other, train, query, table, hot, sems):
+    height, wide = table.shape
+    step = wide // LOOKUP_STEPS
+    asks = [
+        pltpu.make_async_copy(train_hbm, train, sems.at[0]),
+        pltpu.make_async_copy(query_hbm, query, sems.at[1]),
+    ]
+    pieces = []
+    for j in range(LOOKUP_STEPS):
+        span = pl.ds(j * step, step)
+        pieces.append(
+            pltpu.make_async_copy(table_hbm.at[:, span], table.at[:, span], sems.at[2 + j])
+        )
+    for copy in asks + pieces:
+        copy.start()
+    for copy in asks:
+        copy.wait()
+    shard = place[0]
+    core = lax.bitwise_and(shard, 1)
+
+    def column(row):
+        return jnp.broadcast_to(row, (128, 128)).T
+
+    own_train = column(train[pl.ds(core, 1), :])
+    other_train = column(train[pl.ds(1 - core, 1), :])
+    asked = column(query[...])
+    first = core == 0
+    own_query = jnp.where(first, asked[:64], asked[64:])
+    other_query = jnp.where(first, asked[64:], asked[:64])
+    ids = jnp.concatenate([own_train, own_query, other_train, other_query], axis=0)
+    ids = ids - shard * height
+    lane = lax.broadcasted_iota(jnp.int32, ids.shape, 1)
+    for start in range(0, height, 128):
+        width = min(128, height - start)
+        hit = jnp.where(ids == lane + start, 1.0, 0.0).astype(bf16)
+        hot[:, start : start + width] = hit[:, :width]
+    for j in range(LOOKUP_STEPS):
+        pieces[j].wait()
+        found = dot(hot[...], table[:, j * step : (j + 1) * step]).astype(bf16)
+        mine[:, j * step : (j + 1) * step] = found[:192]
+        other[:, j * step : (j + 1) * step] = found[192:]
+
+
+def lookup(train_ids, query_ids, embed):
     height, wide = embed.shape
-    step = 256
-    place = jnp.stack([core, lax.axis_index("shard")])
     out = shape((192, wide), bf16)
-    return pl.pallas_call(
+    return local_call(
         lookup_kernel,
-        grid=(wide // step,),
-        out_shape=(out, out),
-        in_specs=[SMEM, VMEM, VMEM, pl.BlockSpec((height, step), lambda j: (0, j))],
-        out_specs=[pl.BlockSpec((192, step), lambda j: (0, j))] * 2,
-        scratch_shapes=[pltpu.VMEM((384, height), bf16)],
-        compiler_params=pltpu.CompilerParams(vmem_limit_bytes=24 * 2**20),
-    )(place, train_ids.reshape(2, 128), query_ids.reshape(1, 128), embed)
+        (out, out),
+        lax.axis_index("shard").reshape(1),
+        train_ids.reshape(2, 128),
+        query_ids.reshape(1, 128),
+        embed,
+        specs=[SMEM, HBM, HBM, HBM],
+        scratch_shapes=[
+            pltpu.VMEM((2, 128), jnp.int32),
+            pltpu.VMEM((1, 128), jnp.int32),
+            pltpu.VMEM((height, wide), bf16),
+            pltpu.VMEM((384, height), bf16),
+            pltpu.SemaphoreType.DMA((2 + LOOKUP_STEPS,)),
+        ],
+    )
 
 
 def norm_kernel(parts, gain, out):
@@ -128,20 +151,25 @@
         out[i] = normed
 
 
-def acts_kernel(normed, w_gate, w_up, w_gate_other, w_up_other, out):
+def acts_kernel(normed, *refs):
+    weights, (out, held, sems) = refs[:4], refs[4:]
+    copies = [pltpu.make_async_copy(weights[i], held.at[i], sems.at[i]) for i in range(4)]
+    for copy in copies:
+        copy.start()
     rows = normed[...]
 
-    def product(w):
+    def product(i):
+        copies[i].wait()
         return lax.dot_general(
-            w[...], rows, (((1,), (1,)), ((), ())), preferred_element_type=f32
-        )
-
-    def hidden(gate_w, up_w):
-        gate = product(gate_w)
-        return (gate / (1.0 + jnp.exp(-gate))) * product(up_w)
-
-    own = hidden(w_gate, w_up)
-    other = hidden(w_gate_other, w_up_other)
+            held[i], rows, (((1,), (1,)), ((), ())), preferred_element_type=f32
+        )
+
+    def hidden(i):
+        gate = product(i)
+        return (gate / (1.0 + jnp.exp(-gate))) * product(i + 1)
+
+    own = hidden(0)
+    other = hidden(2)
     asked = jnp.concatenate([own[:, 128:], other[:, 128:]], axis=1)
     fill = jnp.zeros((PACK - 3 * UNITS, 128), f32)
     out[...] = jnp.concatenate([own[:, :128], other[:, :128], asked, fill], axis=0).astype(bf16)
@@ -157,34 +185,38 @@
     def across(v):
         return lax.ppermute(v, "dp", YLO)
 
-    same, twin = {0: own}, {0: across(own)}
-    same[-1], same[1] = up(own), down(own)
-    twin[1], twin[-1] = across(same[1]), up(twin[0])
-    same[-2], same[2] = up(same[-1]), down(same[1])
-    twin[2], twin[-2] = across(same[2]), up(twin[-1])
-    same[-3], same[3] = up(same[-2]), down(same[2])
-    twin[3] = across(same[3])
-    same[4] = down(same[3])
-    twin[-3] = across(same[-3])
-    twin[4] = down(twin[3])
+    def together(*values):
+        return lax.optimization_barrier(values)
+
+    same, twin = {0: own}, {}
+    twin[0], same[-1], same[1] = together(across(own), up(own), down(own))
+    twin[1], same[-2], same[2] = together(across(same[1]), up(same[-1]), down(same[1]))
+    twin[2], twin[-1], same[-3], same[3] = together(
+        across(same[2]), up(twin[0]), up(same[-2]), down(same[2])
+    )
+    twin[3], twin[-2], same[4] = together(across(same[3]), up(twin[-1]), down(same[3]))
+    twin[-3], twin[4] = across(same[-3]), down(twin[3])
     return [group[step] for step in STEPS for group in (same, twin)]
 
 
-def group_order():
-    me = lax.axis_index("dp")
-    y, z = me // 8, me % 8
-    order = []
-    for step in STEPS:
-        for flip in range(2):
-            order.append((y ^ flip) * 8 + (z + step) % 8)
-    return jnp.stack(order)
-
-
 def rhs_kernel(scale, *refs):
-    blocks, (wide, part, flip) = refs[:16], refs[16:]
+    blocks, (me, columns, part, flip) = refs[:16], refs[16:]
+    y = lax.shift_right_logical(me[0], 3)
+    z = lax.bitwise_and(me[0], 7)
+    empty = jnp.zeros((64, 128), bf16)
     out = jnp.zeros((PACK - BOTH, 256), f32)
     for b in range(16):
-        out = out + dot(blocks[b][BOTH:, :], wide[b])
+        side = y if b % 2 == 0 else 1 - y
+        group = side * 8 + lax.bitwise_and(z + STEPS[b // 2], 7)
+        seen = columns[group]
+        wide = jnp.concatenate(
+            [
+                jnp.concatenate([seen, empty], axis=1),
+                jnp.concatenate([empty, seen], axis=1),
+            ],
+            axis=0,
+        )
+        out = out + dot(blocks[b][BOTH:, :], wide)
     out = out * scale
     part[:UNITS] = out[:UNITS, :128]
     part[UNITS:] = out[:UNITS, 128:]
@@ -357,8 +389,14 @@
     w_gate, w_up = w_gate.T, w_up.T
     w_gate_other, w_up_other = swap_core(w_gate), swap_core(w_up)
 
+    with jax.named_scope("cotangent"):
+        columns = lax.dynamic_slice_in_dim(cotangent, core * 64, 64, axis=0)
+        columns = lax.all_to_all(
+            columns.reshape(64, 16, 128).transpose(1, 0, 2), "dp", 0, 0, tiled=True
+        )
     with jax.named_scope("rows"):
-        mine, other = lookup(train_ids, query_ids, embed, core)
+        mine, other = lookup(train_ids, query_ids, embed)
+        mine, other, columns = lax.optimization_barrier((mine, other, columns))
         rows = (mine + swap_core(other)).reshape(8, 24, wide)
         rows = exchange_chips(rows)
     with jax.named_scope("normed"):
@@ -366,26 +404,21 @@
         normed = exchange_chips(normed).reshape(192, wide)
     with jax.named_scope("acts"):
         package = local_call(
-            acts_kernel, shape((PACK, 128), bf16), normed, w_gate, w_up, w_gate_other, w_up_other
+            acts_kernel,
+            shape((PACK, 128), bf16),
+            normed,
+            w_gate,
+            w_up,
+            w_gate_other,
+            w_up_other,
+            specs=[VMEM] + [HBM] * 4,
+            scratch_shapes=[
+                pltpu.VMEM((4, UNITS, wide), bf16),
+                pltpu.SemaphoreType.DMA((4,)),
+            ],
         )
     with jax.named_scope("groups"):
         blocks = gather_groups(package)
-    with jax.named_scope("cotangent"):
-        cotangent, _ = lax.optimization_barrier((cotangent, package))
-        mine = lax.dynamic_slice_in_dim(cotangent, core * 64, 64, axis=0)
-        columns = lax.all_to_all(
-            mine.reshape(64, 16, 128).transpose(1, 0, 2), "dp", 0, 0, tiled=True
-        )
-        columns = jnp.take(columns, group_order(), axis=0)
-        empty = jnp.zeros_like(columns)
-        columns = jnp.concatenate(
-            [
-                jnp.concatenate([columns, empty], axis=2),
-                jnp.concatenate([empty, columns], axis=2),
-            ],
-            axis=1,
-        )
-
     vector = shape((BOTH, 128), f32)
     longer = shape((BOTH + 8, 128), f32)
     small = shape((8, 128), f32)
@@ -399,7 +432,9 @@
             functools.partial(rhs_kernel, 1.0 / math.sqrt(2048)),
             (vector, vector),
             *blocks,
+            lax.axis_index("dp").reshape(1),
             columns,
+            specs=[VMEM] * 16 + [SMEM, VMEM],
         )
         got = swap_core(flip)
     with jax.named_scope("first"):

time: 224 us -> 243 us (1.085)
  waiting for transfers between devices: 34.4 us -> 42.9 us
  Pallas kernels: 19.9 us -> 26.5 us
  local copies, waits for them, and re-layouts: 7.9 us -> 13 us
  blocking collectives: 111 us -> 114 us
  starting transfers between devices: 48 us -> 45.5 us
    pallas_call x13 -> x14, Pallas kernels: 13.1 us -> 26.5 us  [local_call(): pl.pallas_call(kernel, out_shape=outs, in_specs=specs or [VMEM] * len(arg...]
    ppermute x5, waiting for transfers between devices: 5.72 us -> 15.1 us  [up(): return lax.ppermute(v, 'dp', z_shift(1))]
    unnamed x12 -> x28, local copies, waits for them, and re-layouts: 4.72 us -> 12.2 us
    pallas_call x1 -> x0, Pallas kernels: 6.82 us -> none  [lookup(): pl.pallas_call(lookup_kernel, grid=(wide // step,), out_shape=(out, out),...]
    all_to_all x1, starting transfers between devices: 4.19 us -> 10.1 us  [body(): lax.all_to_all(columns.reshape(64, 16, 128).transpose(1, 0, 2), 'dp', 0,...]
    ppermute x5, starting transfers between devices: 4.11 us -> 0.01 us  [up(): return lax.ppermute(v, 'dp', z_shift(1))]
    all_to_all x1, waiting for transfers between devices: 3.74 us -> 0.01 us  [body(): lax.all_to_all(columns.reshape(64, 16, 128).transpose(1, 0, 2), 'dp', 0,...]
    ppermute x6, starting transfers between devices: 18.2 us -> 15.5 us  [swap_core(): return lax.ppermute(v, 'shard', CORE)]
  transfers between devices with their start and end apart: 23 -> 23, of which waited for: 11 -> 15; matrix products, arithmetic and copies ran while one was open for 2% -> 0% of each run, Pallas kernels for 1% -> 3%
where the time goes in v4:
time: 243 us; the launch traced here: 242 us
  blocking collectives  114 us (47%)
  starting transfers between devices  45.5 us (19%)
  waiting for transfers between devices  42.9 us (18%)
  Pallas kernels  26.5 us (11%)
  local copies, waits for them, and re-layouts  13 us (5%)
    all_to_all x6, blocking collectives, exchange_chips(): return lax.all_to_all(v, 'shard', 0, 0, axis_index_groups=CHIPS, tiled=True)  89.3 us
    pallas_call x14, Pallas kernels, local_call(): pl.pallas_call(kernel, out_shape=outs, in_specs=specs or [VMEM] * len(arg...  26.5 us
    ppermute x6, starting transfers between devices, swap_core(): return lax.ppermute(v, 'shard', CORE)  15.5 us
    ppermute x5, waiting for transfers between devices, up(): return lax.ppermute(v, 'dp', z_shift(1))  15.1 us
    ppermute x5, starting transfers between devices, down(): return lax.ppermute(v, 'dp', z_shift(-1))  12.8 us
    unnamed x28, local copies, waits for them, and re-layouts  12.2 us
    all_to_all x1, blocking collectives, body(): every = lax.all_to_all(mine, 'dp', 0, 0, tiled=True)  12.2 us
    all_to_all x1, blocking collectives, body(): partials = lax.all_to_all(partials, 'shard', 0, 0, tiled=True)  12.1 us
  transfers between devices with their start and end apart: 23, of which 15 were waited for; matrix products, arithmetic and copies ran while one was open for 0% of the time, Pallas kernels for 3%

profile of v4, /device:TPU:1, one launch (start us, length us, event | category | flops | bytes accessed | tf_op | source)
XLA Modules:
  0.0 241.9 jit_solution(13826808018482378450)
XLA Ops:
  1.8 10.1 %all-to-all-start = ((bf16[16,64,128]{2,1,0:T(8,128)(2,1)}), bf16[16,64,128]{2,1,0:T(8,128)(2,1)S(1)}, u32[]{:S(2)}, u32[]{:S(2)}) async-start(bf16[16,64,128]{2,1,0:T(8,128)(2,1)} %bitcast_bitcast_fusion), calls=%async_computation | async-start | bytes 524288 | tf_op jit(solution)/shard_map/cotangent/all_to_all | solution.py:394
  12.0 3.3 %copy-done.5 = bf16[2000,2048]{1,0:T(8,128)(2,1)S(1)} copy-done((bf16[2000,2048]{1,0:T(8,128)(2,1)S(1)}, bf16[2000,2048]{1,0:T(8,128)(2,1)}, u32[]{:S(2)}) %copy-start.5) | copy-done | bytes 8192024
  16.6 6.4 %rows.1 = (bf16[192,2048]{1,0:T(8,128)(2,1)S(1)}, bf16[192,2048]{1,0:T(8,128)(2,1)S(1)}) custom-call(s32[1]{0:T(128)} %bitcast.1.place, s32[2,128]{1,0:T(2,128)S(1)} %bitcast.22, s32[1,128]{1,0:T(1,128)S(1)} %bitcast.23, bf16[2000,2048]{1,0:T(8,128)(2,1)S(1)} %copy-done.5), custom_call_target="tpu_custom_call" | custom-call | tf_op jit(solution)/shard_map/rows/pallas_call | solution.py:43
  27.4 18.9 %all_to_all.50.parts = bf16[8,24,2048]{2,1,0:T(8,128)(2,1)S(1)} all-to-all(bf16[8,24,2048]{2,1,0:T(8,128)(2,1)S(1)} %bitcast.24), channel_id=1, replica_groups={{0,2,4,6,8,10,12,14},{1,3,5,7,9,11,13,15},{16,18,20,22,24,26,28,30},{17..., dimensions={0} | all-to-all | bytes 1572864 | tf_op jit(solution)/shard_map/rows/all_to_all | solution.py:39
  47.5 3.9 %all-to-all-start.2 = ((bf16[8,24,2048]{2,1,0:T(8,128)(2,1)}), bf16[8,24,2048]{2,1,0:T(8,128)(2,1)S(1)}, u32[]{:S(2)}, u32[]{:S(2)}) async-start(bf16[8,24,2048]{2,1,0:T(8,128)(2,1)} %normed.1), calls=%async_computation.2 | async-start | bytes 1572864 | tf_op jit(solution)/shard_map/normed/all_to_all | solution.py:39
  51.4 12.0 %all-to-all-done.2 = bf16[8,24,2048]{2,1,0:T(8,128)(2,1)S(1)} async-done(((bf16[8,24,2048]{2,1,0:T(8,128)(2,1)}), bf16[8,24,2048]{2,1,0:T(8,128)(2,1)S(1)}, u32[]{:S(2)}, u32[]{:S(2)}) %all-to-all-start.2) | async-done | bytes 786464 | tf_op jit(solution)/shard_map/normed/all_to_all | solution.py:39
  64.7 4.2 %acts.1.refs_0_ = bf16[1040,128]{1,0:T(8,128)(2,1)S(1)} custom-call(bf16[192,2048]{1,0:T(8,128)(2,1)S(1)} %bitcast.16, bf16[344,2048]{1,0:T(8,128)(2,1)S(1)} %bitcast.18, bf16[344,2048]{1,0:T(8,128)(2,1)S(1)} %bitcast.20, bf16[344,2048]{1,0:T(8,128)(2,1)} %collective-permute-done.1.refs_2_, bf16[344,2048]{1,0:T(8,128)(2,1)} %collective-permute-done.2.refs_3_), custom_call_target="tpu_custom_call" | custom-call | tf_op jit(solution)/shard_map/acts/pallas_call | solution.py:43
  68.9 2.9 %collective-permute-start.5 = (bf16[1040,128]{1,0:T(8,128)(2,1)S(1)}, bf16[1040,128]{1,0:T(8,128)(2,1)S(1)}, u32[]{:S(2)}, u32[]{:S(2)}) collective-permute-start(bf16[1040,128]{1,0:T(8,128)(2,1)S(1)} %acts.1.refs_0_), channel_id=1, source_target_pairs={{0,112},{16,0},{32,16},{48,32},{64,48},{80,64},{96,80},{112,96},{1... | collective-permute-start | bytes 798728 | tf_op jit(solution)/shard_map/groups/ppermute | solution.py:183
  72.5 2.8 %collective-permute-done.5.refs_4_ = bf16[1040,128]{1,0:T(8,128)(2,1)S(1)} collective-permute-done((bf16[1040,128]{1,0:T(8,128)(2,1)S(1)}, bf16[1040,128]{1,0:T(8,128)(2,1)S(1)}, u32[]{:S(2)}, u32[]{:S(2)}) %collective-permute-start.5) | collective-permute-done | bytes 266272 | tf_op jit(solution)/shard_map/groups/ppermute | solution.py:183
  75.2 3.1 %collective-permute-done.4.refs_2_ = bf16[1040,128]{1,0:T(8,128)(2,1)S(1)} collective-permute-done((bf16[1040,128]{1,0:T(8,128)(2,1)S(1)}, bf16[1040,128]{1,0:T(8,128)(2,1)S(1)}, u32[]{:S(2)}, u32[]{:S(2)}) %collective-permute-start.4) | collective-permute-done | bytes 266272 | tf_op jit(solution)/shard_map/groups/ppermute | solution.py:180
  78.4 2.7 %collective-permute-start.8 = (bf16[1040,128]{1,0:T(8,128)(2,1)S(1)}, bf16[1040,128]{1,0:T(8,128)(2,1)S(1)}, u32[]{:S(2)}, u32[]{:S(2)}) collective-permute-start(bf16[1040,128]{1,0:T(8,128)(2,1)S(1)} %collective-permute-done.5.refs_4_), channel_id=1, source_target_pairs={{0,112},{16,0},{32,16},{48,32},{64,48},{80,64},{96,80},{112,96},{1... | collective-permute-start | bytes 798728 | tf_op jit(solution)/shard_map/groups/ppermute | solution.py:183
  81.6 3.2 %collective-permute-done.7.refs_6_ = bf16[1040,128]{1,0:T(8,128)(2,1)S(1)} collective-permute-done((bf16[1040,128]{1,0:T(8,128)(2,1)S(1)}, bf16[1040,128]{1,0:T(8,128)(2,1)S(1)}, u32[]{:S(2)}, u32[]{:S(2)}) %collective-permute-start.7) | collective-permute-done | bytes 266272 | tf_op jit(solution)/shard_map/groups/ppermute | solution.py:180
  86.6 2.7 %collective-permute-start.12 = (bf16[1040,128]{1,0:T(8,128)(2,1)S(1)}, bf16[1040,128]{1,0:T(8,128)(2,1)S(1)}, u32[]{:S(2)}, u32[]{:S(2)}) collective-permute-start(bf16[1040,128]{1,0:T(8,128)(2,1)S(1)} %collective-permute-done.8.refs_8_), channel_id=1, source_target_pairs={{0,112},{16,0},{32,16},{48,32},{64,48},{80,64},{96,80},{112,96},{1... | collective-permute-start | bytes 798728 | tf_op jit(solution)/shard_map/groups/ppermute | solution.py:183
  90.1 6.2 %collective-permute-done.11.refs_10_ = bf16[1040,128]{1,0:T(8,128)(2,1)S(1)} collective-permute-done((bf16[1040,128]{1,0:T(8,128)(2,1)S(1)}, bf16[1040,128]{1,0:T(8,128)(2,1)S(1)}, u32[]{:S(2)}, u32[]{:S(2)}) %collective-permute-start.11) | collective-permute-done | bytes 266272 | tf_op jit(solution)/shard_map/groups/ppermute | solution.py:180
  96.3 2.7 %collective-permute-start.15 = (bf16[1040,128]{1,0:T(8,128)(2,1)S(1)}, bf16[1040,128]{1,0:T(8,128)(2,1)S(1)}, u32[]{:S(2)}, u32[]{:S(2)}) collective-permute-start(bf16[1040,128]{1,0:T(8,128)(2,1)S(1)} %collective-permute-done.12.refs_12_), channel_id=1, source_target_pairs={{0,112},{16,0},{32,16},{48,32},{64,48},{80,64},{96,80},{112,96},{1... | collective-permute-start | bytes 798728 | tf_op jit(solution)/shard_map/groups/ppermute | solution.py:183
  100.5 2.3 collective-permute-done.14.refs_7_
  107.4 4.3 %collective-permute-done.17.refs_15_ = bf16[1040,128]{1,0:T(8,128)(2,1)} collective-permute-done((bf16[1040,128]{1,0:T(8,128)(2,1)}, bf16[1040,128]{1,0:T(8,128)(2,1)}, u32[]{:S(2)}, u32[]{:S(2)}) %collective-permute-start.17) | collective-permute-done | bytes 266272 | tf_op jit(solution)/shard_map/groups/ppermute | solution.py:183
  114.6 2.0 rhs.1
  116.6 8.0 %collective-permute-start.18 = (f32[688,128]{1,0:T(8,128)S(1)}, f32[688,128]{1,0:T(8,128)S(1)}, u32[]{:S(2)}, u32[]{:S(2)}) collective-permute-start(f32[688,128]{1,0:T(8,128)S(1)} %get-tuple-element.64), channel_id=1, source_target_pairs={{0,1},{1,0},{2,3},{3,2},{4,5},{5,4},{6,7},{7,6},{8,9},{9,8},{10,11... | collective-permute-start | bytes 1056776 | tf_op jit(solution)/shard_map/rhs/ppermute | solution.py:35
  127.7 17.4 %all_to_all.51.parts = bf16[8,128,256]{2,1,0:T(8,128)(2,1)S(1)} all-to-all(bf16[8,128,256]{2,1,0:T(8,128)(2,1)S(1)} %get-tuple-element.65), channel_id=1, replica_groups={{0,2,4,6,8,10,12,14},{1,3,5,7,9,11,13,15},{16,18,20,22,24,26,28,30},{17..., dimensions={0} | all-to-all | bytes 1048576 | tf_op jit(solution)/shard_map/first/all_to_all | solution.py:39
  145.3 14.0 %all_to_all.52.refs_16_ = bf16[8,144,256]{2,1,0:T(8,128)(2,1)S(1)} all-to-all(bf16[8,144,256]{2,1,0:T(8,128)(2,1)S(1)} %get-tuple-element.67), channel_id=1, replica_groups={{0,2,4,6,8,10,12,14},{1,3,5,7,9,11,13,15},{16,18,20,22,24,26,28,30},{17..., dimensions={0} | all-to-all | bytes 1179648 | tf_op jit(solution)/shard_map/first/all_to_all | solution.py:39
  159.3 2.0 first.5
  161.3 3.0 %collective-permute-start.19 = (f32[696,128]{1,0:T(8,128)S(1)}, f32[696,128]{1,0:T(8,128)S(1)}, u32[]{:S(2)}, u32[]{:S(2)}) collective-permute-start(f32[696,128]{1,0:T(8,128)S(1)} %get-tuple-element.69), channel_id=1, source_target_pairs={{0,1},{1,0},{2,3},{3,2},{4,5},{5,4},{6,7},{7,6},{8,9},{9,8},{10,11... | collective-permute-start | bytes 1069064 | tf_op jit(solution)/shard_map/first/ppermute | solution.py:35
  165.6 2.0 second.3
  167.6 12.7 %all_to_all.53.parts = bf16[8,128,256]{2,1,0:T(8,128)(2,1)S(1)} all-to-all(bf16[8,128,256]{2,1,0:T(8,128)(2,1)S(1)} %get-tuple-element.72), channel_id=1, replica_groups={{0,2,4,6,8,10,12,14},{1,3,5,7,9,11,13,15},{16,18,20,22,24,26,28,30},{17..., dimensions={0} | all-to-all | bytes 1048576 | tf_op jit(solution)/shard_map/second/all_to_all | solution.py:39
  180.5 13.6 %all_to_all.54.refs_16_ = bf16[8,144,256]{2,1,0:T(8,128)(2,1)S(1)} all-to-all(bf16[8,144,256]{2,1,0:T(8,128)(2,1)S(1)} %get-tuple-element.75), channel_id=1, replica_groups={{0,2,4,6,8,10,12,14},{1,3,5,7,9,11,13,15},{16,18,20,22,24,26,28,30},{17..., dimensions={0} | all-to-all | bytes 1179648 | tf_op jit(solution)/shard_map/second/all_to_all | solution.py:39
  194.1 2.3 second.5
  196.4 3.1 %collective-permute-start.20 = (f32[696,128]{1,0:T(8,128)S(1)}, f32[696,128]{1,0:T(8,128)S(1)}, u32[]{:S(2)}, u32[]{:S(2)}) collective-permute-start(f32[696,128]{1,0:T(8,128)S(1)} %get-tuple-element.78), channel_id=1, source_target_pairs={{0,1},{1,0},{2,3},{3,2},{4,5},{5,4},{6,7},{7,6},{8,9},{9,8},{10,11... | collective-permute-start | bytes 1069064 | tf_op jit(solution)/shard_map/second/ppermute | solution.py:35
  200.7 2.2 third.2
  202.9 12.7 %all_to_all.55.parts = bf16[8,128,256]{2,1,0:T(8,128)(2,1)S(1)} all-to-all(bf16[8,128,256]{2,1,0:T(8,128)(2,1)S(1)} %get-tuple-element.81), channel_id=1, replica_groups={{0,2,4,6,8,10,12,14},{1,3,5,7,9,11,13,15},{16,18,20,22,24,26,28,30},{17..., dimensions={0} | all-to-all | bytes 1048576 | tf_op jit(solution)/shard_map/third/all_to_all | solution.py:39
  216.0 12.1 %all_to_all.56.got = f32[16,8,128]{2,1,0:T(8,128)S(1)} all-to-all(f32[16,8,128]{2,1,0:T(8,128)S(1)} %third.3), channel_id=1, replica_groups=mesh['dp'=16,'shard'=16] {'shard'}, dimensions={0} | all-to-all | bytes 131072 | tf_op jit(solution)/shard_map/third/all_to_all | solution.py:475
  228.5 12.2 %all_to_all.57.got = f32[16,8,128]{2,1,0:T(8,128)S(1)} all-to-all(f32[16,8,128]{2,1,0:T(8,128)S(1)} %whole.2), channel_id=1, replica_groups=mesh['dp'=16,'shard'=16] {'dp'}, dimensions={0} | all-to-all | bytes 131072 | tf_op jit(solution)/shard_map/whole/all_to_all | solution.py:478
  (66 shorter events, 30.8 us)
Async XLA Ops:
  0.0 1.0 copy-start
  1.8 22.2 %all-to-all-start = ((bf16[16,64,128]{2,1,0:T(8,128)(2,1)}), bf16[16,64,128]{2,1,0:T(8,128)(2,1)S(1)}, u32[]{:S(2)}, u32[]{:S(2)}) async-start(bf16[16,64,128]{2,1,0:T(8,128)(2,1)} %bitcast_bitcast_fusion), calls=%async_computation | async-start | bytes 524288 | tf_op jit(solution)/shard_map/cotangent/all_to_all | solution.py:394
  12.0 3.3 %copy-start.5 = (bf16[2000,2048]{1,0:T(8,128)(2,1)S(1)}, bf16[2000,2048]{1,0:T(8,128)(2,1)}, u32[]{:S(2)}) copy-start(bf16[2000,2048]{1,0:T(8,128)(2,1)} %table_hbm.1) | copy-start | bytes 24576004
  16.6 8.3 %copy-start.6 = (bf16[2048,344]{0,1:T(8,128)(2,1)S(1)}, bf16[2048,344]{0,1:T(8,128)(2,1)}, u32[]{:S(2)}) copy-start(bf16[2048,344]{0,1:T(8,128)(2,1)} %param.11) | copy-start | bytes 4227076
  24.0 22.4 %copy-start.8 = (bf16[16,64,128]{2,1,0:T(8,128)(2,1)}, bf16[16,64,128]{2,1,0:T(8,128)(2,1)S(1)}, u32[]{:S(2)}) copy-start(bf16[16,64,128]{2,1,0:T(8,128)(2,1)S(1)} %all-to-all-done.refs_17_) | copy-start | bytes 786436
  24.0 3.2 %collective-permute-start = (bf16[192,2048]{1,0:T(8,128)(2,1)}, bf16[192,2048]{1,0:T(8,128)(2,1)S(1)}, u32[]{:S(2)}, u32[]{:S(2)}) collective-permute-start(bf16[192,2048]{1,0:T(8,128)(2,1)} %copy-done.13), channel_id=1, source_target_pairs={{0,1},{1,0},{2,3},{3,2},{4,5},{5,4},{6,7},{7,6},{8,9},{9,8},{10,11... | collective-permute-start | bytes 2359304 | tf_op jit(solution)/shard_map/rows/ppermute | solution.py:35
  24.9 26.4 %collective-permute-start.1 = (bf16[344,2048]{1,0:T(8,128)(2,1)S(1)}, bf16[344,2048]{1,0:T(8,128)(2,1)}, u32[]{:S(2)}, u32[]{:S(2)}) collective-permute-start(bf16[344,2048]{1,0:T(8,128)(2,1)S(1)} %bitcast.17), channel_id=1, source_target_pairs={{0,1},{1,0},{2,3},{3,2},{4,5},{5,4},{6,7},{7,6},{8,9},{9,8},{10,11... | collective-permute-start | bytes 4227080 | tf_op jit(solution)/shard_map/ppermute | solution.py:35
  25.0 21.3 %copy-start.10 = (f32[2048]{0:T(1024)S(1)}, f32[2048]{0:T(1024)}, u32[]{:S(2)}) copy-start(f32[2048]{0:T(1024)} %param.10) | copy-start | bytes 24580
  25.0 26.3 %collective-permute-start.2 = (bf16[344,2048]{1,0:T(8,128)(2,1)}, bf16[344,2048]{1,0:T(8,128)(2,1)}, u32[]{:S(2)}, u32[]{:S(2)}) collective-permute-start(bf16[344,2048]{1,0:T(8,128)(2,1)} %bitcast.19), channel_id=1, source_target_pairs={{0,1},{1,0},{2,3},{3,2},{4,5},{5,4},{6,7},{7,6},{8,9},{9,8},{10,11... | collective-permute-start | bytes 4227080 | tf_op jit(solution)/shard_map/ppermute | solution.py:35
  47.5 15.9 %all-to-all-start.2 = ((bf16[8,24,2048]{2,1,0:T(8,128)(2,1)}), bf16[8,24,2048]{2,1,0:T(8,128)(2,1)S(1)}, u32[]{:S(2)}, u32[]{:S(2)}) async-start(bf16[8,24,2048]{2,1,0:T(8,128)(2,1)} %normed.1), calls=%async_computation.2 | async-start | bytes 1572864 | tf_op jit(solution)/shard_map/normed/all_to_all | solution.py:39
  63.4 1.4 copy-start.7
  68.9 6.3 %collective-permute-start.5 = (bf16[1040,128]{1,0:T(8,128)(2,1)S(1)}, bf16[1040,128]{1,0:T(8,128)(2,1)S(1)}, u32[]{:S(2)}, u32[]{:S(2)}) collective-permute-start(bf16[1040,128]{1,0:T(8,128)(2,1)S(1)} %acts.1.refs_0_), channel_id=1, source_target_pairs={{0,112},{16,0},{32,16},{48,32},{64,48},{80,64},{96,80},{112,96},{1... | collective-permute-start | bytes 798728 | tf_op jit(solution)/shard_map/groups/ppermute | solution.py:183
  71.9 6.5 %collective-permute-start.4 = (bf16[1040,128]{1,0:T(8,128)(2,1)S(1)}, bf16[1040,128]{1,0:T(8,128)(2,1)S(1)}, u32[]{:S(2)}, u32[]{:S(2)}) collective-permute-start(bf16[1040,128]{1,0:T(8,128)(2,1)S(1)} %acts.1.refs_0_), channel_id=1, source_target_pairs={{0,16},{16,32},{32,48},{48,64},{64,80},{80,96},{96,112},{112,0},{1... | collective-permute-start | bytes 798728 | tf_op jit(solution)/shard_map/groups/ppermute | solution.py:180
  71.9 6.5 %collective-permute-start.3 = (bf16[1040,128]{1,0:T(8,128)(2,1)S(1)}, bf16[1040,128]{1,0:T(8,128)(2,1)S(1)}, u32[]{:S(2)}, u32[]{:S(2)}) collective-permute-start(bf16[1040,128]{1,0:T(8,128)(2,1)S(1)} %acts.1.refs_0_), channel_id=1, source_target_pairs={{0,128},{16,144},{32,160},{48,176},{64,192},{80,208},{96,224},{112... | collective-permute-start | bytes 798728 | tf_op jit(solution)/shard_map/groups/ppermute | solution.py:186
  78.4 6.5 %collective-permute-start.7 = (bf16[1040,128]{1,0:T(8,128)(2,1)S(1)}, bf16[1040,128]{1,0:T(8,128)(2,1)S(1)}, u32[]{:S(2)}, u32[]{:S(2)}) collective-permute-start(bf16[1040,128]{1,0:T(8,128)(2,1)S(1)} %collective-permute-done.4.refs_2_), channel_id=1, source_target_pairs={{0,16},{16,32},{32,48},{48,64},{64,80},{80,96},{96,112},{112,0},{1... | collective-permute-start | bytes 798728 | tf_op jit(solution)/shard_map/groups/ppermute | solution.py:180
  78.4 6.5 %collective-permute-start.8 = (bf16[1040,128]{1,0:T(8,128)(2,1)S(1)}, bf16[1040,128]{1,0:T(8,128)(2,1)S(1)}, u32[]{:S(2)}, u32[]{:S(2)}) collective-permute-start(bf16[1040,128]{1,0:T(8,128)(2,1)S(1)} %collective-permute-done.5.refs_4_), channel_id=1, source_target_pairs={{0,112},{16,0},{32,16},{48,32},{64,48},{80,64},{96,80},{112,96},{1... | collective-permute-start | bytes 798728 | tf_op jit(solution)/shard_map/groups/ppermute | solution.py:183
  81.0 5.6 %collective-permute-start.6 = (bf16[1040,128]{1,0:T(8,128)(2,1)S(1)}, bf16[1040,128]{1,0:T(8,128)(2,1)S(1)}, u32[]{:S(2)}, u32[]{:S(2)}) collective-permute-start(bf16[1040,128]{1,0:T(8,128)(2,1)S(1)} %collective-permute-done.5.refs_4_), channel_id=1, source_target_pairs={{0,128},{16,144},{32,160},{48,176},{64,192},{80,208},{96,224},{112... | collective-permute-start | bytes 798728 | tf_op jit(solution)/shard_map/groups/ppermute | solution.py:186
  81.6 8.5 %collective-permute-start.10 = (bf16[1040,128]{1,0:T(8,128)(2,1)S(1)}, bf16[1040,128]{1,0:T(8,128)(2,1)S(1)}, u32[]{:S(2)}, u32[]{:S(2)}) collective-permute-start(bf16[1040,128]{1,0:T(8,128)(2,1)S(1)} %collective-permute-done.3.refs_1_), channel_id=1, source_target_pairs={{0,16},{16,32},{32,48},{48,64},{64,80},{80,96},{96,112},{112,0},{1... | collective-permute-start | bytes 798728 | tf_op jit(solution)/shard_map/groups/ppermute | solution.py:180
  86.6 9.7 %collective-permute-start.11 = (bf16[1040,128]{1,0:T(8,128)(2,1)S(1)}, bf16[1040,128]{1,0:T(8,128)(2,1)S(1)}, u32[]{:S(2)}, u32[]{:S(2)}) collective-permute-start(bf16[1040,128]{1,0:T(8,128)(2,1)S(1)} %collective-permute-done.7.refs_6_), channel_id=1, source_target_pairs={{0,16},{16,32},{32,48},{48,64},{64,80},{80,96},{96,112},{112,0},{1... | collective-permute-start | bytes 798728 | tf_op jit(solution)/shard_map/groups/ppermute | solution.py:180
  86.6 9.7 %collective-permute-start.12 = (bf16[1040,128]{1,0:T(8,128)(2,1)S(1)}, bf16[1040,128]{1,0:T(8,128)(2,1)S(1)}, u32[]{:S(2)}, u32[]{:S(2)}) collective-permute-start(bf16[1040,128]{1,0:T(8,128)(2,1)S(1)} %collective-permute-done.8.refs_8_), channel_id=1, source_target_pairs={{0,112},{16,0},{32,16},{48,32},{64,48},{80,64},{96,80},{112,96},{1... | collective-permute-start | bytes 798728 | tf_op jit(solution)/shard_map/groups/ppermute | solution.py:183
  89.3 7.0 %collective-permute-start.9 = (bf16[1040,128]{1,0:T(8,128)(2,1)S(1)}, bf16[1040,128]{1,0:T(8,128)(2,1)S(1)}, u32[]{:S(2)}, u32[]{:S(2)}) collective-permute-start(bf16[1040,128]{1,0:T(8,128)(2,1)S(1)} %collective-permute-done.8.refs_8_), channel_id=1, source_target_pairs={{0,128},{16,144},{32,160},{48,176},{64,192},{80,208},{96,224},{112... | collective-permute-start | bytes 798728 | tf_op jit(solution)/shard_map/groups/ppermute | solution.py:186
  96.3 6.5 %collective-permute-start.14 = (bf16[1040,128]{1,0:T(8,128)(2,1)S(1)}, bf16[1040,128]{1,0:T(8,128)(2,1)S(1)}, u32[]{:S(2)}, u32[]{:S(2)}) collective-permute-start(bf16[1040,128]{1,0:T(8,128)(2,1)S(1)} %collective-permute-done.10.refs_3_), channel_id=1, source_target_pairs={{0,16},{16,32},{32,48},{48,64},{64,80},{80,96},{96,112},{112,0},{1... | collective-permute-start | bytes 798728 | tf_op jit(solution)/shard_map/groups/ppermute | solution.py:180
  96.3 7.2 %collective-permute-start.15 = (bf16[1040,128]{1,0:T(8,128)(2,1)S(1)}, bf16[1040,128]{1,0:T(8,128)(2,1)S(1)}, u32[]{:S(2)}, u32[]{:S(2)}) collective-permute-start(bf16[1040,128]{1,0:T(8,128)(2,1)S(1)} %collective-permute-done.12.refs_12_), channel_id=1, source_target_pairs={{0,112},{16,0},{32,16},{48,32},{64,48},{80,64},{96,80},{112,96},{1... | collective-permute-start | bytes 798728 | tf_op jit(solution)/shard_map/groups/ppermute | solution.py:183
  99.0 5.4 %collective-permute-start.13 = (bf16[1040,128]{1,0:T(8,128)(2,1)S(1)}, bf16[1040,128]{1,0:T(8,128)(2,1)}, u32[]{:S(2)}, u32[]{:S(2)}) collective-permute-start(bf16[1040,128]{1,0:T(8,128)(2,1)S(1)} %collective-permute-done.12.refs_12_), channel_id=1, source_target_pairs={{0,128},{16,144},{32,160},{48,176},{64,192},{80,208},{96,224},{112... | collective-permute-start | bytes 798728 | tf_op jit(solution)/shard_map/groups/ppermute | solution.py:186
  99.8 7.6 %collective-permute-start.16 = (bf16[1040,128]{1,0:T(8,128)(2,1)S(1)}, bf16[1040,128]{1,0:T(8,128)(2,1)}, u32[]{:S(2)}, u32[]{:S(2)}) collective-permute-start(bf16[1040,128]{1,0:T(8,128)(2,1)S(1)} %collective-permute-done.11.refs_10_), channel_id=1, source_target_pairs={{0,128},{16,144},{32,160},{48,176},{64,192},{80,208},{96,224},{112... | collective-permute-start | bytes 798728 | tf_op jit(solution)/shard_map/groups/ppermute | solution.py:186
  104.4 7.3 %collective-permute-start.17 = (bf16[1040,128]{1,0:T(8,128)(2,1)}, bf16[1040,128]{1,0:T(8,128)(2,1)}, u32[]{:S(2)}, u32[]{:S(2)}) collective-permute-start(bf16[1040,128]{1,0:T(8,128)(2,1)} %collective-permute-done.13.refs_13_), channel_id=1, source_target_pairs={{0,112},{16,0},{32,16},{48,32},{64,48},{80,64},{96,80},{112,96},{1... | collective-permute-start | bytes 798728 | tf_op jit(solution)/shard_map/groups/ppermute | solution.py:183
  111.7 1.0 copy-start.2
  112.6 1.0 copy-start.4
  113.6 0.9 copy-start.9
  116.6 9.3 %collective-permute-start.18 = (f32[688,128]{1,0:T(8,128)S(1)}, f32[688,128]{1,0:T(8,128)S(1)}, u32[]{:S(2)}, u32[]{:S(2)}) collective-permute-start(f32[688,128]{1,0:T(8,128)S(1)} %get-tuple-element.64), channel_id=1, source_target_pairs={{0,1},{1,0},{2,3},{3,2},{4,5},{5,4},{6,7},{7,6},{8,9},{9,8},{10,11... | collective-permute-start | bytes 1056776 | tf_op jit(solution)/shard_map/rhs/ppermute | solution.py:35
  161.3 4.3 %collective-permute-start.19 = (f32[696,128]{1,0:T(8,128)S(1)}, f32[696,128]{1,0:T(8,128)S(1)}, u32[]{:S(2)}, u32[]{:S(2)}) collective-permute-start(f32[696,128]{1,0:T(8,128)S(1)} %get-tuple-element.69), channel_id=1, source_target_pairs={{0,1},{1,0},{2,3},{3,2},{4,5},{5,4},{6,7},{7,6},{8,9},{9,8},{10,11... | collective-permute-start | bytes 1069064 | tf_op jit(solution)/shard_map/first/ppermute | solution.py:35
  196.4 4.4 %collective-permute-start.20 = (f32[696,128]{1,0:T(8,128)S(1)}, f32[696,128]{1,0:T(8,128)S(1)}, u32[]{:S(2)}, u32[]{:S(2)}) collective-permute-start(f32[696,128]{1,0:T(8,128)S(1)} %get-tuple-element.78), channel_id=1, source_target_pairs={{0,1},{1,0},{2,3},{3,2},{4,5},{5,4},{6,7},{7,6},{8,9},{9,8},{10,11... | collective-permute-start | bytes 1069064 | tf_op jit(solution)/shard_map/second/ppermute | solution.py:35
  (5 other events, 3.6 us)

commit v5 on v4

--- a/solution.py
+++ b/solution.py
@@ -39,15 +39,19 @@
     return lax.all_to_all(v, "shard", 0, 0, axis_index_groups=CHIPS, tiled=True)
 
 
-def local_call(kernel, outs, *args, specs=None, **more):
+def local_call(kernel, outs, *args, specs=None, vmem=16, **more):
     return pl.pallas_call(
         kernel,
         out_shape=outs,
         in_specs=specs or [VMEM] * len(args),
         out_specs=jax.tree.map(lambda _: VMEM, outs),
-        compiler_params=pltpu.CompilerParams(vmem_limit_bytes=24 * 2**20),
+        compiler_params=pltpu.CompilerParams(vmem_limit_bytes=vmem * 2**20),
         **more,
     )(*args)
+
+
+def in_hbm(*values):
+    return [pltpu.with_memory_space_constraint(v, pltpu.HBM) for v in values]
 
 
 def shape(dims, dtype):
@@ -129,10 +133,9 @@
         lookup_kernel,
         (out, out),
         lax.axis_index("shard").reshape(1),
-        train_ids.reshape(2, 128),
-        query_ids.reshape(1, 128),
-        embed,
+        *in_hbm(train_ids.reshape(2, 128), query_ids.reshape(1, 128), embed),
         specs=[SMEM, HBM, HBM, HBM],
+        vmem=24,
         scratch_shapes=[
             pltpu.VMEM((2, 128), jnp.int32),
             pltpu.VMEM((1, 128), jnp.int32),
@@ -143,6 +146,11 @@
     )
 
 
+def add_kernel(mine, got, out):
+    for i in range(8):
+        out[i] = mine[i] + got[i]
+
+
 def norm_kernel(parts, gain, out):
     rows = jnp.sum(parts[...].astype(f32), axis=0)
     inv_scale = lax.rsqrt(jnp.mean(rows * rows, axis=-1, keepdims=True) + norm_eps)
@@ -151,31 +159,26 @@
         out[i] = normed
 
 
-def acts_kernel(normed, *refs):
-    weights, (out, held, sems) = refs[:4], refs[4:]
-    copies = [pltpu.make_async_copy(weights[i], held.at[i], sems.at[i]) for i in range(4)]
-    for copy in copies:
-        copy.start()
+def acts_kernel(normed, w_gate, w_up, w_gate_other, w_up_other, out):
     rows = normed[...]
 
-    def product(i):
-        copies[i].wait()
+    def product(w):
         return lax.dot_general(
-            held[i], rows, (((1,), (1,)), ((), ())), preferred_element_type=f32
-        )
-
-    def hidden(i):
-        gate = product(i)
-        return (gate / (1.0 + jnp.exp(-gate))) * product(i + 1)
-
-    own = hidden(0)
-    other = hidden(2)
+            w[...], rows, (((1,), (1,)), ((), ())), preferred_element_type=f32
+        )
+
+    def hidden(gate_w, up_w):
+        gate = product(gate_w)
+        return (gate / (1.0 + jnp.exp(-gate))) * product(up_w)
+
+    own = hidden(w_gate, w_up)
+    other = hidden(w_gate_other, w_up_other)
     asked = jnp.concatenate([own[:, 128:], other[:, 128:]], axis=1)
     fill = jnp.zeros((PACK - 3 * UNITS, 128), f32)
     out[...] = jnp.concatenate([own[:, :128], other[:, :128], asked, fill], axis=0).astype(bf16)
 
 
-def gather_groups(own):
+def gather_groups(own, columns):
     def up(v):
         return lax.ppermute(v, "dp", z_shift(1))
 
@@ -189,18 +192,17 @@
         return lax.optimization_barrier(values)
 
     same, twin = {0: own}, {}
-    twin[0], same[-1], same[1] = together(across(own), up(own), down(own))
-    twin[1], same[-2], same[2] = together(across(same[1]), up(same[-1]), down(same[1]))
-    twin[2], twin[-1], same[-3], same[3] = together(
-        across(same[2]), up(twin[0]), up(same[-2]), down(same[2])
-    )
-    twin[3], twin[-2], same[4] = together(across(same[3]), up(twin[-1]), down(same[3]))
+    twin[0], same[-1], same[1] = across(own), up(own), down(own)
+    twin[1], same[-2], same[2] = across(same[1]), up(same[-1]), down(same[1])
+    same[-2], same[2], columns = together(same[-2], same[2], columns)
+    twin[2], twin[-1], same[-3], same[3] = across(same[2]), up(twin[0]), up(same[-2]), down(same[2])
+    twin[3], twin[-2], same[4] = across(same[3]), up(twin[-1]), down(same[3])
     twin[-3], twin[4] = across(same[-3]), down(twin[3])
-    return [group[step] for step in STEPS for group in (same, twin)]
+    return [group[step] for step in STEPS for group in (same, twin)], columns
 
 
 def rhs_kernel(scale, *refs):
-    blocks, (me, columns, part, flip) = refs[:16], refs[16:]
+    blocks, (me, columns, part, flip, acts) = refs[:16], refs[16:]
     y = lax.shift_right_logical(me[0], 3)
     z = lax.bitwise_and(me[0], 7)
     empty = jnp.zeros((64, 128), bf16)
@@ -217,6 +219,7 @@
             axis=0,
         )
         out = out + dot(blocks[b][BOTH:, :], wide)
+        acts[:, b * 128 : (b + 1) * 128] = blocks[b][:BOTH, :]
     out = out * scale
     part[:UNITS] = out[:UNITS, :128]
     part[UNITS:] = out[:UNITS, 128:]
@@ -224,19 +227,17 @@
     flip[UNITS:] = out[:UNITS, :128]
 
 
-def spread_tangent(res, blocks, tangent):
+def spread_tangent(res, acts, tangent):
     res_t = res.T.astype(bf16)
     for i in range(8):
-        acts = jnp.concatenate([blocks[2 * i][:BOTH, :], blocks[2 * i + 1][:BOTH, :]], axis=1)
-        tangent[i] = dot(res_t, acts).astype(bf16)
-
-
-def first_kernel(*refs):
-    blocks, (part, got, res_out, sums, tangent) = refs[:16], refs[16:]
+        tangent[i] = dot(res_t, acts[:, i * 256 : (i + 1) * 256]).astype(bf16)
+
+
+def first_kernel(acts, part, got, res_out, sums, tangent):
     res = part[...] + got[...]
     res_out[...] = res
     sums[...] = lanes([total(res * res)], (8, 128))
-    spread_tangent(res, blocks, tangent)
+    spread_tangent(res, acts, tangent)
 
 
 def share_kernel(parts, sums, *refs):
@@ -261,8 +262,7 @@
         message[i] = whole
 
 
-def curve_kernel(*refs):
-    blocks, got, refs = refs[:16], refs[16], refs[17:]
+def curve_kernel(acts, got, *refs):
     if len(refs) == 4:
         tangent_out, part, flip, sums_out = refs
     else:
@@ -280,9 +280,11 @@
             tangent_out[i] = tangent
         else:
             tangent = (tangent.astype(f32) + beta * past[i].astype(f32)).astype(bf16)
-        acts = jnp.concatenate([blocks[2 * i][:BOTH, :], blocks[2 * i + 1][:BOTH, :]], axis=1)
         out = out + lax.dot_general(
-            acts, tangent, (((1,), (1,)), ((), ())), preferred_element_type=f32
+            acts[:, i * 256 : (i + 1) * 256],
+            tangent,
+            (((1,), (1,)), ((), ())),
+            preferred_element_type=f32,
         )
     row = lax.broadcasted_iota(jnp.int32, (8, 128), 0)
     sums = jnp.where(row == 0, jnp.broadcast_to(sums, (8, 128)), 0.0)
@@ -293,8 +295,7 @@
     flip[BOTH:] = sums
 
 
-def second_kernel(*refs):
-    blocks, (part, got, sums, res, res_out, state, tangent) = refs[:16], refs[16:]
+def second_kernel(acts, part, got, sums, res, res_out, state, tangent):
     rr = sums[0:1, 0:1]
     tt = sums[0:1, 1:2] + got[BOTH : BOTH + 1, 1:2]
     inv_alpha = guarded(tt / TOKENS + damping * rr, rr)
@@ -303,12 +304,10 @@
     new = old - alpha * ((part[...] + got[:BOTH]) / TOKENS + damping * old)
     res_out[...] = new
     state[...] = lanes([total(new * new), rr, tt, rr, inv_alpha], (8, 128))
-    spread_tangent(new, blocks, tangent)
-
-
-def third_kernel(*refs):
-    blocks, refs = refs[:16], refs[16:]
-    part, got, sums, past, res, res_before, res_out, state, tangent = refs
+    spread_tangent(new, acts, tangent)
+
+
+def third_kernel(acts, part, got, sums, past, res, res_before, res_out, state, tangent):
     rr = sums[0:1, 0:1]
     ww = sums[0:1, 1:2] + got[BOTH : BOTH + 1, 1:2]
     cross = sums[0:1, 2:3] + got[BOTH : BOTH + 1, 2:3]
@@ -325,7 +324,7 @@
     state[...] = lanes(
         [total(new * new), rr0, rr, tt, pp, inv_alpha0, inv_alpha, beta], (8, 128)
     )
-    spread_tangent(new, blocks, tangent)
+    spread_tangent(new, acts, tangent)
 
 
 def partial_kernel(parts, state, block0, block1, message):
@@ -389,36 +388,29 @@
     w_gate, w_up = w_gate.T, w_up.T
     w_gate_other, w_up_other = swap_core(w_gate), swap_core(w_up)
 
-    with jax.named_scope("cotangent"):
-        columns = lax.dynamic_slice_in_dim(cotangent, core * 64, 64, axis=0)
-        columns = lax.all_to_all(
-            columns.reshape(64, 16, 128).transpose(1, 0, 2), "dp", 0, 0, tiled=True
-        )
     with jax.named_scope("rows"):
         mine, other = lookup(train_ids, query_ids, embed)
-        mine, other, columns = lax.optimization_barrier((mine, other, columns))
-        rows = (mine + swap_core(other)).reshape(8, 24, wide)
+        other = swap_core(other).reshape(8, 24, wide)
+        rows = local_call(
+            add_kernel, pltpu.VMEM((8, 24, wide), bf16), mine.reshape(8, 24, wide), other
+        )
         rows = exchange_chips(rows)
     with jax.named_scope("normed"):
-        normed = local_call(norm_kernel, shape((8, 24, wide), bf16), rows, norm_gain.reshape(1, wide))
+        normed = local_call(
+            norm_kernel, pltpu.VMEM((8, 24, wide), bf16), rows, norm_gain.reshape(1, wide)
+        )
+    with jax.named_scope("normed"):
         normed = exchange_chips(normed).reshape(192, wide)
     with jax.named_scope("acts"):
         package = local_call(
-            acts_kernel,
-            shape((PACK, 128), bf16),
-            normed,
-            w_gate,
-            w_up,
-            w_gate_other,
-            w_up_other,
-            specs=[VMEM] + [HBM] * 4,
-            scratch_shapes=[
-                pltpu.VMEM((4, UNITS, wide), bf16),
-                pltpu.SemaphoreType.DMA((4,)),
-            ],
+            acts_kernel, shape((PACK, 128), bf16), normed, w_gate, w_up, w_gate_other, w_up_other
         )
     with jax.named_scope("groups"):
-        blocks = gather_groups(package)
+        columns = lax.dynamic_slice_in_dim(cotangent, core * 64, 64, axis=0)
+        columns = columns.reshape(64, 16, 128).transpose(1, 0, 2)
+        columns, package = lax.optimization_barrier((columns, package))
+        columns = lax.all_to_all(columns, "dp", 0, 0, tiled=True)
+        blocks, columns = gather_groups(package, columns)
     vector = shape((BOTH, 128), f32)
     longer = shape((BOTH + 8, 128), f32)
     small = shape((8, 128), f32)
@@ -428,9 +420,9 @@
     table = shape((16, 8, 128), f32)
 
     with jax.named_scope("rhs"):
-        part, flip = local_call(
+        part, flip, acts = local_call(
             functools.partial(rhs_kernel, 1.0 / math.sqrt(2048)),
-            (vector, vector),
+            (vector, vector, pltpu.VMEM((BOTH, TOKENS // 2), bf16)),
             *blocks,
             lax.axis_index("dp").reshape(1),
             columns,
@@ -438,31 +430,31 @@
         )
         got = swap_core(flip)
     with jax.named_scope("first"):
-        res0, sums, tangent = local_call(first_kernel, (vector, small, spread), *blocks, part, got)
+        res0, sums, tangent = local_call(first_kernel, (vector, small, spread), acts, part, got)
         parts = exchange_chips(tangent)
         block0, shared = local_call(share_kernel, (block, message), parts, sums)
         shared = exchange_chips(shared)
         tangent0, part, flip, sums = local_call(
-            curve_kernel, (spread, vector, longer, small), *blocks, shared
+            curve_kernel, (spread, vector, longer, small), acts, shared
         )
         got = swap_core(flip)
     with jax.named_scope("second"):
         res1, state, tangent = local_call(
-            second_kernel, (vector, small, spread), *blocks, part, got, sums, res0
+            second_kernel, (vector, small, spread), acts, part, got, sums, res0
         )
         parts = exchange_chips(tangent)
         block1, shared = local_call(share_kernel, (block, message), parts, state, block0)
         shared = exchange_chips(shared)
         past = state
         part, flip, sums = local_call(
-            curve_kernel, (vector, longer, small), *blocks, shared, tangent0, state
+            curve_kernel, (vector, longer, small), acts, shared, tangent0, state
         )
         got = swap_core(flip)
     with jax.named_scope("third"):
         res2, state, tangent = local_call(
             third_kernel,
             (vector, small, spread),
-            *blocks,
+            acts,
             part,
             got,
             sums,

time: 243 us -> 216 us (0.89)
  local copies, waits for them, and re-layouts: 13 us -> 0.78 us
  Pallas kernels: 26.5 us -> 21 us
  blocking collectives: 114 us -> 110 us
  starting transfers between devices: 45.5 us -> 41.7 us
    unnamed x28 -> x6, local copies, waits for them, and re-layouts: 12.2 us -> 0.01 us
    ppermute x5, waiting for transfers between devices: 15.1 us -> 4.72 us  [up(): return lax.ppermute(v, 'dp', z_shift(1))]
    ppermute x5, waiting for transfers between devices: 3.15 us -> 10.3 us  [across(): return lax.ppermute(v, 'dp', YLO)]
    all_to_all x1, starting transfers between devices: 10.1 us -> 4.3 us  [body(): columns = lax.all_to_all(columns, 'dp', 0, 0, tiled=True)]
    pallas_call x14 -> x15, Pallas kernels: 26.5 us -> 21 us  [local_call(): pl.pallas_call(kernel, out_shape=outs, in_specs=specs or [VMEM] * len(arg...]
    all_to_all x6, blocking collectives: 89.3 us -> 85.1 us  [exchange_chips(): return lax.all_to_all(v, 'shard', 0, 0, axis_index_groups=CHIPS, tiled=True)]
    all_to_all x1, waiting for transfers between devices: 0.01 us -> 3.97 us  [body(): columns = lax.all_to_all(columns, 'dp', 0, 0, tiled=True)]
    ppermute x5, starting transfers between devices: 3.2 us -> 6.08 us  [across(): return lax.ppermute(v, 'dp', YLO)]
  transfers between devices with their start and end apart: 23 -> 23, of which waited for: 15 -> 13; matrix products, arithmetic and copies ran while one was open for 0% -> 0% of each run, Pallas kernels for 3% -> 1%
where the time goes in v5:
time: 216 us; the launch traced here: 215 us
  blocking collectives  110 us (51%)
  starting transfers between devices  41.7 us (19%)
  waiting for transfers between devices  41.4 us (19%)
  Pallas kernels  21 us (10%)
    all_to_all x6, blocking collectives, exchange_chips(): return lax.all_to_all(v, 'shard', 0, 0, axis_index_groups=CHIPS, tiled=True)  85.1 us
    pallas_call x15, Pallas kernels, local_call(): pl.pallas_call(kernel, out_shape=outs, in_specs=specs or [VMEM] * len(arg...  21 us
    ppermute x6, starting transfers between devices, swap_core(): return lax.ppermute(v, 'shard', CORE)  13.5 us
    ppermute x5, starting transfers between devices, down(): return lax.ppermute(v, 'dp', z_shift(-1))  13.1 us
    all_to_all x1, blocking collectives, body(): every = lax.all_to_all(mine, 'dp', 0, 0, tiled=True)  12.9 us
    all_to_all x1, blocking collectives, body(): partials = lax.all_to_all(partials, 'shard', 0, 0, tiled=True)  12.2 us
    all_to_all x1, waiting for transfers between devices, exchange_chips(): return lax.all_to_all(v, 'shard', 0, 0, axis_index_groups=CHIPS, tiled=True)  11.2 us
    ppermute x5, waiting for transfers between devices, across(): return lax.ppermute(v, 'dp', YLO)  10.3 us
  transfers between devices with their start and end apart: 23, of which 13 were waited for; matrix products, arithmetic and copies ran while one was open for 0% of the time, Pallas kernels for 1%

profile of v5, /device:TPU:1, one launch (start us, length us, event | category | flops | bytes accessed | tf_op | source)
XLA Modules:
  0.0 215.2 jit_solution(1651047387007405073)
XLA Ops:
  0.0 5.7 %rows.2 = (bf16[192,2048]{1,0:T(8,128)(2,1)S(1)}, bf16[192,2048]{1,0:T(8,128)(2,1)S(1)}) custom-call(s32[1]{0:T(128)} %bitcast.2.place, s32[2,128]{1,0:T(2,128)} %bitcast.23, s32[1,128]{1,0:T(1,128)} %bitcast.24, bf16[2000,2048]{1,0:T(8,128)(2,1)} %table_hbm.1), custom_call_target="tpu_custom_call" | custom-call | tf_op jit(solution)/shard_map/rows/pallas_call | solution.py:43
  5.7 3.3 %collective-permute-start = (bf16[192,2048]{1,0:T(8,128)(2,1)S(1)}, bf16[192,2048]{1,0:T(8,128)(2,1)S(1)}, u32[]{:S(2)}, u32[]{:S(2)}) collective-permute-start(bf16[192,2048]{1,0:T(8,128)(2,1)S(1)} %get-tuple-element.36), channel_id=1, source_target_pairs={{0,1},{1,0},{2,3},{3,2},{4,5},{5,4},{6,7},{7,6},{8,9},{9,8},{10,11... | collective-permute-start | bytes 2359304 | tf_op jit(solution)/shard_map/rows/ppermute | solution.py:35
  9.6 1.4 collective-permute-done
  11.1 17.5 %all_to_all.50.parts = bf16[8,24,2048]{2,1,0:T(8,128)(2,1)S(1)} all-to-all(bf16[8,24,2048]{2,1,0:T(8,128)(2,1)S(1)} %rows.3), channel_id=1, replica_groups={{0,2,4,6,8,10,12,14},{1,3,5,7,9,11,13,15},{16,18,20,22,24,26,28,30},{17..., dimensions={0} | all-to-all | bytes 1572864 | tf_op jit(solution)/shard_map/rows/all_to_all | solution.py:39
  29.7 3.9 %all-to-all-start.1 = ((bf16[8,24,2048]{2,1,0:T(8,128)(2,1)}), bf16[8,24,2048]{2,1,0:T(8,128)(2,1)S(1)}, u32[]{:S(2)}, u32[]{:S(2)}) async-start(bf16[8,24,2048]{2,1,0:T(8,128)(2,1)} %normed.1), calls=%async_computation.1 | async-start | bytes 1572864 | tf_op jit(solution)/shard_map/normed/all_to_all | solution.py:39
  34.3 11.2 %all-to-all-done.1 = bf16[8,24,2048]{2,1,0:T(8,128)(2,1)S(1)} async-done(((bf16[8,24,2048]{2,1,0:T(8,128)(2,1)}), bf16[8,24,2048]{2,1,0:T(8,128)(2,1)S(1)}, u32[]{:S(2)}, u32[]{:S(2)}) %all-to-all-start.1) | async-done | bytes 786464 | tf_op jit(solution)/shard_map/normed/all_to_all | solution.py:39
  45.5 4.0 %acts.1.refs_0_ = bf16[1040,128]{1,0:T(8,128)(2,1)S(1)} custom-call(bf16[192,2048]{1,0:T(8,128)(2,1)S(1)} %bitcast.17, bf16[344,2048]{1,0:T(8,128)(2,1)S(1)} %bitcast.19, bf16[344,2048]{1,0:T(8,128)(2,1)} %bitcast.10.w_up, bf16[344,2048]{1,0:T(8,128)(2,1)} %collective-permute-done.1.w_gate_other, bf16[344,2048]{1,0:T(8,128)(2,1)} %collective-permute-done.2.w_up_other), custom_call_target="tpu_custom_call" | custom-call | tf_op jit(solution)/shard_map/acts/pallas_call | solution.py:43
  49.5 5.7 %collective-permute-start.6 = (bf16[1040,128]{1,0:T(8,128)(2,1)S(1)}, bf16[1040,128]{1,0:T(8,128)(2,1)S(1)}, u32[]{:S(2)}, u32[]{:S(2)}) collective-permute-start(bf16[1040,128]{1,0:T(8,128)(2,1)S(1)} %acts.1.refs_0_), channel_id=1, source_target_pairs={{0,112},{16,0},{32,16},{48,32},{64,48},{80,64},{96,80},{112,96},{1... | collective-permute-start | bytes 798728 | tf_op jit(solution)/shard_map/groups/ppermute | solution.py:186
  55.2 4.3 %all-to-all-start.2 = ((bf16[16,64,128]{2,1,0:T(8,128)(2,1)}), bf16[16,64,128]{2,1,0:T(8,128)(2,1)S(1)}, u32[]{:S(2)}, u32[]{:S(2)}) async-start(bf16[16,64,128]{2,1,0:T(8,128)(2,1)} %bitcast_bitcast_fusion), calls=%async_computation.2 | async-start | bytes 524288 | tf_op jit(solution)/shard_map/groups/all_to_all | solution.py:412
  59.5 2.7 %collective-permute-start.9 = (bf16[1040,128]{1,0:T(8,128)(2,1)S(1)}, bf16[1040,128]{1,0:T(8,128)(2,1)S(1)}, u32[]{:S(2)}, u32[]{:S(2)}) collective-permute-start(bf16[1040,128]{1,0:T(8,128)(2,1)S(1)} %collective-permute-done.6.refs_4_), channel_id=1, source_target_pairs={{0,112},{16,0},{32,16},{48,32},{64,48},{80,64},{96,80},{112,96},{1... | collective-permute-start | bytes 798728 | tf_op jit(solution)/shard_map/groups/ppermute | solution.py:186
  63.3 4.0 %all-to-all-done.2.refs_17_ = bf16[16,64,128]{2,1,0:T(8,128)(2,1)S(1)} async-done(((bf16[16,64,128]{2,1,0:T(8,128)(2,1)}), bf16[16,64,128]{2,1,0:T(8,128)(2,1)S(1)}, u32[]{:S(2)}, u32[]{:S(2)}) %all-to-all-start.2) | async-done | bytes 262176 | tf_op jit(solution)/shard_map/groups/all_to_all | solution.py:412
  67.3 3.7 %collective-permute-done.9.refs_8_ = bf16[1040,128]{1,0:T(8,128)(2,1)S(1)} collective-permute-done((bf16[1040,128]{1,0:T(8,128)(2,1)S(1)}, bf16[1040,128]{1,0:T(8,128)(2,1)S(1)}, u32[]{:S(2)}, u32[]{:S(2)}) %collective-permute-start.9) | collective-permute-done | bytes 266272 | tf_op jit(solution)/shard_map/groups/ppermute | solution.py:186
  71.0 2.3 %collective-permute-done.8.refs_6_ = bf16[1040,128]{1,0:T(8,128)(2,1)S(1)} collective-permute-done((bf16[1040,128]{1,0:T(8,128)(2,1)S(1)}, bf16[1040,128]{1,0:T(8,128)(2,1)S(1)}, u32[]{:S(2)}, u32[]{:S(2)}) %collective-permute-start.8) | collective-permute-done | bytes 266272 | tf_op jit(solution)/shard_map/groups/ppermute | solution.py:183
  74.8 1.6 collective-permute-start.7
  76.5 2.1 collective-permute-done.14.refs_12_
  78.6 2.0 collective-permute-start.15
  80.7 2.7 %collective-permute-start.16 = (bf16[1040,128]{1,0:T(8,128)(2,1)S(1)}, bf16[1040,128]{1,0:T(8,128)(2,1)}, u32[]{:S(2)}, u32[]{:S(2)}) collective-permute-start(bf16[1040,128]{1,0:T(8,128)(2,1)S(1)} %collective-permute-done.14.refs_12_), channel_id=1, source_target_pairs={{0,112},{16,0},{32,16},{48,32},{64,48},{80,64},{96,80},{112,96},{1... | collective-permute-start | bytes 798728 | tf_op jit(solution)/shard_map/groups/ppermute | solution.py:186
  83.3 2.4 %collective-permute-done.12.refs_10_ = bf16[1040,128]{1,0:T(8,128)(2,1)S(1)} collective-permute-done((bf16[1040,128]{1,0:T(8,128)(2,1)S(1)}, bf16[1040,128]{1,0:T(8,128)(2,1)S(1)}, u32[]{:S(2)}, u32[]{:S(2)}) %collective-permute-start.12) | collective-permute-done | bytes 266272 | tf_op jit(solution)/shard_map/groups/ppermute | solution.py:183
  87.3 1.6 collective-permute-start.17
  88.9 4.2 %collective-permute-done.11.refs_9_ = bf16[1040,128]{1,0:T(8,128)(2,1)} collective-permute-done((bf16[1040,128]{1,0:T(8,128)(2,1)S(1)}, bf16[1040,128]{1,0:T(8,128)(2,1)}, u32[]{:S(2)}, u32[]{:S(2)}) %collective-permute-start.11) | collective-permute-done | bytes 266272 | tf_op jit(solution)/shard_map/groups/ppermute | solution.py:189
  93.1 5.7 %collective-permute-done.13.refs_11_ = bf16[1040,128]{1,0:T(8,128)(2,1)} collective-permute-done((bf16[1040,128]{1,0:T(8,128)(2,1)S(1)}, bf16[1040,128]{1,0:T(8,128)(2,1)}, u32[]{:S(2)}, u32[]{:S(2)}) %collective-permute-start.13) | collective-permute-done | bytes 266272 | tf_op jit(solution)/shard_map/groups/ppermute | solution.py:189
  98.8 3.1 %rhs.1 = (f32[688,128]{1,0:T(8,128)S(1)}, f32[688,128]{1,0:T(8,128)S(1)}, bf16[688,2048]{1,0:T(8,128)(2,1)S(1)}) custom-call(bf16[1040,128]{1,0:T(8,128)(2,1)S(1)} %acts.1.refs_0_, bf16[1040,128]{1,0:T(8,128)(2,1)S(1)} %collective-permute-done.3.refs_1_, bf16[1040,128]{1,0:T(8,128)(2,1)S(1)} %collective-permute-done.4.refs_2_, ...), custom_call_target="tpu_custom_call" | custom-call | tf_op jit(solution)/shard_map/rhs/pallas_call | solution.py:43
  101.9 3.6 %collective-permute-start.18 = (f32[688,128]{1,0:T(8,128)S(1)}, f32[688,128]{1,0:T(8,128)S(1)}, u32[]{:S(2)}, u32[]{:S(2)}) collective-permute-start(f32[688,128]{1,0:T(8,128)S(1)} %get-tuple-element.44), channel_id=1, source_target_pairs={{0,1},{1,0},{2,3},{3,2},{4,5},{5,4},{6,7},{7,6},{8,9},{9,8},{10,11... | collective-permute-start | bytes 1056776 | tf_op jit(solution)/shard_map/rhs/ppermute | solution.py:35
  107.4 14.7 %all_to_all.51.parts = bf16[8,128,256]{2,1,0:T(8,128)(2,1)S(1)} all-to-all(bf16[8,128,256]{2,1,0:T(8,128)(2,1)S(1)} %get-tuple-element.45), channel_id=1, replica_groups={{0,2,4,6,8,10,12,14},{1,3,5,7,9,11,13,15},{16,18,20,22,24,26,28,30},{17..., dimensions={0} | all-to-all | bytes 1048576 | tf_op jit(solution)/shard_map/first/all_to_all | solution.py:39
  122.4 14.0 %all_to_all.52.got = bf16[8,144,256]{2,1,0:T(8,128)(2,1)S(1)} all-to-all(bf16[8,144,256]{2,1,0:T(8,128)(2,1)S(1)} %get-tuple-element.47), channel_id=1, replica_groups={{0,2,4,6,8,10,12,14},{1,3,5,7,9,11,13,15},{16,18,20,22,24,26,28,30},{17..., dimensions={0} | all-to-all | bytes 1179648 | tf_op jit(solution)/shard_map/first/all_to_all | solution.py:39
  137.3 3.0 %collective-permute-start.19 = (f32[696,128]{1,0:T(8,128)S(1)}, f32[696,128]{1,0:T(8,128)S(1)}, u32[]{:S(2)}, u32[]{:S(2)}) collective-permute-start(f32[696,128]{1,0:T(8,128)S(1)} %get-tuple-element.49), channel_id=1, source_target_pairs={{0,1},{1,0},{2,3},{3,2},{4,5},{5,4},{6,7},{7,6},{8,9},{9,8},{10,11... | collective-permute-start | bytes 1069064 | tf_op jit(solution)/shard_map/first/ppermute | solution.py:35
  142.4 12.7 %all_to_all.53.parts = bf16[8,128,256]{2,1,0:T(8,128)(2,1)S(1)} all-to-all(bf16[8,128,256]{2,1,0:T(8,128)(2,1)S(1)} %get-tuple-element.52), channel_id=1, replica_groups={{0,2,4,6,8,10,12,14},{1,3,5,7,9,11,13,15},{16,18,20,22,24,26,28,30},{17..., dimensions={0} | all-to-all | bytes 1048576 | tf_op jit(solution)/shard_map/second/all_to_all | solution.py:39
  155.4 13.5 %all_to_all.54.got = bf16[8,144,256]{2,1,0:T(8,128)(2,1)S(1)} all-to-all(bf16[8,144,256]{2,1,0:T(8,128)(2,1)S(1)} %get-tuple-element.55), channel_id=1, replica_groups={{0,2,4,6,8,10,12,14},{1,3,5,7,9,11,13,15},{16,18,20,22,24,26,28,30},{17..., dimensions={0} | all-to-all | bytes 1179648 | tf_op jit(solution)/shard_map/second/all_to_all | solution.py:39
  170.1 3.1 %collective-permute-start.20 = (f32[696,128]{1,0:T(8,128)S(1)}, f32[696,128]{1,0:T(8,128)S(1)}, u32[]{:S(2)}, u32[]{:S(2)}) collective-permute-start(f32[696,128]{1,0:T(8,128)S(1)} %get-tuple-element.58), channel_id=1, source_target_pairs={{0,1},{1,0},{2,3},{3,2},{4,5},{5,4},{6,7},{7,6},{8,9},{9,8},{10,11... | collective-permute-start | bytes 1069064 | tf_op jit(solution)/shard_map/second/ppermute | solution.py:35
  175.5 12.7 %all_to_all.55.parts = bf16[8,128,256]{2,1,0:T(8,128)(2,1)S(1)} all-to-all(bf16[8,128,256]{2,1,0:T(8,128)(2,1)S(1)} %get-tuple-element.61), channel_id=1, replica_groups={{0,2,4,6,8,10,12,14},{1,3,5,7,9,11,13,15},{16,18,20,22,24,26,28,30},{17..., dimensions={0} | all-to-all | bytes 1048576 | tf_op jit(solution)/shard_map/third/all_to_all | solution.py:39
  188.5 12.2 %all_to_all.56.got = f32[16,8,128]{2,1,0:T(8,128)S(1)} all-to-all(f32[16,8,128]{2,1,0:T(8,128)S(1)} %third.3), channel_id=1, replica_groups=mesh['dp'=16,'shard'=16] {'shard'}, dimensions={0} | all-to-all | bytes 131072 | tf_op jit(solution)/shard_map/third/all_to_all | solution.py:467
  201.1 12.9 %all_to_all.57.got = f32[16,8,128]{2,1,0:T(8,128)S(1)} all-to-all(f32[16,8,128]{2,1,0:T(8,128)S(1)} %whole.2), channel_id=1, replica_groups=mesh['dp'=16,'shard'=16] {'dp'}, dimensions={0} | all-to-all | bytes 131072 | tf_op jit(solution)/shard_map/whole/all_to_all | solution.py:470
  (44 shorter events, 17.8 us)
Async XLA Ops:
  0.0 33.6 %copy-start = (bf16[128,2048]{1,0:T(8,128)(2,1)S(1)}, bf16[128,2048]{1,0:T(8,128)(2,1)}, u32[]{:S(2)}) copy-start(bf16[128,2048]{1,0:T(8,128)(2,1)} %param.13) | copy-start | bytes 1572868
  0.0 9.1 %copy-start.1 = (bf16[2048,344]{0,1:T(8,128)(2,1)S(1)}, bf16[2048,344]{0,1:T(8,128)(2,1)}, u32[]{:S(2)}) copy-start(bf16[2048,344]{0,1:T(8,128)(2,1)} %param.11) | copy-start | bytes 4227076
  5.7 5.3 %collective-permute-start = (bf16[192,2048]{1,0:T(8,128)(2,1)S(1)}, bf16[192,2048]{1,0:T(8,128)(2,1)S(1)}, u32[]{:S(2)}, u32[]{:S(2)}) collective-permute-start(bf16[192,2048]{1,0:T(8,128)(2,1)S(1)} %get-tuple-element.36), channel_id=1, source_target_pairs={{0,1},{1,0},{2,3},{3,2},{4,5},{5,4},{6,7},{7,6},{8,9},{9,8},{10,11... | collective-permute-start | bytes 2359304 | tf_op jit(solution)/shard_map/rows/ppermute | solution.py:35
  9.1 25.3 %collective-permute-start.1 = (bf16[344,2048]{1,0:T(8,128)(2,1)S(1)}, bf16[344,2048]{1,0:T(8,128)(2,1)}, u32[]{:S(2)}, u32[]{:S(2)}) collective-permute-start(bf16[344,2048]{1,0:T(8,128)(2,1)S(1)} %bitcast.18), channel_id=1, source_target_pairs={{0,1},{1,0},{2,3},{3,2},{4,5},{5,4},{6,7},{7,6},{8,9},{9,8},{10,11... | collective-permute-start | bytes 4227080 | tf_op jit(solution)/shard_map/ppermute | solution.py:35
  9.2 25.2 %collective-permute-start.2 = (bf16[344,2048]{1,0:T(8,128)(2,1)}, bf16[344,2048]{1,0:T(8,128)(2,1)}, u32[]{:S(2)}, u32[]{:S(2)}) collective-permute-start(bf16[344,2048]{1,0:T(8,128)(2,1)} %bitcast.10.w_up), channel_id=1, source_target_pairs={{0,1},{1,0},{2,3},{3,2},{4,5},{5,4},{6,7},{7,6},{8,9},{9,8},{10,11... | collective-permute-start | bytes 4227080 | tf_op jit(solution)/shard_map/ppermute | solution.py:35
  11.0 17.6 %copy-start.2 = (f32[2048]{0:T(1024)S(1)}, f32[2048]{0:T(1024)}, u32[]{:S(2)}) copy-start(f32[2048]{0:T(1024)} %param.10) | copy-start | bytes 24580
  29.7 15.9 %all-to-all-start.1 = ((bf16[8,24,2048]{2,1,0:T(8,128)(2,1)}), bf16[8,24,2048]{2,1,0:T(8,128)(2,1)S(1)}, u32[]{:S(2)}, u32[]{:S(2)}) async-start(bf16[8,24,2048]{2,1,0:T(8,128)(2,1)} %normed.1), calls=%async_computation.1 | async-start | bytes 1572864 | tf_op jit(solution)/shard_map/normed/all_to_all | solution.py:39
  49.5 10.0 %collective-permute-start.6 = (bf16[1040,128]{1,0:T(8,128)(2,1)S(1)}, bf16[1040,128]{1,0:T(8,128)(2,1)S(1)}, u32[]{:S(2)}, u32[]{:S(2)}) collective-permute-start(bf16[1040,128]{1,0:T(8,128)(2,1)S(1)} %acts.1.refs_0_), channel_id=1, source_target_pairs={{0,112},{16,0},{32,16},{48,32},{64,48},{80,64},{96,80},{112,96},{1... | collective-permute-start | bytes 798728 | tf_op jit(solution)/shard_map/groups/ppermute | solution.py:186
  55.2 7.0 %collective-permute-start.4 = (bf16[1040,128]{1,0:T(8,128)(2,1)S(1)}, bf16[1040,128]{1,0:T(8,128)(2,1)S(1)}, u32[]{:S(2)}, u32[]{:S(2)}) collective-permute-start(bf16[1040,128]{1,0:T(8,128)(2,1)S(1)} %acts.1.refs_0_), channel_id=1, source_target_pairs={{0,16},{16,32},{32,48},{48,64},{64,80},{80,96},{96,112},{112,0},{1... | collective-permute-start | bytes 798728 | tf_op jit(solution)/shard_map/groups/ppermute | solution.py:183
  55.2 12.1 %all-to-all-start.2 = ((bf16[16,64,128]{2,1,0:T(8,128)(2,1)}), bf16[16,64,128]{2,1,0:T(8,128)(2,1)S(1)}, u32[]{:S(2)}, u32[]{:S(2)}) async-start(bf16[16,64,128]{2,1,0:T(8,128)(2,1)} %bitcast_bitcast_fusion), calls=%async_computation.2 | async-start | bytes 524288 | tf_op jit(solution)/shard_map/groups/all_to_all | solution.py:412
  59.5 11.6 %collective-permute-start.9 = (bf16[1040,128]{1,0:T(8,128)(2,1)S(1)}, bf16[1040,128]{1,0:T(8,128)(2,1)S(1)}, u32[]{:S(2)}, u32[]{:S(2)}) collective-permute-start(bf16[1040,128]{1,0:T(8,128)(2,1)S(1)} %collective-permute-done.6.refs_4_), channel_id=1, source_target_pairs={{0,112},{16,0},{32,16},{48,32},{64,48},{80,64},{96,80},{112,96},{1... | collective-permute-start | bytes 798728 | tf_op jit(solution)/shard_map/groups/ppermute | solution.py:186
  62.1 11.2 %collective-permute-start.8 = (bf16[1040,128]{1,0:T(8,128)(2,1)S(1)}, bf16[1040,128]{1,0:T(8,128)(2,1)S(1)}, u32[]{:S(2)}, u32[]{:S(2)}) collective-permute-start(bf16[1040,128]{1,0:T(8,128)(2,1)S(1)} %collective-permute-done.4.refs_2_), channel_id=1, source_target_pairs={{0,16},{16,32},{32,48},{48,64},{64,80},{80,96},{96,112},{112,0},{1... | collective-permute-start | bytes 798728 | tf_op jit(solution)/shard_map/groups/ppermute | solution.py:183
  62.2 11.8 %collective-permute-start.3 = (bf16[1040,128]{1,0:T(8,128)(2,1)S(1)}, bf16[1040,128]{1,0:T(8,128)(2,1)S(1)}, u32[]{:S(2)}, u32[]{:S(2)}) collective-permute-start(bf16[1040,128]{1,0:T(8,128)(2,1)S(1)} %acts.1.refs_0_), channel_id=1, source_target_pairs={{0,128},{16,144},{32,160},{48,176},{64,192},{80,208},{96,224},{112... | collective-permute-start | bytes 798728 | tf_op jit(solution)/shard_map/groups/ppermute | solution.py:189
  73.4 5.3 %collective-permute-start.14 = (bf16[1040,128]{1,0:T(8,128)(2,1)S(1)}, bf16[1040,128]{1,0:T(8,128)(2,1)S(1)}, u32[]{:S(2)}, u32[]{:S(2)}) collective-permute-start(bf16[1040,128]{1,0:T(8,128)(2,1)S(1)} %collective-permute-done.9.refs_8_), channel_id=1, source_target_pairs={{0,112},{16,0},{32,16},{48,32},{64,48},{80,64},{96,80},{112,96},{1... | collective-permute-start | bytes 798728 | tf_op jit(solution)/shard_map/groups/ppermute | solution.py:186
  73.9 6.7 %collective-permute-start.5 = (bf16[1040,128]{1,0:T(8,128)(2,1)S(1)}, bf16[1040,128]{1,0:T(8,128)(2,1)S(1)}, u32[]{:S(2)}, u32[]{:S(2)}) collective-permute-start(bf16[1040,128]{1,0:T(8,128)(2,1)S(1)} %collective-permute-done.3.refs_1_), channel_id=1, source_target_pairs={{0,16},{16,32},{32,48},{48,64},{64,80},{80,96},{96,112},{112,0},{1... | collective-permute-start | bytes 798728 | tf_op jit(solution)/shard_map/groups/ppermute | solution.py:183
  74.8 5.8 %collective-permute-start.7 = (bf16[1040,128]{1,0:T(8,128)(2,1)S(1)}, bf16[1040,128]{1,0:T(8,128)(2,1)S(1)}, u32[]{:S(2)}, u32[]{:S(2)}) collective-permute-start(bf16[1040,128]{1,0:T(8,128)(2,1)S(1)} %collective-permute-done.6.refs_4_), channel_id=1, source_target_pairs={{0,128},{16,144},{32,160},{48,176},{64,192},{80,208},{96,224},{112... | collective-permute-start | bytes 798728 | tf_op jit(solution)/shard_map/groups/ppermute | solution.py:189
  76.5 9.3 %collective-permute-start.12 = (bf16[1040,128]{1,0:T(8,128)(2,1)S(1)}, bf16[1040,128]{1,0:T(8,128)(2,1)S(1)}, u32[]{:S(2)}, u32[]{:S(2)}) collective-permute-start(bf16[1040,128]{1,0:T(8,128)(2,1)S(1)} %collective-permute-done.8.refs_6_), channel_id=1, source_target_pairs={{0,16},{16,32},{32,48},{48,64},{64,80},{80,96},{96,112},{112,0},{1... | collective-permute-start | bytes 798728 | tf_op jit(solution)/shard_map/groups/ppermute | solution.py:183
  78.6 8.7 %collective-permute-start.15 = (bf16[1040,128]{1,0:T(8,128)(2,1)S(1)}, bf16[1040,128]{1,0:T(8,128)(2,1)}, u32[]{:S(2)}, u32[]{:S(2)}) collective-permute-start(bf16[1040,128]{1,0:T(8,128)(2,1)S(1)} %collective-permute-done.14.refs_12_), channel_id=1, source_target_pairs={{0,128},{16,144},{32,160},{48,176},{64,192},{80,208},{96,224},{112... | collective-permute-start | bytes 798728 | tf_op jit(solution)/shard_map/groups/ppermute | solution.py:189
  80.6 12.5 %collective-permute-start.11 = (bf16[1040,128]{1,0:T(8,128)(2,1)S(1)}, bf16[1040,128]{1,0:T(8,128)(2,1)}, u32[]{:S(2)}, u32[]{:S(2)}) collective-permute-start(bf16[1040,128]{1,0:T(8,128)(2,1)S(1)} %collective-permute-done.9.refs_8_), channel_id=1, source_target_pairs={{0,128},{16,144},{32,160},{48,176},{64,192},{80,208},{96,224},{112... | collective-permute-start | bytes 798728 | tf_op jit(solution)/shard_map/groups/ppermute | solution.py:189
  80.7 12.5 %collective-permute-start.10 = (bf16[1040,128]{1,0:T(8,128)(2,1)S(1)}, bf16[1040,128]{1,0:T(8,128)(2,1)}, u32[]{:S(2)}, u32[]{:S(2)}) collective-permute-start(bf16[1040,128]{1,0:T(8,128)(2,1)S(1)} %collective-permute-done.5.refs_3_), channel_id=1, source_target_pairs={{0,16},{16,32},{32,48},{48,64},{64,80},{80,96},{96,112},{112,0},{1... | collective-permute-start | bytes 798728 | tf_op jit(solution)/shard_map/groups/ppermute | solution.py:183
  80.7 18.2 %collective-permute-start.16 = (bf16[1040,128]{1,0:T(8,128)(2,1)S(1)}, bf16[1040,128]{1,0:T(8,128)(2,1)}, u32[]{:S(2)}, u32[]{:S(2)}) collective-permute-start(bf16[1040,128]{1,0:T(8,128)(2,1)S(1)} %collective-permute-done.14.refs_12_), channel_id=1, source_target_pairs={{0,112},{16,0},{32,16},{48,32},{64,48},{80,64},{96,80},{112,96},{1... | collective-permute-start | bytes 798728 | tf_op jit(solution)/shard_map/groups/ppermute | solution.py:186
  85.7 13.1 %collective-permute-start.13 = (bf16[1040,128]{1,0:T(8,128)(2,1)S(1)}, bf16[1040,128]{1,0:T(8,128)(2,1)}, u32[]{:S(2)}, u32[]{:S(2)}) collective-permute-start(bf16[1040,128]{1,0:T(8,128)(2,1)S(1)} %collective-permute-done.12.refs_10_), channel_id=1, source_target_pairs={{0,128},{16,144},{32,160},{48,176},{64,192},{80,208},{96,224},{112... | collective-permute-start | bytes 798728 | tf_op jit(solution)/shard_map/groups/ppermute | solution.py:189
  87.3 11.5 %collective-permute-start.17 = (bf16[1040,128]{1,0:T(8,128)(2,1)}, bf16[1040,128]{1,0:T(8,128)(2,1)}, u32[]{:S(2)}, u32[]{:S(2)}) collective-permute-start(bf16[1040,128]{1,0:T(8,128)(2,1)} %collective-permute-done.15.refs_13_), channel_id=1, source_target_pairs={{0,112},{16,0},{32,16},{48,32},{64,48},{80,64},{96,80},{112,96},{1... | collective-permute-start | bytes 798728 | tf_op jit(solution)/shard_map/groups/ppermute | solution.py:186
  101.9 4.9 %collective-permute-start.18 = (f32[688,128]{1,0:T(8,128)S(1)}, f32[688,128]{1,0:T(8,128)S(1)}, u32[]{:S(2)}, u32[]{:S(2)}) collective-permute-start(f32[688,128]{1,0:T(8,128)S(1)} %get-tuple-element.44), channel_id=1, source_target_pairs={{0,1},{1,0},{2,3},{3,2},{4,5},{5,4},{6,7},{7,6},{8,9},{9,8},{10,11... | collective-permute-start | bytes 1056776 | tf_op jit(solution)/shard_map/rhs/ppermute | solution.py:35
  137.3 4.3 %collective-permute-start.19 = (f32[696,128]{1,0:T(8,128)S(1)}, f32[696,128]{1,0:T(8,128)S(1)}, u32[]{:S(2)}, u32[]{:S(2)}) collective-permute-start(f32[696,128]{1,0:T(8,128)S(1)} %get-tuple-element.49), channel_id=1, source_target_pairs={{0,1},{1,0},{2,3},{3,2},{4,5},{5,4},{6,7},{7,6},{8,9},{9,8},{10,11... | collective-permute-start | bytes 1069064 | tf_op jit(solution)/shard_map/first/ppermute | solution.py:35
  170.1 4.4 %collective-permute-start.20 = (f32[696,128]{1,0:T(8,128)S(1)}, f32[696,128]{1,0:T(8,128)S(1)}, u32[]{:S(2)}, u32[]{:S(2)}) collective-permute-start(f32[696,128]{1,0:T(8,128)S(1)} %get-tuple-element.58), channel_id=1, source_target_pairs={{0,1},{1,0},{2,3},{3,2},{4,5},{5,4},{6,7},{7,6},{8,9},{9,8},{10,11... | collective-permute-start | bytes 1069064 | tf_op jit(solution)/shard_map/second/ppermute | solution.py:35

commit v6 on v5

--- a/solution.py
+++ b/solution.py
@@ -152,7 +152,10 @@
 
 
 def norm_kernel(parts, gain, out):
-    rows = jnp.sum(parts[...].astype(f32), axis=0)
+    rows = parts[0]
+    for i in range(1, 8):
+        rows = rows + parts[i]
+    rows = rows.astype(f32)
     inv_scale = lax.rsqrt(jnp.mean(rows * rows, axis=-1, keepdims=True) + norm_eps)
     normed = (rows * inv_scale * gain[...]).astype(bf16)
     for i in range(8):
@@ -160,12 +163,10 @@
 
 
 def acts_kernel(normed, w_gate, w_up, w_gate_other, w_up_other, out):
-    rows = normed[...]
+    rows = normed[...].T
 
     def product(w):
-        return lax.dot_general(
-            w[...], rows, (((1,), (1,)), ((), ())), preferred_element_type=f32
-        )
+        return dot(w[...], rows)
 
     def hidden(gate_w, up_w):
         gate = product(gate_w)
@@ -194,7 +195,6 @@
     same, twin = {0: own}, {}
     twin[0], same[-1], same[1] = across(own), up(own), down(own)
     twin[1], same[-2], same[2] = across(same[1]), up(same[-1]), down(same[1])
-    same[-2], same[2], columns = together(same[-2], same[2], columns)
     twin[2], twin[-1], same[-3], same[3] = across(same[2]), up(twin[0]), up(same[-2]), down(same[2])
     twin[3], twin[-2], same[4] = across(same[3]), up(twin[-1]), down(same[3])
     twin[-3], twin[4] = across(same[-3]), down(twin[3])
@@ -207,19 +207,17 @@
     z = lax.bitwise_and(me[0], 7)
     empty = jnp.zeros((64, 128), bf16)
     out = jnp.zeros((PACK - BOTH, 256), f32)
-    for b in range(16):
-        side = y if b % 2 == 0 else 1 - y
-        group = side * 8 + lax.bitwise_and(z + STEPS[b // 2], 7)
-        seen = columns[group]
-        wide = jnp.concatenate(
-            [
-                jnp.concatenate([seen, empty], axis=1),
-                jnp.concatenate([empty, seen], axis=1),
-            ],
-            axis=0,
-        )
-        out = out + dot(blocks[b][BOTH:, :], wide)
-        acts[:, b * 128 : (b + 1) * 128] = blocks[b][:BOTH, :]
+    for i, step in enumerate(STEPS):
+        pieces = []
+        for side in (y, 1 - y):
+            seen = columns[side * 8 + lax.bitwise_and(z + step, 7)]
+            pieces.append(jnp.concatenate([seen, empty], axis=1))
+            pieces.append(jnp.concatenate([empty, seen], axis=1))
+        pair = blocks[2 * i], blocks[2 * i + 1]
+        asked = jnp.concatenate([block[BOTH:, :] for block in pair], axis=1)
+        out = out + dot(asked, jnp.concatenate(pieces, axis=0))
+        for j, block in enumerate(pair):
+            acts[:, (2 * i + j) * 128 : (2 * i + j + 1) * 128] = block[:BOTH, :]
     out = out * scale
     part[:UNITS] = out[:UNITS, :128]
     part[UNITS:] = out[:UNITS, 128:]
@@ -331,26 +329,26 @@
     block2 = jnp.sum(parts[...].astype(f32), axis=0)
     beta = state[0:1, 7:8]
     step1 = block1[...].astype(f32) + beta * block0[...].astype(f32)
-    out = lanes([0.5 * state[0:1, 0:1], total(block2 * block2), total(block2 * step1)], (8, 128))
+    out = lanes([0.5 * state[0:1, 0:1], total(block2 * block2), total(block2 * step1)], (1, 128))
     for i in range(16):
         message[i] = out
 
 
 def group_kernel(got, state, message):
-    sums = jnp.sum(jnp.sum(got[...], axis=0), axis=0, keepdims=True)
+    sums = jnp.sum(got[...], axis=0)
     rr0, rr1, tt1, pp1, inv_alpha0, inv_alpha1, beta0 = (state[0:1, i : i + 1] for i in range(1, 8))
     rr2 = sums[:, 0:1]
     beta1 = guarded(rr2, rr1)
     tt2 = sums[:, 1:2] + 2.0 * beta1 * sums[:, 2:3] + beta1 * beta1 * tt1
     pp2 = rr2 + beta1 * beta1 * pp1
     inv_alpha2 = guarded(tt2 / TOKENS + damping * pp2, rr2)
-    out = lanes([rr0, rr1, rr2, inv_alpha0, inv_alpha1, inv_alpha2, beta0, beta1], (8, 128))
+    out = lanes([rr0, rr1, rr2, inv_alpha0, inv_alpha1, inv_alpha2, beta0, beta1], (1, 128))
     for i in range(16):
         message[i] = out
 
 
 def whole_kernel(me, got, res0, res1, res2, out):
-    every = jnp.sum(got[...], axis=1)
+    every = jnp.concatenate([got[i] for i in range(16)], axis=0)
     n0, n1, n2, ia0, ia1, ia2, b0, b1 = (every[:, i : i + 1] for i in range(8))
 
     def apply_whole(u):
@@ -417,7 +415,7 @@
     spread = shape((8, 128, 256), bf16)
     block = shape((128, 256), bf16)
     message = shape((8, 144, 256), bf16)
-    table = shape((16, 8, 128), f32)
+    table = shape((16, 1, 128), f32)
 
     with jax.named_scope("rhs"):
         part, flip, acts = local_call(

time: 216 us -> 215 us (level)
  waiting for transfers between devices: 41.4 us -> 37.6 us
  blocking collectives: 110 us -> 113 us
    ppermute x5, waiting for transfers between devices: 10.3 us -> 3.02 us  [across(): return lax.ppermute(v, 'dp', YLO)]
    ppermute x5, waiting for transfers between devices: 5.89 us -> 9.75 us  [down(): return lax.ppermute(v, 'dp', z_shift(-1))]
    ppermute x5, starting transfers between devices: 6.08 us -> 2.92 us  [across(): return lax.ppermute(v, 'dp', YLO)]
    all_to_all x6, blocking collectives: 85.1 us -> 88.1 us  [exchange_chips(): return lax.all_to_all(v, 'shard', 0, 0, axis_index_groups=CHIPS, tiled=True)]
  transfers between devices with their start and end apart: 23 -> 23, of which waited for: 13 -> 12; matrix products, arithmetic and copies ran while one was open for 0% -> 0% of each run, Pallas kernels for 1% -> 1%
where the time goes in v6:
time: 215 us; the launch traced here: 214 us
  blocking collectives  113 us (53%)
  starting transfers between devices  41.3 us (19%)
  waiting for transfers between devices  37.6 us (17%)
  Pallas kernels  20.8 us (10%)
    all_to_all x6, blocking collectives, exchange_chips(): return lax.all_to_all(v, 'shard', 0, 0, axis_index_groups=CHIPS, tiled=True)  88.1 us
    pallas_call x15, Pallas kernels, local_call(): pl.pallas_call(kernel, out_shape=outs, in_specs=specs or [VMEM] * len(arg...  20.8 us
    ppermute x5, starting transfers between devices, down(): return lax.ppermute(v, 'dp', z_shift(-1))  14.5 us
    ppermute x6, starting transfers between devices, swap_core(): return lax.ppermute(v, 'shard', CORE)  13.6 us
    all_to_all x1, blocking collectives, body(): every = lax.all_to_all(mine, 'dp', 0, 0, tiled=True)  13.6 us
    all_to_all x1, blocking collectives, body(): partials = lax.all_to_all(partials, 'shard', 0, 0, tiled=True)  11.8 us
    all_to_all x1, waiting for transfers between devices, exchange_chips(): return lax.all_to_all(v, 'shard', 0, 0, axis_index_groups=CHIPS, tiled=True)  11.2 us
    ppermute x5, waiting for transfers between devices, down(): return lax.ppermute(v, 'dp', z_shift(-1))  9.75 us
  transfers between devices with their start and end apart: 23, of which 12 were waited for; matrix products, arithmetic and copies ran while one was open for 0% of the time, Pallas kernels for 1%

profile of v6, /device:TPU:1, one launch (start us, length us, event | category | flops | bytes accessed | tf_op | source)
XLA Modules:
  0.0 214.1 jit_solution(8739547507922153303)
XLA Ops:
  0.0 5.7 %rows.2 = (bf16[192,2048]{1,0:T(8,128)(2,1)S(1)}, bf16[192,2048]{1,0:T(8,128)(2,1)S(1)}) custom-call(s32[1]{0:T(128)} %bitcast.2.place, s32[2,128]{1,0:T(2,128)} %bitcast.23, s32[1,128]{1,0:T(1,128)} %bitcast.24, bf16[2000,2048]{1,0:T(8,128)(2,1)} %table_hbm.1), custom_call_target="tpu_custom_call" | custom-call | tf_op jit(solution)/shard_map/rows/pallas_call | solution.py:43
  5.7 3.3 %collective-permute-start = (bf16[192,2048]{1,0:T(8,128)(2,1)S(1)}, bf16[192,2048]{1,0:T(8,128)(2,1)S(1)}, u32[]{:S(2)}, u32[]{:S(2)}) collective-permute-start(bf16[192,2048]{1,0:T(8,128)(2,1)S(1)} %get-tuple-element.33), channel_id=1, source_target_pairs={{0,1},{1,0},{2,3},{3,2},{4,5},{5,4},{6,7},{7,6},{8,9},{9,8},{10,11... | collective-permute-start | bytes 2359304 | tf_op jit(solution)/shard_map/rows/ppermute | solution.py:35
  9.6 1.4 collective-permute-done
  11.1 17.5 %all_to_all.50.parts = bf16[8,24,2048]{2,1,0:T(8,128)(2,1)S(1)} all-to-all(bf16[8,24,2048]{2,1,0:T(8,128)(2,1)S(1)} %rows.3), channel_id=1, replica_groups={{0,2,4,6,8,10,12,14},{1,3,5,7,9,11,13,15},{16,18,20,22,24,26,28,30},{17..., dimensions={0} | all-to-all | bytes 1572864 | tf_op jit(solution)/shard_map/rows/all_to_all | solution.py:39
  29.6 3.9 %all-to-all-start.1 = ((bf16[8,24,2048]{2,1,0:T(8,128)(2,1)}), bf16[8,24,2048]{2,1,0:T(8,128)(2,1)S(1)}, u32[]{:S(2)}, u32[]{:S(2)}) async-start(bf16[8,24,2048]{2,1,0:T(8,128)(2,1)} %normed.1), calls=%async_computation.1 | async-start | bytes 1572864 | tf_op jit(solution)/shard_map/normed/all_to_all | solution.py:39
  34.3 11.2 %all-to-all-done.1 = bf16[8,24,2048]{2,1,0:T(8,128)(2,1)S(1)} async-done(((bf16[8,24,2048]{2,1,0:T(8,128)(2,1)}), bf16[8,24,2048]{2,1,0:T(8,128)(2,1)S(1)}, u32[]{:S(2)}, u32[]{:S(2)}) %all-to-all-start.1) | async-done | bytes 786464 | tf_op jit(solution)/shard_map/normed/all_to_all | solution.py:39
  45.5 4.0 %acts.1.refs_0_ = bf16[1040,128]{1,0:T(8,128)(2,1)S(1)} custom-call(bf16[192,2048]{1,0:T(8,128)(2,1)S(1)} %bitcast.17, bf16[344,2048]{1,0:T(8,128)(2,1)S(1)} %bitcast.19, bf16[344,2048]{1,0:T(8,128)(2,1)} %bitcast.10.w_up, bf16[344,2048]{1,0:T(8,128)(2,1)} %collective-permute-done.1.w_gate_other, bf16[344,2048]{1,0:T(8,128)(2,1)} %collective-permute-done.2.w_up_other), custom_call_target="tpu_custom_call" | custom-call | tf_op jit(solution)/shard_map/acts/pallas_call | solution.py:43
  49.5 5.7 %collective-permute-start.6 = (bf16[1040,128]{1,0:T(8,128)(2,1)S(1)}, bf16[1040,128]{1,0:T(8,128)(2,1)S(1)}, u32[]{:S(2)}, u32[]{:S(2)}) collective-permute-start(bf16[1040,128]{1,0:T(8,128)(2,1)S(1)} %acts.1.refs_0_), channel_id=1, source_target_pairs={{0,112},{16,0},{32,16},{48,32},{64,48},{80,64},{96,80},{112,96},{1... | collective-permute-start | bytes 798728 | tf_op jit(solution)/shard_map/groups/ppermute | solution.py:187
  55.1 3.4 %collective-permute-done.6.refs_4_ = bf16[1040,128]{1,0:T(8,128)(2,1)S(1)} collective-permute-done((bf16[1040,128]{1,0:T(8,128)(2,1)S(1)}, bf16[1040,128]{1,0:T(8,128)(2,1)S(1)}, u32[]{:S(2)}, u32[]{:S(2)}) %collective-permute-start.6) | collective-permute-done | bytes 266272 | tf_op jit(solution)/shard_map/groups/ppermute | solution.py:187
  58.5 3.1 %collective-permute-start.10 = (bf16[1040,128]{1,0:T(8,128)(2,1)S(1)}, bf16[1040,128]{1,0:T(8,128)(2,1)S(1)}, u32[]{:S(2)}, u32[]{:S(2)}) collective-permute-start(bf16[1040,128]{1,0:T(8,128)(2,1)S(1)} %collective-permute-done.6.refs_4_), channel_id=1, source_target_pairs={{0,112},{16,0},{32,16},{48,32},{64,48},{80,64},{96,80},{112,96},{1... | collective-permute-start | bytes 798728 | tf_op jit(solution)/shard_map/groups/ppermute | solution.py:187
  62.0 3.0 %collective-permute-done.10.refs_8_ = bf16[1040,128]{1,0:T(8,128)(2,1)S(1)} collective-permute-done((bf16[1040,128]{1,0:T(8,128)(2,1)S(1)}, bf16[1040,128]{1,0:T(8,128)(2,1)S(1)}, u32[]{:S(2)}, u32[]{:S(2)}) %collective-permute-start.10) | collective-permute-done | bytes 266272 | tf_op jit(solution)/shard_map/groups/ppermute | solution.py:187
  65.0 3.1 %collective-permute-start.14 = (bf16[1040,128]{1,0:T(8,128)(2,1)S(1)}, bf16[1040,128]{1,0:T(8,128)(2,1)S(1)}, u32[]{:S(2)}, u32[]{:S(2)}) collective-permute-start(bf16[1040,128]{1,0:T(8,128)(2,1)S(1)} %collective-permute-done.10.refs_8_), channel_id=1, source_target_pairs={{0,112},{16,0},{32,16},{48,32},{64,48},{80,64},{96,80},{112,96},{1... | collective-permute-start | bytes 798728 | tf_op jit(solution)/shard_map/groups/ppermute | solution.py:187
  68.5 3.4 %collective-permute-done.14.refs_12_ = bf16[1040,128]{1,0:T(8,128)(2,1)S(1)} collective-permute-done((bf16[1040,128]{1,0:T(8,128)(2,1)S(1)}, bf16[1040,128]{1,0:T(8,128)(2,1)S(1)}, u32[]{:S(2)}, u32[]{:S(2)}) %collective-permute-start.14) | collective-permute-done | bytes 266272 | tf_op jit(solution)/shard_map/groups/ppermute | solution.py:187
  72.3 5.3 %all-to-all-start.2 = ((bf16[16,64,128]{2,1,0:T(8,128)(2,1)}), bf16[16,64,128]{2,1,0:T(8,128)(2,1)S(1)}, u32[]{:S(2)}, u32[]{:S(2)}) async-start(bf16[16,64,128]{2,1,0:T(8,128)(2,1)} %bitcast_bitcast_fusion), calls=%async_computation.2 | async-start | bytes 524288 | tf_op jit(solution)/shard_map/groups/all_to_all | solution.py:410
  77.6 1.4 collective-permute-start.11
  80.2 1.5 collective-permute-start.16
  83.1 3.0 %all-to-all-done.2.refs_17_ = bf16[16,64,128]{2,1,0:T(8,128)(2,1)S(1)} async-done(((bf16[16,64,128]{2,1,0:T(8,128)(2,1)}), bf16[16,64,128]{2,1,0:T(8,128)(2,1)S(1)}, u32[]{:S(2)}, u32[]{:S(2)}) %all-to-all-start.2) | async-done | bytes 262176 | tf_op jit(solution)/shard_map/groups/all_to_all | solution.py:410
  86.2 1.4 collective-permute-done.11.refs_9_
  87.6 5.3 %collective-permute-done.9.refs_7_ = bf16[1040,128]{1,0:T(8,128)(2,1)} collective-permute-done((bf16[1040,128]{1,0:T(8,128)(2,1)S(1)}, bf16[1040,128]{1,0:T(8,128)(2,1)}, u32[]{:S(2)}, u32[]{:S(2)}) %collective-permute-start.9) | collective-permute-done | bytes 266272 | tf_op jit(solution)/shard_map/groups/ppermute | solution.py:184
  92.9 1.6 collective-permute-done.13.refs_11_
  94.5 2.7 %rhs.1 = (f32[688,128]{1,0:T(8,128)S(1)}, f32[688,128]{1,0:T(8,128)S(1)}, bf16[688,2048]{1,0:T(8,128)(2,1)S(1)}) custom-call(bf16[1040,128]{1,0:T(8,128)(2,1)S(1)} %acts.1.refs_0_, bf16[1040,128]{1,0:T(8,128)(2,1)S(1)} %collective-permute-done.3.refs_1_, bf16[1040,128]{1,0:T(8,128)(2,1)S(1)} %collective-permute-done.4.refs_2_, ...), custom_call_target="tpu_custom_call" | custom-call | tf_op jit(solution)/shard_map/rhs/pallas_call | solution.py:43
  97.2 3.7 %collective-permute-start.18 = (f32[688,128]{1,0:T(8,128)S(1)}, f32[688,128]{1,0:T(8,128)S(1)}, u32[]{:S(2)}, u32[]{:S(2)}) collective-permute-start(f32[688,128]{1,0:T(8,128)S(1)} %get-tuple-element.38), channel_id=1, source_target_pairs={{0,1},{1,0},{2,3},{3,2},{4,5},{5,4},{6,7},{7,6},{8,9},{9,8},{10,11... | collective-permute-start | bytes 1056776 | tf_op jit(solution)/shard_map/rhs/ppermute | solution.py:35
  102.9 17.7 %all_to_all.51.parts = bf16[8,128,256]{2,1,0:T(8,128)(2,1)S(1)} all-to-all(bf16[8,128,256]{2,1,0:T(8,128)(2,1)S(1)} %get-tuple-element.39), channel_id=1, replica_groups={{0,2,4,6,8,10,12,14},{1,3,5,7,9,11,13,15},{16,18,20,22,24,26,28,30},{17..., dimensions={0} | all-to-all | bytes 1048576 | tf_op jit(solution)/shard_map/first/all_to_all | solution.py:39
  120.8 14.0 %all_to_all.52.got = bf16[8,144,256]{2,1,0:T(8,128)(2,1)S(1)} all-to-all(bf16[8,144,256]{2,1,0:T(8,128)(2,1)S(1)} %get-tuple-element.41), channel_id=1, replica_groups={{0,2,4,6,8,10,12,14},{1,3,5,7,9,11,13,15},{16,18,20,22,24,26,28,30},{17..., dimensions={0} | all-to-all | bytes 1179648 | tf_op jit(solution)/shard_map/first/all_to_all | solution.py:39
  135.8 3.0 %collective-permute-start.19 = (f32[696,128]{1,0:T(8,128)S(1)}, f32[696,128]{1,0:T(8,128)S(1)}, u32[]{:S(2)}, u32[]{:S(2)}) collective-permute-start(f32[696,128]{1,0:T(8,128)S(1)} %get-tuple-element.43), channel_id=1, source_target_pairs={{0,1},{1,0},{2,3},{3,2},{4,5},{5,4},{6,7},{7,6},{8,9},{9,8},{10,11... | collective-permute-start | bytes 1069064 | tf_op jit(solution)/shard_map/first/ppermute | solution.py:35
  140.9 12.7 %all_to_all.53.parts = bf16[8,128,256]{2,1,0:T(8,128)(2,1)S(1)} all-to-all(bf16[8,128,256]{2,1,0:T(8,128)(2,1)S(1)} %get-tuple-element.46), channel_id=1, replica_groups={{0,2,4,6,8,10,12,14},{1,3,5,7,9,11,13,15},{16,18,20,22,24,26,28,30},{17..., dimensions={0} | all-to-all | bytes 1048576 | tf_op jit(solution)/shard_map/second/all_to_all | solution.py:39
  153.8 13.5 %all_to_all.54.got = bf16[8,144,256]{2,1,0:T(8,128)(2,1)S(1)} all-to-all(bf16[8,144,256]{2,1,0:T(8,128)(2,1)S(1)} %get-tuple-element.49), channel_id=1, replica_groups={{0,2,4,6,8,10,12,14},{1,3,5,7,9,11,13,15},{16,18,20,22,24,26,28,30},{17..., dimensions={0} | all-to-all | bytes 1179648 | tf_op jit(solution)/shard_map/second/all_to_all | solution.py:39
  168.5 3.1 %collective-permute-start.20 = (f32[696,128]{1,0:T(8,128)S(1)}, f32[696,128]{1,0:T(8,128)S(1)}, u32[]{:S(2)}, u32[]{:S(2)}) collective-permute-start(f32[696,128]{1,0:T(8,128)S(1)} %get-tuple-element.52), channel_id=1, source_target_pairs={{0,1},{1,0},{2,3},{3,2},{4,5},{5,4},{6,7},{7,6},{8,9},{9,8},{10,11... | collective-permute-start | bytes 1069064 | tf_op jit(solution)/shard_map/second/ppermute | solution.py:35
  174.0 12.7 %all_to_all.55.parts = bf16[8,128,256]{2,1,0:T(8,128)(2,1)S(1)} all-to-all(bf16[8,128,256]{2,1,0:T(8,128)(2,1)S(1)} %get-tuple-element.55), channel_id=1, replica_groups={{0,2,4,6,8,10,12,14},{1,3,5,7,9,11,13,15},{16,18,20,22,24,26,28,30},{17..., dimensions={0} | all-to-all | bytes 1048576 | tf_op jit(solution)/shard_map/third/all_to_all | solution.py:39
  186.9 11.8 %all_to_all.56.got = f32[16,1,128]{2,1,0:T(1,128)S(1)} all-to-all(f32[16,1,128]{2,1,0:T(1,128)S(1)} %third.3), channel_id=1, replica_groups=mesh['dp'=16,'shard'=16] {'shard'}, dimensions={0} | all-to-all | bytes 16384 | tf_op jit(solution)/shard_map/third/all_to_all | solution.py:465
  199.1 13.6 %all_to_all.57.got = f32[16,1,128]{2,1,0:T(1,128)S(1)} all-to-all(f32[16,1,128]{2,1,0:T(1,128)S(1)} %whole.2), channel_id=1, replica_groups=mesh['dp'=16,'shard'=16] {'dp'}, dimensions={0} | all-to-all | bytes 16384 | tf_op jit(solution)/shard_map/whole/all_to_all | solution.py:468
  212.7 1.4 whole.3
  (44 shorter events, 16.0 us)
Async XLA Ops:
  0.0 33.5 %copy-start = (bf16[128,2048]{1,0:T(8,128)(2,1)S(1)}, bf16[128,2048]{1,0:T(8,128)(2,1)}, u32[]{:S(2)}) copy-start(bf16[128,2048]{1,0:T(8,128)(2,1)} %param.13) | copy-start | bytes 1572868
  0.0 9.1 %copy-start.1 = (bf16[2048,344]{0,1:T(8,128)(2,1)S(1)}, bf16[2048,344]{0,1:T(8,128)(2,1)}, u32[]{:S(2)}) copy-start(bf16[2048,344]{0,1:T(8,128)(2,1)} %param.11) | copy-start | bytes 4227076
  5.7 5.3 %collective-permute-start = (bf16[192,2048]{1,0:T(8,128)(2,1)S(1)}, bf16[192,2048]{1,0:T(8,128)(2,1)S(1)}, u32[]{:S(2)}, u32[]{:S(2)}) collective-permute-start(bf16[192,2048]{1,0:T(8,128)(2,1)S(1)} %get-tuple-element.33), channel_id=1, source_target_pairs={{0,1},{1,0},{2,3},{3,2},{4,5},{5,4},{6,7},{7,6},{8,9},{9,8},{10,11... | collective-permute-start | bytes 2359304 | tf_op jit(solution)/shard_map/rows/ppermute | solution.py:35
  9.1 25.2 %collective-permute-start.1 = (bf16[344,2048]{1,0:T(8,128)(2,1)S(1)}, bf16[344,2048]{1,0:T(8,128)(2,1)}, u32[]{:S(2)}, u32[]{:S(2)}) collective-permute-start(bf16[344,2048]{1,0:T(8,128)(2,1)S(1)} %bitcast.18), channel_id=1, source_target_pairs={{0,1},{1,0},{2,3},{3,2},{4,5},{5,4},{6,7},{7,6},{8,9},{9,8},{10,11... | collective-permute-start | bytes 4227080 | tf_op jit(solution)/shard_map/ppermute | solution.py:35
  9.2 25.1 %collective-permute-start.2 = (bf16[344,2048]{1,0:T(8,128)(2,1)}, bf16[344,2048]{1,0:T(8,128)(2,1)}, u32[]{:S(2)}, u32[]{:S(2)}) collective-permute-start(bf16[344,2048]{1,0:T(8,128)(2,1)} %bitcast.10.w_up), channel_id=1, source_target_pairs={{0,1},{1,0},{2,3},{3,2},{4,5},{5,4},{6,7},{7,6},{8,9},{9,8},{10,11... | collective-permute-start | bytes 4227080 | tf_op jit(solution)/shard_map/ppermute | solution.py:35
  11.0 17.6 %copy-start.2 = (f32[2048]{0:T(1024)S(1)}, f32[2048]{0:T(1024)}, u32[]{:S(2)}) copy-start(f32[2048]{0:T(1024)} %param.10) | copy-start | bytes 24580
  29.6 15.9 %all-to-all-start.1 = ((bf16[8,24,2048]{2,1,0:T(8,128)(2,1)}), bf16[8,24,2048]{2,1,0:T(8,128)(2,1)S(1)}, u32[]{:S(2)}, u32[]{:S(2)}) async-start(bf16[8,24,2048]{2,1,0:T(8,128)(2,1)} %normed.1), calls=%async_computation.1 | async-start | bytes 1572864 | tf_op jit(solution)/shard_map/normed/all_to_all | solution.py:39
  49.5 9.0 %collective-permute-start.6 = (bf16[1040,128]{1,0:T(8,128)(2,1)S(1)}, bf16[1040,128]{1,0:T(8,128)(2,1)S(1)}, u32[]{:S(2)}, u32[]{:S(2)}) collective-permute-start(bf16[1040,128]{1,0:T(8,128)(2,1)S(1)} %acts.1.refs_0_), channel_id=1, source_target_pairs={{0,112},{16,0},{32,16},{48,32},{64,48},{80,64},{96,80},{112,96},{1... | collective-permute-start | bytes 798728 | tf_op jit(solution)/shard_map/groups/ppermute | solution.py:187
  55.1 6.9 %collective-permute-start.4 = (bf16[1040,128]{1,0:T(8,128)(2,1)S(1)}, bf16[1040,128]{1,0:T(8,128)(2,1)S(1)}, u32[]{:S(2)}, u32[]{:S(2)}) collective-permute-start(bf16[1040,128]{1,0:T(8,128)(2,1)S(1)} %acts.1.refs_0_), channel_id=1, source_target_pairs={{0,16},{16,32},{32,48},{48,64},{64,80},{80,96},{96,112},{112,0},{1... | collective-permute-start | bytes 798728 | tf_op jit(solution)/shard_map/groups/ppermute | solution.py:184
  58.5 6.5 %collective-permute-start.10 = (bf16[1040,128]{1,0:T(8,128)(2,1)S(1)}, bf16[1040,128]{1,0:T(8,128)(2,1)S(1)}, u32[]{:S(2)}, u32[]{:S(2)}) collective-permute-start(bf16[1040,128]{1,0:T(8,128)(2,1)S(1)} %collective-permute-done.6.refs_4_), channel_id=1, source_target_pairs={{0,112},{16,0},{32,16},{48,32},{64,48},{80,64},{96,80},{112,96},{1... | collective-permute-start | bytes 798728 | tf_op jit(solution)/shard_map/groups/ppermute | solution.py:187
  61.6 6.5 %collective-permute-start.3 = (bf16[1040,128]{1,0:T(8,128)(2,1)S(1)}, bf16[1040,128]{1,0:T(8,128)(2,1)S(1)}, u32[]{:S(2)}, u32[]{:S(2)}) collective-permute-start(bf16[1040,128]{1,0:T(8,128)(2,1)S(1)} %acts.1.refs_0_), channel_id=1, source_target_pairs={{0,128},{16,144},{32,160},{48,176},{64,192},{80,208},{96,224},{112... | collective-permute-start | bytes 798728 | tf_op jit(solution)/shard_map/groups/ppermute | solution.py:190
  62.0 6.5 %collective-permute-start.8 = (bf16[1040,128]{1,0:T(8,128)(2,1)S(1)}, bf16[1040,128]{1,0:T(8,128)(2,1)S(1)}, u32[]{:S(2)}, u32[]{:S(2)}) collective-permute-start(bf16[1040,128]{1,0:T(8,128)(2,1)S(1)} %collective-permute-done.4.refs_2_), channel_id=1, source_target_pairs={{0,16},{16,32},{32,48},{48,64},{64,80},{80,96},{96,112},{112,0},{1... | collective-permute-start | bytes 798728 | tf_op jit(solution)/shard_map/groups/ppermute | solution.py:184
  65.0 7.0 %collective-permute-start.14 = (bf16[1040,128]{1,0:T(8,128)(2,1)S(1)}, bf16[1040,128]{1,0:T(8,128)(2,1)S(1)}, u32[]{:S(2)}, u32[]{:S(2)}) collective-permute-start(bf16[1040,128]{1,0:T(8,128)(2,1)S(1)} %collective-permute-done.10.refs_8_), channel_id=1, source_target_pairs={{0,112},{16,0},{32,16},{48,32},{64,48},{80,64},{96,80},{112,96},{1... | collective-permute-start | bytes 798728 | tf_op jit(solution)/shard_map/groups/ppermute | solution.py:187
  68.1 10.9 %collective-permute-start.5 = (bf16[1040,128]{1,0:T(8,128)(2,1)S(1)}, bf16[1040,128]{1,0:T(8,128)(2,1)S(1)}, u32[]{:S(2)}, u32[]{:S(2)}) collective-permute-start(bf16[1040,128]{1,0:T(8,128)(2,1)S(1)} %collective-permute-done.3.refs_1_), channel_id=1, source_target_pairs={{0,16},{16,32},{32,48},{48,64},{64,80},{80,96},{96,112},{112,0},{1... | collective-permute-start | bytes 798728 | tf_op jit(solution)/shard_map/groups/ppermute | solution.py:184
  68.1 12.1 %collective-permute-start.7 = (bf16[1040,128]{1,0:T(8,128)(2,1)S(1)}, bf16[1040,128]{1,0:T(8,128)(2,1)S(1)}, u32[]{:S(2)}, u32[]{:S(2)}) collective-permute-start(bf16[1040,128]{1,0:T(8,128)(2,1)S(1)} %collective-permute-done.6.refs_4_), channel_id=1, source_target_pairs={{0,128},{16,144},{32,160},{48,176},{64,192},{80,208},{96,224},{112... | collective-permute-start | bytes 798728 | tf_op jit(solution)/shard_map/groups/ppermute | solution.py:190
  68.5 13.2 %collective-permute-start.12 = (bf16[1040,128]{1,0:T(8,128)(2,1)S(1)}, bf16[1040,128]{1,0:T(8,128)(2,1)S(1)}, u32[]{:S(2)}, u32[]{:S(2)}) collective-permute-start(bf16[1040,128]{1,0:T(8,128)(2,1)S(1)} %collective-permute-done.8.refs_6_), channel_id=1, source_target_pairs={{0,16},{16,32},{32,48},{48,64},{64,80},{80,96},{96,112},{112,0},{1... | collective-permute-start | bytes 798728 | tf_op jit(solution)/shard_map/groups/ppermute | solution.py:184
  71.9 10.1 %collective-permute-start.15 = (bf16[1040,128]{1,0:T(8,128)(2,1)S(1)}, bf16[1040,128]{1,0:T(8,128)(2,1)}, u32[]{:S(2)}, u32[]{:S(2)}) collective-permute-start(bf16[1040,128]{1,0:T(8,128)(2,1)S(1)} %collective-permute-done.14.refs_12_), channel_id=1, source_target_pairs={{0,128},{16,144},{32,160},{48,176},{64,192},{80,208},{96,224},{112... | collective-permute-start | bytes 798728 | tf_op jit(solution)/shard_map/groups/ppermute | solution.py:190
  72.3 13.9 %all-to-all-start.2 = ((bf16[16,64,128]{2,1,0:T(8,128)(2,1)}), bf16[16,64,128]{2,1,0:T(8,128)(2,1)S(1)}, u32[]{:S(2)}, u32[]{:S(2)}) async-start(bf16[16,64,128]{2,1,0:T(8,128)(2,1)} %bitcast_bitcast_fusion), calls=%async_computation.2 | async-start | bytes 524288 | tf_op jit(solution)/shard_map/groups/all_to_all | solution.py:410
  77.6 10.0 %collective-permute-start.11 = (bf16[1040,128]{1,0:T(8,128)(2,1)S(1)}, bf16[1040,128]{1,0:T(8,128)(2,1)}, u32[]{:S(2)}, u32[]{:S(2)}) collective-permute-start(bf16[1040,128]{1,0:T(8,128)(2,1)S(1)} %collective-permute-done.10.refs_8_), channel_id=1, source_target_pairs={{0,128},{16,144},{32,160},{48,176},{64,192},{80,208},{96,224},{112... | collective-permute-start | bytes 798728 | tf_op jit(solution)/shard_map/groups/ppermute | solution.py:190
  79.0 13.9 %collective-permute-start.9 = (bf16[1040,128]{1,0:T(8,128)(2,1)S(1)}, bf16[1040,128]{1,0:T(8,128)(2,1)}, u32[]{:S(2)}, u32[]{:S(2)}) collective-permute-start(bf16[1040,128]{1,0:T(8,128)(2,1)S(1)} %collective-permute-done.5.refs_3_), channel_id=1, source_target_pairs={{0,16},{16,32},{32,48},{48,64},{64,80},{80,96},{96,112},{112,0},{1... | collective-permute-start | bytes 798728 | tf_op jit(solution)/shard_map/groups/ppermute | solution.py:184
  80.2 12.7 %collective-permute-start.16 = (bf16[1040,128]{1,0:T(8,128)(2,1)S(1)}, bf16[1040,128]{1,0:T(8,128)(2,1)}, u32[]{:S(2)}, u32[]{:S(2)}) collective-permute-start(bf16[1040,128]{1,0:T(8,128)(2,1)S(1)} %collective-permute-done.14.refs_12_), channel_id=1, source_target_pairs={{0,112},{16,0},{32,16},{48,32},{64,48},{80,64},{96,80},{112,96},{1... | collective-permute-start | bytes 798728 | tf_op jit(solution)/shard_map/groups/ppermute | solution.py:187
  81.7 12.8 %collective-permute-start.13 = (bf16[1040,128]{1,0:T(8,128)(2,1)S(1)}, bf16[1040,128]{1,0:T(8,128)(2,1)}, u32[]{:S(2)}, u32[]{:S(2)}) collective-permute-start(bf16[1040,128]{1,0:T(8,128)(2,1)S(1)} %collective-permute-done.12.refs_10_), channel_id=1, source_target_pairs={{0,128},{16,144},{32,160},{48,176},{64,192},{80,208},{96,224},{112... | collective-permute-start | bytes 798728 | tf_op jit(solution)/shard_map/groups/ppermute | solution.py:190
  82.0 12.5 %collective-permute-start.17 = (bf16[1040,128]{1,0:T(8,128)(2,1)}, bf16[1040,128]{1,0:T(8,128)(2,1)}, u32[]{:S(2)}, u32[]{:S(2)}) collective-permute-start(bf16[1040,128]{1,0:T(8,128)(2,1)} %collective-permute-done.15.refs_13_), channel_id=1, source_target_pairs={{0,112},{16,0},{32,16},{48,32},{64,48},{80,64},{96,80},{112,96},{1... | collective-permute-start | bytes 798728 | tf_op jit(solution)/shard_map/groups/ppermute | solution.py:187
  97.2 5.0 %collective-permute-start.18 = (f32[688,128]{1,0:T(8,128)S(1)}, f32[688,128]{1,0:T(8,128)S(1)}, u32[]{:S(2)}, u32[]{:S(2)}) collective-permute-start(f32[688,128]{1,0:T(8,128)S(1)} %get-tuple-element.38), channel_id=1, source_target_pairs={{0,1},{1,0},{2,3},{3,2},{4,5},{5,4},{6,7},{7,6},{8,9},{9,8},{10,11... | collective-permute-start | bytes 1056776 | tf_op jit(solution)/shard_map/rhs/ppermute | solution.py:35
  135.8 4.3 %collective-permute-start.19 = (f32[696,128]{1,0:T(8,128)S(1)}, f32[696,128]{1,0:T(8,128)S(1)}, u32[]{:S(2)}, u32[]{:S(2)}) collective-permute-start(f32[696,128]{1,0:T(8,128)S(1)} %get-tuple-element.43), channel_id=1, source_target_pairs={{0,1},{1,0},{2,3},{3,2},{4,5},{5,4},{6,7},{7,6},{8,9},{9,8},{10,11... | collective-permute-start | bytes 1069064 | tf_op jit(solution)/shard_map/first/ppermute | solution.py:35
  168.5 4.4 %collective-permute-start.20 = (f32[696,128]{1,0:T(8,128)S(1)}, f32[696,128]{1,0:T(8,128)S(1)}, u32[]{:S(2)}, u32[]{:S(2)}) collective-permute-start(f32[696,128]{1,0:T(8,128)S(1)} %get-tuple-element.52), channel_id=1, source_target_pairs={{0,1},{1,0},{2,3},{3,2},{4,5},{5,4},{6,7},{7,6},{8,9},{9,8},{10,11... | collective-permute-start | bytes 1069064 | tf_op jit(solution)/shard_map/second/ppermute | solution.py:35

commit v7 on v6

--- a/solution.py
+++ b/solution.py
@@ -219,10 +219,9 @@
         for j, block in enumerate(pair):
             acts[:, (2 * i + j) * 128 : (2 * i + j + 1) * 128] = block[:BOTH, :]
     out = out * scale
-    part[:UNITS] = out[:UNITS, :128]
-    part[UNITS:] = out[:UNITS, 128:]
-    flip[:UNITS] = out[:UNITS, 128:]
-    flip[UNITS:] = out[:UNITS, :128]
+    part[:UNITS] = out[:UNITS, :128].astype(bf16).astype(f32)
+    part[UNITS:] = out[:UNITS, 128:].astype(bf16).astype(f32)
+    flip[...] = jnp.concatenate([out[:UNITS, 128:], out[:UNITS, :128]], axis=0).astype(bf16)
 
 
 def spread_tangent(res, acts, tangent):
@@ -232,7 +231,7 @@
 
 
 def first_kernel(acts, part, got, res_out, sums, tangent):
-    res = part[...] + got[...]
+    res = part[...] + got[...].astype(f32)
     res_out[...] = res
     sums[...] = lanes([total(res * res)], (8, 128))
     spread_tangent(res, acts, tangent)
@@ -287,28 +286,26 @@
     row = lax.broadcasted_iota(jnp.int32, (8, 128), 0)
     sums = jnp.where(row == 0, jnp.broadcast_to(sums, (8, 128)), 0.0)
     sums_out[...] = sums
-    part[...] = out
-    flip[:UNITS] = out[UNITS:]
-    flip[UNITS:BOTH] = out[:UNITS]
-    flip[BOTH:] = sums
-
-
-def second_kernel(acts, part, got, sums, res, res_out, state, tangent):
+    part[...] = out.astype(bf16).astype(f32)
+    flip[...] = jnp.concatenate([out[UNITS:], out[:UNITS]], axis=0).astype(bf16)
+
+
+def second_kernel(acts, part, got, peer, sums, res, res_out, state, tangent):
     rr = sums[0:1, 0:1]
-    tt = sums[0:1, 1:2] + got[BOTH : BOTH + 1, 1:2]
+    tt = sums[0:1, 1:2] + peer[0:1, 1:2]
     inv_alpha = guarded(tt / TOKENS + damping * rr, rr)
     alpha = guarded(jnp.ones_like(inv_alpha), inv_alpha)
     old = res[...]
-    new = old - alpha * ((part[...] + got[:BOTH]) / TOKENS + damping * old)
+    new = old - alpha * ((part[...] + got[...].astype(f32)) / TOKENS + damping * old)
     res_out[...] = new
     state[...] = lanes([total(new * new), rr, tt, rr, inv_alpha], (8, 128))
     spread_tangent(new, acts, tangent)
 
 
-def third_kernel(acts, part, got, sums, past, res, res_before, res_out, state, tangent):
+def third_kernel(acts, part, got, peer, sums, past, res, res_before, res_out, state, tangent):
     rr = sums[0:1, 0:1]
-    ww = sums[0:1, 1:2] + got[BOTH : BOTH + 1, 1:2]
-    cross = sums[0:1, 2:3] + got[BOTH : BOTH + 1, 2:3]
+    ww = sums[0:1, 1:2] + peer[0:1, 1:2]
+    cross = sums[0:1, 2:3] + peer[0:1, 2:3]
     rr0, tt0, pp0, inv_alpha0 = (past[0:1, i : i + 1] for i in range(1, 5))
     beta = guarded(rr, rr0)
     tt = ww + 2.0 * beta * cross + beta * beta * tt0
@@ -317,7 +314,7 @@
     alpha = guarded(jnp.ones_like(inv_alpha), inv_alpha)
     old = res[...]
     direction = old + beta * res_before[...]
-    new = old - alpha * ((part[...] + got[:BOTH]) / TOKENS + damping * direction)
+    new = old - alpha * ((part[...] + got[...].astype(f32)) / TOKENS + damping * direction)
     res_out[...] = new
     state[...] = lanes(
         [total(new * new), rr0, rr, tt, pp, inv_alpha0, inv_alpha, beta], (8, 128)
@@ -410,7 +407,7 @@
         columns = lax.all_to_all(columns, "dp", 0, 0, tiled=True)
         blocks, columns = gather_groups(package, columns)
     vector = shape((BOTH, 128), f32)
-    longer = shape((BOTH + 8, 128), f32)
+    rounded = shape((BOTH, 128), bf16)
     small = shape((8, 128), f32)
     spread = shape((8, 128, 256), bf16)
     block = shape((128, 256), bf16)
@@ -420,7 +417,7 @@
     with jax.named_scope("rhs"):
         part, flip, acts = local_call(
             functools.partial(rhs_kernel, 1.0 / math.sqrt(2048)),
-            (vector, vector, pltpu.VMEM((BOTH, TOKENS // 2), bf16)),
+            (vector, rounded, pltpu.VMEM((BOTH, TOKENS // 2), bf16)),
             *blocks,
             lax.axis_index("dp").reshape(1),
             columns,
@@ -433,21 +430,21 @@
         block0, shared = local_call(share_kernel, (block, message), parts, sums)
         shared = exchange_chips(shared)
         tangent0, part, flip, sums = local_call(
-            curve_kernel, (spread, vector, longer, small), acts, shared
-        )
-        got = swap_core(flip)
+            curve_kernel, (spread, vector, rounded, small), acts, shared
+        )
+        got, peer = swap_core(flip), swap_core(sums)
     with jax.named_scope("second"):
         res1, state, tangent = local_call(
-            second_kernel, (vector, small, spread), acts, part, got, sums, res0
+            second_kernel, (vector, small, spread), acts, part, got, peer, sums, res0
         )
         parts = exchange_chips(tangent)
         block1, shared = local_call(share_kernel, (block, message), parts, state, block0)
         shared = exchange_chips(shared)
         past = state
         part, flip, sums = local_call(
-            curve_kernel, (vector, longer, small), acts, shared, tangent0, state
-        )
-        got = swap_core(flip)
+            curve_kernel, (vector, rounded, small), acts, shared, tangent0, state
+        )
+        got, peer = swap_core(flip), swap_core(sums)
     with jax.named_scope("third"):
         res2, state, tangent = local_call(
             third_kernel,
@@ -455,6 +452,7 @@
             acts,
             part,
             got,
+            peer,
             sums,
             past,
             res1,

time: 215 us -> 214 us (level)
    ppermute x6 -> x8, waiting for transfers between devices: 5.31 us -> 4.6 us  [swap_core(): return lax.ppermute(v, 'shard', CORE)]
    ppermute x6 -> x8, starting transfers between devices: 13.6 us -> 14.2 us  [swap_core(): return lax.ppermute(v, 'shard', CORE)]
  transfers between devices with their start and end apart: 23 -> 25, of which waited for: 12 -> 12; matrix products, arithmetic and copies ran while one was open for 0% -> 0% of each run, Pallas kernels for 1% -> 1%
where the time goes in v7:
time: 214 us
  blocking collectives  113 us (53%)
  starting transfers between devices  41.9 us (20%)
  waiting for transfers between devices  36.9 us (17%)
  Pallas kernels  20.8 us (10%)
    all_to_all x6, blocking collectives, exchange_chips(): return lax.all_to_all(v, 'shard', 0, 0, axis_index_groups=CHIPS, tiled=True)  88.5 us
    pallas_call x15, Pallas kernels, local_call(): pl.pallas_call(kernel, out_shape=outs, in_specs=specs or [VMEM] * len(arg...  20.8 us
    ppermute x5, starting transfers between devices, down(): return lax.ppermute(v, 'dp', z_shift(-1))  14.5 us
    ppermute x8, starting transfers between devices, swap_core(): return lax.ppermute(v, 'shard', CORE)  14.2 us
    all_to_all x1, blocking collectives, body(): every = lax.all_to_all(mine, 'dp', 0, 0, tiled=True)  13.6 us
    all_to_all x1, waiting for transfers between devices, exchange_chips(): return lax.all_to_all(v, 'shard', 0, 0, axis_index_groups=CHIPS, tiled=True)  11.2 us
    all_to_all x1, blocking collectives, body(): partials = lax.all_to_all(partials, 'shard', 0, 0, tiled=True)  11.1 us
    ppermute x5, waiting for transfers between devices, down(): return lax.ppermute(v, 'dp', z_shift(-1))  9.71 us
  transfers between devices with their start and end apart: 25, of which 12 were waited for; matrix products, arithmetic and copies ran while one was open for 0% of the time, Pallas kernels for 1%

profile of v7, /device:TPU:1, one launch (start us, length us, event | category | flops | bytes accessed | tf_op | source)
XLA Modules:
  0.0 213.8 jit_solution(14072882511835042007)
XLA Ops:
  0.0 5.7 %rows.2 = (bf16[192,2048]{1,0:T(8,128)(2,1)S(1)}, bf16[192,2048]{1,0:T(8,128)(2,1)S(1)}) custom-call(s32[1]{0:T(128)} %bitcast.2.place, s32[2,128]{1,0:T(2,128)} %bitcast.23, s32[1,128]{1,0:T(1,128)} %bitcast.24, bf16[2000,2048]{1,0:T(8,128)(2,1)} %table_hbm.1), custom_call_target="tpu_custom_call" | custom-call | tf_op jit(solution)/shard_map/rows/pallas_call | solution.py:43
  5.7 3.3 %collective-permute-start = (bf16[192,2048]{1,0:T(8,128)(2,1)S(1)}, bf16[192,2048]{1,0:T(8,128)(2,1)S(1)}, u32[]{:S(2)}, u32[]{:S(2)}) collective-permute-start(bf16[192,2048]{1,0:T(8,128)(2,1)S(1)} %get-tuple-element.33), channel_id=1, source_target_pairs={{0,1},{1,0},{2,3},{3,2},{4,5},{5,4},{6,7},{7,6},{8,9},{9,8},{10,11... | collective-permute-start | bytes 2359304 | tf_op jit(solution)/shard_map/rows/ppermute | solution.py:35
  9.6 1.4 collective-permute-done
  11.1 17.5 %all_to_all.50.parts = bf16[8,24,2048]{2,1,0:T(8,128)(2,1)S(1)} all-to-all(bf16[8,24,2048]{2,1,0:T(8,128)(2,1)S(1)} %rows.3), channel_id=1, replica_groups={{0,2,4,6,8,10,12,14},{1,3,5,7,9,11,13,15},{16,18,20,22,24,26,28,30},{17..., dimensions={0} | all-to-all | bytes 1572864 | tf_op jit(solution)/shard_map/rows/all_to_all | solution.py:39
  29.6 3.9 %all-to-all-start.1 = ((bf16[8,24,2048]{2,1,0:T(8,128)(2,1)}), bf16[8,24,2048]{2,1,0:T(8,128)(2,1)S(1)}, u32[]{:S(2)}, u32[]{:S(2)}) async-start(bf16[8,24,2048]{2,1,0:T(8,128)(2,1)} %normed.1), calls=%async_computation.1 | async-start | bytes 1572864 | tf_op jit(solution)/shard_map/normed/all_to_all | solution.py:39
  34.3 11.2 %all-to-all-done.1 = bf16[8,24,2048]{2,1,0:T(8,128)(2,1)S(1)} async-done(((bf16[8,24,2048]{2,1,0:T(8,128)(2,1)}), bf16[8,24,2048]{2,1,0:T(8,128)(2,1)S(1)}, u32[]{:S(2)}, u32[]{:S(2)}) %all-to-all-start.1) | async-done | bytes 786464 | tf_op jit(solution)/shard_map/normed/all_to_all | solution.py:39
  45.5 4.0 %acts.1.refs_0_ = bf16[1040,128]{1,0:T(8,128)(2,1)S(1)} custom-call(bf16[192,2048]{1,0:T(8,128)(2,1)S(1)} %bitcast.17, bf16[344,2048]{1,0:T(8,128)(2,1)S(1)} %bitcast.19, bf16[344,2048]{1,0:T(8,128)(2,1)} %bitcast.10.w_up, bf16[344,2048]{1,0:T(8,128)(2,1)} %collective-permute-done.1.w_gate_other, bf16[344,2048]{1,0:T(8,128)(2,1)} %collective-permute-done.2.w_up_other), custom_call_target="tpu_custom_call" | custom-call | tf_op jit(solution)/shard_map/acts/pallas_call | solution.py:43
  49.4 5.7 %collective-permute-start.6 = (bf16[1040,128]{1,0:T(8,128)(2,1)S(1)}, bf16[1040,128]{1,0:T(8,128)(2,1)S(1)}, u32[]{:S(2)}, u32[]{:S(2)}) collective-permute-start(bf16[1040,128]{1,0:T(8,128)(2,1)S(1)} %acts.1.refs_0_), channel_id=1, source_target_pairs={{0,112},{16,0},{32,16},{48,32},{64,48},{80,64},{96,80},{112,96},{1... | collective-permute-start | bytes 798728 | tf_op jit(solution)/shard_map/groups/ppermute | solution.py:187
  55.1 3.4 %collective-permute-done.6.refs_4_ = bf16[1040,128]{1,0:T(8,128)(2,1)S(1)} collective-permute-done((bf16[1040,128]{1,0:T(8,128)(2,1)S(1)}, bf16[1040,128]{1,0:T(8,128)(2,1)S(1)}, u32[]{:S(2)}, u32[]{:S(2)}) %collective-permute-start.6) | collective-permute-done | bytes 266272 | tf_op jit(solution)/shard_map/groups/ppermute | solution.py:187
  58.5 3.1 %collective-permute-start.10 = (bf16[1040,128]{1,0:T(8,128)(2,1)S(1)}, bf16[1040,128]{1,0:T(8,128)(2,1)S(1)}, u32[]{:S(2)}, u32[]{:S(2)}) collective-permute-start(bf16[1040,128]{1,0:T(8,128)(2,1)S(1)} %collective-permute-done.6.refs_4_), channel_id=1, source_target_pairs={{0,112},{16,0},{32,16},{48,32},{64,48},{80,64},{96,80},{112,96},{1... | collective-permute-start | bytes 798728 | tf_op jit(solution)/shard_map/groups/ppermute | solution.py:187
  62.0 3.0 %collective-permute-done.10.refs_8_ = bf16[1040,128]{1,0:T(8,128)(2,1)S(1)} collective-permute-done((bf16[1040,128]{1,0:T(8,128)(2,1)S(1)}, bf16[1040,128]{1,0:T(8,128)(2,1)S(1)}, u32[]{:S(2)}, u32[]{:S(2)}) %collective-permute-start.10) | collective-permute-done | bytes 266272 | tf_op jit(solution)/shard_map/groups/ppermute | solution.py:187
  64.9 3.1 %collective-permute-start.14 = (bf16[1040,128]{1,0:T(8,128)(2,1)S(1)}, bf16[1040,128]{1,0:T(8,128)(2,1)S(1)}, u32[]{:S(2)}, u32[]{:S(2)}) collective-permute-start(bf16[1040,128]{1,0:T(8,128)(2,1)S(1)} %collective-permute-done.10.refs_8_), channel_id=1, source_target_pairs={{0,112},{16,0},{32,16},{48,32},{64,48},{80,64},{96,80},{112,96},{1... | collective-permute-start | bytes 798728 | tf_op jit(solution)/shard_map/groups/ppermute | solution.py:187
  68.5 3.4 %collective-permute-done.14.refs_12_ = bf16[1040,128]{1,0:T(8,128)(2,1)S(1)} collective-permute-done((bf16[1040,128]{1,0:T(8,128)(2,1)S(1)}, bf16[1040,128]{1,0:T(8,128)(2,1)S(1)}, u32[]{:S(2)}, u32[]{:S(2)}) %collective-permute-start.14) | collective-permute-done | bytes 266272 | tf_op jit(solution)/shard_map/groups/ppermute | solution.py:187
  72.3 5.3 %all-to-all-start.2 = ((bf16[16,64,128]{2,1,0:T(8,128)(2,1)}), bf16[16,64,128]{2,1,0:T(8,128)(2,1)S(1)}, u32[]{:S(2)}, u32[]{:S(2)}) async-start(bf16[16,64,128]{2,1,0:T(8,128)(2,1)} %bitcast_bitcast_fusion), calls=%async_computation.2 | async-start | bytes 524288 | tf_op jit(solution)/shard_map/groups/all_to_all | solution.py:407
  77.6 1.4 collective-permute-start.11
  80.1 1.5 collective-permute-start.16
  83.1 3.0 %all-to-all-done.2.refs_17_ = bf16[16,64,128]{2,1,0:T(8,128)(2,1)S(1)} async-done(((bf16[16,64,128]{2,1,0:T(8,128)(2,1)}), bf16[16,64,128]{2,1,0:T(8,128)(2,1)S(1)}, u32[]{:S(2)}, u32[]{:S(2)}) %all-to-all-start.2) | async-done | bytes 262176 | tf_op jit(solution)/shard_map/groups/all_to_all | solution.py:407
  86.1 1.4 collective-permute-done.11.refs_9_
  87.5 5.3 %collective-permute-done.9.refs_7_ = bf16[1040,128]{1,0:T(8,128)(2,1)} collective-permute-done((bf16[1040,128]{1,0:T(8,128)(2,1)S(1)}, bf16[1040,128]{1,0:T(8,128)(2,1)}, u32[]{:S(2)}, u32[]{:S(2)}) %collective-permute-start.9) | collective-permute-done | bytes 266272 | tf_op jit(solution)/shard_map/groups/ppermute | solution.py:184
  92.9 1.6 collective-permute-done.13.refs_11_
  94.5 2.7 %rhs.1 = (f32[688,128]{1,0:T(8,128)S(1)}, bf16[688,128]{1,0:T(8,128)(2,1)S(1)}, bf16[688,2048]{1,0:T(8,128)(2,1)S(1)}) custom-call(bf16[1040,128]{1,0:T(8,128)(2,1)S(1)} %acts.1.refs_0_, bf16[1040,128]{1,0:T(8,128)(2,1)S(1)} %collective-permute-done.3.refs_1_, bf16[1040,128]{1,0:T(8,128)(2,1)S(1)} %collective-permute-done.4.refs_2_, ...), custom_call_target="tpu_custom_call" | custom-call | tf_op jit(solution)/shard_map/rhs/pallas_call | solution.py:43
  97.2 4.2 %collective-permute-start.18 = (bf16[688,128]{1,0:T(8,128)(2,1)S(1)}, bf16[688,128]{1,0:T(8,128)(2,1)S(1)}, u32[]{:S(2)}, u32[]{:S(2)}) collective-permute-start(bf16[688,128]{1,0:T(8,128)(2,1)S(1)} %get-tuple-element.38), channel_id=1, source_target_pairs={{0,1},{1,0},{2,3},{3,2},{4,5},{5,4},{6,7},{7,6},{8,9},{9,8},{10,11... | collective-permute-start | bytes 528392 | tf_op jit(solution)/shard_map/rhs/ppermute | solution.py:35
  103.1 17.3 %all_to_all.51.parts = bf16[8,128,256]{2,1,0:T(8,128)(2,1)S(1)} all-to-all(bf16[8,128,256]{2,1,0:T(8,128)(2,1)S(1)} %get-tuple-element.39), channel_id=1, replica_groups={{0,2,4,6,8,10,12,14},{1,3,5,7,9,11,13,15},{16,18,20,22,24,26,28,30},{17..., dimensions={0} | all-to-all | bytes 1048576 | tf_op jit(solution)/shard_map/first/all_to_all | solution.py:39
  120.6 14.0 %all_to_all.52.got = bf16[8,144,256]{2,1,0:T(8,128)(2,1)S(1)} all-to-all(bf16[8,144,256]{2,1,0:T(8,128)(2,1)S(1)} %get-tuple-element.41), channel_id=1, replica_groups={{0,2,4,6,8,10,12,14},{1,3,5,7,9,11,13,15},{16,18,20,22,24,26,28,30},{17..., dimensions={0} | all-to-all | bytes 1179648 | tf_op jit(solution)/shard_map/first/all_to_all | solution.py:39
  135.6 3.0 %collective-permute-start.19 = (bf16[688,128]{1,0:T(8,128)(2,1)S(1)}, bf16[688,128]{1,0:T(8,128)(2,1)S(1)}, u32[]{:S(2)}, u32[]{:S(2)}) collective-permute-start(bf16[688,128]{1,0:T(8,128)(2,1)S(1)} %get-tuple-element.43), channel_id=1, source_target_pairs={{0,1},{1,0},{2,3},{3,2},{4,5},{5,4},{6,7},{7,6},{8,9},{9,8},{10,11... | collective-permute-start | bytes 528392 | tf_op jit(solution)/shard_map/first/ppermute | solution.py:35
  140.6 13.4 %all_to_all.53.parts = bf16[8,128,256]{2,1,0:T(8,128)(2,1)S(1)} all-to-all(bf16[8,128,256]{2,1,0:T(8,128)(2,1)S(1)} %get-tuple-element.46), channel_id=1, replica_groups={{0,2,4,6,8,10,12,14},{1,3,5,7,9,11,13,15},{16,18,20,22,24,26,28,30},{17..., dimensions={0} | all-to-all | bytes 1048576 | tf_op jit(solution)/shard_map/second/all_to_all | solution.py:39
  154.2 13.0 %all_to_all.54.got = bf16[8,144,256]{2,1,0:T(8,128)(2,1)S(1)} all-to-all(bf16[8,144,256]{2,1,0:T(8,128)(2,1)S(1)} %get-tuple-element.49), channel_id=1, replica_groups={{0,2,4,6,8,10,12,14},{1,3,5,7,9,11,13,15},{16,18,20,22,24,26,28,30},{17..., dimensions={0} | all-to-all | bytes 1179648 | tf_op jit(solution)/shard_map/second/all_to_all | solution.py:39
  168.4 3.0 %collective-permute-start.21 = (bf16[688,128]{1,0:T(8,128)(2,1)S(1)}, bf16[688,128]{1,0:T(8,128)(2,1)S(1)}, u32[]{:S(2)}, u32[]{:S(2)}) collective-permute-start(bf16[688,128]{1,0:T(8,128)(2,1)S(1)} %get-tuple-element.52), channel_id=1, source_target_pairs={{0,1},{1,0},{2,3},{3,2},{4,5},{5,4},{6,7},{7,6},{8,9},{9,8},{10,11... | collective-permute-start | bytes 528392 | tf_op jit(solution)/shard_map/second/ppermute | solution.py:35
  173.6 13.4 %all_to_all.55.parts = bf16[8,128,256]{2,1,0:T(8,128)(2,1)S(1)} all-to-all(bf16[8,128,256]{2,1,0:T(8,128)(2,1)S(1)} %get-tuple-element.55), channel_id=1, replica_groups={{0,2,4,6,8,10,12,14},{1,3,5,7,9,11,13,15},{16,18,20,22,24,26,28,30},{17..., dimensions={0} | all-to-all | bytes 1048576 | tf_op jit(solution)/shard_map/third/all_to_all | solution.py:39
  187.2 11.1 %all_to_all.56.got = f32[16,1,128]{2,1,0:T(1,128)S(1)} all-to-all(f32[16,1,128]{2,1,0:T(1,128)S(1)} %third.3), channel_id=1, replica_groups=mesh['dp'=16,'shard'=16] {'shard'}, dimensions={0} | all-to-all | bytes 16384 | tf_op jit(solution)/shard_map/third/all_to_all | solution.py:463
  198.7 13.6 %all_to_all.57.got = f32[16,1,128]{2,1,0:T(1,128)S(1)} all-to-all(f32[16,1,128]{2,1,0:T(1,128)S(1)} %whole.2), channel_id=1, replica_groups=mesh['dp'=16,'shard'=16] {'dp'}, dimensions={0} | all-to-all | bytes 16384 | tf_op jit(solution)/shard_map/whole/all_to_all | solution.py:466
  212.3 1.4 whole.3
  (48 shorter events, 15.5 us)
Async XLA Ops:
  0.0 33.5 %copy-start = (bf16[128,2048]{1,0:T(8,128)(2,1)S(1)}, bf16[128,2048]{1,0:T(8,128)(2,1)}, u32[]{:S(2)}) copy-start(bf16[128,2048]{1,0:T(8,128)(2,1)} %param.13) | copy-start | bytes 1572868
  0.0 9.1 %copy-start.1 = (bf16[2048,344]{0,1:T(8,128)(2,1)S(1)}, bf16[2048,344]{0,1:T(8,128)(2,1)}, u32[]{:S(2)}) copy-start(bf16[2048,344]{0,1:T(8,128)(2,1)} %param.11) | copy-start | bytes 4227076
  5.7 5.3 %collective-permute-start = (bf16[192,2048]{1,0:T(8,128)(2,1)S(1)}, bf16[192,2048]{1,0:T(8,128)(2,1)S(1)}, u32[]{:S(2)}, u32[]{:S(2)}) collective-permute-start(bf16[192,2048]{1,0:T(8,128)(2,1)S(1)} %get-tuple-element.33), channel_id=1, source_target_pairs={{0,1},{1,0},{2,3},{3,2},{4,5},{5,4},{6,7},{7,6},{8,9},{9,8},{10,11... | collective-permute-start | bytes 2359304 | tf_op jit(solution)/shard_map/rows/ppermute | solution.py:35
  9.1 25.2 %collective-permute-start.1 = (bf16[344,2048]{1,0:T(8,128)(2,1)S(1)}, bf16[344,2048]{1,0:T(8,128)(2,1)}, u32[]{:S(2)}, u32[]{:S(2)}) collective-permute-start(bf16[344,2048]{1,0:T(8,128)(2,1)S(1)} %bitcast.18), channel_id=1, source_target_pairs={{0,1},{1,0},{2,3},{3,2},{4,5},{5,4},{6,7},{7,6},{8,9},{9,8},{10,11... | collective-permute-start | bytes 4227080 | tf_op jit(solution)/shard_map/ppermute | solution.py:35
  9.2 25.1 %collective-permute-start.2 = (bf16[344,2048]{1,0:T(8,128)(2,1)}, bf16[344,2048]{1,0:T(8,128)(2,1)}, u32[]{:S(2)}, u32[]{:S(2)}) collective-permute-start(bf16[344,2048]{1,0:T(8,128)(2,1)} %bitcast.10.w_up), channel_id=1, source_target_pairs={{0,1},{1,0},{2,3},{3,2},{4,5},{5,4},{6,7},{7,6},{8,9},{9,8},{10,11... | collective-permute-start | bytes 4227080 | tf_op jit(solution)/shard_map/ppermute | solution.py:35
  11.0 17.6 %copy-start.2 = (f32[2048]{0:T(1024)S(1)}, f32[2048]{0:T(1024)}, u32[]{:S(2)}) copy-start(f32[2048]{0:T(1024)} %param.10) | copy-start | bytes 24580
  29.6 15.9 %all-to-all-start.1 = ((bf16[8,24,2048]{2,1,0:T(8,128)(2,1)}), bf16[8,24,2048]{2,1,0:T(8,128)(2,1)S(1)}, u32[]{:S(2)}, u32[]{:S(2)}) async-start(bf16[8,24,2048]{2,1,0:T(8,128)(2,1)} %normed.1), calls=%async_computation.1 | async-start | bytes 1572864 | tf_op jit(solution)/shard_map/normed/all_to_all | solution.py:39
  49.4 9.0 %collective-permute-start.6 = (bf16[1040,128]{1,0:T(8,128)(2,1)S(1)}, bf16[1040,128]{1,0:T(8,128)(2,1)S(1)}, u32[]{:S(2)}, u32[]{:S(2)}) collective-permute-start(bf16[1040,128]{1,0:T(8,128)(2,1)S(1)} %acts.1.refs_0_), channel_id=1, source_target_pairs={{0,112},{16,0},{32,16},{48,32},{64,48},{80,64},{96,80},{112,96},{1... | collective-permute-start | bytes 798728 | tf_op jit(solution)/shard_map/groups/ppermute | solution.py:187
  55.1 6.9 %collective-permute-start.4 = (bf16[1040,128]{1,0:T(8,128)(2,1)S(1)}, bf16[1040,128]{1,0:T(8,128)(2,1)S(1)}, u32[]{:S(2)}, u32[]{:S(2)}) collective-permute-start(bf16[1040,128]{1,0:T(8,128)(2,1)S(1)} %acts.1.refs_0_), channel_id=1, source_target_pairs={{0,16},{16,32},{32,48},{48,64},{64,80},{80,96},{96,112},{112,0},{1... | collective-permute-start | bytes 798728 | tf_op jit(solution)/shard_map/groups/ppermute | solution.py:184
  58.5 6.5 %collective-permute-start.10 = (bf16[1040,128]{1,0:T(8,128)(2,1)S(1)}, bf16[1040,128]{1,0:T(8,128)(2,1)S(1)}, u32[]{:S(2)}, u32[]{:S(2)}) collective-permute-start(bf16[1040,128]{1,0:T(8,128)(2,1)S(1)} %collective-permute-done.6.refs_4_), channel_id=1, source_target_pairs={{0,112},{16,0},{32,16},{48,32},{64,48},{80,64},{96,80},{112,96},{1... | collective-permute-start | bytes 798728 | tf_op jit(solution)/shard_map/groups/ppermute | solution.py:187
  61.6 6.5 %collective-permute-start.3 = (bf16[1040,128]{1,0:T(8,128)(2,1)S(1)}, bf16[1040,128]{1,0:T(8,128)(2,1)S(1)}, u32[]{:S(2)}, u32[]{:S(2)}) collective-permute-start(bf16[1040,128]{1,0:T(8,128)(2,1)S(1)} %acts.1.refs_0_), channel_id=1, source_target_pairs={{0,128},{16,144},{32,160},{48,176},{64,192},{80,208},{96,224},{112... | collective-permute-start | bytes 798728 | tf_op jit(solution)/shard_map/groups/ppermute | solution.py:190
  62.0 6.5 %collective-permute-start.8 = (bf16[1040,128]{1,0:T(8,128)(2,1)S(1)}, bf16[1040,128]{1,0:T(8,128)(2,1)S(1)}, u32[]{:S(2)}, u32[]{:S(2)}) collective-permute-start(bf16[1040,128]{1,0:T(8,128)(2,1)S(1)} %collective-permute-done.4.refs_2_), channel_id=1, source_target_pairs={{0,16},{16,32},{32,48},{48,64},{64,80},{80,96},{96,112},{112,0},{1... | collective-permute-start | bytes 798728 | tf_op jit(solution)/shard_map/groups/ppermute | solution.py:184
  64.9 6.9 %collective-permute-start.14 = (bf16[1040,128]{1,0:T(8,128)(2,1)S(1)}, bf16[1040,128]{1,0:T(8,128)(2,1)S(1)}, u32[]{:S(2)}, u32[]{:S(2)}) collective-permute-start(bf16[1040,128]{1,0:T(8,128)(2,1)S(1)} %collective-permute-done.10.refs_8_), channel_id=1, source_target_pairs={{0,112},{16,0},{32,16},{48,32},{64,48},{80,64},{96,80},{112,96},{1... | collective-permute-start | bytes 798728 | tf_op jit(solution)/shard_map/groups/ppermute | solution.py:187
  68.1 10.9 %collective-permute-start.5 = (bf16[1040,128]{1,0:T(8,128)(2,1)S(1)}, bf16[1040,128]{1,0:T(8,128)(2,1)S(1)}, u32[]{:S(2)}, u32[]{:S(2)}) collective-permute-start(bf16[1040,128]{1,0:T(8,128)(2,1)S(1)} %collective-permute-done.3.refs_1_), channel_id=1, source_target_pairs={{0,16},{16,32},{32,48},{48,64},{64,80},{80,96},{96,112},{112,0},{1... | collective-permute-start | bytes 798728 | tf_op jit(solution)/shard_map/groups/ppermute | solution.py:184
  68.1 12.1 %collective-permute-start.7 = (bf16[1040,128]{1,0:T(8,128)(2,1)S(1)}, bf16[1040,128]{1,0:T(8,128)(2,1)S(1)}, u32[]{:S(2)}, u32[]{:S(2)}) collective-permute-start(bf16[1040,128]{1,0:T(8,128)(2,1)S(1)} %collective-permute-done.6.refs_4_), channel_id=1, source_target_pairs={{0,128},{16,144},{32,160},{48,176},{64,192},{80,208},{96,224},{112... | collective-permute-start | bytes 798728 | tf_op jit(solution)/shard_map/groups/ppermute | solution.py:190
  68.5 13.1 %collective-permute-start.12 = (bf16[1040,128]{1,0:T(8,128)(2,1)S(1)}, bf16[1040,128]{1,0:T(8,128)(2,1)S(1)}, u32[]{:S(2)}, u32[]{:S(2)}) collective-permute-start(bf16[1040,128]{1,0:T(8,128)(2,1)S(1)} %collective-permute-done.8.refs_6_), channel_id=1, source_target_pairs={{0,16},{16,32},{32,48},{48,64},{64,80},{80,96},{96,112},{112,0},{1... | collective-permute-start | bytes 798728 | tf_op jit(solution)/shard_map/groups/ppermute | solution.py:184
  71.9 10.1 %collective-permute-start.15 = (bf16[1040,128]{1,0:T(8,128)(2,1)S(1)}, bf16[1040,128]{1,0:T(8,128)(2,1)}, u32[]{:S(2)}, u32[]{:S(2)}) collective-permute-start(bf16[1040,128]{1,0:T(8,128)(2,1)S(1)} %collective-permute-done.14.refs_12_), channel_id=1, source_target_pairs={{0,128},{16,144},{32,160},{48,176},{64,192},{80,208},{96,224},{112... | collective-permute-start | bytes 798728 | tf_op jit(solution)/shard_map/groups/ppermute | solution.py:190
  72.3 13.8 %all-to-all-start.2 = ((bf16[16,64,128]{2,1,0:T(8,128)(2,1)}), bf16[16,64,128]{2,1,0:T(8,128)(2,1)S(1)}, u32[]{:S(2)}, u32[]{:S(2)}) async-start(bf16[16,64,128]{2,1,0:T(8,128)(2,1)} %bitcast_bitcast_fusion), calls=%async_computation.2 | async-start | bytes 524288 | tf_op jit(solution)/shard_map/groups/all_to_all | solution.py:407
  77.6 10.0 %collective-permute-start.11 = (bf16[1040,128]{1,0:T(8,128)(2,1)S(1)}, bf16[1040,128]{1,0:T(8,128)(2,1)}, u32[]{:S(2)}, u32[]{:S(2)}) collective-permute-start(bf16[1040,128]{1,0:T(8,128)(2,1)S(1)} %collective-permute-done.10.refs_8_), channel_id=1, source_target_pairs={{0,128},{16,144},{32,160},{48,176},{64,192},{80,208},{96,224},{112... | collective-permute-start | bytes 798728 | tf_op jit(solution)/shard_map/groups/ppermute | solution.py:190
  78.9 13.9 %collective-permute-start.9 = (bf16[1040,128]{1,0:T(8,128)(2,1)S(1)}, bf16[1040,128]{1,0:T(8,128)(2,1)}, u32[]{:S(2)}, u32[]{:S(2)}) collective-permute-start(bf16[1040,128]{1,0:T(8,128)(2,1)S(1)} %collective-permute-done.5.refs_3_), channel_id=1, source_target_pairs={{0,16},{16,32},{32,48},{48,64},{64,80},{80,96},{96,112},{112,0},{1... | collective-permute-start | bytes 798728 | tf_op jit(solution)/shard_map/groups/ppermute | solution.py:184
  80.1 12.8 %collective-permute-start.16 = (bf16[1040,128]{1,0:T(8,128)(2,1)S(1)}, bf16[1040,128]{1,0:T(8,128)(2,1)}, u32[]{:S(2)}, u32[]{:S(2)}) collective-permute-start(bf16[1040,128]{1,0:T(8,128)(2,1)S(1)} %collective-permute-done.14.refs_12_), channel_id=1, source_target_pairs={{0,112},{16,0},{32,16},{48,32},{64,48},{80,64},{96,80},{112,96},{1... | collective-permute-start | bytes 798728 | tf_op jit(solution)/shard_map/groups/ppermute | solution.py:187
  81.6 12.9 %collective-permute-start.13 = (bf16[1040,128]{1,0:T(8,128)(2,1)S(1)}, bf16[1040,128]{1,0:T(8,128)(2,1)}, u32[]{:S(2)}, u32[]{:S(2)}) collective-permute-start(bf16[1040,128]{1,0:T(8,128)(2,1)S(1)} %collective-permute-done.12.refs_10_), channel_id=1, source_target_pairs={{0,128},{16,144},{32,160},{48,176},{64,192},{80,208},{96,224},{112... | collective-permute-start | bytes 798728 | tf_op jit(solution)/shard_map/groups/ppermute | solution.py:190
  82.0 12.5 %collective-permute-start.17 = (bf16[1040,128]{1,0:T(8,128)(2,1)}, bf16[1040,128]{1,0:T(8,128)(2,1)}, u32[]{:S(2)}, u32[]{:S(2)}) collective-permute-start(bf16[1040,128]{1,0:T(8,128)(2,1)} %collective-permute-done.15.refs_13_), channel_id=1, source_target_pairs={{0,112},{16,0},{32,16},{48,32},{64,48},{80,64},{96,80},{112,96},{1... | collective-permute-start | bytes 798728 | tf_op jit(solution)/shard_map/groups/ppermute | solution.py:187
  97.2 5.2 %collective-permute-start.18 = (bf16[688,128]{1,0:T(8,128)(2,1)S(1)}, bf16[688,128]{1,0:T(8,128)(2,1)S(1)}, u32[]{:S(2)}, u32[]{:S(2)}) collective-permute-start(bf16[688,128]{1,0:T(8,128)(2,1)S(1)} %get-tuple-element.38), channel_id=1, source_target_pairs={{0,1},{1,0},{2,3},{3,2},{4,5},{5,4},{6,7},{7,6},{8,9},{9,8},{10,11... | collective-permute-start | bytes 528392 | tf_op jit(solution)/shard_map/rhs/ppermute | solution.py:35
  135.6 4.1 %collective-permute-start.19 = (bf16[688,128]{1,0:T(8,128)(2,1)S(1)}, bf16[688,128]{1,0:T(8,128)(2,1)S(1)}, u32[]{:S(2)}, u32[]{:S(2)}) collective-permute-start(bf16[688,128]{1,0:T(8,128)(2,1)S(1)} %get-tuple-element.43), channel_id=1, source_target_pairs={{0,1},{1,0},{2,3},{3,2},{4,5},{5,4},{6,7},{7,6},{8,9},{9,8},{10,11... | collective-permute-start | bytes 528392 | tf_op jit(solution)/shard_map/first/ppermute | solution.py:35
  138.5 1.2 collective-permute-start.20
  168.4 4.1 %collective-permute-start.21 = (bf16[688,128]{1,0:T(8,128)(2,1)S(1)}, bf16[688,128]{1,0:T(8,128)(2,1)S(1)}, u32[]{:S(2)}, u32[]{:S(2)}) collective-permute-start(bf16[688,128]{1,0:T(8,128)(2,1)S(1)} %get-tuple-element.52), channel_id=1, source_target_pairs={{0,1},{1,0},{2,3},{3,2},{4,5},{5,4},{6,7},{7,6},{8,9},{9,8},{10,11... | collective-permute-start | bytes 528392 | tf_op jit(solution)/shard_map/second/ppermute | solution.py:35
  171.4 1.2 collective-permute-start.22

commit v8 on v6

--- a/solution.py
+++ b/solution.py
@@ -179,7 +179,24 @@
     out[...] = jnp.concatenate([own[:, :128], other[:, :128], asked, fill], axis=0).astype(bf16)
 
 
-def gather_groups(own, columns):
+def deal_kernel(place, cotangent, *outs):
+    y = lax.shift_right_logical(place[0], 3)
+    z = lax.bitwise_and(place[0], 7)
+    rows = pl.ds(pl.multiple_of(place[1] * 64, 64), 64)
+    for step, out in zip(STEPS, outs):
+        there = lax.bitwise_and(z - step, 7)
+        for side in range(2):
+            group = (1 - y if side else y) * 8 + there
+            columns = pl.ds(pl.multiple_of(group * 128, 128), 128)
+            out[side * 64 : (side + 1) * 64, :] = cotangent[rows, columns]
+
+
+def pass_kernel(*refs):
+    for i in range(8):
+        refs[8][i * 64 : (i + 1) * 64, :] = refs[i][64:, :]
+
+
+def gather_groups(own):
     def up(v):
         return lax.ppermute(v, "dp", z_shift(1))
 
@@ -198,19 +215,17 @@
     twin[2], twin[-1], same[-3], same[3] = across(same[2]), up(twin[0]), up(same[-2]), down(same[2])
     twin[3], twin[-2], same[4] = across(same[3]), up(twin[-1]), down(same[3])
     twin[-3], twin[4] = across(same[-3]), down(twin[3])
-    return [group[step] for step in STEPS for group in (same, twin)], columns
+    return [group[step] for step in STEPS for group in (same, twin)]
 
 
 def rhs_kernel(scale, *refs):
-    blocks, (me, columns, part, flip, acts) = refs[:16], refs[16:]
-    y = lax.shift_right_logical(me[0], 3)
-    z = lax.bitwise_and(me[0], 7)
+    blocks, columns, (part, flip, acts) = refs[:16], refs[16:25], refs[25:]
     empty = jnp.zeros((64, 128), bf16)
     out = jnp.zeros((PACK - BOTH, 256), f32)
-    for i, step in enumerate(STEPS):
+    for i in range(8):
         pieces = []
-        for side in (y, 1 - y):
-            seen = columns[side * 8 + lax.bitwise_and(z + step, 7)]
+        for side in range(2):
+            seen = columns[8][i * 64 : (i + 1) * 64, :] if side else columns[i][:64, :]
             pieces.append(jnp.concatenate([seen, empty], axis=1))
             pieces.append(jnp.concatenate([empty, seen], axis=1))
         pair = blocks[2 * i], blocks[2 * i + 1]
@@ -392,23 +407,36 @@
         rows = local_call(
             add_kernel, pltpu.VMEM((8, 24, wide), bf16), mine.reshape(8, 24, wide), other
         )
+        dealt = local_call(
+            deal_kernel,
+            (shape((128, 128), bf16),) * 8,
+            jnp.stack([lax.axis_index("dp"), core]),
+            cotangent,
+            specs=[SMEM, VMEM],
+        )
+        rows, *dealt = lax.optimization_barrier((rows, *dealt))
         rows = exchange_chips(rows)
+        columns = [dealt[0]] + [
+            lax.ppermute(v, "dp", z_shift(-step)) for step, v in zip(STEPS[1:5], dealt[1:5])
+        ]
+        rows, *columns = lax.optimization_barrier((rows, *columns))
     with jax.named_scope("normed"):
         normed = local_call(
             norm_kernel, pltpu.VMEM((8, 24, wide), bf16), rows, norm_gain.reshape(1, wide)
         )
     with jax.named_scope("normed"):
+        normed, *dealt = lax.optimization_barrier((normed, *dealt[5:]))
         normed = exchange_chips(normed).reshape(192, wide)
+        columns += [lax.ppermute(v, "dp", z_shift(-step)) for step, v in zip(STEPS[5:], dealt)]
+        normed, *columns = lax.optimization_barrier((normed, *columns))
+        passed = local_call(pass_kernel, shape((512, 128), bf16), *columns)
+        columns.append(lax.ppermute(passed, "dp", YLO))
     with jax.named_scope("acts"):
         package = local_call(
             acts_kernel, shape((PACK, 128), bf16), normed, w_gate, w_up, w_gate_other, w_up_other
         )
     with jax.named_scope("groups"):
-        columns = lax.dynamic_slice_in_dim(cotangent, core * 64, 64, axis=0)
-        columns = columns.reshape(64, 16, 128).transpose(1, 0, 2)
-        columns, package = lax.optimization_barrier((columns, package))
-        columns = lax.all_to_all(columns, "dp", 0, 0, tiled=True)
-        blocks, columns = gather_groups(package, columns)
+        blocks = gather_groups(package)
     vector = shape((BOTH, 128), f32)
     longer = shape((BOTH + 8, 128), f32)
     small = shape((8, 128), f32)
@@ -422,9 +450,7 @@
             functools.partial(rhs_kernel, 1.0 / math.sqrt(2048)),
             (vector, vector, pltpu.VMEM((BOTH, TOKENS // 2), bf16)),
             *blocks,
-            lax.axis_index("dp").reshape(1),
-            columns,
-            specs=[VMEM] * 16 + [SMEM, VMEM],
+            *columns,
         )
         got = swap_core(flip)
     with jax.named_scope("first"):

time: 215 us -> 219 us (1.019)
  starting transfers between devices: 41.3 us -> 68.7 us
  blocking collectives: 113 us -> 94.6 us
  waiting for transfers between devices: 37.6 us -> 33.5 us
    ppermute x0 -> x8, starting transfers between devices: none -> 19.4 us  [the longest x7 18.2 us: body(): lax.ppermute(v, 'dp', z_shift(-step))]
    all_to_all x6 -> x5, blocking collectives: 88.1 us -> 70.3 us  [exchange_chips(): return lax.all_to_all(v, 'shard', 0, 0, axis_index_groups=CHIPS, tiled=True)]
    ppermute x0 -> x8, waiting for transfers between devices: none -> 13.3 us  [the longest x1 7.22 us: body(): columns.append(lax.ppermute(passed, 'dp', YLO))]
    all_to_all x1 -> x2, waiting for transfers between devices: 11.2 us -> 1.28 us  [exchange_chips(): return lax.all_to_all(v, 'shard', 0, 0, axis_index_groups=CHIPS, tiled=True)]
    all_to_all x1 -> x2, starting transfers between devices: 3.86 us -> 10 us  [exchange_chips(): return lax.all_to_all(v, 'shard', 0, 0, axis_index_groups=CHIPS, tiled=True)]
    ppermute x6, starting transfers between devices: 13.6 us -> 19.7 us  [swap_core(): return lax.ppermute(v, 'shard', CORE)]
    all_to_all x1 -> x0, starting transfers between devices: 5.3 us -> none  [body(): columns = lax.all_to_all(columns, 'dp', 0, 0, tiled=True)]
    ppermute x5, waiting for transfers between devices: 5.33 us -> 0.86 us  [up(): return lax.ppermute(v, 'dp', z_shift(1))]
  transfers between devices with their start and end apart: 23 -> 31, of which waited for: 12 -> 17; matrix products, arithmetic and copies ran while one was open for 0% -> 0% of each run, Pallas kernels for 1% -> 1%
where the time goes in v8:
time: 219 us
  blocking collectives  94.6 us (43%)
  starting transfers between devices  68.7 us (31%)
  waiting for transfers between devices  33.5 us (15%)
  Pallas kernels  21.4 us (10%)
    all_to_all x5, blocking collectives, exchange_chips(): return lax.all_to_all(v, 'shard', 0, 0, axis_index_groups=CHIPS, tiled=True)  70.3 us
    pallas_call x17, Pallas kernels, local_call(): pl.pallas_call(kernel, out_shape=outs, in_specs=specs or [VMEM] * len(arg...  21.4 us
    ppermute x6, starting transfers between devices, swap_core(): return lax.ppermute(v, 'shard', CORE)  19.7 us
    ppermute x7, starting transfers between devices, body(): lax.ppermute(v, 'dp', z_shift(-step))  18.2 us
    ppermute x5, starting transfers between devices, down(): return lax.ppermute(v, 'dp', z_shift(-1))  17 us
    all_to_all x1, blocking collectives, body(): every = lax.all_to_all(mine, 'dp', 0, 0, tiled=True)  12.6 us
    all_to_all x1, blocking collectives, body(): partials = lax.all_to_all(partials, 'shard', 0, 0, tiled=True)  11.8 us
    ppermute x5, waiting for transfers between devices, down(): return lax.ppermute(v, 'dp', z_shift(-1))  10.9 us
  transfers between devices with their start and end apart: 31, of which 17 were waited for; matrix products, arithmetic and copies ran while one was open for 0% of the time, Pallas kernels for 1%

profile of v8, /device:TPU:1, one launch (start us, length us, event | category | flops | bytes accessed | tf_op | source)
XLA Modules:
  0.0 218.6 jit_solution(7171236894878183843)
XLA Ops:
  0.0 6.6 %rows.3 = (bf16[192,2048]{1,0:T(8,128)(2,1)S(1)}, bf16[192,2048]{1,0:T(8,128)(2,1)}) custom-call(s32[1]{0:T(128)} %bitcast.1.place, s32[2,128]{1,0:T(2,128)} %bitcast.17, s32[1,128]{1,0:T(1,128)} %bitcast.18, bf16[2000,2048]{1,0:T(8,128)(2,1)} %table_hbm.1), custom_call_target="tpu_custom_call" | custom-call | tf_op jit(solution)/shard_map/rows/pallas_call | solution.py:43
  6.6 3.3 %collective-permute-start = (bf16[192,2048]{1,0:T(8,128)(2,1)}, bf16[192,2048]{1,0:T(8,128)(2,1)S(1)}, u32[]{:S(2)}, u32[]{:S(2)}) collective-permute-start(bf16[192,2048]{1,0:T(8,128)(2,1)} %get-tuple-element.67), channel_id=1, source_target_pairs={{0,1},{1,0},{2,3},{3,2},{4,5},{5,4},{6,7},{7,6},{8,9},{9,8},{10,11... | collective-permute-start | bytes 2359304 | tf_op jit(solution)/shard_map/rows/ppermute | solution.py:35
  13.1 4.9 %all-to-all-start = ((bf16[8,24,2048]{2,1,0:T(8,128)(2,1)}), bf16[8,24,2048]{2,1,0:T(8,128)(2,1)S(1)}, u32[]{:S(2)}, u32[]{:S(2)}) async-start(bf16[8,24,2048]{2,1,0:T(8,128)(2,1)} %rows.4), calls=%async_computation | async-start | bytes 1572864 | tf_op jit(solution)/shard_map/rows/all_to_all | solution.py:39
  18.1 1.7 collective-permute-start.1
  19.8 4.0 %collective-permute-start.2 = (bf16[128,128]{1,0:T(8,128)(2,1)S(1)}, bf16[128,128]{1,0:T(8,128)(2,1)S(1)}, u32[]{:S(2)}, u32[]{:S(2)}) collective-permute-start(bf16[128,128]{1,0:T(8,128)(2,1)S(1)} %copy-done.14), channel_id=1, source_target_pairs={{0,112},{16,0},{32,16},{48,32},{64,48},{80,64},{96,80},{112,96},{1... | collective-permute-start | bytes 98312 | tf_op jit(solution)/shard_map/rows/ppermute | solution.py:420
  25.0 2.4 %collective-permute-start.4 = (bf16[128,128]{1,0:T(8,128)(2,1)S(1)}, bf16[128,128]{1,0:T(8,128)(2,1)S(1)}, u32[]{:S(2)}, u32[]{:S(2)}) collective-permute-start(bf16[128,128]{1,0:T(8,128)(2,1)S(1)} %copy-done.10), channel_id=1, source_target_pairs={{0,96},{16,112},{32,0},{48,16},{64,32},{80,48},{96,64},{112,80},{1... | collective-permute-start | bytes 98312 | tf_op jit(solution)/shard_map/rows/ppermute | solution.py:420
  27.4 1.8 collective-permute-done.3.refs_3_.refs_19_
  32.1 5.1 %all-to-all-start.1 = ((bf16[8,24,2048]{2,1,0:T(8,128)(2,1)}), bf16[8,24,2048]{2,1,0:T(8,128)(2,1)S(1)}, u32[]{:S(2)}, u32[]{:S(2)}) async-start(bf16[8,24,2048]{2,1,0:T(8,128)(2,1)} %normed.2), calls=%async_computation.1 | async-start | bytes 1572864 | tf_op jit(solution)/shard_map/normed/all_to_all | solution.py:39
  37.2 3.1 %collective-permute-start.5 = (bf16[128,128]{1,0:T(8,128)(2,1)S(1)}, bf16[128,128]{1,0:T(8,128)(2,1)S(1)}, u32[]{:S(2)}, u32[]{:S(2)}) collective-permute-start(bf16[128,128]{1,0:T(8,128)(2,1)S(1)} %copy-done.8), channel_id=1, source_target_pairs={{0,48},{16,64},{32,80},{48,96},{64,112},{80,0},{96,16},{112,32},{1... | collective-permute-start | bytes 98312 | tf_op jit(solution)/shard_map/normed/ppermute | solution.py:430
  40.3 2.2 %collective-permute-start.6 = (bf16[128,128]{1,0:T(8,128)(2,1)S(1)}, bf16[128,128]{1,0:T(8,128)(2,1)S(1)}, u32[]{:S(2)}, u32[]{:S(2)}) collective-permute-start(bf16[128,128]{1,0:T(8,128)(2,1)S(1)} %copy-done.6), channel_id=1, source_target_pairs={{0,80},{16,96},{32,112},{48,0},{64,16},{80,32},{96,48},{112,64},{1... | collective-permute-start | bytes 98312 | tf_op jit(solution)/shard_map/normed/ppermute | solution.py:430
  42.5 4.8 %collective-permute-start.7 = (bf16[128,128]{1,0:T(8,128)(2,1)S(1)}, bf16[128,128]{1,0:T(8,128)(2,1)S(1)}, u32[]{:S(2)}, u32[]{:S(2)}) collective-permute-start(bf16[128,128]{1,0:T(8,128)(2,1)S(1)} %copy-done.4), channel_id=1, source_target_pairs={{0,64},{16,80},{32,96},{48,112},{64,0},{80,16},{96,32},{112,48},{1... | collective-permute-start | bytes 98312 | tf_op jit(solution)/shard_map/normed/ppermute | solution.py:430
  47.3 2.5 %collective-permute-done.7.refs_7_.refs_23_ = bf16[128,128]{1,0:T(8,128)(2,1)S(1)} collective-permute-done((bf16[128,128]{1,0:T(8,128)(2,1)S(1)}, bf16[128,128]{1,0:T(8,128)(2,1)S(1)}, u32[]{:S(2)}, u32[]{:S(2)}) %collective-permute-start.7) | collective-permute-done | bytes 32800 | tf_op jit(solution)/shard_map/normed/ppermute | solution.py:430
  49.9 4.0 %acts.1.refs_0_ = bf16[1040,128]{1,0:T(8,128)(2,1)S(1)} custom-call(bf16[192,2048]{1,0:T(8,128)(2,1)S(1)} %bitcast.11, bf16[344,2048]{1,0:T(8,128)(2,1)S(1)} %bitcast.13, bf16[344,2048]{1,0:T(8,128)(2,1)} %bitcast.10.w_up, bf16[344,2048]{1,0:T(8,128)(2,1)} %collective-permute-done.8.w_gate_other, bf16[344,2048]{1,0:T(8,128)(2,1)} %collective-permute-done.9.w_up_other), custom_call_target="tpu_custom_call" | custom-call | tf_op jit(solution)/shard_map/acts/pallas_call | solution.py:43
  53.8 4.5 %collective-permute-start.13 = (bf16[1040,128]{1,0:T(8,128)(2,1)S(1)}, bf16[1040,128]{1,0:T(8,128)(2,1)S(1)}, u32[]{:S(2)}, u32[]{:S(2)}) collective-permute-start(bf16[1040,128]{1,0:T(8,128)(2,1)S(1)} %acts.1.refs_0_), channel_id=1, source_target_pairs={{0,112},{16,0},{32,16},{48,32},{64,48},{80,64},{96,80},{112,96},{1... | collective-permute-start | bytes 798728 | tf_op jit(solution)/shard_map/groups/ppermute | solution.py:204
  58.3 4.0 %collective-permute-done.13.refs_4_ = bf16[1040,128]{1,0:T(8,128)(2,1)S(1)} collective-permute-done((bf16[1040,128]{1,0:T(8,128)(2,1)S(1)}, bf16[1040,128]{1,0:T(8,128)(2,1)S(1)}, u32[]{:S(2)}, u32[]{:S(2)}) %collective-permute-start.13) | collective-permute-done | bytes 266272 | tf_op jit(solution)/shard_map/groups/ppermute | solution.py:204
  62.3 3.4 %collective-permute-start.17 = (bf16[1040,128]{1,0:T(8,128)(2,1)S(1)}, bf16[1040,128]{1,0:T(8,128)(2,1)S(1)}, u32[]{:S(2)}, u32[]{:S(2)}) collective-permute-start(bf16[1040,128]{1,0:T(8,128)(2,1)S(1)} %collective-permute-done.13.refs_4_), channel_id=1, source_target_pairs={{0,112},{16,0},{32,16},{48,32},{64,48},{80,64},{96,80},{112,96},{1... | collective-permute-start | bytes 798728 | tf_op jit(solution)/shard_map/groups/ppermute | solution.py:204
  66.1 3.0 %collective-permute-done.17.refs_8_ = bf16[1040,128]{1,0:T(8,128)(2,1)S(1)} collective-permute-done((bf16[1040,128]{1,0:T(8,128)(2,1)S(1)}, bf16[1040,128]{1,0:T(8,128)(2,1)S(1)}, u32[]{:S(2)}, u32[]{:S(2)}) %collective-permute-start.17) | collective-permute-done | bytes 266272 | tf_op jit(solution)/shard_map/groups/ppermute | solution.py:204
  69.1 3.1 %collective-permute-start.21 = (bf16[1040,128]{1,0:T(8,128)(2,1)S(1)}, bf16[1040,128]{1,0:T(8,128)(2,1)S(1)}, u32[]{:S(2)}, u32[]{:S(2)}) collective-permute-start(bf16[1040,128]{1,0:T(8,128)(2,1)S(1)} %collective-permute-done.17.refs_8_), channel_id=1, source_target_pairs={{0,112},{16,0},{32,16},{48,32},{64,48},{80,64},{96,80},{112,96},{1... | collective-permute-start | bytes 798728 | tf_op jit(solution)/shard_map/groups/ppermute | solution.py:204
  72.6 3.0 %collective-permute-done.21.refs_12_ = bf16[1040,128]{1,0:T(8,128)(2,1)S(1)} collective-permute-done((bf16[1040,128]{1,0:T(8,128)(2,1)S(1)}, bf16[1040,128]{1,0:T(8,128)(2,1)S(1)}, u32[]{:S(2)}, u32[]{:S(2)}) %collective-permute-start.21) | collective-permute-done | bytes 266272 | tf_op jit(solution)/shard_map/groups/ppermute | solution.py:204
  77.1 7.2 %collective-permute-done.25.refs_24_ = bf16[512,128]{1,0:T(8,128)(2,1)S(1)} collective-permute-done((bf16[512,128]{1,0:T(8,128)(2,1)S(1)}, bf16[512,128]{1,0:T(8,128)(2,1)S(1)}, u32[]{:S(2)}, u32[]{:S(2)}) %collective-permute-start.25) | collective-permute-done | bytes 131104 | tf_op jit(solution)/shard_map/normed/ppermute | solution.py:433
  84.7 4.6 %collective-permute-start.23 = (bf16[1040,128]{1,0:T(8,128)(2,1)S(1)}, bf16[1040,128]{1,0:T(8,128)(2,1)S(1)}, u32[]{:S(2)}, u32[]{:S(2)}) collective-permute-start(bf16[1040,128]{1,0:T(8,128)(2,1)S(1)} %collective-permute-done.21.refs_12_), channel_id=1, source_target_pairs={{0,112},{16,0},{32,16},{48,32},{64,48},{80,64},{96,80},{112,96},{1... | collective-permute-start | bytes 798728 | tf_op jit(solution)/shard_map/groups/ppermute | solution.py:204
  93.0 2.0 collective-permute-done.20.refs_11_
  97.1 9.8 %collective-permute-start.26 = (f32[688,128]{1,0:T(8,128)S(1)}, f32[688,128]{1,0:T(8,128)S(1)}, u32[]{:S(2)}, u32[]{:S(2)}) collective-permute-start(f32[688,128]{1,0:T(8,128)S(1)} %get-tuple-element.106), channel_id=1, source_target_pairs={{0,1},{1,0},{2,3},{3,2},{4,5},{5,4},{6,7},{7,6},{8,9},{9,8},{10,11... | collective-permute-start | bytes 1056776 | tf_op jit(solution)/shard_map/rhs/ppermute | solution.py:35
  108.8 17.3 %all_to_all.45.parts = bf16[8,128,256]{2,1,0:T(8,128)(2,1)S(1)} all-to-all(bf16[8,128,256]{2,1,0:T(8,128)(2,1)S(1)} %get-tuple-element.107), channel_id=1, replica_groups={{0,2,4,6,8,10,12,14},{1,3,5,7,9,11,13,15},{16,18,20,22,24,26,28,30},{17..., dimensions={0} | all-to-all | bytes 1048576 | tf_op jit(solution)/shard_map/first/all_to_all | solution.py:39
  126.4 14.0 %all_to_all.46.got = bf16[8,144,256]{2,1,0:T(8,128)(2,1)S(1)} all-to-all(bf16[8,144,256]{2,1,0:T(8,128)(2,1)S(1)} %get-tuple-element.109), channel_id=1, replica_groups={{0,2,4,6,8,10,12,14},{1,3,5,7,9,11,13,15},{16,18,20,22,24,26,28,30},{17..., dimensions={0} | all-to-all | bytes 1179648 | tf_op jit(solution)/shard_map/first/all_to_all | solution.py:39
  141.3 3.0 %collective-permute-start.27 = (f32[696,128]{1,0:T(8,128)S(1)}, f32[696,128]{1,0:T(8,128)S(1)}, u32[]{:S(2)}, u32[]{:S(2)}) collective-permute-start(f32[696,128]{1,0:T(8,128)S(1)} %get-tuple-element.111), channel_id=1, source_target_pairs={{0,1},{1,0},{2,3},{3,2},{4,5},{5,4},{6,7},{7,6},{8,9},{9,8},{10,11... | collective-permute-start | bytes 1069064 | tf_op jit(solution)/shard_map/first/ppermute | solution.py:35
  146.4 12.7 %all_to_all.47.parts = bf16[8,128,256]{2,1,0:T(8,128)(2,1)S(1)} all-to-all(bf16[8,128,256]{2,1,0:T(8,128)(2,1)S(1)} %get-tuple-element.114), channel_id=1, replica_groups={{0,2,4,6,8,10,12,14},{1,3,5,7,9,11,13,15},{16,18,20,22,24,26,28,30},{17..., dimensions={0} | all-to-all | bytes 1048576 | tf_op jit(solution)/shard_map/second/all_to_all | solution.py:39
  159.4 13.5 %all_to_all.48.got = bf16[8,144,256]{2,1,0:T(8,128)(2,1)S(1)} all-to-all(bf16[8,144,256]{2,1,0:T(8,128)(2,1)S(1)} %get-tuple-element.117), channel_id=1, replica_groups={{0,2,4,6,8,10,12,14},{1,3,5,7,9,11,13,15},{16,18,20,22,24,26,28,30},{17..., dimensions={0} | all-to-all | bytes 1179648 | tf_op jit(solution)/shard_map/second/all_to_all | solution.py:39
  174.1 3.1 %collective-permute-start.28 = (f32[696,128]{1,0:T(8,128)S(1)}, f32[696,128]{1,0:T(8,128)S(1)}, u32[]{:S(2)}, u32[]{:S(2)}) collective-permute-start(f32[696,128]{1,0:T(8,128)S(1)} %get-tuple-element.120), channel_id=1, source_target_pairs={{0,1},{1,0},{2,3},{3,2},{4,5},{5,4},{6,7},{7,6},{8,9},{9,8},{10,11... | collective-permute-start | bytes 1069064 | tf_op jit(solution)/shard_map/second/ppermute | solution.py:35
  179.5 12.7 %all_to_all.49.parts = bf16[8,128,256]{2,1,0:T(8,128)(2,1)S(1)} all-to-all(bf16[8,128,256]{2,1,0:T(8,128)(2,1)S(1)} %get-tuple-element.123), channel_id=1, replica_groups={{0,2,4,6,8,10,12,14},{1,3,5,7,9,11,13,15},{16,18,20,22,24,26,28,30},{17..., dimensions={0} | all-to-all | bytes 1048576 | tf_op jit(solution)/shard_map/third/all_to_all | solution.py:39
  192.5 11.8 %all_to_all.50.got = f32[16,1,128]{2,1,0:T(1,128)S(1)} all-to-all(f32[16,1,128]{2,1,0:T(1,128)S(1)} %third.3), channel_id=1, replica_groups=mesh['dp'=16,'shard'=16] {'shard'}, dimensions={0} | all-to-all | bytes 16384 | tf_op jit(solution)/shard_map/third/all_to_all | solution.py:491
  204.6 12.6 %all_to_all.51.got = f32[16,1,128]{2,1,0:T(1,128)S(1)} all-to-all(f32[16,1,128]{2,1,0:T(1,128)S(1)} %whole.2), channel_id=1, replica_groups=mesh['dp'=16,'shard'=16] {'dp'}, dimensions={0} | all-to-all | bytes 16384 | tf_op jit(solution)/shard_map/whole/all_to_all | solution.py:494
  (89 shorter events, 26.6 us)
Async XLA Ops:
  6.6 5.5 %collective-permute-start = (bf16[192,2048]{1,0:T(8,128)(2,1)}, bf16[192,2048]{1,0:T(8,128)(2,1)S(1)}, u32[]{:S(2)}, u32[]{:S(2)}) collective-permute-start(bf16[192,2048]{1,0:T(8,128)(2,1)} %get-tuple-element.67), channel_id=1, source_target_pairs={{0,1},{1,0},{2,3},{3,2},{4,5},{5,4},{6,7},{7,6},{8,9},{9,8},{10,11... | collective-permute-start | bytes 2359304 | tf_op jit(solution)/shard_map/rows/ppermute | solution.py:35
  9.9 39.9 %collective-permute-start.8 = (bf16[344,2048]{1,0:T(8,128)(2,1)S(1)}, bf16[344,2048]{1,0:T(8,128)(2,1)}, u32[]{:S(2)}, u32[]{:S(2)}) collective-permute-start(bf16[344,2048]{1,0:T(8,128)(2,1)S(1)} %bitcast.12), channel_id=1, source_target_pairs={{0,1},{1,0},{2,3},{3,2},{4,5},{5,4},{6,7},{7,6},{8,9},{9,8},{10,11... | collective-permute-start | bytes 4227080 | tf_op jit(solution)/shard_map/ppermute | solution.py:35
  10.1 39.8 %collective-permute-start.9 = (bf16[344,2048]{1,0:T(8,128)(2,1)}, bf16[344,2048]{1,0:T(8,128)(2,1)}, u32[]{:S(2)}, u32[]{:S(2)}) collective-permute-start(bf16[344,2048]{1,0:T(8,128)(2,1)} %bitcast.10.w_up), channel_id=1, source_target_pairs={{0,1},{1,0},{2,3},{3,2},{4,5},{5,4},{6,7},{7,6},{8,9},{9,8},{10,11... | collective-permute-start | bytes 4227080 | tf_op jit(solution)/shard_map/ppermute | solution.py:35
  12.1 18.9 %copy-start.2 = (f32[2048]{0:T(1024)S(1)}, f32[2048]{0:T(1024)}, u32[]{:S(2)}) copy-start(f32[2048]{0:T(1024)} %param.10) | copy-start | bytes 24580
  13.1 17.9 %all-to-all-start = ((bf16[8,24,2048]{2,1,0:T(8,128)(2,1)}), bf16[8,24,2048]{2,1,0:T(8,128)(2,1)S(1)}, u32[]{:S(2)}, u32[]{:S(2)}) async-start(bf16[8,24,2048]{2,1,0:T(8,128)(2,1)} %rows.4), calls=%async_computation | async-start | bytes 1572864 | tf_op jit(solution)/shard_map/rows/all_to_all | solution.py:39
  18.1 7.0 %collective-permute-start.1 = (bf16[128,128]{1,0:T(8,128)(2,1)S(1)}, bf16[128,128]{1,0:T(8,128)(2,1)S(1)}, u32[]{:S(2)}, u32[]{:S(2)}) collective-permute-start(bf16[128,128]{1,0:T(8,128)(2,1)S(1)} %copy-done.16), channel_id=1, source_target_pairs={{0,16},{16,32},{32,48},{48,64},{64,80},{80,96},{96,112},{112,0},{1... | collective-permute-start | bytes 98312 | tf_op jit(solution)/shard_map/rows/ppermute | solution.py:420
  19.8 7.6 %collective-permute-start.2 = (bf16[128,128]{1,0:T(8,128)(2,1)S(1)}, bf16[128,128]{1,0:T(8,128)(2,1)S(1)}, u32[]{:S(2)}, u32[]{:S(2)}) collective-permute-start(bf16[128,128]{1,0:T(8,128)(2,1)S(1)} %copy-done.14), channel_id=1, source_target_pairs={{0,112},{16,0},{32,16},{48,32},{64,48},{80,64},{96,80},{112,96},{1... | collective-permute-start | bytes 98312 | tf_op jit(solution)/shard_map/rows/ppermute | solution.py:420
  23.8 5.4 %collective-permute-start.3 = (bf16[128,128]{1,0:T(8,128)(2,1)S(1)}, bf16[128,128]{1,0:T(8,128)(2,1)S(1)}, u32[]{:S(2)}, u32[]{:S(2)}) collective-permute-start(bf16[128,128]{1,0:T(8,128)(2,1)S(1)} %copy-done.12), channel_id=1, source_target_pairs={{0,32},{16,48},{32,64},{48,80},{64,96},{80,112},{96,0},{112,16},{1... | collective-permute-start | bytes 98312 | tf_op jit(solution)/shard_map/rows/ppermute | solution.py:420
  25.0 4.7 %collective-permute-start.4 = (bf16[128,128]{1,0:T(8,128)(2,1)S(1)}, bf16[128,128]{1,0:T(8,128)(2,1)S(1)}, u32[]{:S(2)}, u32[]{:S(2)}) collective-permute-start(bf16[128,128]{1,0:T(8,128)(2,1)S(1)} %copy-done.10), channel_id=1, source_target_pairs={{0,96},{16,112},{32,0},{48,16},{64,32},{80,48},{96,64},{112,80},{1... | collective-permute-start | bytes 98312 | tf_op jit(solution)/shard_map/rows/ppermute | solution.py:420
  32.1 17.8 %all-to-all-start.1 = ((bf16[8,24,2048]{2,1,0:T(8,128)(2,1)}), bf16[8,24,2048]{2,1,0:T(8,128)(2,1)S(1)}, u32[]{:S(2)}, u32[]{:S(2)}) async-start(bf16[8,24,2048]{2,1,0:T(8,128)(2,1)} %normed.2), calls=%async_computation.1 | async-start | bytes 1572864 | tf_op jit(solution)/shard_map/normed/all_to_all | solution.py:39
  37.2 10.1 %collective-permute-start.5 = (bf16[128,128]{1,0:T(8,128)(2,1)S(1)}, bf16[128,128]{1,0:T(8,128)(2,1)S(1)}, u32[]{:S(2)}, u32[]{:S(2)}) collective-permute-start(bf16[128,128]{1,0:T(8,128)(2,1)S(1)} %copy-done.8), channel_id=1, source_target_pairs={{0,48},{16,64},{32,80},{48,96},{64,112},{80,0},{96,16},{112,32},{1... | collective-permute-start | bytes 98312 | tf_op jit(solution)/shard_map/normed/ppermute | solution.py:430
  40.3 7.0 %collective-permute-start.6 = (bf16[128,128]{1,0:T(8,128)(2,1)S(1)}, bf16[128,128]{1,0:T(8,128)(2,1)S(1)}, u32[]{:S(2)}, u32[]{:S(2)}) collective-permute-start(bf16[128,128]{1,0:T(8,128)(2,1)S(1)} %copy-done.6), channel_id=1, source_target_pairs={{0,80},{16,96},{32,112},{48,0},{64,16},{80,32},{96,48},{112,64},{1... | collective-permute-start | bytes 98312 | tf_op jit(solution)/shard_map/normed/ppermute | solution.py:430
  42.5 7.4 %collective-permute-start.7 = (bf16[128,128]{1,0:T(8,128)(2,1)S(1)}, bf16[128,128]{1,0:T(8,128)(2,1)S(1)}, u32[]{:S(2)}, u32[]{:S(2)}) collective-permute-start(bf16[128,128]{1,0:T(8,128)(2,1)S(1)} %copy-done.4), channel_id=1, source_target_pairs={{0,64},{16,80},{32,96},{48,112},{64,0},{80,16},{96,32},{112,48},{1... | collective-permute-start | bytes 98312 | tf_op jit(solution)/shard_map/normed/ppermute | solution.py:430
  53.8 8.4 %collective-permute-start.13 = (bf16[1040,128]{1,0:T(8,128)(2,1)S(1)}, bf16[1040,128]{1,0:T(8,128)(2,1)S(1)}, u32[]{:S(2)}, u32[]{:S(2)}) collective-permute-start(bf16[1040,128]{1,0:T(8,128)(2,1)S(1)} %acts.1.refs_0_), channel_id=1, source_target_pairs={{0,112},{16,0},{32,16},{48,32},{64,48},{80,64},{96,80},{112,96},{1... | collective-permute-start | bytes 798728 | tf_op jit(solution)/shard_map/groups/ppermute | solution.py:204
  58.3 7.8 %collective-permute-start.11 = (bf16[1040,128]{1,0:T(8,128)(2,1)S(1)}, bf16[1040,128]{1,0:T(8,128)(2,1)S(1)}, u32[]{:S(2)}, u32[]{:S(2)}) collective-permute-start(bf16[1040,128]{1,0:T(8,128)(2,1)S(1)} %acts.1.refs_0_), channel_id=1, source_target_pairs={{0,16},{16,32},{32,48},{48,64},{64,80},{80,96},{96,112},{112,0},{1... | collective-permute-start | bytes 798728 | tf_op jit(solution)/shard_map/groups/ppermute | solution.py:201
  62.3 6.8 %collective-permute-start.17 = (bf16[1040,128]{1,0:T(8,128)(2,1)S(1)}, bf16[1040,128]{1,0:T(8,128)(2,1)S(1)}, u32[]{:S(2)}, u32[]{:S(2)}) collective-permute-start(bf16[1040,128]{1,0:T(8,128)(2,1)S(1)} %collective-permute-done.13.refs_4_), channel_id=1, source_target_pairs={{0,112},{16,0},{32,16},{48,32},{64,48},{80,64},{96,80},{112,96},{1... | collective-permute-start | bytes 798728 | tf_op jit(solution)/shard_map/groups/ppermute | solution.py:204
  65.7 6.5 %collective-permute-start.10 = (bf16[1040,128]{1,0:T(8,128)(2,1)S(1)}, bf16[1040,128]{1,0:T(8,128)(2,1)S(1)}, u32[]{:S(2)}, u32[]{:S(2)}) collective-permute-start(bf16[1040,128]{1,0:T(8,128)(2,1)S(1)} %acts.1.refs_0_), channel_id=1, source_target_pairs={{0,128},{16,144},{32,160},{48,176},{64,192},{80,208},{96,224},{112... | collective-permute-start | bytes 798728 | tf_op jit(solution)/shard_map/groups/ppermute | solution.py:207
  66.1 6.5 %collective-permute-start.15 = (bf16[1040,128]{1,0:T(8,128)(2,1)S(1)}, bf16[1040,128]{1,0:T(8,128)(2,1)S(1)}, u32[]{:S(2)}, u32[]{:S(2)}) collective-permute-start(bf16[1040,128]{1,0:T(8,128)(2,1)S(1)} %collective-permute-done.11.refs_2_), channel_id=1, source_target_pairs={{0,16},{16,32},{32,48},{48,64},{64,80},{80,96},{96,112},{112,0},{1... | collective-permute-start | bytes 798728 | tf_op jit(solution)/shard_map/groups/ppermute | solution.py:201
  69.1 6.5 %collective-permute-start.21 = (bf16[1040,128]{1,0:T(8,128)(2,1)S(1)}, bf16[1040,128]{1,0:T(8,128)(2,1)S(1)}, u32[]{:S(2)}, u32[]{:S(2)}) collective-permute-start(bf16[1040,128]{1,0:T(8,128)(2,1)S(1)} %collective-permute-done.17.refs_8_), channel_id=1, source_target_pairs={{0,112},{16,0},{32,16},{48,32},{64,48},{80,64},{96,80},{112,96},{1... | collective-permute-start | bytes 798728 | tf_op jit(solution)/shard_map/groups/ppermute | solution.py:204
  72.2 12.5 %collective-permute-start.12 = (bf16[1040,128]{1,0:T(8,128)(2,1)S(1)}, bf16[1040,128]{1,0:T(8,128)(2,1)S(1)}, u32[]{:S(2)}, u32[]{:S(2)}) collective-permute-start(bf16[1040,128]{1,0:T(8,128)(2,1)S(1)} %collective-permute-done.10.refs_1_), channel_id=1, source_target_pairs={{0,16},{16,32},{32,48},{48,64},{64,80},{80,96},{96,112},{112,0},{1... | collective-permute-start | bytes 798728 | tf_op jit(solution)/shard_map/groups/ppermute | solution.py:201
  72.2 12.5 %collective-permute-start.14 = (bf16[1040,128]{1,0:T(8,128)(2,1)S(1)}, bf16[1040,128]{1,0:T(8,128)(2,1)S(1)}, u32[]{:S(2)}, u32[]{:S(2)}) collective-permute-start(bf16[1040,128]{1,0:T(8,128)(2,1)S(1)} %collective-permute-done.13.refs_4_), channel_id=1, source_target_pairs={{0,128},{16,144},{32,160},{48,176},{64,192},{80,208},{96,224},{112... | collective-permute-start | bytes 798728 | tf_op jit(solution)/shard_map/groups/ppermute | solution.py:207
  72.6 16.8 %collective-permute-start.19 = (bf16[1040,128]{1,0:T(8,128)(2,1)S(1)}, bf16[1040,128]{1,0:T(8,128)(2,1)S(1)}, u32[]{:S(2)}, u32[]{:S(2)}) collective-permute-start(bf16[1040,128]{1,0:T(8,128)(2,1)S(1)} %collective-permute-done.15.refs_6_), channel_id=1, source_target_pairs={{0,16},{16,32},{32,48},{48,64},{64,80},{80,96},{96,112},{112,0},{1... | collective-permute-start | bytes 798728 | tf_op jit(solution)/shard_map/groups/ppermute | solution.py:201
  75.5 14.9 %collective-permute-start.22 = (bf16[1040,128]{1,0:T(8,128)(2,1)S(1)}, bf16[1040,128]{1,0:T(8,128)(2,1)S(1)}, u32[]{:S(2)}, u32[]{:S(2)}) collective-permute-start(bf16[1040,128]{1,0:T(8,128)(2,1)S(1)} %collective-permute-done.21.refs_12_), channel_id=1, source_target_pairs={{0,128},{16,144},{32,160},{48,176},{64,192},{80,208},{96,224},{112... | collective-permute-start | bytes 798728 | tf_op jit(solution)/shard_map/groups/ppermute | solution.py:207
  75.9 8.4 %collective-permute-start.25 = (bf16[512,128]{1,0:T(8,128)(2,1)S(1)}, bf16[512,128]{1,0:T(8,128)(2,1)S(1)}, u32[]{:S(2)}, u32[]{:S(2)}) collective-permute-start(bf16[512,128]{1,0:T(8,128)(2,1)S(1)} %normed.3), channel_id=1, source_target_pairs={{0,128},{16,144},{32,160},{48,176},{64,192},{80,208},{96,224},{112... | collective-permute-start | bytes 393224 | tf_op jit(solution)/shard_map/normed/ppermute | solution.py:433
  84.3 7.8 %collective-permute-start.18 = (bf16[1040,128]{1,0:T(8,128)(2,1)S(1)}, bf16[1040,128]{1,0:T(8,128)(2,1)S(1)}, u32[]{:S(2)}, u32[]{:S(2)}) collective-permute-start(bf16[1040,128]{1,0:T(8,128)(2,1)S(1)} %collective-permute-done.17.refs_8_), channel_id=1, source_target_pairs={{0,128},{16,144},{32,160},{48,176},{64,192},{80,208},{96,224},{112... | collective-permute-start | bytes 798728 | tf_op jit(solution)/shard_map/groups/ppermute | solution.py:207
  84.7 8.4 %collective-permute-start.16 = (bf16[1040,128]{1,0:T(8,128)(2,1)S(1)}, bf16[1040,128]{1,0:T(8,128)(2,1)S(1)}, u32[]{:S(2)}, u32[]{:S(2)}) collective-permute-start(bf16[1040,128]{1,0:T(8,128)(2,1)S(1)} %collective-permute-done.12.refs_3_), channel_id=1, source_target_pairs={{0,16},{16,32},{32,48},{48,64},{64,80},{80,96},{96,112},{112,0},{1... | collective-permute-start | bytes 798728 | tf_op jit(solution)/shard_map/groups/ppermute | solution.py:201
  84.7 8.4 %collective-permute-start.23 = (bf16[1040,128]{1,0:T(8,128)(2,1)S(1)}, bf16[1040,128]{1,0:T(8,128)(2,1)S(1)}, u32[]{:S(2)}, u32[]{:S(2)}) collective-permute-start(bf16[1040,128]{1,0:T(8,128)(2,1)S(1)} %collective-permute-done.21.refs_12_), channel_id=1, source_target_pairs={{0,112},{16,0},{32,16},{48,32},{64,48},{80,64},{96,80},{112,96},{1... | collective-permute-start | bytes 798728 | tf_op jit(solution)/shard_map/groups/ppermute | solution.py:204
  89.3 5.7 %collective-permute-start.20 = (bf16[1040,128]{1,0:T(8,128)(2,1)S(1)}, bf16[1040,128]{1,0:T(8,128)(2,1)S(1)}, u32[]{:S(2)}, u32[]{:S(2)}) collective-permute-start(bf16[1040,128]{1,0:T(8,128)(2,1)S(1)} %collective-permute-done.19.refs_10_), channel_id=1, source_target_pairs={{0,128},{16,144},{32,160},{48,176},{64,192},{80,208},{96,224},{112... | collective-permute-start | bytes 798728 | tf_op jit(solution)/shard_map/groups/ppermute | solution.py:207
  90.4 5.6 %collective-permute-start.24 = (bf16[1040,128]{1,0:T(8,128)(2,1)S(1)}, bf16[1040,128]{1,0:T(8,128)(2,1)S(1)}, u32[]{:S(2)}, u32[]{:S(2)}) collective-permute-start(bf16[1040,128]{1,0:T(8,128)(2,1)S(1)} %collective-permute-done.22.refs_13_), channel_id=1, source_target_pairs={{0,112},{16,0},{32,16},{48,32},{64,48},{80,64},{96,80},{112,96},{1... | collective-permute-start | bytes 798728 | tf_op jit(solution)/shard_map/groups/ppermute | solution.py:204
  97.1 11.1 %collective-permute-start.26 = (f32[688,128]{1,0:T(8,128)S(1)}, f32[688,128]{1,0:T(8,128)S(1)}, u32[]{:S(2)}, u32[]{:S(2)}) collective-permute-start(f32[688,128]{1,0:T(8,128)S(1)} %get-tuple-element.106), channel_id=1, source_target_pairs={{0,1},{1,0},{2,3},{3,2},{4,5},{5,4},{6,7},{7,6},{8,9},{9,8},{10,11... | collective-permute-start | bytes 1056776 | tf_op jit(solution)/shard_map/rhs/ppermute | solution.py:35
  141.3 4.3 %collective-permute-start.27 = (f32[696,128]{1,0:T(8,128)S(1)}, f32[696,128]{1,0:T(8,128)S(1)}, u32[]{:S(2)}, u32[]{:S(2)}) collective-permute-start(f32[696,128]{1,0:T(8,128)S(1)} %get-tuple-element.111), channel_id=1, source_target_pairs={{0,1},{1,0},{2,3},{3,2},{4,5},{5,4},{6,7},{7,6},{8,9},{9,8},{10,11... | collective-permute-start | bytes 1069064 | tf_op jit(solution)/shard_map/first/ppermute | solution.py:35
  174.1 4.4 %collective-permute-start.28 = (f32[696,128]{1,0:T(8,128)S(1)}, f32[696,128]{1,0:T(8,128)S(1)}, u32[]{:S(2)}, u32[]{:S(2)}) collective-permute-start(f32[696,128]{1,0:T(8,128)S(1)} %get-tuple-element.120), channel_id=1, source_target_pairs={{0,1},{1,0},{2,3},{3,2},{4,5},{5,4},{6,7},{7,6},{8,9},{9,8},{10,11... | collective-permute-start | bytes 1069064 | tf_op jit(solution)/shard_map/second/ppermute | solution.py:35
  (16 other events, 94.9 us)

commit v9 on v8

--- a/solution.py
+++ b/solution.py
@@ -407,6 +407,7 @@
         rows = local_call(
             add_kernel, pltpu.VMEM((8, 24, wide), bf16), mine.reshape(8, 24, wide), other
         )
+        rows, cotangent = lax.optimization_barrier((rows, cotangent))
         dealt = local_call(
             deal_kernel,
             (shape((128, 128), bf16),) * 8,
@@ -414,7 +415,6 @@
             cotangent,
             specs=[SMEM, VMEM],
         )
-        rows, *dealt = lax.optimization_barrier((rows, *dealt))
         rows = exchange_chips(rows)
         columns = [dealt[0]] + [
             lax.ppermute(v, "dp", z_shift(-step)) for step, v in zip(STEPS[1:5], dealt[1:5])
@@ -428,7 +428,6 @@
         normed, *dealt = lax.optimization_barrier((normed, *dealt[5:]))
         normed = exchange_chips(normed).reshape(192, wide)
         columns += [lax.ppermute(v, "dp", z_shift(-step)) for step, v in zip(STEPS[5:], dealt)]
-        normed, *columns = lax.optimization_barrier((normed, *columns))
         passed = local_call(pass_kernel, shape((512, 128), bf16), *columns)
         columns.append(lax.ppermute(passed, "dp", YLO))
     with jax.named_scope("acts"):

time: 219 us -> 233 us (1.064)
  waiting for transfers between devices: 33.5 us -> 56.8 us
  starting transfers between devices: 68.7 us -> 61.9 us
    ppermute x7, waiting for transfers between devices: 6.08 us -> 20.9 us  [body(): lax.ppermute(v, 'dp', z_shift(-step))]
    all_to_all x2, waiting for transfers between devices: 1.28 us -> 10.5 us  [exchange_chips(): return lax.all_to_all(v, 'shard', 0, 0, axis_index_groups=CHIPS, tiled=True)]
    ppermute x7, starting transfers between devices: 18.2 us -> 10.4 us  [body(): lax.ppermute(v, 'dp', z_shift(-step))]
    ppermute x1, waiting for transfers between devices: 7.22 us -> 2.36 us  [body(): columns.append(lax.ppermute(passed, 'dp', YLO))]
  transfers between devices with their start and end apart: 31 -> 31, of which waited for: 17 -> 21; matrix products, arithmetic and copies ran while one was open for 0% -> 0% of each run, Pallas kernels for 1% -> 1%
where the time goes in v9:
time: 233 us; the launch traced here: 232 us
  blocking collectives  92.5 us (40%)
  starting transfers between devices  61.9 us (27%)
  waiting for transfers between devices  56.8 us (24%)
  Pallas kernels  20.6 us (9%)
    all_to_all x5, blocking collectives, exchange_chips(): return lax.all_to_all(v, 'shard', 0, 0, axis_index_groups=CHIPS, tiled=True)  70.3 us
    ppermute x6, starting transfers between devices, swap_core(): return lax.ppermute(v, 'shard', CORE)  21.6 us
    ppermute x7, waiting for transfers between devices, body(): lax.ppermute(v, 'dp', z_shift(-step))  20.9 us
    pallas_call x17, Pallas kernels, local_call(): pl.pallas_call(kernel, out_shape=outs, in_specs=specs or [VMEM] * len(arg...  20.6 us
    ppermute x5, starting transfers between devices, down(): return lax.ppermute(v, 'dp', z_shift(-1))  14.8 us
    ppermute x5, waiting for transfers between devices, down(): return lax.ppermute(v, 'dp', z_shift(-1))  12.6 us
    all_to_all x1, blocking collectives, body(): partials = lax.all_to_all(partials, 'shard', 0, 0, tiled=True)  11.8 us
    all_to_all x2, starting transfers between devices, exchange_chips(): return lax.all_to_all(v, 'shard', 0, 0, axis_index_groups=CHIPS, tiled=True)  10.8 us
  transfers between devices with their start and end apart: 31, of which 21 were waited for; matrix products, arithmetic and copies ran while one was open for 0% of the time, Pallas kernels for 1%

profile of v9, /device:TPU:1, one launch (start us, length us, event | category | flops | bytes accessed | tf_op | source)
XLA Modules:
  0.0 232.1 jit_solution(2530046002284661434)
XLA Ops:
  0.0 5.7 %rows.3 = (bf16[192,2048]{1,0:T(8,128)(2,1)S(1)}, bf16[192,2048]{1,0:T(8,128)(2,1)S(1)}) custom-call(s32[1]{0:T(128)} %bitcast.1.place, s32[2,128]{1,0:T(2,128)} %bitcast.17, s32[1,128]{1,0:T(1,128)} %bitcast.18, bf16[2000,2048]{1,0:T(8,128)(2,1)} %table_hbm.1), custom_call_target="tpu_custom_call" | custom-call | tf_op jit(solution)/shard_map/rows/pallas_call | solution.py:43
  5.7 3.3 %collective-permute-start = (bf16[192,2048]{1,0:T(8,128)(2,1)S(1)}, bf16[192,2048]{1,0:T(8,128)(2,1)S(1)}, u32[]{:S(2)}, u32[]{:S(2)}) collective-permute-start(bf16[192,2048]{1,0:T(8,128)(2,1)S(1)} %get-tuple-element.51), channel_id=1, source_target_pairs={{0,1},{1,0},{2,3},{3,2},{4,5},{5,4},{6,7},{7,6},{8,9},{9,8},{10,11... | collective-permute-start | bytes 2359304 | tf_op jit(solution)/shard_map/rows/ppermute | solution.py:35
  11.9 5.0 %all-to-all-start = ((bf16[8,24,2048]{2,1,0:T(8,128)(2,1)}), bf16[8,24,2048]{2,1,0:T(8,128)(2,1)S(1)}, u32[]{:S(2)}, u32[]{:S(2)}) async-start(bf16[8,24,2048]{2,1,0:T(8,128)(2,1)} %rows.4), calls=%async_computation | async-start | bytes 1572864 | tf_op jit(solution)/shard_map/rows/all_to_all | solution.py:39
  19.4 4.0 %collective-permute-start.2 = (bf16[128,128]{1,0:T(8,128)(2,1)S(1)}, bf16[128,128]{1,0:T(8,128)(2,1)S(1)}, u32[]{:S(2)}, u32[]{:S(2)}) collective-permute-start(bf16[128,128]{1,0:T(8,128)(2,1)S(1)} %get-tuple-element.56), channel_id=1, source_target_pairs={{0,112},{16,0},{32,16},{48,32},{64,48},{80,64},{96,80},{112,96},{1... | collective-permute-start | bytes 98312 | tf_op jit(solution)/shard_map/rows/ppermute | solution.py:420
  24.9 2.1 collective-permute-start.4
  27.0 1.8 collective-permute-done.3.refs_3_.refs_19_
  31.0 5.8 %all-to-all-start.1 = ((bf16[8,24,2048]{2,1,0:T(8,128)(2,1)}), bf16[8,24,2048]{2,1,0:T(8,128)(2,1)S(1)}, u32[]{:S(2)}, u32[]{:S(2)}) async-start(bf16[8,24,2048]{2,1,0:T(8,128)(2,1)} %normed.2), calls=%async_computation.1 | async-start | bytes 1572864 | tf_op jit(solution)/shard_map/normed/all_to_all | solution.py:39
  36.8 9.9 %all-to-all-done.1 = bf16[8,24,2048]{2,1,0:T(8,128)(2,1)S(1)} async-done(((bf16[8,24,2048]{2,1,0:T(8,128)(2,1)}), bf16[8,24,2048]{2,1,0:T(8,128)(2,1)S(1)}, u32[]{:S(2)}, u32[]{:S(2)}) %all-to-all-start.1) | async-done | bytes 786464 | tf_op jit(solution)/shard_map/normed/all_to_all | solution.py:39
  46.7 4.0 %acts.1.refs_0_ = bf16[1040,128]{1,0:T(8,128)(2,1)S(1)} custom-call(bf16[192,2048]{1,0:T(8,128)(2,1)S(1)} %bitcast.11, bf16[344,2048]{1,0:T(8,128)(2,1)S(1)} %bitcast.13, bf16[344,2048]{1,0:T(8,128)(2,1)} %bitcast.10.w_up, bf16[344,2048]{1,0:T(8,128)(2,1)} %collective-permute-done.5.w_gate_other, bf16[344,2048]{1,0:T(8,128)(2,1)} %collective-permute-done.6.w_up_other), custom_call_target="tpu_custom_call" | custom-call | tf_op jit(solution)/shard_map/acts/pallas_call | solution.py:43
  50.7 5.5 %collective-permute-start.10 = (bf16[1040,128]{1,0:T(8,128)(2,1)S(1)}, bf16[1040,128]{1,0:T(8,128)(2,1)S(1)}, u32[]{:S(2)}, u32[]{:S(2)}) collective-permute-start(bf16[1040,128]{1,0:T(8,128)(2,1)S(1)} %acts.1.refs_0_), channel_id=1, source_target_pairs={{0,112},{16,0},{32,16},{48,32},{64,48},{80,64},{96,80},{112,96},{1... | collective-permute-start | bytes 798728 | tf_op jit(solution)/shard_map/groups/ppermute | solution.py:204
  56.2 3.4 %collective-permute-done.10.refs_4_ = bf16[1040,128]{1,0:T(8,128)(2,1)S(1)} collective-permute-done((bf16[1040,128]{1,0:T(8,128)(2,1)S(1)}, bf16[1040,128]{1,0:T(8,128)(2,1)S(1)}, u32[]{:S(2)}, u32[]{:S(2)}) %collective-permute-start.10) | collective-permute-done | bytes 266272 | tf_op jit(solution)/shard_map/groups/ppermute | solution.py:204
  59.6 3.1 %collective-permute-start.14 = (bf16[1040,128]{1,0:T(8,128)(2,1)S(1)}, bf16[1040,128]{1,0:T(8,128)(2,1)S(1)}, u32[]{:S(2)}, u32[]{:S(2)}) collective-permute-start(bf16[1040,128]{1,0:T(8,128)(2,1)S(1)} %collective-permute-done.10.refs_4_), channel_id=1, source_target_pairs={{0,112},{16,0},{32,16},{48,32},{64,48},{80,64},{96,80},{112,96},{1... | collective-permute-start | bytes 798728 | tf_op jit(solution)/shard_map/groups/ppermute | solution.py:204
  63.1 3.0 %collective-permute-done.14.refs_8_ = bf16[1040,128]{1,0:T(8,128)(2,1)S(1)} collective-permute-done((bf16[1040,128]{1,0:T(8,128)(2,1)S(1)}, bf16[1040,128]{1,0:T(8,128)(2,1)S(1)}, u32[]{:S(2)}, u32[]{:S(2)}) %collective-permute-start.14) | collective-permute-done | bytes 266272 | tf_op jit(solution)/shard_map/groups/ppermute | solution.py:204
  66.0 3.1 %collective-permute-start.18 = (bf16[1040,128]{1,0:T(8,128)(2,1)S(1)}, bf16[1040,128]{1,0:T(8,128)(2,1)S(1)}, u32[]{:S(2)}, u32[]{:S(2)}) collective-permute-start(bf16[1040,128]{1,0:T(8,128)(2,1)S(1)} %collective-permute-done.14.refs_8_), channel_id=1, source_target_pairs={{0,112},{16,0},{32,16},{48,32},{64,48},{80,64},{96,80},{112,96},{1... | collective-permute-start | bytes 798728 | tf_op jit(solution)/shard_map/groups/ppermute | solution.py:204
  69.6 4.2 %collective-permute-done.18.refs_12_ = bf16[1040,128]{1,0:T(8,128)(2,1)S(1)} collective-permute-done((bf16[1040,128]{1,0:T(8,128)(2,1)S(1)}, bf16[1040,128]{1,0:T(8,128)(2,1)S(1)}, u32[]{:S(2)}, u32[]{:S(2)}) %collective-permute-start.18) | collective-permute-done | bytes 266272 | tf_op jit(solution)/shard_map/groups/ppermute | solution.py:204
  74.2 2.2 collective-permute-start.22
  76.4 5.9 %collective-permute-done.22.refs_5_.refs_21_ = bf16[128,128]{1,0:T(8,128)(2,1)S(1)} collective-permute-done((bf16[128,128]{1,0:T(8,128)(2,1)S(1)}, bf16[128,128]{1,0:T(8,128)(2,1)S(1)}, u32[]{:S(2)}, u32[]{:S(2)}) %collective-permute-start.22) | collective-permute-done | bytes 32800 | tf_op jit(solution)/shard_map/normed/ppermute | solution.py:430
  82.7 4.5 %collective-permute-done.23.refs_6_.refs_22_ = bf16[128,128]{1,0:T(8,128)(2,1)S(1)} collective-permute-done((bf16[128,128]{1,0:T(8,128)(2,1)S(1)}, bf16[128,128]{1,0:T(8,128)(2,1)S(1)}, u32[]{:S(2)}, u32[]{:S(2)}) %collective-permute-start.23) | collective-permute-done | bytes 32800 | tf_op jit(solution)/shard_map/normed/ppermute | solution.py:430
  87.2 6.7 %collective-permute-done.24.refs_7_.refs_23_ = bf16[128,128]{1,0:T(8,128)(2,1)S(1)} collective-permute-done((bf16[128,128]{1,0:T(8,128)(2,1)S(1)}, bf16[128,128]{1,0:T(8,128)(2,1)S(1)}, u32[]{:S(2)}, u32[]{:S(2)}) %collective-permute-start.24) | collective-permute-done | bytes 32800 | tf_op jit(solution)/shard_map/normed/ppermute | solution.py:430
  95.5 2.4 %collective-permute-done.25.refs_24_ = bf16[512,128]{1,0:T(8,128)(2,1)S(1)} collective-permute-done((bf16[512,128]{1,0:T(8,128)(2,1)S(1)}, bf16[512,128]{1,0:T(8,128)(2,1)S(1)}, u32[]{:S(2)}, u32[]{:S(2)}) %collective-permute-start.25) | collective-permute-done | bytes 131104 | tf_op jit(solution)/shard_map/normed/ppermute | solution.py:432
  99.4 2.7 %collective-permute-start.20 = (bf16[1040,128]{1,0:T(8,128)(2,1)S(1)}, bf16[1040,128]{1,0:T(8,128)(2,1)S(1)}, u32[]{:S(2)}, u32[]{:S(2)}) collective-permute-start(bf16[1040,128]{1,0:T(8,128)(2,1)S(1)} %collective-permute-done.18.refs_12_), channel_id=1, source_target_pairs={{0,112},{16,0},{32,16},{48,32},{64,48},{80,64},{96,80},{112,96},{1... | collective-permute-start | bytes 798728 | tf_op jit(solution)/shard_map/groups/ppermute | solution.py:204
  103.1 2.7 %collective-permute-done.13.refs_7_ = bf16[1040,128]{1,0:T(8,128)(2,1)S(1)} collective-permute-done((bf16[1040,128]{1,0:T(8,128)(2,1)S(1)}, bf16[1040,128]{1,0:T(8,128)(2,1)S(1)}, u32[]{:S(2)}, u32[]{:S(2)}) %collective-permute-start.13) | collective-permute-done | bytes 266272 | tf_op jit(solution)/shard_map/groups/ppermute | solution.py:201
  110.6 11.7 %collective-permute-start.26 = (f32[688,128]{1,0:T(8,128)S(1)}, f32[688,128]{1,0:T(8,128)S(1)}, u32[]{:S(2)}, u32[]{:S(2)}) collective-permute-start(f32[688,128]{1,0:T(8,128)S(1)} %get-tuple-element.74), channel_id=1, source_target_pairs={{0,1},{1,0},{2,3},{3,2},{4,5},{5,4},{6,7},{7,6},{8,9},{9,8},{10,11... | collective-permute-start | bytes 1056776 | tf_op jit(solution)/shard_map/rhs/ppermute | solution.py:35
  124.3 17.3 %all_to_all.45.parts = bf16[8,128,256]{2,1,0:T(8,128)(2,1)S(1)} all-to-all(bf16[8,128,256]{2,1,0:T(8,128)(2,1)S(1)} %get-tuple-element.75), channel_id=1, replica_groups={{0,2,4,6,8,10,12,14},{1,3,5,7,9,11,13,15},{16,18,20,22,24,26,28,30},{17..., dimensions={0} | all-to-all | bytes 1048576 | tf_op jit(solution)/shard_map/first/all_to_all | solution.py:39
  141.9 14.0 %all_to_all.46.got = bf16[8,144,256]{2,1,0:T(8,128)(2,1)S(1)} all-to-all(bf16[8,144,256]{2,1,0:T(8,128)(2,1)S(1)} %get-tuple-element.77), channel_id=1, replica_groups={{0,2,4,6,8,10,12,14},{1,3,5,7,9,11,13,15},{16,18,20,22,24,26,28,30},{17..., dimensions={0} | all-to-all | bytes 1179648 | tf_op jit(solution)/shard_map/first/all_to_all | solution.py:39
  156.8 3.0 %collective-permute-start.27 = (f32[696,128]{1,0:T(8,128)S(1)}, f32[696,128]{1,0:T(8,128)S(1)}, u32[]{:S(2)}, u32[]{:S(2)}) collective-permute-start(f32[696,128]{1,0:T(8,128)S(1)} %get-tuple-element.79), channel_id=1, source_target_pairs={{0,1},{1,0},{2,3},{3,2},{4,5},{5,4},{6,7},{7,6},{8,9},{9,8},{10,11... | collective-permute-start | bytes 1069064 | tf_op jit(solution)/shard_map/first/ppermute | solution.py:35
  161.9 12.7 %all_to_all.47.parts = bf16[8,128,256]{2,1,0:T(8,128)(2,1)S(1)} all-to-all(bf16[8,128,256]{2,1,0:T(8,128)(2,1)S(1)} %get-tuple-element.82), channel_id=1, replica_groups={{0,2,4,6,8,10,12,14},{1,3,5,7,9,11,13,15},{16,18,20,22,24,26,28,30},{17..., dimensions={0} | all-to-all | bytes 1048576 | tf_op jit(solution)/shard_map/second/all_to_all | solution.py:39
  174.9 13.5 %all_to_all.48.got = bf16[8,144,256]{2,1,0:T(8,128)(2,1)S(1)} all-to-all(bf16[8,144,256]{2,1,0:T(8,128)(2,1)S(1)} %get-tuple-element.85), channel_id=1, replica_groups={{0,2,4,6,8,10,12,14},{1,3,5,7,9,11,13,15},{16,18,20,22,24,26,28,30},{17..., dimensions={0} | all-to-all | bytes 1179648 | tf_op jit(solution)/shard_map/second/all_to_all | solution.py:39
  189.6 3.1 %collective-permute-start.28 = (f32[696,128]{1,0:T(8,128)S(1)}, f32[696,128]{1,0:T(8,128)S(1)}, u32[]{:S(2)}, u32[]{:S(2)}) collective-permute-start(f32[696,128]{1,0:T(8,128)S(1)} %get-tuple-element.88), channel_id=1, source_target_pairs={{0,1},{1,0},{2,3},{3,2},{4,5},{5,4},{6,7},{7,6},{8,9},{9,8},{10,11... | collective-permute-start | bytes 1069064 | tf_op jit(solution)/shard_map/second/ppermute | solution.py:35
  195.0 12.7 %all_to_all.49.parts = bf16[8,128,256]{2,1,0:T(8,128)(2,1)S(1)} all-to-all(bf16[8,128,256]{2,1,0:T(8,128)(2,1)S(1)} %get-tuple-element.91), channel_id=1, replica_groups={{0,2,4,6,8,10,12,14},{1,3,5,7,9,11,13,15},{16,18,20,22,24,26,28,30},{17..., dimensions={0} | all-to-all | bytes 1048576 | tf_op jit(solution)/shard_map/third/all_to_all | solution.py:39
  208.0 11.8 %all_to_all.50.got = f32[16,1,128]{2,1,0:T(1,128)S(1)} all-to-all(f32[16,1,128]{2,1,0:T(1,128)S(1)} %third.3), channel_id=1, replica_groups=mesh['dp'=16,'shard'=16] {'shard'}, dimensions={0} | all-to-all | bytes 16384 | tf_op jit(solution)/shard_map/third/all_to_all | solution.py:490
  220.2 10.5 %all_to_all.51.got = f32[16,1,128]{2,1,0:T(1,128)S(1)} all-to-all(f32[16,1,128]{2,1,0:T(1,128)S(1)} %whole.2), channel_id=1, replica_groups=mesh['dp'=16,'shard'=16] {'dp'}, dimensions={0} | all-to-all | bytes 16384 | tf_op jit(solution)/shard_map/whole/all_to_all | solution.py:493
  (61 shorter events, 30.7 us)
Async XLA Ops:
  5.7 5.3 %collective-permute-start = (bf16[192,2048]{1,0:T(8,128)(2,1)S(1)}, bf16[192,2048]{1,0:T(8,128)(2,1)S(1)}, u32[]{:S(2)}, u32[]{:S(2)}) collective-permute-start(bf16[192,2048]{1,0:T(8,128)(2,1)S(1)} %get-tuple-element.51), channel_id=1, source_target_pairs={{0,1},{1,0},{2,3},{3,2},{4,5},{5,4},{6,7},{7,6},{8,9},{9,8},{10,11... | collective-permute-start | bytes 2359304 | tf_op jit(solution)/shard_map/rows/ppermute | solution.py:35
  9.0 27.8 %collective-permute-start.5 = (bf16[344,2048]{1,0:T(8,128)(2,1)S(1)}, bf16[344,2048]{1,0:T(8,128)(2,1)}, u32[]{:S(2)}, u32[]{:S(2)}) collective-permute-start(bf16[344,2048]{1,0:T(8,128)(2,1)S(1)} %bitcast.12), channel_id=1, source_target_pairs={{0,1},{1,0},{2,3},{3,2},{4,5},{5,4},{6,7},{7,6},{8,9},{9,8},{10,11... | collective-permute-start | bytes 4227080 | tf_op jit(solution)/shard_map/ppermute | solution.py:35
  9.1 27.7 %collective-permute-start.6 = (bf16[344,2048]{1,0:T(8,128)(2,1)}, bf16[344,2048]{1,0:T(8,128)(2,1)}, u32[]{:S(2)}, u32[]{:S(2)}) collective-permute-start(bf16[344,2048]{1,0:T(8,128)(2,1)} %bitcast.10.w_up), channel_id=1, source_target_pairs={{0,1},{1,0},{2,3},{3,2},{4,5},{5,4},{6,7},{7,6},{8,9},{9,8},{10,11... | collective-permute-start | bytes 4227080 | tf_op jit(solution)/shard_map/ppermute | solution.py:35
  11.9 18.0 %copy-start.2 = (f32[2048]{0:T(1024)S(1)}, f32[2048]{0:T(1024)}, u32[]{:S(2)}) copy-start(f32[2048]{0:T(1024)} %param.10) | copy-start | bytes 24580
  11.9 18.0 %all-to-all-start = ((bf16[8,24,2048]{2,1,0:T(8,128)(2,1)}), bf16[8,24,2048]{2,1,0:T(8,128)(2,1)S(1)}, u32[]{:S(2)}, u32[]{:S(2)}) async-start(bf16[8,24,2048]{2,1,0:T(8,128)(2,1)} %rows.4), calls=%async_computation | async-start | bytes 1572864 | tf_op jit(solution)/shard_map/rows/all_to_all | solution.py:39
  17.7 7.3 %collective-permute-start.1 = (bf16[128,128]{1,0:T(8,128)(2,1)S(1)}, bf16[128,128]{1,0:T(8,128)(2,1)S(1)}, u32[]{:S(2)}, u32[]{:S(2)}) collective-permute-start(bf16[128,128]{1,0:T(8,128)(2,1)S(1)} %get-tuple-element.55), channel_id=1, source_target_pairs={{0,16},{16,32},{32,48},{48,64},{64,80},{80,96},{96,112},{112,0},{1... | collective-permute-start | bytes 98312 | tf_op jit(solution)/shard_map/rows/ppermute | solution.py:420
  19.4 7.6 %collective-permute-start.2 = (bf16[128,128]{1,0:T(8,128)(2,1)S(1)}, bf16[128,128]{1,0:T(8,128)(2,1)S(1)}, u32[]{:S(2)}, u32[]{:S(2)}) collective-permute-start(bf16[128,128]{1,0:T(8,128)(2,1)S(1)} %get-tuple-element.56), channel_id=1, source_target_pairs={{0,112},{16,0},{32,16},{48,32},{64,48},{80,64},{96,80},{112,96},{1... | collective-permute-start | bytes 98312 | tf_op jit(solution)/shard_map/rows/ppermute | solution.py:420
  23.4 5.4 %collective-permute-start.3 = (bf16[128,128]{1,0:T(8,128)(2,1)S(1)}, bf16[128,128]{1,0:T(8,128)(2,1)S(1)}, u32[]{:S(2)}, u32[]{:S(2)}) collective-permute-start(bf16[128,128]{1,0:T(8,128)(2,1)S(1)} %get-tuple-element.57), channel_id=1, source_target_pairs={{0,32},{16,48},{32,64},{48,80},{64,96},{80,112},{96,0},{112,16},{1... | collective-permute-start | bytes 98312 | tf_op jit(solution)/shard_map/rows/ppermute | solution.py:420
  24.9 4.3 %collective-permute-start.4 = (bf16[128,128]{1,0:T(8,128)(2,1)S(1)}, bf16[128,128]{1,0:T(8,128)(2,1)S(1)}, u32[]{:S(2)}, u32[]{:S(2)}) collective-permute-start(bf16[128,128]{1,0:T(8,128)(2,1)S(1)} %get-tuple-element.58), channel_id=1, source_target_pairs={{0,96},{16,112},{32,0},{48,16},{64,32},{80,48},{96,64},{112,80},{1... | collective-permute-start | bytes 98312 | tf_op jit(solution)/shard_map/rows/ppermute | solution.py:420
  31.0 15.7 %all-to-all-start.1 = ((bf16[8,24,2048]{2,1,0:T(8,128)(2,1)}), bf16[8,24,2048]{2,1,0:T(8,128)(2,1)S(1)}, u32[]{:S(2)}, u32[]{:S(2)}) async-start(bf16[8,24,2048]{2,1,0:T(8,128)(2,1)} %normed.2), calls=%async_computation.1 | async-start | bytes 1572864 | tf_op jit(solution)/shard_map/normed/all_to_all | solution.py:39
  50.7 8.9 %collective-permute-start.10 = (bf16[1040,128]{1,0:T(8,128)(2,1)S(1)}, bf16[1040,128]{1,0:T(8,128)(2,1)S(1)}, u32[]{:S(2)}, u32[]{:S(2)}) collective-permute-start(bf16[1040,128]{1,0:T(8,128)(2,1)S(1)} %acts.1.refs_0_), channel_id=1, source_target_pairs={{0,112},{16,0},{32,16},{48,32},{64,48},{80,64},{96,80},{112,96},{1... | collective-permute-start | bytes 798728 | tf_op jit(solution)/shard_map/groups/ppermute | solution.py:204
  56.2 6.9 %collective-permute-start.8 = (bf16[1040,128]{1,0:T(8,128)(2,1)S(1)}, bf16[1040,128]{1,0:T(8,128)(2,1)S(1)}, u32[]{:S(2)}, u32[]{:S(2)}) collective-permute-start(bf16[1040,128]{1,0:T(8,128)(2,1)S(1)} %acts.1.refs_0_), channel_id=1, source_target_pairs={{0,16},{16,32},{32,48},{48,64},{64,80},{80,96},{96,112},{112,0},{1... | collective-permute-start | bytes 798728 | tf_op jit(solution)/shard_map/groups/ppermute | solution.py:201
  59.6 6.5 %collective-permute-start.14 = (bf16[1040,128]{1,0:T(8,128)(2,1)S(1)}, bf16[1040,128]{1,0:T(8,128)(2,1)S(1)}, u32[]{:S(2)}, u32[]{:S(2)}) collective-permute-start(bf16[1040,128]{1,0:T(8,128)(2,1)S(1)} %collective-permute-done.10.refs_4_), channel_id=1, source_target_pairs={{0,112},{16,0},{32,16},{48,32},{64,48},{80,64},{96,80},{112,96},{1... | collective-permute-start | bytes 798728 | tf_op jit(solution)/shard_map/groups/ppermute | solution.py:204
  62.7 6.5 %collective-permute-start.7 = (bf16[1040,128]{1,0:T(8,128)(2,1)S(1)}, bf16[1040,128]{1,0:T(8,128)(2,1)S(1)}, u32[]{:S(2)}, u32[]{:S(2)}) collective-permute-start(bf16[1040,128]{1,0:T(8,128)(2,1)S(1)} %acts.1.refs_0_), channel_id=1, source_target_pairs={{0,128},{16,144},{32,160},{48,176},{64,192},{80,208},{96,224},{112... | collective-permute-start | bytes 798728 | tf_op jit(solution)/shard_map/groups/ppermute | solution.py:207
  63.1 6.5 %collective-permute-start.12 = (bf16[1040,128]{1,0:T(8,128)(2,1)S(1)}, bf16[1040,128]{1,0:T(8,128)(2,1)S(1)}, u32[]{:S(2)}, u32[]{:S(2)}) collective-permute-start(bf16[1040,128]{1,0:T(8,128)(2,1)S(1)} %collective-permute-done.8.refs_2_), channel_id=1, source_target_pairs={{0,16},{16,32},{32,48},{48,64},{64,80},{80,96},{96,112},{112,0},{1... | collective-permute-start | bytes 798728 | tf_op jit(solution)/shard_map/groups/ppermute | solution.py:201
  66.0 7.7 %collective-permute-start.18 = (bf16[1040,128]{1,0:T(8,128)(2,1)S(1)}, bf16[1040,128]{1,0:T(8,128)(2,1)S(1)}, u32[]{:S(2)}, u32[]{:S(2)}) collective-permute-start(bf16[1040,128]{1,0:T(8,128)(2,1)S(1)} %collective-permute-done.14.refs_8_), channel_id=1, source_target_pairs={{0,112},{16,0},{32,16},{48,32},{64,48},{80,64},{96,80},{112,96},{1... | collective-permute-start | bytes 798728 | tf_op jit(solution)/shard_map/groups/ppermute | solution.py:204
  69.2 30.2 %collective-permute-start.9 = (bf16[1040,128]{1,0:T(8,128)(2,1)S(1)}, bf16[1040,128]{1,0:T(8,128)(2,1)S(1)}, u32[]{:S(2)}, u32[]{:S(2)}) collective-permute-start(bf16[1040,128]{1,0:T(8,128)(2,1)S(1)} %collective-permute-done.7.refs_1_), channel_id=1, source_target_pairs={{0,16},{16,32},{32,48},{48,64},{64,80},{80,96},{96,112},{112,0},{1... | collective-permute-start | bytes 798728 | tf_op jit(solution)/shard_map/groups/ppermute | solution.py:201
  69.2 30.2 %collective-permute-start.11 = (bf16[1040,128]{1,0:T(8,128)(2,1)S(1)}, bf16[1040,128]{1,0:T(8,128)(2,1)S(1)}, u32[]{:S(2)}, u32[]{:S(2)}) collective-permute-start(bf16[1040,128]{1,0:T(8,128)(2,1)S(1)} %collective-permute-done.10.refs_4_), channel_id=1, source_target_pairs={{0,128},{16,144},{32,160},{48,176},{64,192},{80,208},{96,224},{112... | collective-permute-start | bytes 798728 | tf_op jit(solution)/shard_map/groups/ppermute | solution.py:207
  69.6 32.5 %collective-permute-start.16 = (bf16[1040,128]{1,0:T(8,128)(2,1)S(1)}, bf16[1040,128]{1,0:T(8,128)(2,1)S(1)}, u32[]{:S(2)}, u32[]{:S(2)}) collective-permute-start(bf16[1040,128]{1,0:T(8,128)(2,1)S(1)} %collective-permute-done.12.refs_6_), channel_id=1, source_target_pairs={{0,16},{16,32},{32,48},{48,64},{64,80},{80,96},{96,112},{112,0},{1... | collective-permute-start | bytes 798728 | tf_op jit(solution)/shard_map/groups/ppermute | solution.py:201
  73.8 28.2 %collective-permute-start.19 = (bf16[1040,128]{1,0:T(8,128)(2,1)S(1)}, bf16[1040,128]{1,0:T(8,128)(2,1)S(1)}, u32[]{:S(2)}, u32[]{:S(2)}) collective-permute-start(bf16[1040,128]{1,0:T(8,128)(2,1)S(1)} %collective-permute-done.18.refs_12_), channel_id=1, source_target_pairs={{0,128},{16,144},{32,160},{48,176},{64,192},{80,208},{96,224},{112... | collective-permute-start | bytes 798728 | tf_op jit(solution)/shard_map/groups/ppermute | solution.py:207
  74.2 8.1 %collective-permute-start.22 = (bf16[128,128]{1,0:T(8,128)(2,1)S(1)}, bf16[128,128]{1,0:T(8,128)(2,1)S(1)}, u32[]{:S(2)}, u32[]{:S(2)}) collective-permute-start(bf16[128,128]{1,0:T(8,128)(2,1)S(1)} %get-tuple-element.69), channel_id=1, source_target_pairs={{0,48},{16,64},{32,80},{48,96},{64,112},{80,0},{96,16},{112,32},{1... | collective-permute-start | bytes 98312 | tf_op jit(solution)/shard_map/normed/ppermute | solution.py:430
  82.3 4.9 %collective-permute-start.23 = (bf16[128,128]{1,0:T(8,128)(2,1)S(1)}, bf16[128,128]{1,0:T(8,128)(2,1)S(1)}, u32[]{:S(2)}, u32[]{:S(2)}) collective-permute-start(bf16[128,128]{1,0:T(8,128)(2,1)S(1)} %get-tuple-element.70), channel_id=1, source_target_pairs={{0,80},{16,96},{32,112},{48,0},{64,16},{80,32},{96,48},{112,64},{1... | collective-permute-start | bytes 98312 | tf_op jit(solution)/shard_map/normed/ppermute | solution.py:430
  87.2 6.7 %collective-permute-start.24 = (bf16[128,128]{1,0:T(8,128)(2,1)S(1)}, bf16[128,128]{1,0:T(8,128)(2,1)S(1)}, u32[]{:S(2)}, u32[]{:S(2)}) collective-permute-start(bf16[128,128]{1,0:T(8,128)(2,1)S(1)} %get-tuple-element.71), channel_id=1, source_target_pairs={{0,64},{16,80},{32,96},{48,112},{64,0},{80,16},{96,32},{112,48},{1... | collective-permute-start | bytes 98312 | tf_op jit(solution)/shard_map/normed/ppermute | solution.py:430
  93.9 4.0 %collective-permute-start.25 = (bf16[512,128]{1,0:T(8,128)(2,1)S(1)}, bf16[512,128]{1,0:T(8,128)(2,1)S(1)}, u32[]{:S(2)}, u32[]{:S(2)}) collective-permute-start(bf16[512,128]{1,0:T(8,128)(2,1)S(1)} %normed.3), channel_id=1, source_target_pairs={{0,128},{16,144},{32,160},{48,176},{64,192},{80,208},{96,224},{112... | collective-permute-start | bytes 393224 | tf_op jit(solution)/shard_map/normed/ppermute | solution.py:432
  97.9 5.3 %collective-permute-start.15 = (bf16[1040,128]{1,0:T(8,128)(2,1)S(1)}, bf16[1040,128]{1,0:T(8,128)(2,1)S(1)}, u32[]{:S(2)}, u32[]{:S(2)}) collective-permute-start(bf16[1040,128]{1,0:T(8,128)(2,1)S(1)} %collective-permute-done.14.refs_8_), channel_id=1, source_target_pairs={{0,128},{16,144},{32,160},{48,176},{64,192},{80,208},{96,224},{112... | collective-permute-start | bytes 798728 | tf_op jit(solution)/shard_map/groups/ppermute | solution.py:207
  99.3 6.5 %collective-permute-start.13 = (bf16[1040,128]{1,0:T(8,128)(2,1)S(1)}, bf16[1040,128]{1,0:T(8,128)(2,1)S(1)}, u32[]{:S(2)}, u32[]{:S(2)}) collective-permute-start(bf16[1040,128]{1,0:T(8,128)(2,1)S(1)} %collective-permute-done.9.refs_3_), channel_id=1, source_target_pairs={{0,16},{16,32},{32,48},{48,64},{64,80},{80,96},{96,112},{112,0},{1... | collective-permute-start | bytes 798728 | tf_op jit(solution)/shard_map/groups/ppermute | solution.py:201
  99.4 7.7 %collective-permute-start.20 = (bf16[1040,128]{1,0:T(8,128)(2,1)S(1)}, bf16[1040,128]{1,0:T(8,128)(2,1)S(1)}, u32[]{:S(2)}, u32[]{:S(2)}) collective-permute-start(bf16[1040,128]{1,0:T(8,128)(2,1)S(1)} %collective-permute-done.18.refs_12_), channel_id=1, source_target_pairs={{0,112},{16,0},{32,16},{48,32},{64,48},{80,64},{96,80},{112,96},{1... | collective-permute-start | bytes 798728 | tf_op jit(solution)/shard_map/groups/ppermute | solution.py:204
  102.0 6.7 %collective-permute-start.17 = (bf16[1040,128]{1,0:T(8,128)(2,1)S(1)}, bf16[1040,128]{1,0:T(8,128)(2,1)S(1)}, u32[]{:S(2)}, u32[]{:S(2)}) collective-permute-start(bf16[1040,128]{1,0:T(8,128)(2,1)S(1)} %collective-permute-done.16.refs_10_), channel_id=1, source_target_pairs={{0,128},{16,144},{32,160},{48,176},{64,192},{80,208},{96,224},{112... | collective-permute-start | bytes 798728 | tf_op jit(solution)/shard_map/groups/ppermute | solution.py:207
  102.0 7.6 %collective-permute-start.21 = (bf16[1040,128]{1,0:T(8,128)(2,1)S(1)}, bf16[1040,128]{1,0:T(8,128)(2,1)S(1)}, u32[]{:S(2)}, u32[]{:S(2)}) collective-permute-start(bf16[1040,128]{1,0:T(8,128)(2,1)S(1)} %collective-permute-done.19.refs_13_), channel_id=1, source_target_pairs={{0,112},{16,0},{32,16},{48,32},{64,48},{80,64},{96,80},{112,96},{1... | collective-permute-start | bytes 798728 | tf_op jit(solution)/shard_map/groups/ppermute | solution.py:204
  110.6 13.0 %collective-permute-start.26 = (f32[688,128]{1,0:T(8,128)S(1)}, f32[688,128]{1,0:T(8,128)S(1)}, u32[]{:S(2)}, u32[]{:S(2)}) collective-permute-start(f32[688,128]{1,0:T(8,128)S(1)} %get-tuple-element.74), channel_id=1, source_target_pairs={{0,1},{1,0},{2,3},{3,2},{4,5},{5,4},{6,7},{7,6},{8,9},{9,8},{10,11... | collective-permute-start | bytes 1056776 | tf_op jit(solution)/shard_map/rhs/ppermute | solution.py:35
  156.8 4.3 %collective-permute-start.27 = (f32[696,128]{1,0:T(8,128)S(1)}, f32[696,128]{1,0:T(8,128)S(1)}, u32[]{:S(2)}, u32[]{:S(2)}) collective-permute-start(f32[696,128]{1,0:T(8,128)S(1)} %get-tuple-element.79), channel_id=1, source_target_pairs={{0,1},{1,0},{2,3},{3,2},{4,5},{5,4},{6,7},{7,6},{8,9},{9,8},{10,11... | collective-permute-start | bytes 1069064 | tf_op jit(solution)/shard_map/first/ppermute | solution.py:35
  189.6 4.4 %collective-permute-start.28 = (f32[696,128]{1,0:T(8,128)S(1)}, f32[696,128]{1,0:T(8,128)S(1)}, u32[]{:S(2)}, u32[]{:S(2)}) collective-permute-start(f32[696,128]{1,0:T(8,128)S(1)} %get-tuple-element.88), channel_id=1, source_target_pairs={{0,1},{1,0},{2,3},{3,2},{4,5},{5,4},{6,7},{7,6},{8,9},{9,8},{10,11... | collective-permute-start | bytes 1069064 | tf_op jit(solution)/shard_map/second/ppermute | solution.py:35
  (2 other events, 15.1 us)
